TPU v7x, 32 devices: a whole 2x2x4 slice. The times are simulated.
32 devices in a mesh: ctx: 16 (over z, x, core), fsdp: 2 (over y).
Axes of the slice: x: 2, y: 2, z: 4, core: 2. Of those that a mesh axis runs over, the one named last changes fastest.
Arguments:
- inputs: float32 [2, 2048, 1024], P('fsdp', 'ctx'), may hold values from -6 to 6
- qkv_weight: bfloat16 [1024, 3072], P('fsdp'), may hold values from -0.1875 to 0.1875
- gate_weight: bfloat16 [1024, 1024], P('fsdp'), may hold values from -0.1875 to 0.1875
- out_weight: bfloat16 [1024, 1024], P('fsdp'), may hold values from -0.75 to 0.75
- up_weight: bfloat16 [1024, 5632], P('fsdp'), may hold values from -0.1875 to 0.1875
- down_weight: bfloat16 [2816, 1024], P('fsdp'), may hold values from -0.109375 to 0.109375
- conv_taps: bfloat16 [4, 3072], P(None, 'fsdp'), may hold values from -3 to 3
- gain_attn: bfloat16 [1024], P('fsdp'), may hold values from 0.5 to 1.5
- gain_ffn: bfloat16 [1024], P('fsdp'), may hold values from 0.5 to 1.5
- ridge_terms: bfloat16 [1024], P('fsdp'), may hold values from 0.099609375 to 1
- forget: float32 [2, 2048, 8], P('fsdp', 'ctx'), may hold values from 0 to 1, as said below
- cotangent: float32 [2, 2048, 1024], P('fsdp', 'ctx'), may hold values from -6 to 6
Outputs:
- output: float32 [2, 2048, 1024], P('fsdp', 'ctx')
- grad_inputs: float32 [2, 2048, 1024], P('fsdp', 'ctx')
- grad_qkv: float32 [1024, 3072], P(('ctx', 'fsdp'))
- grad_gate: float32 [1024, 1024], P(('ctx', 'fsdp'))
- grad_out: float32 [1024, 1024], P(('ctx', 'fsdp'))
- grad_up: float32 [1024, 5632], P(('ctx', 'fsdp'))
- grad_down: float32 [2816, 1024], P(('ctx', 'fsdp'))
- grad_taps: float32 [4, 3072], P(None, ('ctx', 'fsdp'))
- grad_gain_attn: float32 [1024], P(('ctx', 'fsdp'))
- grad_gain_ffn: float32 [1024], P(('ctx', 'fsdp'))
- grad_ridge: float32 [1024], P(('ctx', 'fsdp'))
Inputs may be any that keep to these rules, and one draw needn't show every extreme that they name: forget gates lie strictly between 0 and 1.
All inputs are finite; a program needn't handle non-finite values.
Results may differ from a plain program's by a relative error of at most 0.024.
Values may be sent and summed in bfloat16 or wider, within the bound.
No kernel may reach another device: no remote copies, remote signals or barrier semaphores. Data moves between devices by JAX's collectives and lax.ppermute only.
A program may use at most 576 MiB of HBM per device.

v0:
```python
import jax
import jax.numpy as jnp
from jax import lax
from jax.sharding import PartitionSpec as P

D = 1024
HEADS = 8
FF = 2816
KW = 4
ITERS = 8
HEAD_DIM = 128


highest = lax.Precision.HIGHEST


def shifted(x, axis, by):
    peers = lax.axis_size(axis)
    pairs = [(i, i + by) for i in range(peers) if 0 <= i + by < peers]
    return lax.ppermute(x, axis, pairs)


def entering(x, axis, combine, identity):
    peers, here = (lax.axis_size(axis), lax.axis_index(axis))
    everything = jax.tree.map(
        lambda part, kind: lax.all_gather(part.astype(kind), axis),
        x,
        (jnp.bfloat16, jnp.bfloat16, jnp.bfloat16),
    )
    start = jax.tree.map(
        lambda part, zero: jnp.broadcast_to(jnp.asarray(zero, part.dtype), part.shape), x, identity
    )

    def entering_hop(k, before):
        reached = k < here
        new = combine(
            before, jax.tree.map(lambda part, own: part[k].astype(own.dtype), everything, x)
        )
        return jax.tree.map(lambda a, b: jnp.where(reached, a, b), new, before)

    return lax.fori_loop(0, peers, entering_hop, start)


def carried_in(x, axis, combine, identity):
    peers, here = (lax.axis_size(axis), lax.axis_index(axis))
    everything = jax.tree.map(
        lambda part, kind: lax.all_gather(part.astype(kind), axis),
        x,
        jax.tree.map(lambda a: jnp.bfloat16 if a.dtype == jnp.float32 else a.dtype, x),
    )
    start = jax.tree.map(
        lambda part, zero: jnp.broadcast_to(jnp.asarray(zero, part.dtype), part.shape), x, identity
    )

    def carried_hop(k, before):
        at = peers - 1 - k
        reached = at > here
        new = combine(
            before, jax.tree.map(lambda part, own: part[at].astype(own.dtype), everything, x)
        )
        return jax.tree.map(lambda a, b: jnp.where(reached, a, b), new, before)

    return lax.fori_loop(0, peers, carried_hop, start)


def rms_scale(values, gain):
    return values * lax.rsqrt(jnp.mean(values * values, axis=-1, keepdims=True) + 1e-05) * gain


def unit_rows(values):
    return values * lax.rsqrt(jnp.sum(values * values, axis=-1, keepdims=True) + 1e-06)


def decay_tables(gate_logarithm, strength):
    cumulative = jnp.cumsum(gate_logarithm, axis=-1)
    length_here = gate_logarithm.shape[-1]
    causal = jnp.arange(length_here)[:, None] >= jnp.arange(length_here)[None, :]
    spread = cumulative[..., :, None] - cumulative[..., None, :]
    within = (
        jnp.where(causal, jnp.exp(jnp.where(causal, spread, 0.0)), 0.0) * strength[..., None, :]
    )
    start_decay = jnp.exp(cumulative)
    ending = jnp.exp(cumulative[..., -1:] - cumulative) * strength
    return (within, start_decay, ending, jnp.exp(cumulative[..., -1]))


def block_states(key_rows, value_rows, ending):
    own_key = jnp.einsum("hsi,hsj->hij", key_rows * ending[..., None], key_rows, precision=highest)
    own_value = jnp.einsum(
        "hsi,hsj->hij", value_rows * ending[..., None], key_rows, precision=highest
    )
    return (own_key, own_value)


def solve_heads(
    queries, key_rows, value_rows, state_key, state_value, ridge_heads, within, start_decay
):
    solution = jnp.zeros_like(queries)
    residual = queries
    direction = queries
    norm_now = jnp.sum(residual * residual, axis=-1, keepdims=True)
    for iteration in range(ITERS):
        operator_from_state = start_decay[..., None] * jnp.einsum(
            "htj,hij->hti", direction, state_key, precision=highest
        )
        operator_scores = (
            jnp.einsum("htd,hsd->hts", direction, key_rows, precision=highest) * within
        )
        local_part = jnp.einsum("hts,hsd->htd", operator_scores, key_rows, precision=highest)
        image_rows = operator_from_state + local_part + direction * ridge_heads[:, None, :]
        step_size = norm_now / jnp.sum(direction * image_rows, axis=-1, keepdims=True)
        solution = solution + step_size * direction
        residual = residual - step_size * image_rows
        norm_next = jnp.sum(residual * residual, axis=-1, keepdims=True)
        direction = residual + norm_next / norm_now * direction
        norm_now = norm_next
    from_state = start_decay[..., None] * jnp.einsum(
        "htj,hij->hti", solution, state_value, precision=highest
    )
    scores = jnp.einsum("htd,hsd->hts", solution, key_rows, precision=highest) * within
    return from_state + jnp.einsum("hts,hsd->htd", scores, value_rows, precision=highest)


def combine_states(earlier, later):
    factor = later[2][:, None, None]
    return (factor * earlier[0] + later[0], factor * earlier[1] + later[1], earlier[2] * later[2])


def right_product(left, right):
    return lax.dot_general(
        left, right, (((1,), (1,)), ((), ())), preferred_element_type=jnp.float32
    )


def left_product(left, right):
    return lax.dot_general(
        left, right, (((0,), (0,)), ((), ())), preferred_element_type=jnp.float32
    )


def local(
    inputs,
    qkv_weight,
    gate_weight,
    out_weight,
    up_weight,
    down_weight,
    conv_taps,
    gain_attn,
    gain_ffn,
    ridge_terms,
    forget,
    cotangent,
):
    tokens = inputs[0]
    row_count = tokens.shape[0]
    shards = (
        qkv_weight,
        gate_weight,
        out_weight,
        up_weight,
        down_weight,
        conv_taps,
        gain_attn,
        gain_ffn,
        ridge_terms,
    )
    gathered = (
        lax.all_gather(shards[0], "fsdp", axis=0, tiled=True),
        lax.all_gather(shards[1], "fsdp", axis=0, tiled=True),
        lax.all_gather(shards[2], "fsdp", axis=0, tiled=True),
        lax.all_gather(shards[3], "fsdp", axis=0, tiled=True),
        lax.all_gather(shards[4], "fsdp", axis=0, tiled=True),
        lax.all_gather(shards[5], "fsdp", axis=1, tiled=True),
        lax.all_gather(shards[6], "fsdp", axis=0, tiled=True),
        lax.all_gather(shards[7], "fsdp", axis=0, tiled=True),
        lax.all_gather(shards[8], "fsdp", axis=0, tiled=True),
    )
    qkv_full, gate_full, out_full, up_full, down_full = (
        gathered[0],
        gathered[1],
        gathered[2],
        gathered[3],
        gathered[4],
    )
    taps_float = gathered[5].astype(jnp.float32)
    gain_first = gathered[6].astype(jnp.float32)
    gain_second = gathered[7].astype(jnp.float32)
    ridge_heads = gathered[8].astype(jnp.float32).reshape(HEADS, HEAD_DIM)
    gate_logarithm = jnp.log(forget[0]).T
    strength = (1.0 - forget[0]).T
    within, start_decay, ending, decay_all = decay_tables(gate_logarithm, strength)

    def features(projected, before, taps_here):
        padded = jnp.concatenate([before, projected], axis=0)
        conv_sum = taps_here[0] * padded[0:row_count]
        for offset in range(1, KW):
            conv_sum = conv_sum + taps_here[offset] * padded[offset : offset + row_count]
        activated = jax.nn.silu(conv_sum)
        queries = unit_rows(activated[:, :D].reshape(row_count, HEADS, HEAD_DIM)).transpose(1, 0, 2)
        key_rows = unit_rows(activated[:, D : 2 * D].reshape(row_count, HEADS, HEAD_DIM)).transpose(
            1, 0, 2
        )
        value_rows = activated[:, 2 * D :].reshape(row_count, HEADS, HEAD_DIM).transpose(1, 0, 2)
        own_key, own_value = block_states(key_rows, value_rows, ending)
        return (queries, key_rows, value_rows, own_key, own_value)

    def mixer_core(queries, key_rows, value_rows, state_key, state_value, ridge_here):
        return solve_heads(
            queries, key_rows, value_rows, state_key, state_value, ridge_here, within, start_decay
        )

    identity = (
        jnp.zeros((HEADS, HEAD_DIM, HEAD_DIM), jnp.float32),
        jnp.zeros((HEADS, HEAD_DIM, HEAD_DIM), jnp.float32),
        jnp.ones((HEADS,), jnp.float32),
    )
    normed = rms_scale(tokens, gain_first)
    normed_low = normed.astype(jnp.bfloat16)
    projected = jnp.dot(normed_low, qkv_full, preferred_element_type=jnp.float32)
    tail_rows = projected[row_count - (KW - 1) :]
    before = shifted(tail_rows.astype(jnp.bfloat16), "ctx", 1).astype(tail_rows.dtype)
    queries, key_rows, value_rows, own_key, own_value = features(projected, before, taps_float)
    scanned = entering((own_key, own_value, decay_all), "ctx", combine_states, identity)
    state_key, state_value = (scanned[0], scanned[1])
    attended_heads = mixer_core(queries, key_rows, value_rows, state_key, state_value, ridge_heads)
    attended = attended_heads.transpose(1, 0, 2).reshape(row_count, D)
    gate_logit = jnp.dot(normed_low, gate_full, preferred_element_type=jnp.float32)
    gate_sig = jax.nn.sigmoid(gate_logit)
    gated_mix = (attended * gate_sig).astype(jnp.bfloat16)
    hidden = tokens + jnp.dot(gated_mix, out_full, preferred_element_type=jnp.float32)
    normed_ffn = rms_scale(hidden, gain_second)
    normed_ffn_low = normed_ffn.astype(jnp.bfloat16)
    gate_up = jnp.dot(normed_ffn_low, up_full, preferred_element_type=jnp.float32)
    gate_part = gate_up[:, :FF]
    up_part = gate_up[:, FF:]
    inner = (jax.nn.silu(gate_part) * up_part).astype(jnp.bfloat16)
    output = hidden + jnp.dot(inner, down_full, preferred_element_type=jnp.float32)
    grad_output = cotangent[0]
    grad_branch = grad_output.astype(jnp.bfloat16)
    grad_inner = right_product(grad_branch, down_full)
    grad_down_full = left_product(inner, grad_branch)
    gate_sigmoid = jax.nn.sigmoid(gate_part)
    grad_gate_part = grad_inner * up_part * gate_sigmoid * (1.0 + gate_part * (1.0 - gate_sigmoid))
    grad_up_part = grad_inner * gate_part * gate_sigmoid
    grad_gate_up = jnp.concatenate([grad_gate_part, grad_up_part], axis=1).astype(jnp.bfloat16)
    grad_up_full = left_product(normed_ffn_low, grad_gate_up)
    grad_normed_ffn = right_product(grad_gate_up, up_full)
    second_value, second_pull = jax.vjp(rms_scale, hidden, gain_second)
    grad_hidden_norm, grad_second_gain = second_pull(grad_normed_ffn)
    grad_hidden = grad_output + grad_hidden_norm
    grad_attn_branch = grad_hidden.astype(jnp.bfloat16)
    grad_mixed = right_product(grad_attn_branch, out_full)
    grad_out_full = left_product(gated_mix, grad_attn_branch)
    grad_attended = grad_mixed * gate_sig
    grad_logit = (grad_mixed * attended * gate_sig * (1.0 - gate_sig)).astype(jnp.bfloat16)
    grad_gate_full = left_product(normed_low, grad_logit)
    grad_normed = right_product(grad_logit, gate_full)
    rescanned = entering((own_key, own_value, decay_all), "ctx", combine_states, identity)
    state_key, state_value = (rescanned[0], rescanned[1])
    core_value, core_pull = jax.vjp(
        mixer_core, queries, key_rows, value_rows, state_key, state_value, ridge_heads
    )
    grad_heads = grad_attended.reshape(row_count, HEADS, HEAD_DIM).transpose(1, 0, 2)
    core_grads = core_pull(grad_heads)
    returned = carried_in(
        (core_grads[3], core_grads[4], decay_all), "ctx", combine_states, identity
    )
    feature_value, feature_pull = jax.vjp(features, projected, before, taps_float)
    grad_projected, grad_before, grad_taps_full = feature_pull(
        (core_grads[0], core_grads[1], core_grads[2], returned[0], returned[1])
    )
    from_next = shifted(grad_before.astype(jnp.bfloat16), "ctx", -1).astype(grad_before.dtype)
    padding = jnp.zeros((row_count - (KW - 1), 3 * D), jnp.float32)
    grad_projected = grad_projected + jnp.concatenate([padding, from_next], axis=0)
    grad_projected_low = grad_projected.astype(jnp.bfloat16)
    grad_qkv_full = left_product(normed_low, grad_projected_low)
    grad_normed = grad_normed + right_product(grad_projected_low, qkv_full)
    first_value, first_pull = jax.vjp(rms_scale, tokens, gain_first)
    grad_tokens_norm, grad_first_gain = first_pull(grad_normed)
    grad_tokens = grad_hidden + grad_tokens_norm
    totals = (
        grad_qkv_full,
        grad_gate_full,
        grad_out_full,
        grad_up_full,
        grad_down_full,
        grad_taps_full.T,
        grad_first_gain,
        grad_second_gain,
        core_grads[5].reshape(D),
    )
    owned = (
        lax.psum_scatter(totals[0], ("ctx", "fsdp"), scatter_dimension=0, tiled=True),
        lax.psum_scatter(totals[1], ("ctx", "fsdp"), scatter_dimension=0, tiled=True),
        lax.psum_scatter(totals[2], ("ctx", "fsdp"), scatter_dimension=0, tiled=True),
        lax.psum_scatter(totals[3], ("ctx", "fsdp"), scatter_dimension=0, tiled=True),
        lax.psum_scatter(totals[4], ("ctx", "fsdp"), scatter_dimension=0, tiled=True),
        lax.psum_scatter(totals[5], ("ctx", "fsdp"), scatter_dimension=0, tiled=True),
        lax.psum_scatter(totals[6], ("ctx", "fsdp"), scatter_dimension=0, tiled=True),
        lax.psum_scatter(totals[7], ("ctx", "fsdp"), scatter_dimension=0, tiled=True),
        lax.psum_scatter(totals[8], ("ctx", "fsdp"), scatter_dimension=0, tiled=True),
    )
    return (
        output[None],
        grad_tokens[None],
        owned[0],
        owned[1],
        owned[2],
        owned[3],
        owned[4],
        owned[5].T,
        owned[6],
        owned[7],
        owned[8],
    )


def solution(mesh):
    return jax.shard_map(
        local,
        mesh=mesh,
        in_specs=(
            P("fsdp", "ctx", None),
            P("fsdp", None),
            P("fsdp", None),
            P("fsdp", None),
            P("fsdp", None),
            P("fsdp", None),
            P(None, "fsdp"),
            P("fsdp"),
            P("fsdp"),
            P("fsdp"),
            P("fsdp", "ctx", None),
            P("fsdp", "ctx", None),
        ),
        out_specs=(
            P("fsdp", "ctx", None),
            P("fsdp", "ctx", None),
            P(("ctx", "fsdp"), None),
            P(("ctx", "fsdp"), None),
            P(("ctx", "fsdp"), None),
            P(("ctx", "fsdp"), None),
            P(("ctx", "fsdp"), None),
            P(None, ("ctx", "fsdp")),
            P(("ctx", "fsdp")),
            P(("ctx", "fsdp")),
            P(("ctx", "fsdp")),
        ),
        check_vma=False,
    )
```

profile of v0, /device:TPU:0, one launch (start us, length us, event | category | flops | bytes accessed | tf_op | source)
XLA Modules:
  0.0 2016.9 jit_solution(7584096173320419008)
XLA Ops:
  8.0 5.3 all-gather.5
  13.6 4.4 all_gather.63
  19.1 73.6 %all-gather.18.cloned.1.call-done = bf16[1024,3072]{1,0:T(8,128)(2,1)} async-done(((bf16[512,3072]{1,0:T(8,128)(2,1)}), bf16[1024,3072]{1,0:T(8,128)(2,1)}) %all-gather.18.cloned.1.call-update) | async-done | bytes 6291472 | tf_op jit(solution)/shard_map/all_gather | solution.py:169
  92.7 3.8 fusion.298
  99.1 2.1 fusion.13
  102.0 1.9 convolution_convert_fusion.2
  104.2 1.9 convolution_convert_fusion.1
  109.0 4.3 all-gather.6
  114.9 33.4 %all-reduce.12 = bf16[128]{0:T(256)(128)(2,1)S(1)} all-reduce(bf16[128]{0:T(256)(128)(2,1)S(1)} %dynamic-update-slice), channel_id=2, replica_groups=mesh['ctx'=16,'fsdp'=2] {'ctx'}, use_global_device_ids=true, to_apply=%add.12 | all-reduce | flops 128 | bytes 512
  148.4 4.3 all-gather.7
  154.5 2.6 all-gather.28.cloned.1.call-done
  157.1 52.3 %all-gather.30.cloned.1.call-done = bf16[128,128,128]{2,1,0:T(8,128)(2,1)} async-done(((bf16[8,128,128]{2,1,0:T(8,128)(2,1)}), bf16[128,128,128]{2,1,0:T(8,128)(2,1)}) %all-gather.30.cloned.1.call-update) | async-done | bytes 4194320 | tf_op jit(solution)/shard_map/all_gather | solution.py:26
  209.4 22.9 %while.40 = (s32[]{:T(128)}, f32[8,128,128]{2,1,0:T(8,128)S(1)}, f32[8,128,128]{2,1,0:T(8,128)S(1)}, s32[]{:T(128)}, bf16[16,8]{1,0:T(8,128)(2,1)S(1)}, /*index=...) while((s32[]{:T(128)}, f32[8,128,128]{2,1,0:T(8,128)S(1)}, ...), condition=%wide.region_6.7_spmd.clone, body=%wide.region_5.6_spmd.clone.sunk | while | flops 1310732 | bytes 2621649 | solution.py:41
  233.0 2.1 fusion.142
  237.0 2.1 multiply_reduce_fusion.48
  241.6 2.1 multiply_reduce_fusion.46
  246.3 2.1 multiply_reduce_fusion.44
  251.2 2.1 multiply_reduce_fusion.42
  255.9 2.1 multiply_reduce_fusion.40
  260.6 2.1 multiply_reduce_fusion.38
  265.3 2.1 multiply_reduce_fusion.36
  271.3 2.0 fusion.28
  273.3 2.0 copy.437
  275.3 3.0 multiply_convert_fusion.5
  278.4 3.0 multiply_reduce_fusion.35
  282.4 137.0 %all-gather.24.cloned.1.call-done = bf16[1024,5632]{1,0:T(8,128)(2,1)} async-done(((bf16[512,5632]{1,0:T(8,128)(2,1)}), bf16[1024,5632]{1,0:T(8,128)(2,1)}) %all-gather.24.cloned.1.call-update) | async-done | bytes 11534352 | tf_op jit(solution)/shard_map/all_gather | solution.py:172
  419.4 7.8 fusion.283
  427.2 68.2 %all-gather.26.cloned.1.call-done = bf16[2816,1024]{1,0:T(8,128)(2,1)} async-done(((bf16[1408,1024]{1,0:T(8,128)(2,1)}), bf16[2816,1024]{1,0:T(8,128)(2,1)}) %all-gather.26.cloned.1.call-update) | async-done | bytes 5767184 | tf_op jit(solution)/shard_map/all_gather | solution.py:173
  495.5 6.9 multiply_convert_fusion.1
  502.5 5.2 multiply_reduce_fusion.10
  509.5 2.8 fusion.291
  512.3 2.0 copy.439
  514.4 2.4 convolution_multiply_fusion.8
  522.9 2.8 multiply_reduce_fusion.30
  531.0 1.9 multiply_reduce_fusion.27
  537.8 1.9 multiply_reduce_fusion.24
  544.8 1.9 multiply_reduce_fusion.21
  552.0 1.9 multiply_reduce_fusion.18
  558.8 2.0 multiply_reduce_fusion.15
  565.6 2.4 fusion.151
  577.0 1.9 fusion.31
  579.0 3.1 convolution_convert_fusion
  585.3 2.1 convolution_multiply_fusion
  587.6 8.1 fusion.23
  597.7 2.1 copy.581
  621.1 8.6 all-gather.32.cloned.1.call-done
  629.7 51.3 %all-gather.34.cloned.1.call-done = bf16[128,128,128]{2,1,0:T(8,128)(2,1)} async-done(((bf16[8,128,128]{2,1,0:T(8,128)(2,1)}), bf16[128,128,128]{2,1,0:T(8,128)(2,1)}) %all-gather.34.cloned.1.call-update) | async-done | bytes 4194320 | tf_op jit(solution)/shard_map/all_gather | solution.py:47
  680.9 33.2 %while.41 = (s32[]{:T(128)}, f32[8,128,128]{2,1,0:T(8,128)S(1)}, f32[8,128,128]{2,1,0:T(8,128)S(1)}, s32[]{:T(128)}, bf16[16,8]{1,0:T(8,128)(2,1)}, /*index=5*/b...) while((s32[]{:T(128)}, f32[8,128,128]{2,1,0:T(8,128)S(1)}, ...), condition=%wide.region_47.48_spmd.clone, body=%wide.region_46.47_spmd.clone.sunk | while | flops 1310736 | bytes 2621711 | solution.py:63
  718.7 2.6 fusion.27
  722.6 3.5 multiply_reduce_fusion.2
  727.9 2.8 fusion.308
  731.9 2.7 fusion.209
  735.9 5.9 fusion.294
  747.7 6.4 fusion.213
  755.2 10.9 fusion.32
  766.8 2.4 fusion.306
  769.3 4.6 fusion.30
  773.9 5.2 multiply_reduce_fusion.11
  779.2 41.2 %all-reduce.16 = (f32[1024]{0:T(1024)S(1)}, f32[1024]{0:T(1024)S(1)}, f32[1024]{0:T(1024)S(1)}) all-reduce(f32[1024]{0:T(1024)S(1)} %get-tuple-element.387, f32[1024]{0:T(1024)S(1)} %copy-done.213, f32[1024]{0:T(1024)S(1)} %add_bitcast_fusion.1), channel_id=13, replica_groups=mesh['ctx'=16,'fsdp'=2] {'ctx','fsdp'}, use_global_device_ids=true, to_apply=%region_62.63.clone | all-reduce | flops 3072 | bytes 24576
  825.0 142.2 %reduce-scatter.11.cloned.1.call-done = f32[32,1024]{1,0:T(8,128)} async-done(((f32[1024,1024]{1,0:T(8,128)}), f32[32,1024]{1,0:T(8,128)}) %reduce-scatter.11.cloned.1.call-update) | async-done | bytes 131088 | tf_op jit(solution)/shard_map/reduce_scatter | solution.py:295
  967.2 141.2 %reduce-scatter.13.cloned.1.call-done = f32[32,1024]{1,0:T(8,128)} async-done(((f32[1024,1024]{1,0:T(8,128)}), f32[32,1024]{1,0:T(8,128)}) %reduce-scatter.13.cloned.1.call-update) | async-done | bytes 131088 | tf_op jit(solution)/shard_map/reduce_scatter | solution.py:296
  1108.4 248.4 %reduce-scatter.17.cloned.1.call-done = f32[88,1024]{1,0:T(8,128)} async-done(((f32[2816,1024]{1,0:T(8,128)}), f32[88,1024]{1,0:T(8,128)}) %reduce-scatter.17.cloned.1.call-update) | async-done | bytes 360464 | tf_op jit(solution)/shard_map/reduce_scatter | solution.py:298
  1356.8 163.0 %reduce-scatter.9.cloned.1.call-done = f32[32,3072]{1,0:T(8,128)} async-done(((f32[1024,3072]{1,0:T(8,128)}), f32[32,3072]{1,0:T(8,128)}) %reduce-scatter.9.cloned.1.call-update) | async-done | bytes 393232 | tf_op jit(solution)/shard_map/reduce_scatter | solution.py:294
  1519.8 490.0 %reduce-scatter.15.cloned.1.call-done = f32[32,5632]{1,0:T(8,128)} async-done(((f32[1024,5632]{1,0:T(8,128)}), f32[32,5632]{1,0:T(8,128)}) %reduce-scatter.15.cloned.1.call-update) | async-done | bytes 720912 | tf_op jit(solution)/shard_map/reduce_scatter | solution.py:297
  (777 shorter events, 183.4 us)
Async XLA Ops:
  7.2 6.4 copy-start.224
  7.2 11.0 copy-start.37
  7.2 85.5 %all-gather.18.cloned.1.call-start = ((), (), s32[]{:S(2)}) async-start(), calls=%async_computation.6 | async-start | bytes 9437184 | tf_op jit(solution)/shard_map/all_gather | solution.py:169
  8.0 149.1 %all-gather.28.cloned.1.call-start = ((), (), s32[]{:S(2)}) async-start(), calls=%async_computation.16 | async-start | bytes 4456448 | tf_op jit(solution)/shard_map/all_gather | solution.py:26
  18.2 80.1 %copy-start.225 = (f32[8]{0:T(128)}, f32[8]{0:T(128)S(1)}, u32[]{:S(2)}) copy-start(f32[8]{0:T(128)S(1)} %slice_reduce_fusion) | copy-start | bytes 100
  19.1 80.0 %copy-start.145 = (f32[1,3072]{1,0:T(1,128)}, f32[1,3072]{1,0:T(1,128)S(1)}, u32[]{:S(2)}) copy-start(f32[1,3072]{1,0:T(1,128)S(1)} %get-tuple-element.525) | copy-start | bytes 36868
  19.1 80.0 %copy-start.147 = (f32[1,3072]{1,0:T(1,128)}, f32[1,3072]{1,0:T(1,128)S(1)}, u32[]{:S(2)}) copy-start(f32[1,3072]{1,0:T(1,128)S(1)} %get-tuple-element.526) | copy-start | bytes 36868
  19.1 80.0 %copy-start.149 = (f32[1,3072]{1,0:T(1,128)}, f32[1,3072]{1,0:T(1,128)S(1)}, u32[]{:S(2)}) copy-start(f32[1,3072]{1,0:T(1,128)S(1)} %get-tuple-element.527) | copy-start | bytes 36868
  19.1 80.0 %copy-start.151 = (f32[1,3072]{1,0:T(1,128)}, f32[1,3072]{1,0:T(1,128)S(1)}, u32[]{:S(2)}) copy-start(f32[1,3072]{1,0:T(1,128)S(1)} %get-tuple-element.528) | copy-start | bytes 36868
  96.5 2.6 collective-permute-start
  104.0 105.4 %all-gather.30.cloned.1.call-start = ((), (), s32[]{:S(2)}) async-start(), calls=%async_computation.17 | async-start | bytes 4456448 | tf_op jit(solution)/shard_map/all_gather | solution.py:26
  106.2 169.2 %all-gather.20.cloned.1.call-start = ((), (), s32[]{:S(2)}) async-start(), calls=%async_computation.7 | async-start | bytes 3145728 | tf_op jit(solution)/shard_map/all_gather | solution.py:170
  106.7 171.6 %all-gather.22.cloned.1.call-start = ((), (), s32[]{:S(2)}) async-start(), calls=%async_computation.8 | async-start | bytes 3145728 | tf_op jit(solution)/shard_map/all_gather | solution.py:171
  107.3 312.1 %all-gather.24.cloned.1.call-start = ((), (), s32[]{:S(2)}) async-start(), calls=%async_computation.9 | async-start | bytes 17301504 | tf_op jit(solution)/shard_map/all_gather | solution.py:172
  107.9 40.4 %copy-start.237 = (bf16[512]{0:T(512)(128)(2,1)S(1)}, bf16[512]{0:T(512)(128)(2,1)}, u32[]{:S(2)}) copy-start(bf16[512]{0:T(512)(128)(2,1)} %param.24) | copy-start | bytes 3076
  108.0 387.5 %all-gather.26.cloned.1.call-start = ((), (), s32[]{:S(2)}) async-start(), calls=%async_computation.10 | async-start | bytes 8650752 | tf_op jit(solution)/shard_map/all_gather | solution.py:173
  108.7 521.0 %all-gather.32.cloned.1.call-start = ((), (), s32[]{:S(2)}) async-start(), calls=%async_computation.18 | async-start | bytes 4456448 | tf_op jit(solution)/shard_map/all_gather | solution.py:47
  153.3 56.0 %copy-start.193 = (f32[128,8]{0,1:T(8,128)}, f32[128,8]{0,1:T(8,128)S(1)}, u32[]{:S(2)}) copy-start(f32[128,8]{0,1:T(8,128)S(1)} %copy.403) | copy-start | bytes 12292
  154.5 78.5 %copy-start.96 = (f32[8,128,128]{2,1,0:T(8,128)}, f32[8,128,128]{2,1,0:T(8,128)S(1)}, u32[]{:S(2)}) copy-start(f32[8,128,128]{2,1,0:T(8,128)S(1)} %convolution_multiply_fusion.17) | copy-start | bytes 1572868
  239.1 28.8 %copy-start.160 = (f32[8,128]{1,0:T(8,128)}, f32[8,128]{1,0:T(8,128)S(1)}, u32[]{:S(2)}) copy-start(f32[8,128]{1,0:T(8,128)S(1)} %div.502) | copy-start | bytes 12292
  243.7 24.3 %copy-start.162 = (f32[8,128]{1,0:T(8,128)}, f32[8,128]{1,0:T(8,128)S(1)}, u32[]{:S(2)}) copy-start(f32[8,128]{1,0:T(8,128)S(1)} %div.504) | copy-start | bytes 12292
  244.5 23.4 %copy-start.1 = (f32[8,128,128]{1,2,0:T(8,128)}, f32[8,128,128]{1,2,0:T(8,128)S(1)}, u32[]{:S(2)}) copy-start(f32[8,128,128]{1,2,0:T(8,128)S(1)} %multiply_add_fusion.17) | copy-start | bytes 1572868
  249.0 19.0 copy-start.164
  249.2 18.8 copy-start.4
  253.3 14.7 copy-start.166
  254.1 13.9 copy-start.7
  258.0 10.0 copy-start.168
  258.8 9.2 copy-start.10
  495.5 6.9 copy-start
  495.5 7.0 copy-start.20
  495.5 7.0 copy-start.211
  502.5 6.7 copy-start.118
  519.0 6.7 copy-start.176
  519.0 49.0 %copy-start.13 = (f32[8,128,128]{1,2,0:T(8,128)}, f32[8,128,128]{1,2,0:T(8,128)S(1)}, u32[]{:S(2)}) copy-start(f32[8,128,128]{1,2,0:T(8,128)S(1)} %get-tuple-element.574) | copy-start | bytes 1572868
  525.7 7.2 copy-start.183
  527.8 41.8 %copy-start.49 = (f32[8,128,128]{1,2,0:T(8,128)}, f32[8,128,128]{1,2,0:T(8,128)S(1)}, u32[]{:S(2)}) copy-start(f32[8,128,128]{1,2,0:T(8,128)S(1)} %get-tuple-element.437) | copy-start | bytes 1572868
  532.9 6.8 copy-start.184
  534.6 36.2 %copy-start.39 = (f32[8,128,128]{1,2,0:T(8,128)}, f32[8,128,128]{1,2,0:T(8,128)S(1)}, u32[]{:S(2)}) copy-start(f32[8,128,128]{1,2,0:T(8,128)S(1)} %get-tuple-element.439) | copy-start | bytes 1572868
  539.7 7.0 copy-start.185
  540.5 6.2 copy-start.179
  541.4 30.7 %copy-start.41 = (f32[8,128,128]{1,2,0:T(8,128)}, f32[8,128,128]{1,2,0:T(8,128)S(1)}, u32[]{:S(2)}) copy-start(f32[8,128,128]{1,2,0:T(8,128)S(1)} %get-tuple-element.441) | copy-start | bytes 1572868
  546.7 7.2 copy-start.159
  548.9 24.4 %copy-start.43 = (f32[8,128,128]{1,2,0:T(8,128)}, f32[8,128,128]{1,2,0:T(8,128)S(1)}, u32[]{:S(2)}) copy-start(f32[8,128,128]{1,2,0:T(8,128)S(1)} %get-tuple-element.443) | copy-start | bytes 1572868
  554.0 6.8 copy-start.186
  555.6 18.9 copy-start.45
  560.8 7.2 copy-start.187
  561.6 6.4 copy-start.182
  562.5 13.3 copy-start.47
  569.6 7.4 copy-start.28
  577.0 6.8 copy-start.142
  579.0 102.0 %all-gather.34.cloned.1.call-start = ((), (), s32[]{:S(2)}) async-start(), calls=%async_computation.19 | async-start | bytes 4456448 | tf_op jit(solution)/shard_map/all_gather | solution.py:47
  582.1 241.5 %reduce-scatter.19.cloned.1.call-start = ((), (), s32[]{:S(2)}) async-start(), calls=%async_computation.20 | async-start | bytes 1622016
  587.5 8.2 copy-start.128
  587.6 8.1 copy-start.29
  619.4 61.5 %copy-start.15 = (f32[8,128,128]{2,1,0:T(8,128)S(1)}, f32[8,128,128]{2,1,0:T(8,128)}, u32[]{:S(2)}) copy-start(f32[8,128,128]{2,1,0:T(8,128)} %custom-call.2) | copy-start | bytes 1572868
  619.4 61.5 %copy-start.16 = (f32[8,128,128]{2,1,0:T(8,128)S(1)}, f32[8,128,128]{2,1,0:T(8,128)}, u32[]{:S(2)}) copy-start(f32[8,128,128]{2,1,0:T(8,128)} %custom-call.3) | copy-start | bytes 1572868
  680.9 33.3 %copy-start.154 = (f32[8,128]{1,0:T(8,128)S(1)}, f32[8,128]{1,0:T(8,128)}, u32[]{:S(2)}) copy-start(f32[8,128]{1,0:T(8,128)} %copy-done.153) | copy-start | bytes 12292
  727.9 239.3 %reduce-scatter.11.cloned.1.call-start = ((), (), s32[]{:S(2)}) async-start(), calls=%async_computation.12 | async-start | bytes 4325376 | tf_op jit(solution)/shard_map/reduce_scatter | solution.py:295
  730.8 377.6 %reduce-scatter.13.cloned.1.call-start = ((), (), s32[]{:S(2)}) async-start(), calls=%async_computation.13 | async-start | bytes 4325376 | tf_op jit(solution)/shard_map/reduce_scatter | solution.py:296
  734.6 622.2 %reduce-scatter.17.cloned.1.call-start = ((), (), s32[]{:S(2)}) async-start(), calls=%async_computation.15 | async-start | bytes 11894784 | tf_op jit(solution)/shard_map/reduce_scatter | solution.py:298
  741.8 778.0 %reduce-scatter.9.cloned.1.call-start = ((), (), s32[]{:S(2)}) async-start(), calls=%async_computation.11 | async-start | bytes 12976128 | tf_op jit(solution)/shard_map/reduce_scatter | solution.py:294
  744.6 3.1 collective-permute-start.1
  754.2 1255.7 %reduce-scatter.15.cloned.1.call-start = ((), (), s32[]{:S(2)}) async-start(), calls=%async_computation.14 | async-start | bytes 23789568 | tf_op jit(solution)/shard_map/reduce_scatter | solution.py:297
  773.9 48.2 %copy-start.239 = (f32[128]{0:T(128)S(1)}, f32[128]{0:T(128)}, u32[]{:S(2)}) copy-start(f32[128]{0:T(128)} %copy-done.238) | copy-start | bytes 1540
  (196 other events, 449.7 us)
Sparse Core Ops, SparseCore 0:
  9.6 83.0 all-gather.17
  104.1 52.9 all-gather.27
  159.8 49.5 all-gather.29
  210.8 31.6 all-gather.19
  243.8 33.1 all-gather.21
  278.4 141.0 all-gather.23
  421.0 74.4 all-gather.25
  579.1 50.5 all-gather.31
  631.8 49.0 all-gather.33
  728.0 95.5 reduce-scatter.18
  826.4 140.7 reduce-scatter.10
  969.9 138.4 reduce-scatter.12
  1111.3 245.4 reduce-scatter.16
  1363.3 156.5 reduce-scatter.8
  1522.7 487.1 reduce-scatter.14
where the time goes:
time: 2030 us; the launch traced here: 2020 us
  waiting for transfers between devices  1580 us (78%)
  matrix products  192 us (9%)
  blocking collectives  92.9 us (5%)
  other arithmetic  83.6 us (4%)
  local copies, waits for them, and re-layouts  41.1 us (2%)
    reduce_scatter x1, waiting for transfers between devices, local(): lax.psum_scatter(totals[3], ('ctx', 'fsdp'), scatter_dimension=0, tiled=T...  490 us
    reduce_scatter x1, waiting for transfers between devices, local(): lax.psum_scatter(totals[4], ('ctx', 'fsdp'), scatter_dimension=0, tiled=T...  248 us
    reduce_scatter x1, waiting for transfers between devices, local(): lax.psum_scatter(totals[0], ('ctx', 'fsdp'), scatter_dimension=0, tiled=T...  163 us
    reduce_scatter x1, waiting for transfers between devices, local(): lax.psum_scatter(totals[1], ('ctx', 'fsdp'), scatter_dimension=0, tiled=T...  142 us
    reduce_scatter x1, waiting for transfers between devices, local(): lax.psum_scatter(totals[2], ('ctx', 'fsdp'), scatter_dimension=0, tiled=T...  141 us
    all_gather x1, waiting for transfers between devices, local(): lax.all_gather(shards[3], 'fsdp', axis=0, tiled=True)  137 us
    unnamed x2, blocking collectives  74.6 us
    all_gather x1, waiting for transfers between devices, local(): lax.all_gather(shards[0], 'fsdp', axis=0, tiled=True)  73.6 us
  transfers between devices with their start and end apart: 17, of which 15 were waited for; matrix products, arithmetic and copies ran while one was open for 8% of the time, Pallas kernels for 0%

commit v1 on v0

v1 whole, which is shorter than its diff:
```python
import functools
import jax
import jax.numpy as jnp
from jax import lax
from jax.experimental import pallas as pl
from jax.experimental.pallas import tpu as pltpu
from jax.sharding import PartitionSpec as P

D = 1024
HEADS = 8
FF = 2816
KW = 4
ITERS = 8
HEAD_DIM = 128
GROUP = 4

f32 = jnp.float32
bf16 = jnp.bfloat16
VMEM_LIMIT = 56 * 1024 * 1024


def nn(a, b):
    return lax.dot_general(a, b, (((1,), (0,)), ((), ())), preferred_element_type=f32)


def nt(a, b):
    return lax.dot_general(a, b, (((1,), (1,)), ((), ())), preferred_element_type=f32)


def tn(a, b):
    return lax.dot_general(a, b, (((0,), (0,)), ((), ())), preferred_element_type=f32)


def column(row, like):
    return jnp.broadcast_to(row, like).T


def decay_mask(c, b, tokens):
    shape = (tokens, tokens)
    late = lax.broadcasted_iota(jnp.int32, shape, 1) >= lax.broadcasted_iota(jnp.int32, shape, 0)
    spread = jnp.broadcast_to(c, shape) - column(c, shape)
    return jnp.where(late, jnp.exp(jnp.where(late, spread, 0.0)), 0.0) * column(b, shape)


def conv_parts(proj, halo, taps):
    padded = jnp.concatenate([halo, proj], axis=0)
    rows = proj.shape[0]
    shifted = [padded[8 - KW + 1 + j : 8 - KW + 1 + j + rows] for j in range(KW)]
    total = taps[0:1] * shifted[0]
    for j in range(1, KW):
        total = total + taps[j : j + 1] * shifted[j]
    return total, shifted


def features_kernel(pq, pk, pv, hq, hk, hv, tq, tk, tv, c_ref, b_ref, q_out, k_out, v_out, st_out):
    head = pl.program_id(0)
    tokens = pq.shape[0]
    shape = (tokens, HEAD_DIM)

    def activated(p, h, t):
        total, _ = conv_parts(p[...], h[...], t[...])
        return total * jax.nn.sigmoid(total)

    def unit(a):
        return a * lax.rsqrt(jnp.sum(a * a, axis=-1, keepdims=True) + 1e-06)

    c = c_ref[pl.ds(head, 1), :]
    b = b_ref[pl.ds(head, 1), :]
    ending = column(jnp.exp(c[:, tokens - 1 :] - c) * b, (HEAD_DIM, tokens))
    q = unit(activated(pq, hq, tq))
    k = unit(activated(pk, hk, tk))
    v = activated(pv, hv, tv)
    k_low = k.astype(bf16)
    q_out[0] = q.T
    k_out[0] = k_low
    v_out[0] = v.astype(bf16)
    st_out[0, 0] = tn((k * ending).astype(bf16), k_low).astype(bf16)
    st_out[0, 1] = tn((v * ending).astype(bf16), k_low).astype(bf16)


def thirds(rows):
    return [pl.BlockSpec((rows, HEAD_DIM), lambda h, i=i: (0, i * HEADS + h)) for i in range(3)]


def whole(*shape):
    return pl.BlockSpec(shape, lambda h: (0,) * len(shape))


def per_head(*shape):
    return pl.BlockSpec((1,) + shape, lambda h: (h,) + (0,) * len(shape))


def features(proj, halo, taps, c, b):
    tokens = proj.shape[0]
    square = (HEADS, HEAD_DIM, tokens)
    return pl.pallas_call(
        features_kernel,
        grid=(HEADS,),
        in_specs=thirds(tokens) + thirds(8) + thirds(KW) + [whole(HEADS, tokens)] * 2,
        out_specs=[
            per_head(HEAD_DIM, tokens),
            per_head(tokens, HEAD_DIM),
            per_head(tokens, HEAD_DIM),
            per_head(2, HEAD_DIM, HEAD_DIM),
        ],
        out_shape=[
            jax.ShapeDtypeStruct(square, f32),
            jax.ShapeDtypeStruct((HEADS, tokens, HEAD_DIM), bf16),
            jax.ShapeDtypeStruct((HEADS, tokens, HEAD_DIM), bf16),
            jax.ShapeDtypeStruct((HEADS, 2, HEAD_DIM, HEAD_DIM), bf16),
        ],
        cost_estimate=pl.CostEstimate(flops=70_000_000, bytes_accessed=4_000_000, transcendentals=400_000),
        name="features",
    )(proj, proj, proj, halo, halo, halo, taps, taps, taps, c, b)


def solve_kernel(
    q_ref, k_ref, v_ref, st_ref, c_ref, b_ref, ridge_ref,
    att_ref, x_out, p_out, m_out, scal_out,
    left, kt, mask, decay, ridge, x_s, r_s, p_s,
):
    group = pl.program_id(0)
    tokens = q_ref.shape[2]
    shape = (HEAD_DIM, tokens)
    first = []
    for h in range(GROUP):
        c = c_ref[pl.ds(group * GROUP + h, 1), :]
        b = b_ref[pl.ds(group * GROUP + h, 1), :]
        left[h, :HEAD_DIM] = st_ref[h, 0]
        left[h, HEAD_DIM:] = k_ref[h]
        kt[h] = k_ref[h].T
        mask[h] = decay_mask(c, b, tokens)
        decay[h] = jnp.broadcast_to(jnp.exp(c), (8, tokens))
        ridge[h] = column(ridge_ref[pl.ds(group * GROUP + h, 1), :], (tokens, HEAD_DIM))
        q = q_ref[h]
        x_s[h] = jnp.zeros(shape, f32)
        r_s[h] = q
        p_s[h] = q
        first.append(jnp.sum(q * q, axis=0, keepdims=True))

    def step(i, norms):
        after = []
        for h in range(GROUP):
            p = p_s[h]
            p_low = p.astype(bf16)
            both = nn(left[h], p_low)
            scores = (both[HEAD_DIM:] * mask[h]).astype(bf16)
            image = decay[h, 0:1] * both[:HEAD_DIM] + nn(kt[h], scores) + ridge[h] * p
            dot = jnp.sum(p * image, axis=0, keepdims=True)
            size = norms[h] / dot
            p_out[i, h] = p
            m_out[i, h] = image
            scal_out[h, pl.ds(i, 1)] = norms[h]
            scal_out[h, pl.ds(ITERS + i, 1)] = dot
            x_s[h] = x_s[h] + size * p
            r = r_s[h] - size * image
            r_s[h] = r
            norm = jnp.sum(r * r, axis=0, keepdims=True)
            p_s[h] = r + (norm / norms[h]) * p
            after.append(norm)
        return tuple(after)

    lax.fori_loop(0, ITERS, step, tuple(first))
    for h in range(GROUP):
        x_low = x_s[h].astype(bf16)
        x_out[h] = x_low
        scores = (nn(k_ref[h], x_low) * mask[h]).astype(bf16)
        out = decay[h, 0:1] * nn(st_ref[h, 1], x_low) + tn(v_ref[h], scores)
        att_ref[:, h * HEAD_DIM : (h + 1) * HEAD_DIM] = out.T


def grouped(*shape):
    return pl.BlockSpec((GROUP,) + shape, lambda g: (g,) + (0,) * len(shape))


def solve(q, k, v, states, c, b, ridge):
    tokens = q.shape[2]
    steps = pl.BlockSpec((ITERS, GROUP, HEAD_DIM, tokens), lambda g: (0, g, 0, 0))
    square = pltpu.VMEM((GROUP, HEAD_DIM, tokens), f32)
    return pl.pallas_call(
        solve_kernel,
        grid=(HEADS // GROUP,),
        in_specs=[
            grouped(HEAD_DIM, tokens),
            grouped(tokens, HEAD_DIM),
            grouped(tokens, HEAD_DIM),
            grouped(2, HEAD_DIM, HEAD_DIM),
            whole(HEADS, tokens),
            whole(HEADS, tokens),
            whole(HEADS, HEAD_DIM),
        ],
        out_specs=[
            pl.BlockSpec((tokens, GROUP * HEAD_DIM), lambda g: (0, g)),
            grouped(HEAD_DIM, tokens),
            steps,
            steps,
            grouped(2 * ITERS, tokens),
        ],
        out_shape=[
            jax.ShapeDtypeStruct((tokens, D), f32),
            jax.ShapeDtypeStruct((HEADS, HEAD_DIM, tokens), bf16),
            jax.ShapeDtypeStruct((ITERS, HEADS, HEAD_DIM, tokens), f32),
            jax.ShapeDtypeStruct((ITERS, HEADS, HEAD_DIM, tokens), f32),
            jax.ShapeDtypeStruct((HEADS, 2 * ITERS, tokens), f32),
        ],
        scratch_shapes=[
            pltpu.VMEM((GROUP, HEAD_DIM + tokens, HEAD_DIM), bf16),
            pltpu.VMEM((GROUP, HEAD_DIM, tokens), bf16),
            pltpu.VMEM((GROUP, tokens, tokens), f32),
            pltpu.VMEM((GROUP, 8, tokens), f32),
            square, square, square, square,
        ],
        compiler_params=pltpu.CompilerParams(vmem_limit_bytes=VMEM_LIMIT),
        cost_estimate=pl.CostEstimate(flops=900_000_000, bytes_accessed=12_000_000, transcendentals=200_000),
        name="solve",
    )(q, k, v, states, c, b, ridge)


def adjoint_kernel(
    ga_ref, k_ref, v_ref, st_ref, c_ref, b_ref, ridge_ref, x_ref, p_ref, m_ref, scal_ref,
    dq_ref, dk_ref, dv_ref, dst_ref, dridge_ref,
    left, kt, mask, decay, ridge, gx_s, gr_s, gp_s, acc_s, wide, rows, scaled,
):
    group = pl.program_id(0)
    tokens = k_ref.shape[1]
    steps = ITERS * tokens
    first = []
    for h in range(GROUP):
        c = c_ref[pl.ds(group * GROUP + h, 1), :]
        b = b_ref[pl.ds(group * GROUP + h, 1), :]
        k = k_ref[h]
        left[h, :HEAD_DIM] = st_ref[h, 0]
        left[h, HEAD_DIM:] = k
        kt[h] = k.T
        mask[h] = decay_mask(c, b, tokens)
        decay[h] = jnp.broadcast_to(jnp.exp(c), (8, tokens))
        ridge[h] = column(ridge_ref[pl.ds(group * GROUP + h, 1), :], (tokens, HEAD_DIM))
        e = decay[h, 0:1]
        ga = ga_ref[:, h * HEAD_DIM : (h + 1) * HEAD_DIM].T
        ga_low = ga.astype(bf16)
        x = x_ref[h]
        scores = (nn(k, x) * mask[h]).astype(bf16)
        dscores = (nn(v_ref[h], ga_low) * mask[h]).astype(bf16)
        gx = e * tn(st_ref[h, 1], ga_low) + nn(kt[h], dscores)
        gx_s[h] = gx
        dv_ref[h] = nt(scores, ga_low)
        dst_ref[h, 1] = nt((e * ga).astype(bf16), x).astype(bf16)
        wide[h, :, 2 * steps :] = dscores
        rows[h, :, 2 * steps :] = x
        for i in range(ITERS):
            low = p_ref[i, h].astype(bf16)
            rows[h, :, steps + i * tokens : steps + (i + 1) * tokens] = low
            wide[h, :, i * tokens : (i + 1) * tokens] = (nn(k, low) * mask[h]).astype(bf16)
        i = ITERS - 1
        p, m = p_ref[i, h], m_ref[i, h]
        norm = scal_ref[h, i : i + 1]
        dot = scal_ref[h, ITERS + i : ITERS + i + 1]
        size = norm / dot
        gsize = jnp.sum(gx * p, axis=0, keepdims=True)
        gdot = -gsize * size / dot
        gm = gdot * p
        low = gm.astype(bf16)
        gp_s[h] = size * gx + 2.0 * gdot * m
        gr_s[h] = jnp.zeros_like(gx)
        acc_s[h] = gm * p
        rows[h, :, i * tokens : (i + 1) * tokens] = low
        wide[h, :, steps + i * tokens : steps + (i + 1) * tokens] = (nn(k, low) * mask[h]).astype(bf16)
        scaled[h, :, i * tokens : (i + 1) * tokens] = (e * gm).astype(bf16)
        first.append(gsize / dot)

    def step(back, gnorms):
        i = ITERS - 2 - back
        at = pl.multiple_of(i * tokens, tokens)
        after = []
        for h in range(GROUP):
            e = decay[h, 0:1]
            p, m = p_ref[i, h], m_ref[i, h]
            norm = scal_ref[h, pl.ds(i, 1)]
            norm_next = scal_ref[h, pl.ds(i + 1, 1)]
            dot = scal_ref[h, pl.ds(ITERS + i, 1)]
            size = norm / dot
            ratio = norm_next / norm
            gp = gp_s[h]
            gx = gx_s[h]
            gratio = jnp.sum(gp * p, axis=0, keepdims=True)
            gnext = gnorms[h] + gratio / norm
            residual = p_ref[i + 1, h] - ratio * p
            gr = gr_s[h] + gp + 2.0 * gnext * residual
            gsize = jnp.sum(gx * p - gr * m, axis=0, keepdims=True)
            gdot = -gsize * size / dot
            gm = gdot * p - size * gr
            low = gm.astype(bf16)
            both = nn(left[h], low)
            dscores = (both[HEAD_DIM:] * mask[h]).astype(bf16)
            image = e * both[:HEAD_DIM] + nn(kt[h], dscores) + ridge[h] * gm
            gp_s[h] = ratio * gp + size * gx + gdot * m + image
            gr_s[h] = gr
            acc_s[h] = acc_s[h] + gm * p
            rows[h, :, pl.ds(at, tokens)] = low
            wide[h, :, pl.ds(steps + at, tokens)] = dscores
            scaled[h, :, pl.ds(at, tokens)] = (e * gm).astype(bf16)
            after.append(gsize / dot - gratio * ratio / norm)
        return tuple(after)

    gnorms = lax.fori_loop(0, ITERS - 1, step, tuple(first))
    for h in range(GROUP):
        dq_ref[h] = gr_s[h] + gp_s[h] + 2.0 * gnorms[h] * p_ref[0, h]
        dk_ref[h] = nt(wide[h], rows[h])
        dst_ref[h, 0] = nt(scaled[h], rows[h, :, steps : 2 * steps]).astype(bf16)
        dridge_ref[h] = jnp.sum(acc_s[h].T, axis=0, keepdims=True)


def adjoint(ga, k, v, states, c, b, ridge, x, p_all, m_all, scal):
    tokens = k.shape[1]
    steps = pl.BlockSpec((ITERS, GROUP, HEAD_DIM, tokens), lambda g: (0, g, 0, 0))
    square = pltpu.VMEM((GROUP, HEAD_DIM, tokens), f32)
    return pl.pallas_call(
        adjoint_kernel,
        grid=(HEADS // GROUP,),
        in_specs=[
            pl.BlockSpec((tokens, GROUP * HEAD_DIM), lambda g: (0, g)),
            grouped(tokens, HEAD_DIM),
            grouped(tokens, HEAD_DIM),
            grouped(2, HEAD_DIM, HEAD_DIM),
            whole(HEADS, tokens),
            whole(HEADS, tokens),
            whole(HEADS, HEAD_DIM),
            grouped(HEAD_DIM, tokens),
            steps,
            steps,
            grouped(2 * ITERS, tokens),
        ],
        out_specs=[
            grouped(HEAD_DIM, tokens),
            grouped(tokens, HEAD_DIM),
            grouped(tokens, HEAD_DIM),
            grouped(2, HEAD_DIM, HEAD_DIM),
            grouped(1, HEAD_DIM),
        ],
        out_shape=[
            jax.ShapeDtypeStruct((HEADS, HEAD_DIM, tokens), f32),
            jax.ShapeDtypeStruct((HEADS, tokens, HEAD_DIM), f32),
            jax.ShapeDtypeStruct((HEADS, tokens, HEAD_DIM), f32),
            jax.ShapeDtypeStruct((HEADS, 2, HEAD_DIM, HEAD_DIM), bf16),
            jax.ShapeDtypeStruct((HEADS, 1, HEAD_DIM), f32),
        ],
        scratch_shapes=[
            pltpu.VMEM((GROUP, HEAD_DIM + tokens, HEAD_DIM), bf16),
            pltpu.VMEM((GROUP, HEAD_DIM, tokens), bf16),
            pltpu.VMEM((GROUP, tokens, tokens), f32),
            pltpu.VMEM((GROUP, 8, tokens), f32),
            square, square, square, square, square,
            pltpu.VMEM((GROUP, tokens, (2 * ITERS + 1) * tokens), bf16),
            pltpu.VMEM((GROUP, HEAD_DIM, (2 * ITERS + 1) * tokens), bf16),
            pltpu.VMEM((GROUP, HEAD_DIM, ITERS * tokens), bf16),
        ],
        compiler_params=pltpu.CompilerParams(vmem_limit_bytes=VMEM_LIMIT),
        cost_estimate=pl.CostEstimate(flops=1_800_000_000, bytes_accessed=12_000_000, transcendentals=200_000),
        name="adjoint",
    )(ga, k, v, states, c, b, ridge, x, p_all, m_all, scal)


def features_back_kernel(
    pq, pk, pv, hq, hk, hv, tq, tk, tv, c_ref, b_ref, dq_ref, dk_ref, dv_ref, dst_ref,
    gq, gk, gv, bq, bk, bv, dtq, dtk, dtv,
):
    head = pl.program_id(0)
    tokens = pq.shape[0]
    c = c_ref[pl.ds(head, 1), :]
    b = b_ref[pl.ds(head, 1), :]
    ending = column(jnp.exp(c[:, tokens - 1 :] - c) * b, (HEAD_DIM, tokens))

    def forward(p, h, t):
        total, shifted = conv_parts(p[...], h[...], t[...])
        sig = jax.nn.sigmoid(total)
        act = total * sig
        return shifted, sig * (1.0 + total * (1.0 - sig)), act

    def unit_back(act, grad):
        scale = lax.rsqrt(jnp.sum(act * act, axis=-1, keepdims=True) + 1e-06)
        unit = act * scale
        return scale * (grad - unit * jnp.sum(unit * grad, axis=-1, keepdims=True))

    def conv_back(dconv, shifted, t, g, before, dt):
        taps = t[...]
        padded = jnp.concatenate([dconv, jnp.zeros((8, HEAD_DIM), f32)], axis=0)
        total = taps[KW - 1 : KW] * dconv
        for j in range(KW - 1):
            total = total + taps[j : j + 1] * padded[KW - 1 - j : KW - 1 - j + tokens]
        g[...] = total
        ahead = jnp.concatenate([jnp.zeros((8, HEAD_DIM), f32), dconv[:8]], axis=0)
        lead = taps[0:1] * ahead[8:16]
        for j in range(1, KW - 1):
            lead = lead + taps[j : j + 1] * ahead[8 - j : 16 - j]
        before[...] = lead
        dt[...] = jnp.concatenate(
            [jnp.sum(dconv * shifted[j], axis=0, keepdims=True) for j in range(KW)], axis=0
        )

    sh_q, slope_q, act_q = forward(pq, hq, tq)
    sh_k, slope_k, act_k = forward(pk, hk, tk)
    sh_v, slope_v, act_v = forward(pv, hv, tv)
    k = act_k * lax.rsqrt(jnp.sum(act_k * act_k, axis=-1, keepdims=True) + 1e-06)
    k_low = k.astype(bf16)
    v_low = act_v.astype(bf16)
    both = dst_ref[0, 0].astype(f32)
    both = (both + both.T).astype(bf16)
    rv = dst_ref[0, 1].astype(bf16)
    dk = dk_ref[0] + ending * (nn(k_low, both) + nn(v_low, rv))
    dv = dv_ref[0] + ending * nt(k_low, rv)
    conv_back(unit_back(act_q, dq_ref[0].T) * slope_q, sh_q, tq, gq, bq, dtq)
    conv_back(unit_back(act_k, dk) * slope_k, sh_k, tk, gk, bk, dtk)
    conv_back(dv * slope_v, sh_v, tv, gv, bv, dtv)


def features_back(proj, halo, taps, c, b, dq, dk, dv, dst):
    tokens = proj.shape[0]

    def third(rows):
        return pl.BlockSpec((rows, HEAD_DIM), lambda h: (0, h))

    return pl.pallas_call(
        features_back_kernel,
        grid=(HEADS,),
        in_specs=thirds(tokens) + thirds(8) + thirds(KW) + [whole(HEADS, tokens)] * 2
        + [per_head(HEAD_DIM, tokens), per_head(tokens, HEAD_DIM), per_head(tokens, HEAD_DIM), per_head(2, HEAD_DIM, HEAD_DIM)],
        out_specs=[third(tokens)] * 3 + [third(8)] * 3 + [third(KW)] * 3,
        out_shape=[jax.ShapeDtypeStruct((tokens, D), f32)] * 3
        + [jax.ShapeDtypeStruct((8, D), f32)] * 3
        + [jax.ShapeDtypeStruct((KW, D), f32)] * 3,
        cost_estimate=pl.CostEstimate(flops=100_000_000, bytes_accessed=8_000_000, transcendentals=400_000),
        name="features_back",
    )(proj, proj, proj, halo, halo, halo, taps, taps, taps, c, b, dq, dk, dv, dst)


def neighbour(axis, bit):
    return [(i, i ^ bit) for i in range(lax.axis_size(axis))]


def partner(x, axis, bit=1):
    return lax.ppermute(x, axis, neighbour(axis, bit))


def shifted(x, axis, by):
    peers = lax.axis_size(axis)
    return lax.ppermute(x, axis, [(i, i + by) for i in range(peers) if 0 <= i + by < peers])


def pick(x, index, axis=0):
    return lax.dynamic_index_in_dim(x, index, axis, keepdims=False)


def entering(own, logs, axis, reverse):
    peers = lax.axis_size(axis)
    here = lax.axis_index(axis)
    if reverse:
        here = peers - 1 - here
        logs = logs[::-1]
    at = jnp.arange(peers)
    heads = own.shape[0]

    def total_decay(start, stop):
        inside = (at >= start) & (at < stop)
        return jnp.exp(jnp.sum(jnp.where(inside[:, None], logs, 0.0), axis=0))

    def times(coefficients, first, count):
        part = lax.dynamic_slice_in_dim(coefficients, first, count, 0)
        return part[:, None, None, None]

    levels = peers.bit_length() - 1
    halving = min(2, levels)
    now = own
    first, count = 0, heads
    saved = []
    for level in range(halving):
        size = 1 << level
        bit = (here >> level) & 1
        base = (here >> (level + 1)) << (level + 1)
        halves = now.reshape((2, count // 2) + now.shape[1:])
        keep = pick(halves, bit)
        received = partner(pick(halves, 1 - bit), axis, size)
        count = count // 2
        first = first + bit * count
        low = jnp.where(bit == 1, received, keep).astype(f32)
        high = jnp.where(bit == 1, keep, received).astype(f32)
        now = (times(total_decay(base + size, base + 2 * size), first, count) * low + high).astype(bf16)
        saved.append((bit, low, times(total_decay(base, base + size), first, count)))
    unit = (here >> halving) << halving
    before = jnp.zeros(now.shape, f32)
    for level in range(halving, levels):
        size = 1 << level
        bit = (here >> level) & 1
        base = (here >> (level + 1)) << (level + 1)
        start = (here >> level) << level
        received = partner(now, axis, size).astype(f32)
        mine = now.astype(f32)
        before = jnp.where(bit == 1, times(total_decay(start, unit), first, count) * received + before, before)
        low = jnp.where(bit == 1, received, mine)
        high = jnp.where(bit == 1, mine, received)
        now = (times(total_decay(base + size, base + 2 * size), first, count) * low + high).astype(bf16)
    for level in reversed(range(halving)):
        bit, low, decay = saved[level]
        after = decay * before + low
        mine = jnp.where(bit == 1, after, before).astype(bf16)
        other = jnp.where(bit == 1, before, after).astype(bf16)
        received = partner(other, axis, 1 << level)
        before = jnp.concatenate(
            [jnp.where(bit == 1, received, mine), jnp.where(bit == 1, mine, received)], axis=0
        ).astype(f32)
    return before.astype(bf16)


def rms_scale(values, gain):
    return values * lax.rsqrt(jnp.mean(values * values, axis=-1, keepdims=True) + 1e-05) * gain


def right_product(left, right):
    return nt(left, right)


def local(
    inputs,
    qkv_weight,
    gate_weight,
    out_weight,
    up_weight,
    down_weight,
    conv_taps,
    gain_attn,
    gain_ffn,
    ridge_terms,
    forget,
    cotangent,
):
    tokens = inputs[0]
    rows = tokens.shape[0]
    y = lax.axis_index("fsdp")
    peers = lax.axis_size("ctx")
    owners = peers * 2
    small = jnp.concatenate(
        [conv_taps.reshape(-1), gain_attn, gain_ffn, ridge_terms]
    )
    both = lax.all_gather(small, "fsdp", axis=0)
    split = KW * 3 * D // 2
    taps = both[:, :split].reshape(2, KW, 3 * D // 2).transpose(1, 0, 2).reshape(KW, 3 * D).astype(f32)
    rest = both[:, split:].reshape(2, 3, D // 2).transpose(1, 0, 2).reshape(3, D).astype(f32)
    gain_first, gain_second = rest[0], rest[1]
    ridge = rest[2].reshape(HEADS, HEAD_DIM)
    out_full = lax.all_gather(out_weight, "fsdp", axis=0, tiled=True)
    up_full = lax.all_gather(up_weight, "fsdp", axis=0, tiled=True)
    down_full = lax.all_gather(down_weight, "fsdp", axis=0, tiled=True)
    cumulative = jnp.cumsum(jnp.log(forget[0]).T, axis=-1)
    strength = (1.0 - forget[0]).T
    logs = lax.all_gather(cumulative[:, -1], "ctx", axis=0)

    normed_low = rms_scale(tokens, gain_first).astype(bf16)
    halves = normed_low.reshape(rows, 2, D // 2)
    mine = pick(halves, y, 1)
    theirs = partner(pick(halves, 1 - y, 1), "fsdp")
    lent = nn(theirs, qkv_weight).astype(bf16)
    projected = nn(mine, qkv_weight) + partner(lent, "fsdp").astype(f32)
    lent = nn(theirs, gate_weight).astype(bf16)
    gate_logit = nn(mine, gate_weight) + partner(lent, "fsdp").astype(f32)
    tail = shifted(projected[rows - (KW - 1) :].astype(bf16), "ctx", 1).astype(f32)
    halo = jnp.concatenate([jnp.zeros((8 - KW + 1, 3 * D), f32), tail], axis=0)
    queries, keys, values, own = features(projected, halo, taps, cumulative, strength)
    states = entering(own, logs, "ctx", False)
    attended, x, p_all, m_all, scal = solve(queries, keys, values, states, cumulative, strength, ridge)

    gate_sig = jax.nn.sigmoid(gate_logit)
    gated_mix = (attended * gate_sig).astype(bf16)
    hidden = tokens + nn(gated_mix, out_full)
    normed_ffn, second_pull = jax.vjp(rms_scale, hidden, gain_second)
    normed_ffn_low = normed_ffn.astype(bf16)
    gate_up = nn(normed_ffn_low, up_full)
    gate_part = gate_up[:, :FF]
    up_part = gate_up[:, FF:]
    inner = (jax.nn.silu(gate_part) * up_part).astype(bf16)
    output = hidden + nn(inner, down_full)
    grad_output = cotangent[0]
    grad_branch = grad_output.astype(bf16)
    grad_inner = nt(grad_branch, down_full)
    gate_sigmoid = jax.nn.sigmoid(gate_part)
    grad_gate_part = grad_inner * up_part * gate_sigmoid * (1.0 + gate_part * (1.0 - gate_sigmoid))
    grad_up_part = grad_inner * gate_part * gate_sigmoid
    grad_gate_up = jnp.concatenate([grad_gate_part, grad_up_part], axis=1).astype(bf16)
    grad_normed_ffn = nt(grad_gate_up, up_full)
    grad_hidden_norm, grad_second_gain = second_pull(grad_normed_ffn)
    grad_hidden = grad_output + grad_hidden_norm
    grad_attn_branch = grad_hidden.astype(bf16)
    grad_mixed = nt(grad_attn_branch, out_full)
    grad_attended = grad_mixed * gate_sig
    grad_logit = (grad_mixed * attended * gate_sig * (1.0 - gate_sig)).astype(bf16)

    def parity(left):
        flat = left.T.reshape(peers, 2, left.shape[1] // owners, rows)
        kept = pick(flat, y, 1).reshape(-1, rows)
        sent = pick(flat, 1 - y, 1).reshape(-1, rows)
        return jnp.concatenate([kept, partner(sent, "fsdp")], axis=1)

    def share(right):
        return jnp.concatenate([right, partner(right, "fsdp")], axis=0)

    def reduced(left, right):
        return lax.psum_scatter(
            nn(left, right).astype(bf16), "ctx", scatter_dimension=0, tiled=True
        ).astype(f32)

    grad_down = reduced(parity(inner), share(grad_branch))
    grad_up = reduced(parity(normed_ffn_low), share(grad_gate_up))
    grad_out = reduced(parity(gated_mix), share(grad_attn_branch))
    both_logit = share(grad_logit)
    normed_parity = parity(normed_low)
    grad_gate = reduced(normed_parity, both_logit)

    dq, dk, dv, dst, dridge = adjoint(
        grad_attended, keys, values, states, cumulative, strength, ridge, x, p_all, m_all, scal
    )
    returned = entering(dst, logs, "ctx", True)
    parts = features_back(projected, halo, taps, cumulative, strength, dq, dk, dv, returned)
    grad_projected = jnp.concatenate(parts[:3], axis=1)
    grad_before = jnp.concatenate(parts[3:6], axis=1)[: KW - 1]
    grad_taps = jnp.concatenate(parts[6:], axis=1)
    from_next = shifted(grad_before.astype(bf16), "ctx", -1).astype(f32)
    grad_projected = grad_projected + jnp.pad(from_next, ((rows - KW + 1, 0), (0, 0)))
    both_projected = share(grad_projected.astype(bf16))
    grad_qkv = reduced(normed_parity, both_projected)
    lent = nt(both_projected, qkv_weight) + nt(both_logit, gate_weight)
    back = partner(lent[rows:].astype(bf16), "fsdp").astype(f32)
    kept = lent[:rows]
    grad_normed = jnp.where(
        y == 0, jnp.concatenate([kept, back], axis=1), jnp.concatenate([back, kept], axis=1)
    )
    _, first_pull = jax.vjp(rms_scale, tokens, gain_first)
    grad_tokens_norm, grad_first_gain = first_pull(grad_normed)
    grad_tokens = grad_hidden + grad_tokens_norm
    width = 3 * D // owners
    vector = jnp.concatenate(
        [
            grad_taps.reshape(KW, owners, width).transpose(1, 0, 2).reshape(owners, KW * width),
            grad_first_gain.reshape(owners, D // owners),
            grad_second_gain.reshape(owners, D // owners),
            dridge.reshape(owners, D // owners),
        ],
        axis=1,
    )
    vector = lax.psum_scatter(vector, ("ctx", "fsdp"), scatter_dimension=0, tiled=True)[0]
    taps_end = KW * width
    size = D // owners
    return (
        output[None],
        grad_tokens[None],
        grad_qkv,
        grad_gate,
        grad_out,
        grad_up,
        grad_down,
        vector[:taps_end].reshape(KW, width),
        vector[taps_end : taps_end + size],
        vector[taps_end + size : taps_end + 2 * size],
        vector[taps_end + 2 * size :],
    )


def solution(mesh):
    tokens = P("fsdp", "ctx", None)
    rows = P("fsdp", None)
    vector = P("fsdp")
    owned = P(("ctx", "fsdp"), None)
    owned_vector = P(("ctx", "fsdp"))
    return jax.shard_map(
        local,
        mesh=mesh,
        in_specs=(
            tokens, rows, rows, rows, rows, rows, P(None, "fsdp"), vector, vector, vector, tokens, tokens,
        ),
        out_specs=(
            tokens, tokens, owned, owned, owned, owned, owned, P(None, ("ctx", "fsdp")),
            owned_vector, owned_vector, owned_vector,
        ),
        check_vma=False,
    )
```

time: 2030 us -> 762 us (0.38)
  waiting for transfers between devices: 1580 us -> 420 us
  matrix products: 192 us -> 58.7 us
  Pallas kernels: 0 us -> 56.5 us
  other arithmetic: 83.6 us -> 54.6 us
  starting transfers between devices: 3.89 us -> 26.8 us
    reduce_scatter x5, waiting for transfers between devices: 1180 us -> 186 us  [reduced(): lax.psum_scatter(nn(left, right).astype(bf16), 'ctx', scatter_dimension=0...]
    all_gather x9 -> x3, waiting for transfers between devices: 394 us -> 97.9 us  [the longest x1 68.3 us: local(): down_full = lax.all_gather(down_weight, 'fsdp', axis=0, tiled=True)]
    dot_general x102 -> x17, matrix products: 192 us -> 58.7 us  [the longest x12 40.4 us: nn(): lax.dot_general(a, b, (((1,), (0,)), ((), ())), preferred_element_type=f32)]
    ppermute x2 -> x27, waiting for transfers between devices: 1.75 us -> 134 us  [the longest x25 134 us: partner(): return lax.ppermute(x, axis, neighbour(axis, bit))]
    pallas_call x0 -> x4, Pallas kernels: none -> 56.5 us  [the longest x1 21.5 us: adjoint(): pl.pallas_call(adjoint_kernel, grid=(HEADS // GROUP,), in_specs=[pl.Block...]
    select_n x32 -> x8, other arithmetic: 43.8 us -> 5.89 us  [the longest x4 3.88 us: entering(): jnp.where(bit == 1, received, mine)]
    ppermute x2 -> x27, starting transfers between devices: 3.29 us -> 26.2 us  [the longest x25 23.7 us: partner(): return lax.ppermute(x, axis, neighbour(axis, bit))]
  transfers between devices with their start and end apart: 17 -> 35, of which waited for: 15 -> 23; matrix products, arithmetic and copies ran while one was open for 8% -> 16% of each run, Pallas kernels for 0% -> 4%
where the time goes in v1:
time: 762 us; the launch traced here: 759 us
  waiting for transfers between devices  420 us (55%)
  blocking collectives  78.1 us (10%)
  matrix products  58.7 us (8%)
  Pallas kernels  56.5 us (7%)
  other arithmetic  54.6 us (7%)
  local copies, waits for them, and re-layouts  48.4 us (6%)
  starting transfers between devices  26.8 us (4%)
  between operations  15.7 us (2%)
    reduce_scatter x5, waiting for transfers between devices, reduced(): lax.psum_scatter(nn(left, right).astype(bf16), 'ctx', scatter_dimension=0...  186 us
    ppermute x25, waiting for transfers between devices, partner(): return lax.ppermute(x, axis, neighbour(axis, bit))  134 us
    unnamed x2, blocking collectives  72.6 us
    all_gather x1, waiting for transfers between devices, local(): down_full = lax.all_gather(down_weight, 'fsdp', axis=0, tiled=True)  68.3 us
    dot_general x12, matrix products, nn(): lax.dot_general(a, b, (((1,), (0,)), ((), ())), preferred_element_type=f32)  40.4 us
    all_gather x1, waiting for transfers between devices, local(): up_full = lax.all_gather(up_weight, 'fsdp', axis=0, tiled=True)  29.6 us
    ppermute x25, starting transfers between devices, partner(): return lax.ppermute(x, axis, neighbour(axis, bit))  23.7 us
    pallas_call x1, Pallas kernels, adjoint(): pl.pallas_call(adjoint_kernel, grid=(HEADS // GROUP,), in_specs=[pl.Block...  21.5 us
  transfers between devices with their start and end apart: 35, of which 23 were waited for; matrix products, arithmetic and copies ran while one was open for 16% of the time, Pallas kernels for 4%

profile of v1, /device:TPU:0, one launch (start us, length us, event | category | flops | bytes accessed | tf_op | source)
XLA Modules:
  0.0 758.7 jit_solution(17423550413098064602)
XLA Ops:
  8.9 5.5 all-gather.2
  15.7 2.0 copy.40
  21.1 2.1 collective-permute-start
  27.8 2.0 collective-permute-done
  30.4 2.0 collective-permute-start.1
  33.0 31.8 %collective-permute-done.1 = bf16[128,3072]{1,0:T(8,128)(2,1)S(1)} collective-permute-done((bf16[128,3072]{1,0:T(8,128)(2,1)S(1)}, bf16[128,3072]{1,0:T(8,128)(2,1)S(1)}, u32[]{:S(2)}, u32[]{:S(2)}) %collective-permute-start.1) | collective-permute-done | bytes 786464 | tf_op jit(solution)/shard_map/ppermute | solution.py:441
  69.0 7.0 features.1
  76.1 1.8 dynamic-slice_bitcast_fusion.1
  77.8 2.4 collective-permute-start.3
  81.8 34.6 %all-reduce.2 = f32[128]{0:T(128)S(1)} all-reduce(f32[128]{0:T(128)S(1)} %dynamic-update-slice), channel_id=3, replica_groups=mesh['ctx'=16,'fsdp'=2] {'ctx'}, use_global_device_ids=true, to_apply=%add.2 | all-reduce | flops 128 | bytes 1024
  122.3 2.7 collective-permute-done.4
  125.6 1.7 fusion.31
  133.5 1.8 bitcast_convert_fusion
  135.3 4.1 collective-permute-done.6
  140.1 1.8 select_convert_fusion.3
  144.3 2.9 collective-permute-done.7
  149.3 1.9 fusion.14
  157.1 19.7 %solve.1 = (f32[128,1024]{1,0:T(8,128)}, bf16[8,128,128]{2,1,0:T(8,128)(2,1)}, f32[8,8,128,128]{3,2,1,0:T(8,128)}, f32[8,8,128,128]{3,2,1,0:T(8,128)}, f32[8,16,128]{2,1,0:T(8,128)}) custom-call(f32[8,128,128]{2,1,0:T(8,128)} %get-tuple-element.34.q_ref, bf16[8,128,128]{2,1,0:T(8,128)(2,1)} %get-tuple-element.35.k_ref, ...), custom_call_target="tpu_custom_call" | custom-call | flops 900000000 | bytes 12000000 | tf_op jit(solution)/shard_map/solve/pallas_call | solution.py:180
  177.4 2.2 multiply_convert_fusion.6
  179.6 3.0 multiply_reduce_fusion.3
  182.6 29.6 %all-gather.9.cloned.1.call-done = bf16[1024,5632]{1,0:T(8,128)(2,1)} async-done(((bf16[512,5632]{1,0:T(8,128)(2,1)}), bf16[1024,5632]{1,0:T(8,128)(2,1)}) %all-gather.9.cloned.1.call-update) | async-done | bytes 11534352 | tf_op jit(solution)/shard_map/all_gather | solution.py:550
  212.3 7.8 %fusion.67 = f32[128,5632]{1,0:T(8,128)} fusion(bf16[1024,5632]{1,0:T(8,128)(2,1)} %all-gather.9.cloned.1.call-done, f32[128,1024]{1,0:T(8,128)} %get-tuple-element.111, f32[1024]{0:T(1024)S(1)} %bitcast.199, f32[128]{0:T(128)S(1)} %fusion.58), kind=kOutput, calls=%fused_computation.215 | convolution fusion | flops 1476788224 | bytes 14946816 | tf_op jit(solution)/shard_map/dot_general | solution.py:23
  220.1 68.3 %all-gather.11.cloned.1.call-done = bf16[2816,1024]{1,0:T(8,128)(2,1)} async-done(((bf16[1408,1024]{1,0:T(8,128)(2,1)}), bf16[2816,1024]{1,0:T(8,128)(2,1)}) %all-gather.11.cloned.1.call-update) | async-done | bytes 5767184 | tf_op jit(solution)/shard_map/all_gather | solution.py:551
  288.3 6.7 multiply_convert_fusion.1
  295.2 4.4 multiply_reduce_fusion
  301.4 2.9 fusion.69
  304.4 21.5 %adjoint.1 = (f32[8,128,128]{2,1,0:T(8,128)}, f32[8,128,128]{2,1,0:T(8,128)}, f32[8,128,128]{2,1,0:T(8,128)}, bf16[8,2,128,128]{3,2,1,0:T(8,128)(2,1)}, f32[8,1,128]{2,1,0:T(1,128)}) custom-call(f32[128,1024]{1,0:T(8,128)} %get-tuple-element.88.ga_ref, bf16[8,128,128]{2,1,0:T(8,128)(2,1)} %get-tuple-element.35.k_ref, ...), custom_call_target="tpu_custom_call" | custom-call | flops 1800000000 | bytes 12000000 | tf_op jit(solution)/shard_map/adjoint/pallas_call | solution.py:317
  325.9 1.7 dynamic-slice_bitcast_fusion
  334.5 3.0 collective-permute-done.11
  342.1 3.0 collective-permute-done.12
  345.0 1.7 fusion.40
  346.7 2.4 collective-permute-start.13
  350.0 4.3 collective-permute-done.13
  357.7 2.8 collective-permute-done.14
  364.7 8.3 %features_back.1 = (f32[128,1024]{1,0:T(8,128)}, f32[128,1024]{1,0:T(8,128)}, f32[128,1024]{1,0:T(8,128)}, f32[8,1024]{1,0:T(8,128)}, f32[8,1024]{1,0:T(8,128)},...) custom-call(f32[128,3072]{1,0:T(8,128)} %copy-done.1, f32[128,3072]{1,0:T(8,128)} %copy-done.1, ...), custom_call_target="tpu_custom_call" | custom-call | flops 100000000 | bytes 8000000 | tf_op jit(solution)/shard_map/features_back/pallas_call | solution.py:422
  377.8 1.8 copy.46
  379.6 2.4 fusion.5
  382.0 1.7 collective-permute-start.17
  384.7 1.7 collective-permute-start.18
  386.4 19.9 %collective-permute-done.21 = bf16[512,128]{1,0:T(8,128)(2,1)S(1)} collective-permute-done((bf16[512,128]{1,0:T(8,128)(2,1)S(1)}, bf16[512,128]{1,0:T(8,128)(2,1)S(1)}, u32[]{:S(2)}, u32[]{:S(2)}) %collective-permute-start.21) | collective-permute-done | bytes 131104 | tf_op jit(solution)/shard_map/ppermute | solution.py:441
  406.4 2.4 convolution_convert_fusion.4
  408.8 3.2 collective-permute-done.18
  412.0 1.9 fusion.29
  413.9 2.4 convolution_add_fusion.1
  419.4 4.1 collective-permute-done.19
  424.2 2.5 multiply_reduce_fusion.1
  426.7 1.8 copy.44
  430.1 4.4 collective-permute-done.20
  435.2 2.4 convolution_convert_fusion.5
  437.7 2.3 copy.47
  443.2 12.0 %collective-permute-done.26 = bf16[128,1024]{1,0:T(8,128)(2,1)S(1)} collective-permute-done((bf16[128,1024]{1,0:T(8,128)(2,1)}, bf16[128,1024]{1,0:T(8,128)(2,1)S(1)}, u32[]{:S(2)}, u32[]{:S(2)}) %collective-permute-start.26) | collective-permute-done | bytes 262176 | tf_op jit(solution)/shard_map/ppermute | solution.py:441
  455.2 3.4 convolution_convert_fusion.2
  458.7 4.2 convolution_convert_fusion.1
  466.9 31.5 %collective-permute-done.23 = bf16[512,128]{1,0:T(8,128)(2,1)S(1)} collective-permute-done((bf16[512,128]{1,0:T(8,128)(2,1)S(1)}, bf16[512,128]{1,0:T(8,128)(2,1)S(1)}, u32[]{:S(2)}, u32[]{:S(2)}) %collective-permute-start.23) | collective-permute-done | bytes 131104 | tf_op jit(solution)/shard_map/ppermute | solution.py:441
  498.4 7.5 convolution_convert_fusion
  508.6 4.7 fusion.6
  516.7 37.9 %all-reduce.3 = f32[32,480]{1,0:T(8,128)S(1)} all-reduce(f32[32,480]{1,0:T(8,128)S(1)} %pad_maximum_fusion.14), channel_id=9, replica_groups=mesh['ctx'=16,'fsdp'=2] {'ctx','fsdp'}, use_global_device_ids=true, to_apply=%region_26.27.clone | all-reduce | flops 15360 | bytes 122880
  556.6 2.3 fusion.20
  560.4 35.2 %reduce-scatter.14.cloned.1.call-done = bf16[88,1024]{1,0:T(8,128)(2,1)} async-done(((bf16[1408,1024]{1,0:T(8,128)(2,1)}), bf16[88,1024]{1,0:T(8,128)(2,1)}) %reduce-scatter.14.cloned.1.call-update) | async-done | bytes 180240 | tf_op jit(solution)/shard_map/reduce_scatter | solution.py:605
  595.6 1.7 convert_element_type.253
  597.3 67.7 %reduce-scatter.6.cloned.1.call-done = bf16[32,3072]{1,0:T(8,128)(2,1)} async-done(((bf16[512,3072]{1,0:T(8,128)(2,1)}), bf16[32,3072]{1,0:T(8,128)(2,1)}) %reduce-scatter.6.cloned.1.call-update) | async-done | bytes 196624 | tf_op jit(solution)/shard_map/reduce_scatter | solution.py:605
  665.1 1.7 convert_element_type.245
  666.8 83.2 %reduce-scatter.12.cloned.1.call-done = bf16[32,5632]{1,0:T(8,128)(2,1)} async-done(((bf16[512,5632]{1,0:T(8,128)(2,1)}), bf16[32,5632]{1,0:T(8,128)(2,1)}) %reduce-scatter.12.cloned.1.call-update) | async-done | bytes 360464 | tf_op jit(solution)/shard_map/reduce_scatter | solution.py:605
  750.0 1.9 convert_element_type.251
  (299 shorter events, 92.1 us)
Async XLA Ops:
  7.2 22.6 %copy-start = (bf16[512,3072]{1,0:T(8,128)(2,1)S(1)}, bf16[512,3072]{1,0:T(8,128)(2,1)}, u32[]{:S(2)}) copy-start(bf16[512,3072]{1,0:T(8,128)(2,1)} %param.13) | copy-start | bytes 9437188
  7.2 172.4 %all-gather.7.cloned.1.call-start = ((), (), s32[]{:S(2)}) async-start(), calls=%async_computation.5 | async-start | bytes 3145728 | tf_op jit(solution)/shard_map/all_gather | solution.py:549
  8.0 204.3 %all-gather.9.cloned.1.call-start = ((), (), s32[]{:S(2)}) async-start(), calls=%async_computation.6 | async-start | bytes 17301504 | tf_op jit(solution)/shard_map/all_gather | solution.py:550
  8.7 279.6 %all-gather.11.cloned.1.call-start = ((), (), s32[]{:S(2)}) async-start(), calls=%async_computation.7 | async-start | bytes 8650752 | tf_op jit(solution)/shard_map/all_gather | solution.py:551
  20.3 12.1 %copy-start.23 = (bf16[128,2,512]{0,2,1:T(8,128)(2,1)}, bf16[128,2,512]{0,2,1:T(8,128)(2,1)S(1)}, u32[]{:S(2)}) copy-start(bf16[128,2,512]{0,2,1:T(8,128)(2,1)S(1)} %multiply_convert_fusion.7) | copy-start | bytes 786436
  21.1 8.7 %collective-permute-start = (bf16[128,512]{1,0:T(8,128)(2,1)}, bf16[128,512]{1,0:T(8,128)(2,1)S(1)}, u32[]{:S(2)}, u32[]{:S(2)}) collective-permute-start(bf16[128,512]{1,0:T(8,128)(2,1)} %bitcast.206), channel_id=1, source_target_pairs={{0,1},{1,0},{2,3},{3,2},{4,5},{5,4},{6,7},{7,6},{8,9},{9,8},{10,11... | collective-permute-start | bytes 393224 | tf_op jit(solution)/shard_map/ppermute | solution.py:441
  23.2 491.0 %reduce-scatter.10.cloned.1.call-start = ((), (), s32[]{:S(2)}) async-start(), calls=%async_computation.10 | async-start | bytes 1114112 | tf_op jit(solution)/shard_map/reduce_scatter | solution.py:605
  27.6 5.4 copy-start.34
  30.4 34.5 %collective-permute-start.1 = (bf16[128,3072]{1,0:T(8,128)(2,1)S(1)}, bf16[128,3072]{1,0:T(8,128)(2,1)S(1)}, u32[]{:S(2)}, u32[]{:S(2)}) collective-permute-start(bf16[128,3072]{1,0:T(8,128)(2,1)S(1)} %convolution_convert_fusion.3), channel_id=1, source_target_pairs={{0,1},{1,0},{2,3},{3,2},{4,5},{5,4},{6,7},{7,6},{8,9},{9,8},{10,11... | collective-permute-start | bytes 2359304 | tf_op jit(solution)/shard_map/ppermute | solution.py:441
  66.2 2.1 collective-permute-start.2
  69.0 11.3 %copy-start.62 = (u32[32]{0:T(128)S(1)}, u32[32]{0:T(128)}, u32[]{:S(2)}) copy-start(u32[32]{0:T(128)} %constant.108) | copy-start | bytes 388
  69.0 47.5 %copy-start.55 = (pred[16]{0:T(512)(128)(4,1)S(1)}, pred[16]{0:T(512)(128)(4,1)}, u32[]{:S(2)}) copy-start(pred[16]{0:T(512)(128)(4,1)} %compare_and_fusion.13) | copy-start | bytes 52
  69.0 47.5 %copy-start.56 = (pred[16]{0:T(512)(128)(4,1)S(1)}, pred[16]{0:T(512)(128)(4,1)}, u32[]{:S(2)}) copy-start(pred[16]{0:T(512)(128)(4,1)} %compare_and_fusion.7) | copy-start | bytes 52
  69.0 47.5 %copy-start.57 = (pred[16]{0:T(512)(128)(4,1)S(1)}, pred[16]{0:T(512)(128)(4,1)}, u32[]{:S(2)}) copy-start(pred[16]{0:T(512)(128)(4,1)} %compare_and_fusion.9) | copy-start | bytes 52
  69.0 47.5 %copy-start.58 = (pred[16]{0:T(512)(128)(4,1)S(1)}, pred[16]{0:T(512)(128)(4,1)}, u32[]{:S(2)}) copy-start(pred[16]{0:T(512)(128)(4,1)} %compare_and_fusion.11) | copy-start | bytes 52
  77.8 39.5 %collective-permute-start.3 = (bf16[4,2,128,128]{3,2,1,0:T(8,128)(2,1)}, bf16[4,2,128,128]{3,2,1,0:T(8,128)(2,1)S(1)}, u32[]{:S(2)}, u32[]{:S(2)}) collective-permute-start(bf16[4,2,128,128]{3,2,1,0:T(8,128)(2,1)} %dynamic-slice_bitcast_fusion.1), channel_id=1, source_target_pairs={{0,2},{2,0},{4,6},{6,4},{8,10},{10,8},{12,14},{14,12},{16,18},{18,... | collective-permute-start | bytes 786440 | tf_op jit(solution)/shard_map/ppermute | solution.py:441
  119.8 5.2 collective-permute-start.4
  127.3 5.2 collective-permute-start.5
  133.5 5.9 collective-permute-start.6
  141.8 5.3 collective-permute-start.7
  151.2 2.8 collective-permute-start.8
  153.3 23.4 %collective-permute-start.9 = (bf16[128,1024]{1,0:T(8,128)(2,1)S(1)}, bf16[128,1024]{1,0:T(8,128)(2,1)S(1)}, u32[]{:S(2)}, u32[]{:S(2)}) collective-permute-start(bf16[128,1024]{1,0:T(8,128)(2,1)S(1)} %convolution_convert_fusion.6), channel_id=1, source_target_pairs={{0,1},{1,0},{2,3},{3,2},{4,5},{5,4},{6,7},{7,6},{8,9},{9,8},{10,11... | collective-permute-start | bytes 786440 | tf_op jit(solution)/shard_map/ppermute | solution.py:441
  156.2 21.2 %copy-start.22 = (bf16[512,1024]{1,0:T(8,128)(2,1)S(1)}, bf16[512,1024]{1,0:T(8,128)(2,1)}, u32[]{:S(2)}) copy-start(bf16[512,1024]{1,0:T(8,128)(2,1)} %param.14) | copy-start | bytes 3145732
  156.2 21.2 %copy-start.24 = (bf16[128,2,512]{0,2,1:T(8,128)(2,1)S(1)}, bf16[128,2,512]{0,2,1:T(8,128)(2,1)}, u32[]{:S(2)}) copy-start(bf16[128,2,512]{0,2,1:T(8,128)(2,1)} %copy-done.23) | copy-start | bytes 786436
  179.6 32.7 %copy-start.18 = (bf16[128,1024]{1,0:T(8,128)(2,1)}, bf16[128,1024]{1,0:T(8,128)(2,1)S(1)}, u32[]{:S(2)}) copy-start(bf16[128,1024]{1,0:T(8,128)(2,1)S(1)} %get-tuple-element.108) | copy-start | bytes 786436
  212.3 76.1 %copy-start.17 = (bf16[128,1024]{1,0:T(8,128)(2,1)S(1)}, bf16[128,1024]{1,0:T(8,128)(2,1)}, u32[]{:S(2)}) copy-start(bf16[128,1024]{1,0:T(8,128)(2,1)} %bitcast_convert_fusion) | copy-start | bytes 786436
  288.3 6.8 copy-start.2
  288.3 6.8 copy-start.3
  304.4 23.3 %copy-start.45 = (pred[16]{0:T(512)(128)(4,1)S(1)}, pred[16]{0:T(512)(128)(4,1)}, u32[]{:S(2)}) copy-start(pred[16]{0:T(512)(128)(4,1)} %get-tuple-element.115) | copy-start | bytes 52
  304.4 23.3 %copy-start.46 = (pred[16]{0:T(512)(128)(4,1)S(1)}, pred[16]{0:T(512)(128)(4,1)}, u32[]{:S(2)}) copy-start(pred[16]{0:T(512)(128)(4,1)} %get-tuple-element.116) | copy-start | bytes 52
  304.4 23.3 %copy-start.53 = (pred[16]{0:T(512)(128)(4,1)S(1)}, pred[16]{0:T(512)(128)(4,1)}, u32[]{:S(2)}) copy-start(pred[16]{0:T(512)(128)(4,1)} %compare_and_fusion.3) | copy-start | bytes 52
  304.4 23.3 %copy-start.54 = (pred[16]{0:T(512)(128)(4,1)S(1)}, pred[16]{0:T(512)(128)(4,1)}, u32[]{:S(2)}) copy-start(pred[16]{0:T(512)(128)(4,1)} %compare_and_fusion) | copy-start | bytes 52
  327.6 1.7 collective-permute-start.10
  331.8 5.7 collective-permute-start.11
  339.9 5.2 collective-permute-start.12
  346.7 7.6 %collective-permute-start.13 = (bf16[2,2,128,128]{3,2,1,0:T(8,128)(2,1)}, bf16[2,2,128,128]{3,2,1,0:T(8,128)(2,1)}, u32[]{:S(2)}, u32[]{:S(2)}) collective-permute-start(bf16[2,2,128,128]{3,2,1,0:T(8,128)(2,1)} %fusion.40), channel_id=1, source_target_pairs={{0,16},{2,18},{4,20},{6,22},{8,24},{10,26},{12,28},{14,30},{16,0},... | collective-permute-start | bytes 393224 | tf_op jit(solution)/shard_map/ppermute | solution.py:441
  350.0 7.0 copy-start.47
  350.0 11.8 %copy-start.12 = (bf16[8,2,128,128]{3,2,1,0:T(8,128)(2,1)S(1)}, bf16[8,2,128,128]{3,2,1,0:T(8,128)(2,1)}, u32[]{:S(2)}) copy-start(bf16[8,2,128,128]{3,2,1,0:T(8,128)(2,1)} %get-tuple-element.46) | copy-start | bytes 1572868
  355.5 5.0 collective-permute-start.14
  362.0 1.6 collective-permute-start.15
  364.7 11.9 %copy-start.19 = (bf16[128,1024]{1,0:T(8,128)(2,1)S(1)}, bf16[128,1024]{1,0:T(8,128)(2,1)}, u32[]{:S(2)}) copy-start(bf16[128,1024]{1,0:T(8,128)(2,1)} %copy-done.18) | copy-start | bytes 786436
  375.3 4.3 collective-permute-start.16
  377.5 6.2 copy-start.20
  377.5 28.9 %collective-permute-start.22 = (bf16[128,1024]{1,0:T(8,128)(2,1)}, bf16[128,1024]{1,0:T(8,128)(2,1)}, u32[]{:S(2)}, u32[]{:S(2)}) collective-permute-start(bf16[128,1024]{1,0:T(8,128)(2,1)} %copy-done.28), channel_id=1, source_target_pairs={{0,1},{1,0},{2,3},{3,2},{4,5},{5,4},{6,7},{7,6},{8,9},{9,8},{10,11... | collective-permute-start | bytes 786440 | tf_op jit(solution)/shard_map/ppermute | solution.py:441
  379.6 26.8 %copy-start.29 = (bf16[128,1024]{1,0:T(8,128)(2,1)S(1)}, bf16[128,1024]{1,0:T(8,128)(2,1)}, u32[]{:S(2)}) copy-start(bf16[128,1024]{1,0:T(8,128)(2,1)} %copy-done.28) | copy-start | bytes 786436
  382.0 31.9 %collective-permute-start.17 = (bf16[128,3072]{1,0:T(8,128)(2,1)}, bf16[128,3072]{1,0:T(8,128)(2,1)}, u32[]{:S(2)}, u32[]{:S(2)}) collective-permute-start(bf16[128,3072]{1,0:T(8,128)(2,1)} %fusion.5), channel_id=1, source_target_pairs={{0,1},{1,0},{2,3},{3,2},{4,5},{5,4},{6,7},{7,6},{8,9},{9,8},{10,11... | collective-permute-start | bytes 2359304 | tf_op jit(solution)/shard_map/ppermute | solution.py:441
  384.4 21.9 %collective-permute-start.21 = (bf16[512,128]{1,0:T(8,128)(2,1)S(1)}, bf16[512,128]{1,0:T(8,128)(2,1)S(1)}, u32[]{:S(2)}, u32[]{:S(2)}) collective-permute-start(bf16[512,128]{1,0:T(8,128)(2,1)S(1)} %bitcast.205), channel_id=1, source_target_pairs={{0,1},{1,0},{2,3},{3,2},{4,5},{5,4},{6,7},{7,6},{8,9},{9,8},{10,11... | collective-permute-start | bytes 393224 | tf_op jit(solution)/shard_map/ppermute | solution.py:441
  384.7 27.2 %collective-permute-start.18 = (bf16[128,1024]{1,0:T(8,128)(2,1)}, bf16[128,1024]{1,0:T(8,128)(2,1)S(1)}, u32[]{:S(2)}, u32[]{:S(2)}) collective-permute-start(bf16[128,1024]{1,0:T(8,128)(2,1)} %get-tuple-element.89), channel_id=1, source_target_pairs={{0,1},{1,0},{2,3},{3,2},{4,5},{5,4},{6,7},{7,6},{8,9},{9,8},{10,11... | collective-permute-start | bytes 786440 | tf_op jit(solution)/shard_map/ppermute | solution.py:441
  408.8 150.1 %reduce-scatter.8.cloned.1.call-start = ((), (), s32[]{:S(2)}) async-start(), calls=%async_computation.9 | async-start | bytes 1114112 | tf_op jit(solution)/shard_map/reduce_scatter | solution.py:605
  413.9 10.4 %copy-start.42 = (f32[128]{0:T(128)S(1)}, f32[128]{0:T(128)}, u32[]{:S(2)}) copy-start(f32[128]{0:T(128)} %copy-done.41) | copy-start | bytes 1540
  417.8 5.7 collective-permute-start.19
  429.5 5.0 collective-permute-start.20
  437.6 158.0 %reduce-scatter.14.cloned.1.call-start = ((), (), s32[]{:S(2)}) async-start(), calls=%async_computation.12 | async-start | bytes 3063808 | tf_op jit(solution)/shard_map/reduce_scatter | solution.py:605
  441.1 14.1 %collective-permute-start.25 = (bf16[1408,128]{1,0:T(8,128)(2,1)S(1)}, bf16[1408,128]{1,0:T(8,128)(2,1)S(1)}, u32[]{:S(2)}, u32[]{:S(2)}) collective-permute-start(bf16[1408,128]{1,0:T(8,128)(2,1)S(1)} %bitcast.197), channel_id=1, source_target_pairs={{0,1},{1,0},{2,3},{3,2},{4,5},{5,4},{6,7},{7,6},{8,9},{9,8},{10,11... | collective-permute-start | bytes 1081352 | tf_op jit(solution)/shard_map/ppermute | solution.py:441
  441.8 13.4 %collective-permute-start.26 = (bf16[128,1024]{1,0:T(8,128)(2,1)}, bf16[128,1024]{1,0:T(8,128)(2,1)S(1)}, u32[]{:S(2)}, u32[]{:S(2)}) collective-permute-start(bf16[128,1024]{1,0:T(8,128)(2,1)} %bitcast_convert_fusion), channel_id=1, source_target_pairs={{0,1},{1,0},{2,3},{3,2},{4,5},{5,4},{6,7},{7,6},{8,9},{9,8},{10,11... | collective-permute-start | bytes 786440 | tf_op jit(solution)/shard_map/ppermute | solution.py:441
  458.6 206.4 %reduce-scatter.6.cloned.1.call-start = ((), (), s32[]{:S(2)}) async-start(), calls=%async_computation.8 | async-start | bytes 3342336 | tf_op jit(solution)/shard_map/reduce_scatter | solution.py:605
  462.9 35.5 %copy-start.30 = (bf16[16,1,32,128]{3,2,1,0:T(8,128)(2,1)S(1)}, bf16[16,1,32,128]{3,2,1,0:T(8,128)(2,1)}, u32[]{:S(2)}) copy-start(bf16[16,1,32,128]{3,2,1,0:T(8,128)(2,1)} %get-tuple-element.94) | copy-start | bytes 393220
  462.9 287.1 %reduce-scatter.12.cloned.1.call-start = ((), (), s32[]{:S(2)}) async-start(), calls=%async_computation.11 | async-start | bytes 6127616 | tf_op jit(solution)/shard_map/reduce_scatter | solution.py:605
  463.2 35.1 %copy-start.5 = (bf16[128,2816]{1,0:T(8,128)(2,1)S(1)}, bf16[128,2816]{1,0:T(8,128)(2,1)}, u32[]{:S(2)}) copy-start(bf16[128,2816]{1,0:T(8,128)(2,1)} %copy-done.4) | copy-start | bytes 2162692
  463.2 35.1 %copy-start.7 = (bf16[128,2816]{1,0:T(8,128)(2,1)S(1)}, bf16[128,2816]{1,0:T(8,128)(2,1)}, u32[]{:S(2)}) copy-start(bf16[128,2816]{1,0:T(8,128)(2,1)} %copy-done.6) | copy-start | bytes 2162692
  464.8 33.5 %collective-permute-start.24 = (bf16[128,5632]{1,0:T(8,128)(2,1)S(1)}, bf16[128,5632]{1,0:T(8,128)(2,1)S(1)}, u32[]{:S(2)}, u32[]{:S(2)}) collective-permute-start(bf16[128,5632]{1,0:T(8,128)(2,1)S(1)} %pad_maximum_fusion.1), channel_id=1, source_target_pairs={{0,1},{1,0},{2,3},{3,2},{4,5},{5,4},{6,7},{7,6},{8,9},{9,8},{10,11... | collective-permute-start | bytes 4325384 | tf_op jit(solution)/shard_map/ppermute | solution.py:441
  465.3 33.0 %collective-permute-start.23 = (bf16[512,128]{1,0:T(8,128)(2,1)S(1)}, bf16[512,128]{1,0:T(8,128)(2,1)S(1)}, u32[]{:S(2)}, u32[]{:S(2)}) collective-permute-start(bf16[512,128]{1,0:T(8,128)(2,1)S(1)} %bitcast.203), channel_id=1, source_target_pairs={{0,1},{1,0},{2,3},{3,2},{4,5},{5,4},{6,7},{7,6},{8,9},{9,8},{10,11... | collective-permute-start | bytes 393224 | tf_op jit(solution)/shard_map/ppermute | solution.py:441
  508.6 4.7 copy-start.39
  508.6 47.4 %copy-start.52 = (f32[128]{0:T(128)S(1)}, f32[128]{0:T(128)}, u32[]{:S(2)}) copy-start(f32[128]{0:T(128)} %copy-done.51) | copy-start | bytes 1540
  (34 other events, 71.1 us)
Sparse Core Ops, SparseCore 0:
  9.6 54.5 all-gather.6
  65.7 146.5 all-gather.8
  213.8 74.4 all-gather.10
  408.9 58.4 reduce-scatter.9
  471.3 56.4 reduce-scatter.7
  531.4 64.1 reduce-scatter.13
  599.9 65.0 reduce-scatter.5
  669.5 80.4 reduce-scatter.11

commit v2 on v1

--- a/solution.py
+++ b/solution.py
@@ -433,6 +433,150 @@
     )(proj, proj, proj, halo, halo, halo, taps, taps, taps, c, b, dq, dk, dv, dst)
 
 
+def middle_kernel(
+    place, att_ref, logit_ref, tok_ref, cot_ref, gain_ref, own_out, out_a, out_b, out_c, out_d, *refs,
+):
+    own_up = refs[:4]
+    up_parts = refs[4:8]
+    own_down = refs[8]
+    down_parts = refs[9:13]
+    (out_o, hid_o, gab_o, gatt_o, glog_o, mix_o, nf_o, inner_o, ggu_o, dgain_o) = refs[13:23]
+    out_s, up_s, down_s, nf_s, gb_s, hid_s, acc_s, gnf_s = refs[23:]
+    j = pl.program_id(0)
+    y = place[0]
+    quarter = place[1]
+    half = D // 2
+    mine = pl.ds(pl.multiple_of(y * half, half), half)
+    theirs = pl.ds(pl.multiple_of((1 - y) * half, half), half)
+    order = [quarter, quarter ^ 2, quarter ^ 1, quarter ^ 3]
+    tile = own_up[0].shape[1]
+
+    def scale_of(hidden):
+        return lax.rsqrt(jnp.mean(hidden * hidden, axis=-1, keepdims=True) + 1e-05)
+
+    @pl.when(j == 0)
+    def _():
+        out_s[mine, :] = own_out[...]
+        wide = out_a.shape[1]
+        for part, q in zip((out_a, out_b, out_c, out_d), order):
+            out_s[theirs, pl.ds(pl.multiple_of(q * wide, wide), wide)] = part[...]
+        mix = (att_ref[...] * jax.nn.sigmoid(logit_ref[...])).astype(bf16)
+        mix_o[...] = mix.T
+        hidden = tok_ref[...] + nn(mix, out_s[...])
+        hid_s[...] = hidden
+        normed = (hidden * scale_of(hidden) * gain_ref[...]).astype(bf16)
+        nf_s[...] = normed
+        nf_o[...] = normed.T
+        gb_s[...] = cot_ref[...].astype(bf16)
+        acc_s[...] = jnp.zeros_like(acc_s)
+        gnf_s[...] = jnp.zeros_like(gnf_s)
+
+    for i in range(4):
+        up_s[mine, i * tile : (i + 1) * tile] = own_up[i][...]
+    for part, q in zip(up_parts, order):
+        slot = (q >> 1) * 2 + ((q & 1) ^ y)
+        up_s[theirs, pl.ds(pl.multiple_of(slot * tile, tile), tile)] = part[...]
+    down_s[:tile, :] = own_down[...]
+    wide = down_parts[0].shape[1]
+    for part, q in zip(down_parts, order):
+        down_s[tile:, pl.ds(pl.multiple_of(q * wide, wide), wide)] = part[...]
+    product = nn(nf_s[...], up_s[...])
+    gate, up = product[:, : 2 * tile], product[:, 2 * tile :]
+    ginner = nt(gb_s[...], down_s[...])
+    sig = jax.nn.sigmoid(gate)
+    silu = gate * sig
+    inner = (silu * up).astype(bf16)
+    ggate = (ginner * up * (sig * (1.0 + gate * (1.0 - sig)))).astype(bf16)
+    gup = (ginner * silu).astype(bf16)
+    ggu = jnp.concatenate([ggate, gup], axis=1)
+    acc_s[...] += nn(inner, down_s[...])
+    gnf_s[...] += nt(ggu, up_s[...])
+    inner_t = inner.T
+    inner_o[y] = inner_t[:tile]
+    inner_o[1 - y] = inner_t[tile:]
+    ggu_o[y] = ggate[:, :tile]
+    ggu_o[1 - y] = ggate[:, tile:]
+    ggu_o[2 + y] = gup[:, :tile]
+    ggu_o[3 - y] = gup[:, tile:]
+
+    @pl.when(j == pl.num_programs(0) - 1)
+    def _():
+        hidden = hid_s[...]
+        out_o[...] = hidden + acc_s[...]
+        scale = scale_of(hidden)
+        unit = hidden * scale
+        gnf = gnf_s[...]
+        dgain_o[...] = jnp.sum(gnf * unit, axis=0, keepdims=True)
+        gunit = gnf * gain_ref[...]
+        ghid = cot_ref[...] + scale * (gunit - unit * jnp.mean(gunit * unit, axis=-1, keepdims=True))
+        hid_o[...] = ghid
+        low = ghid.astype(bf16)
+        gab_o[...] = low
+        gmix = nt(low, out_s[...])
+        sig = jax.nn.sigmoid(logit_ref[...])
+        gatt = gmix * sig
+        gatt_o[...] = gatt
+        glog_o[...] = (gatt * att_ref[...] * (1.0 - sig)).astype(bf16)
+
+
+def middle(place, att, logit, tok, cot, gain, out_parts, up_parts, down_parts):
+    tokens = att.shape[0]
+    tile = 128
+    share = FF // 2 // tile
+    half = D // 2
+
+    def full(*shape):
+        return pl.BlockSpec(shape, lambda j, s: (0,) * len(shape))
+
+    rows = full(tokens, D)
+    own_up = [
+        pl.BlockSpec((half, tile), lambda j, s: (0, s[0] * share + j)),
+        pl.BlockSpec((half, tile), lambda j, s: (0, (1 - s[0]) * share + j)),
+        pl.BlockSpec((half, tile), lambda j, s: (0, (2 + s[0]) * share + j)),
+        pl.BlockSpec((half, tile), lambda j, s: (0, (3 - s[0]) * share + j)),
+    ]
+    up_specs = [pl.BlockSpec((half, tile), lambda j, s: (0, j))] * 4
+    own_down = pl.BlockSpec((tile, D), lambda j, s: (j, 0))
+    down_specs = [pl.BlockSpec((tile, D // 4), lambda j, s: (j, 0))] * 4
+    act = jax.ShapeDtypeStruct((tokens, D), f32)
+    low = jax.ShapeDtypeStruct((tokens, D), bf16)
+    turned = jax.ShapeDtypeStruct((D, tokens), bf16)
+    return pl.pallas_call(
+        middle_kernel,
+        grid_spec=pltpu.PrefetchScalarGridSpec(
+            num_scalar_prefetch=1,
+            grid=(share,),
+            in_specs=[rows] * 4 + [full(1, D), full(half, D)] + [full(half, D // 4)] * 4
+            + own_up + up_specs + [own_down] + down_specs,
+            out_specs=[
+                rows, rows, rows, rows, rows, full(D, tokens), full(D, tokens),
+                pl.BlockSpec((2, tile, tokens), lambda j, s: (0, j, 0)),
+                pl.BlockSpec((4, tokens, tile), lambda j, s: (0, 0, j)),
+                full(1, D),
+            ],
+            scratch_shapes=[
+                pltpu.VMEM((D, D), bf16),
+                pltpu.VMEM((D, 4 * tile), bf16),
+                pltpu.VMEM((2 * tile, D), bf16),
+                pltpu.VMEM((tokens, D), bf16),
+                pltpu.VMEM((tokens, D), bf16),
+                pltpu.VMEM((tokens, D), f32),
+                pltpu.VMEM((tokens, D), f32),
+                pltpu.VMEM((tokens, D), f32),
+            ],
+        ),
+        out_shape=[
+            act, act, low, act, low, turned, turned,
+            jax.ShapeDtypeStruct((2, FF // 2, tokens), bf16),
+            jax.ShapeDtypeStruct((4, tokens, FF // 2), bf16),
+            jax.ShapeDtypeStruct((1, D), f32),
+        ],
+        compiler_params=pltpu.CompilerParams(vmem_limit_bytes=VMEM_LIMIT),
+        cost_estimate=pl.CostEstimate(flops=5_000_000_000, bytes_accessed=24_000_000, transcendentals=600_000),
+        name="middle",
+    )(place, att, logit, tok, cot, gain, *out_parts, *[up_parts[0]] * 4, *up_parts[1:], *down_parts)
+
+
 def neighbour(axis, bit):
     return [(i, i ^ bit) for i in range(lax.axis_size(axis))]
 
@@ -448,6 +592,19 @@
 
 def pick(x, index, axis=0):
     return lax.dynamic_index_in_dim(x, index, axis, keepdims=False)
+
+
+def collected(row, axis):
+    here = lax.axis_index(axis)
+    for level in range(lax.axis_size(axis).bit_length() - 1):
+        other = partner(row, axis, 1 << level)
+        late = ((here >> level) & 1) == 1
+        row = jnp.where(late, jnp.concatenate([other, row]), jnp.concatenate([row, other]))
+    return row
+
+
+def after(value, *others):
+    return lax.optimization_barrier((value,) + others)[0]
 
 
 def entering(own, logs, axis, reverse):
@@ -510,12 +667,40 @@
     return before.astype(bf16)
 
 
+def gathered(shard):
+    q = lax.axis_index("ctx") % 4
+    wide = shard.shape[1] // 4
+    direct = partner(lax.dynamic_slice_in_dim(shard, q * wide, wide, 1), "fsdp")
+    across = partner(direct, "ctx", 2)
+    return shard, direct, across, partner(direct, "ctx", 1), partner(across, "ctx", 1)
+
+
+def scattered(left, right):
+    peers = lax.axis_size("ctx")
+    here = lax.axis_index("ctx")
+    bit = here % 2
+    shape = (peers // 2, left.shape[0] // peers, right.shape[1])
+    halves = left.reshape(peers // 2, 2, left.shape[0] // peers, left.shape[1])
+    sent = nn(pick(halves, 1 - bit, 1).reshape(-1, left.shape[1]), right).astype(bf16)
+    kept = nn(pick(halves, bit, 1).reshape(-1, left.shape[1]), right)
+    now = (kept + partner(sent, "ctx", 1).astype(f32)).astype(bf16).reshape(shape)
+    return halved(now, "ctx", 1)
+
+
+def halved(now, axis, level):
+    here = lax.axis_index(axis)
+    levels = lax.axis_size(axis).bit_length() - 1
+    kind = now.dtype
+    for level in range(level, levels):
+        bit = (here >> level) & 1
+        pairs = now.reshape((now.shape[0] // 2, 2) + now.shape[1:])
+        total = pick(pairs, bit, 1).astype(f32) + partner(pick(pairs, 1 - bit, 1), axis, 1 << level).astype(f32)
+        now = total if level == levels - 1 else total.astype(kind)
+    return now[0]
+
+
 def rms_scale(values, gain):
     return values * lax.rsqrt(jnp.mean(values * values, axis=-1, keepdims=True) + 1e-05) * gain
-
-
-def right_product(left, right):
-    return nt(left, right)
 
 
 def local(
@@ -537,81 +722,59 @@
     y = lax.axis_index("fsdp")
     peers = lax.axis_size("ctx")
     owners = peers * 2
-    small = jnp.concatenate(
-        [conv_taps.reshape(-1), gain_attn, gain_ffn, ridge_terms]
-    )
-    both = lax.all_gather(small, "fsdp", axis=0)
+    place = jnp.stack([y, lax.axis_index("ctx") % 4]).astype(jnp.int32)
+    small = jnp.concatenate([conv_taps.reshape(-1), gain_attn, gain_ffn, ridge_terms])
+    theirs = partner(small, "fsdp")
+    both = jnp.where(y == 0, jnp.stack([small, theirs]), jnp.stack([theirs, small])).astype(f32)
     split = KW * 3 * D // 2
-    taps = both[:, :split].reshape(2, KW, 3 * D // 2).transpose(1, 0, 2).reshape(KW, 3 * D).astype(f32)
-    rest = both[:, split:].reshape(2, 3, D // 2).transpose(1, 0, 2).reshape(3, D).astype(f32)
-    gain_first, gain_second = rest[0], rest[1]
+    taps = both[:, :split].reshape(2, KW, 3 * D // 2).transpose(1, 0, 2).reshape(KW, 3 * D)
+    rest = both[:, split:].reshape(2, 3, D // 2).transpose(1, 0, 2).reshape(3, D)
+    gain_first, gain_second = rest[0], rest[1:2]
     ridge = rest[2].reshape(HEADS, HEAD_DIM)
-    out_full = lax.all_gather(out_weight, "fsdp", axis=0, tiled=True)
-    up_full = lax.all_gather(up_weight, "fsdp", axis=0, tiled=True)
-    down_full = lax.all_gather(down_weight, "fsdp", axis=0, tiled=True)
     cumulative = jnp.cumsum(jnp.log(forget[0]).T, axis=-1)
     strength = (1.0 - forget[0]).T
-    logs = lax.all_gather(cumulative[:, -1], "ctx", axis=0)
+    logs = collected(cumulative[:, -1][None], "ctx")
 
     normed_low = rms_scale(tokens, gain_first).astype(bf16)
     halves = normed_low.reshape(rows, 2, D // 2)
     mine = pick(halves, y, 1)
     theirs = partner(pick(halves, 1 - y, 1), "fsdp")
-    lent = nn(theirs, qkv_weight).astype(bf16)
-    projected = nn(mine, qkv_weight) + partner(lent, "fsdp").astype(f32)
-    lent = nn(theirs, gate_weight).astype(bf16)
-    gate_logit = nn(mine, gate_weight) + partner(lent, "fsdp").astype(f32)
+    lent = partner(nn(theirs, qkv_weight).astype(bf16), "fsdp")
+    projected = nn(mine, qkv_weight) + lent.astype(f32)
     tail = shifted(projected[rows - (KW - 1) :].astype(bf16), "ctx", 1).astype(f32)
     halo = jnp.concatenate([jnp.zeros((8 - KW + 1, 3 * D), f32), tail], axis=0)
+    out_parts = gathered(after(out_weight, theirs))
+    up_parts = gathered(after(up_weight, lent))
+    down_parts = gathered(after(down_weight, up_parts[1]))
+    lent_gate = partner(nn(after(theirs, lent), gate_weight).astype(bf16), "fsdp")
+    gate_logit = nn(mine, gate_weight) + lent_gate.astype(f32)
     queries, keys, values, own = features(projected, halo, taps, cumulative, strength)
     states = entering(own, logs, "ctx", False)
     attended, x, p_all, m_all, scal = solve(queries, keys, values, states, cumulative, strength, ridge)
 
-    gate_sig = jax.nn.sigmoid(gate_logit)
-    gated_mix = (attended * gate_sig).astype(bf16)
-    hidden = tokens + nn(gated_mix, out_full)
-    normed_ffn, second_pull = jax.vjp(rms_scale, hidden, gain_second)
-    normed_ffn_low = normed_ffn.astype(bf16)
-    gate_up = nn(normed_ffn_low, up_full)
-    gate_part = gate_up[:, :FF]
-    up_part = gate_up[:, FF:]
-    inner = (jax.nn.silu(gate_part) * up_part).astype(bf16)
-    output = hidden + nn(inner, down_full)
-    grad_output = cotangent[0]
-    grad_branch = grad_output.astype(bf16)
-    grad_inner = nt(grad_branch, down_full)
-    gate_sigmoid = jax.nn.sigmoid(gate_part)
-    grad_gate_part = grad_inner * up_part * gate_sigmoid * (1.0 + gate_part * (1.0 - gate_sigmoid))
-    grad_up_part = grad_inner * gate_part * gate_sigmoid
-    grad_gate_up = jnp.concatenate([grad_gate_part, grad_up_part], axis=1).astype(bf16)
-    grad_normed_ffn = nt(grad_gate_up, up_full)
-    grad_hidden_norm, grad_second_gain = second_pull(grad_normed_ffn)
-    grad_hidden = grad_output + grad_hidden_norm
-    grad_attn_branch = grad_hidden.astype(bf16)
-    grad_mixed = nt(grad_attn_branch, out_full)
-    grad_attended = grad_mixed * gate_sig
-    grad_logit = (grad_mixed * attended * gate_sig * (1.0 - gate_sig)).astype(bf16)
+    (output, grad_hidden, grad_attn_branch, grad_attended, grad_logit, mix_t, normed_ffn_t, inner_t,
+     grad_gate_up, grad_second_gain) = middle(
+        place, attended, gate_logit, tokens, cotangent[0], gain_second, out_parts, up_parts, down_parts
+    )
+    grad_branch = cotangent[0].astype(bf16)
 
     def parity(left):
-        flat = left.T.reshape(peers, 2, left.shape[1] // owners, rows)
+        flat = left.reshape(peers, 2, left.shape[0] // owners, rows)
         kept = pick(flat, y, 1).reshape(-1, rows)
         sent = pick(flat, 1 - y, 1).reshape(-1, rows)
         return jnp.concatenate([kept, partner(sent, "fsdp")], axis=1)
 
-    def share(right):
-        return jnp.concatenate([right, partner(right, "fsdp")], axis=0)
-
-    def reduced(left, right):
-        return lax.psum_scatter(
-            nn(left, right).astype(bf16), "ctx", scatter_dimension=0, tiled=True
-        ).astype(f32)
-
-    grad_down = reduced(parity(inner), share(grad_branch))
-    grad_up = reduced(parity(normed_ffn_low), share(grad_gate_up))
-    grad_out = reduced(parity(gated_mix), share(grad_attn_branch))
+    def share(right, axis=0):
+        return jnp.concatenate([right, partner(right, "fsdp")], axis=axis)
+
+    both_up = share(grad_gate_up, 1)
+    normed_ffn_p = parity(normed_ffn_t)
+    grad_up = jnp.concatenate([scattered(normed_ffn_p, both_up[i]) for i in range(4)], axis=1)
+    grad_down = scattered(parity(inner_t.reshape(FF, rows)), share(grad_branch))
+    grad_out = scattered(parity(mix_t), share(grad_attn_branch))
     both_logit = share(grad_logit)
-    normed_parity = parity(normed_low)
-    grad_gate = reduced(normed_parity, both_logit)
+    normed_parity = parity(normed_low.T)
+    grad_gate = scattered(normed_parity, both_logit)
 
     dq, dk, dv, dst, dridge = adjoint(
         grad_attended, keys, values, states, cumulative, strength, ridge, x, p_all, m_all, scal
@@ -624,7 +787,7 @@
     from_next = shifted(grad_before.astype(bf16), "ctx", -1).astype(f32)
     grad_projected = grad_projected + jnp.pad(from_next, ((rows - KW + 1, 0), (0, 0)))
     both_projected = share(grad_projected.astype(bf16))
-    grad_qkv = reduced(normed_parity, both_projected)
+    grad_qkv = scattered(normed_parity, both_projected)
     lent = nt(both_projected, qkv_weight) + nt(both_logit, gate_weight)
     back = partner(lent[rows:].astype(bf16), "fsdp").astype(f32)
     kept = lent[:rows]
@@ -635,18 +798,19 @@
     grad_tokens_norm, grad_first_gain = first_pull(grad_normed)
     grad_tokens = grad_hidden + grad_tokens_norm
     width = 3 * D // owners
+    size = D // owners
     vector = jnp.concatenate(
         [
             grad_taps.reshape(KW, owners, width).transpose(1, 0, 2).reshape(owners, KW * width),
-            grad_first_gain.reshape(owners, D // owners),
-            grad_second_gain.reshape(owners, D // owners),
-            dridge.reshape(owners, D // owners),
+            grad_first_gain.reshape(owners, size),
+            grad_second_gain.reshape(owners, size),
+            dridge.reshape(owners, size),
         ],
         axis=1,
-    )
-    vector = lax.psum_scatter(vector, ("ctx", "fsdp"), scatter_dimension=0, tiled=True)[0]
+    ).reshape(peers, 2, -1)
+    vector = pick(vector, y, 1) + partner(pick(vector, 1 - y, 1), "fsdp")
+    vector = halved(vector, "ctx", 0)
     taps_end = KW * width
-    size = D // owners
     return (
         output[None],
         grad_tokens[None],

time: 762 us -> 500 us (0.66)
  waiting for transfers between devices: 420 us -> 197 us
  blocking collectives: 78.1 us -> 0 us
  starting transfers between devices: 26.8 us -> 83.4 us
  matrix products: 58.7 us -> 27 us
  Pallas kernels: 56.5 us -> 77.5 us
  between operations: 15.7 us -> 2.14 us
  local copies, waits for them, and re-layouts: 48.4 us -> 59.6 us
    reduce_scatter x5 -> x0, waiting for transfers between devices: 186 us -> none  [reduced(): lax.psum_scatter(nn(left, right).astype(bf16), 'ctx', scatter_dimension=0...]
    all_gather x3 -> x0, waiting for transfers between devices: 97.9 us -> none  [the longest x1 68.3 us: local(): down_full = lax.all_gather(down_weight, 'fsdp', axis=0, tiled=True)]
    unnamed x2 -> x0, blocking collectives: 72.6 us -> none
    ppermute x25 -> x79, waiting for transfers between devices: 134 us -> 197 us  [partner(): return lax.ppermute(x, axis, neighbour(axis, bit))]
    ppermute x25 -> x79, starting transfers between devices: 23.7 us -> 80.4 us  [partner(): return lax.ppermute(x, axis, neighbour(axis, bit))]
    pallas_call x0 -> x1, Pallas kernels: none -> 21.6 us  [middle(): pl.pallas_call(middle_kernel, grid_spec=pltpu.PrefetchScalarGridSpec(num_...]
    dot_general x12 -> x20, matrix products: 40.4 us -> 24.4 us  [nn(): lax.dot_general(a, b, (((1,), (0,)), ((), ())), preferred_element_type=f32)]
    dot_general x5 -> x2, matrix products: 18.3 us -> 2.53 us  [nt(): lax.dot_general(a, b, (((1,), (1,)), ((), ())), preferred_element_type=f32)]
  transfers between devices with their start and end apart: 35 -> 81, of which waited for: 23 -> 34; matrix products, arithmetic and copies ran while one was open for 16% -> 26% of each run, Pallas kernels for 4% -> 16%
where the time goes in v2:
time: 500 us; the launch traced here: 497 us
  waiting for transfers between devices  197 us (39%)
  starting transfers between devices  83.4 us (17%)
  Pallas kernels  77.5 us (16%)
  local copies, waits for them, and re-layouts  59.6 us (12%)
  other arithmetic  49.9 us (10%)
  matrix products  27 us (5%)
    ppermute x79, waiting for transfers between devices, partner(): return lax.ppermute(x, axis, neighbour(axis, bit))  197 us
    ppermute x79, starting transfers between devices, partner(): return lax.ppermute(x, axis, neighbour(axis, bit))  80.4 us
    dot_general x20, matrix products, nn(): lax.dot_general(a, b, (((1,), (0,)), ((), ())), preferred_element_type=f32)  24.4 us
    pallas_call x1, Pallas kernels, middle(): pl.pallas_call(middle_kernel, grid_spec=pltpu.PrefetchScalarGridSpec(num_...  21.6 us
    pallas_call x1, Pallas kernels, adjoint(): pl.pallas_call(adjoint_kernel, grid=(HEADS // GROUP,), in_specs=[pl.Block...  21.3 us
    pallas_call x1, Pallas kernels, solve(): pl.pallas_call(solve_kernel, grid=(HEADS // GROUP,), in_specs=[grouped(HE...  19.6 us
    unnamed x146, local copies, waits for them, and re-layouts  16.3 us
  transfers between devices with their start and end apart: 81, of which 34 were waited for; matrix products, arithmetic and copies ran while one was open for 26% of the time, Pallas kernels for 16%

profile of v2, /device:TPU:0, one launch (start us, length us, event | category | flops | bytes accessed | tf_op | source)
XLA Modules:
  0.0 497.1 jit_solution(14806688824395767229)
XLA Ops:
  6.2 2.5 collective-permute-start
  12.6 2.0 copy.52
  18.6 4.8 collective-permute-done.1
  27.7 1.7 collective-permute-start.5
  29.5 1.9 collective-permute-done.5
  31.3 1.9 collective-permute-start.6
  34.6 9.3 %collective-permute-done.2 = bf16[128,3072]{1,0:T(8,128)(2,1)} collective-permute-done((bf16[128,3072]{1,0:T(8,128)(2,1)}, bf16[128,3072]{1,0:T(8,128)(2,1)}, u32[]{:S(2)}, u32[]{:S(2)}) %collective-permute-start.2) | collective-permute-done | bytes 786464 | tf_op jit(solution)/shard_map/ppermute | solution.py:585
  43.9 1.8 convert_add_fusion.1.pq.pk.pv
  48.3 2.6 constant_dynamic-slice_fusion.27
  52.3 6.8 %features.1 = (f32[8,128,128]{2,1,0:T(8,128)}, bf16[8,128,128]{2,1,0:T(8,128)(2,1)}, bf16[8,128,128]{2,1,0:T(8,128)(2,1)}, bf16[8,2,128,128]{3,2,1,0:T(8,128)(2,1)}) custom-call(f32[128,3072]{1,0:T(8,128)} %copy-done.1, f32[128,3072]{1,0:T(8,128)} %copy-done.1, f32[128,3072]{1,0:T(8,128)} %copy-done.1, f32[8,3072]{1,0:T(8,128)} %pad_convert_fusion.hq.hk.hv, ...), custom_call_target="tpu_custom_call" | custom-call | flops 70000000 | bytes 4000000 | tf_op jit(solution)/shard_map/features/pallas_call | solution.py:96
  60.7 1.8 collective-permute-start.8
  62.6 2.7 collective-permute-start.7
  65.2 1.9 collective-permute-done.7
  97.8 1.8 collective-permute-start.11
  102.4 2.7 collective-permute-done.11
  107.9 27.0 %collective-permute-done.12 = bf16[2,2,128,128]{3,2,1,0:T(8,128)(2,1)S(1)} collective-permute-done((bf16[2,2,128,128]{3,2,1,0:T(8,128)(2,1)S(1)}, bf16[2,2,128,128]{3,2,1,0:T(8,128)(2,1)S(1)}, u32[]{:S(2)}, u32[]{:S(2)}) %collective-permute-start.12) | collective-permute-done | bytes 131104 | tf_op jit(solution)/shard_map/ppermute | solution.py:585
  137.5 4.3 collective-permute-done.13
  142.0 8.7 %collective-permute-done.24.refs_10_ = bf16[1408,256]{1,0:T(8,128)(2,1)} collective-permute-done((bf16[1408,256]{1,0:T(8,128)(2,1)}, bf16[1408,256]{1,0:T(8,128)(2,1)}, u32[]{:S(2)}, u32[]{:S(2)}) %collective-permute-start.24) | collective-permute-done | bytes 720928 | tf_op jit(solution)/shard_map/ppermute | solution.py:585
  153.4 19.6 %solve.1 = (f32[128,1024]{1,0:T(8,128)}, bf16[8,128,128]{2,1,0:T(8,128)(2,1)}, f32[8,8,128,128]{3,2,1,0:T(8,128)}, f32[8,8,128,128]{3,2,1,0:T(8,128)}, f32[8,16,128]{2,1,0:T(8,128)}) custom-call(f32[8,128,128]{2,1,0:T(8,128)} %get-tuple-element.48.q_ref, bf16[8,128,128]{2,1,0:T(8,128)(2,1)} %get-tuple-element.49.k_ref, ...), custom_call_target="tpu_custom_call" | custom-call | flops 900000000 | bytes 12000000 | tf_op jit(solution)/shard_map/solve/pallas_call | solution.py:180
  175.0 21.6 %middle.1 = (f32[128,1024]{1,0:T(8,128)}, f32[128,1024]{1,0:T(8,128)}, bf16[128,1024]{1,0:T(8,128)(2,1)}, f32[128,1024]{1,0:T(8,128)}, bf16[128,1024]{1,0:T(8,12...) custom-call(s32[2]{0:T(128)} %pad_add_fusion.place, ...), custom_call_target="tpu_custom_call" | custom-call | flops 5000000000 | bytes 24000000 | tf_op jit(solution)/shard_map/middle/pallas_call | solution.py:544
  196.6 21.3 %adjoint.1 = (f32[8,128,128]{2,1,0:T(8,128)}, f32[8,128,128]{2,1,0:T(8,128)}, f32[8,128,128]{2,1,0:T(8,128)}, bf16[8,2,128,128]{3,2,1,0:T(8,128)(2,1)}, f32[8,1,128]{2,1,0:T(1,128)}) custom-call(f32[128,1024]{1,0:T(8,128)} %get-tuple-element.59.ga_ref, bf16[8,128,128]{2,1,0:T(8,128)(2,1)} %get-tuple-element.49.k_ref, ...), custom_call_target="tpu_custom_call" | custom-call | flops 1800000000 | bytes 12000000 | tf_op jit(solution)/shard_map/adjoint/pallas_call | solution.py:317
  217.9 1.7 dynamic-slice_bitcast_fusion.10
  226.4 1.8 constant_dynamic-update-slice_fusion.2
  230.7 1.9 reduce.11
  243.4 31.1 %collective-permute-done.47 = bf16[128,1024]{1,0:T(8,128)(2,1)S(1)} collective-permute-done((bf16[128,1024]{1,0:T(8,128)(2,1)}, bf16[128,1024]{1,0:T(8,128)(2,1)S(1)}, u32[]{:S(2)}, u32[]{:S(2)}) %collective-permute-start.47) | collective-permute-done | bytes 262176 | tf_op jit(solution)/shard_map/ppermute | solution.py:585
  276.4 4.2 collective-permute-done.70
  281.5 1.8 collective-permute-start.30
  283.3 2.7 convolution_convert_fusion.6
  286.0 3.2 collective-permute-done.30
  291.9 3.4 collective-permute-done.31
  302.3 8.3 %features_back.1 = (f32[128,1024]{1,0:T(8,128)}, f32[128,1024]{1,0:T(8,128)}, f32[128,1024]{1,0:T(8,128)}, f32[8,1024]{1,0:T(8,128)}, f32[8,1024]{1,0:T(8,128)},...) custom-call(f32[128,3072]{1,0:T(8,128)} %copy-done.1, f32[128,3072]{1,0:T(8,128)} %copy-done.1, ...), custom_call_target="tpu_custom_call" | custom-call | flops 100000000 | bytes 8000000 | tf_op jit(solution)/shard_map/features_back/pallas_call | solution.py:422
  317.7 4.0 collective-permute-start.51
  323.5 1.9 collective-permute-done.51
  331.7 11.2 %collective-permute-done.34 = bf16[128,3072]{1,0:T(8,128)(2,1)S(1)} collective-permute-done((bf16[128,3072]{1,0:T(8,128)(2,1)S(1)}, bf16[128,3072]{1,0:T(8,128)(2,1)S(1)}, u32[]{:S(2)}, u32[]{:S(2)}) %collective-permute-start.34) | collective-permute-done | bytes 786464 | tf_op jit(solution)/shard_map/ppermute | solution.py:585
  346.4 2.9 collective-permute-done.36
  353.5 3.3 add_convert_fusion
  360.1 2.0 dynamic-slice_bitcast_fusion.1
  367.6 2.3 fusion.25
  371.1 2.1 collective-permute-start.80
  373.9 1.8 collective-permute-done.80
  378.5 2.3 collective-permute-done.37
  380.8 2.0 collective-permute-start.73
  391.7 2.1 collective-permute-start.59
  395.4 11.6 %collective-permute-done.55 = bf16[4,32,1408]{2,1,0:T(8,128)(2,1)S(1)} collective-permute-done((bf16[4,32,1408]{2,1,0:T(8,128)(2,1)S(1)}, bf16[4,32,1408]{2,1,0:T(8,128)(2,1)S(1)}, u32[]{:S(2)}, u32[]{:S(2)}) %collective-permute-start.55) | collective-permute-done | bytes 360480 | tf_op jit(solution)/shard_map/ppermute | solution.py:585
  406.9 2.5 collective-permute-start.63
  409.5 5.1 %collective-permute-done.59 = bf16[4,32,1408]{2,1,0:T(8,128)(2,1)S(1)} collective-permute-done((bf16[4,32,1408]{2,1,0:T(8,128)(2,1)S(1)}, bf16[4,32,1408]{2,1,0:T(8,128)(2,1)S(1)}, u32[]{:S(2)}, u32[]{:S(2)}) %collective-permute-start.59) | collective-permute-done | bytes 360480 | tf_op jit(solution)/shard_map/ppermute | solution.py:585
  414.7 2.5 collective-permute-start.67
  417.2 5.0 collective-permute-done.63
  422.2 2.0 collective-permute-start.56
  424.4 2.6 collective-permute-done.67
  429.5 1.7 collective-permute-start.68
  432.1 2.3 collective-permute-done.60
  436.1 3.2 collective-permute-done.64
  440.0 5.1 %collective-permute-done.68 = bf16[2,32,1408]{2,1,0:T(8,128)(2,1)S(1)} collective-permute-done((bf16[2,32,1408]{2,1,0:T(8,128)(2,1)S(1)}, bf16[2,32,1408]{2,1,0:T(8,128)(2,1)S(1)}, u32[]{:S(2)}, u32[]{:S(2)}) %collective-permute-start.68) | collective-permute-done | bytes 180256 | tf_op jit(solution)/shard_map/ppermute | solution.py:585
  445.2 4.3 collective-permute-done.57
  449.5 3.6 collective-permute-start.65
  453.1 1.8 collective-permute-done.61
  455.0 2.8 collective-permute-done.65
  457.8 3.5 collective-permute-done.69
  464.4 2.6 collective-permute-start.44
  467.0 11.3 %collective-permute-done.39 = bf16[4,32,3072]{2,1,0:T(8,128)(2,1)S(1)} collective-permute-done((bf16[4,32,3072]{2,1,0:T(8,128)(2,1)S(1)}, bf16[4,32,3072]{2,1,0:T(8,128)(2,1)S(1)}, u32[]{:S(2)}, u32[]{:S(2)}) %collective-permute-start.39) | collective-permute-done | bytes 786464 | tf_op jit(solution)/shard_map/ppermute | solution.py:585
  478.7 2.4 collective-permute-start.45
  481.9 6.3 %collective-permute-done.40 = bf16[2,32,3072]{2,1,0:T(8,128)(2,1)S(1)} collective-permute-done((bf16[2,32,3072]{2,1,0:T(8,128)(2,1)S(1)}, bf16[2,32,3072]{2,1,0:T(8,128)(2,1)S(1)}, u32[]{:S(2)}, u32[]{:S(2)}) %collective-permute-start.40) | collective-permute-done | bytes 393248 | tf_op jit(solution)/shard_map/ppermute | solution.py:585
  489.3 7.0 %collective-permute-done.41 = bf16[1,32,3072]{2,1,0:T(8,128)(2,1)S(1)} collective-permute-done((bf16[1,32,3072]{2,1,0:T(8,128)(2,1)S(1)}, bf16[1,32,3072]{2,1,0:T(8,128)(2,1)S(1)}, u32[]{:S(2)}, u32[]{:S(2)}) %collective-permute-start.41) | collective-permute-done | bytes 196640 | tf_op jit(solution)/shard_map/ppermute | solution.py:585
  (464 shorter events, 159.3 us)
Async XLA Ops:
  2.5 24.4 %collective-permute-start.4 = (f32[1,8]{1,0:T(1,128)S(1)}, f32[1,8]{1,0:T(1,128)}, u32[]{:S(2)}, u32[]{:S(2)}) collective-permute-start(f32[1,8]{1,0:T(1,128)S(1)} %bitcast.440), channel_id=1, source_target_pairs={{0,2},{2,0},{4,6},{6,4},{8,10},{10,8},{12,14},{14,12},{16,18},{18,... | collective-permute-start | bytes 104 | tf_op jit(solution)/shard_map/ppermute | solution.py:585
  6.2 8.4 %collective-permute-start = (bf16[7680]{0:T(1024)(128)(2,1)S(1)}, bf16[7680]{0:T(1024)(128)(2,1)S(1)}, u32[]{:S(2)}, u32[]{:S(2)}) collective-permute-start(bf16[7680]{0:T(1024)(128)(2,1)S(1)} %constant_dynamic-update-slice_fusion.7), channel_id=1, source_target_pairs={{0,1},{1,0},{2,3},{3,2},{4,5},{5,4},{6,7},{7,6},{8,9},{9,8},{10,11... | collective-permute-start | bytes 46088 | tf_op jit(solution)/shard_map/ppermute | solution.py:585
  24.8 19.2 %collective-permute-start.2 = (bf16[128,3072]{1,0:T(8,128)(2,1)}, bf16[128,3072]{1,0:T(8,128)(2,1)}, u32[]{:S(2)}, u32[]{:S(2)}) collective-permute-start(bf16[128,3072]{1,0:T(8,128)(2,1)} %convolution_convert_fusion.1), channel_id=1, source_target_pairs={{0,1},{1,0},{2,3},{3,2},{4,5},{5,4},{6,7},{7,6},{8,9},{9,8},{10,11... | collective-permute-start | bytes 2359304 | tf_op jit(solution)/shard_map/ppermute | solution.py:585
  31.3 31.2 %collective-permute-start.6 = (f32[4,8]{1,0:T(4,128)S(1)}, f32[4,8]{1,0:T(4,128)S(1)}, u32[]{:S(2)}, u32[]{:S(2)}) collective-permute-start(f32[4,8]{1,0:T(4,128)S(1)} %maximum_select_fusion.3), channel_id=1, source_target_pairs={{0,8},{2,10},{4,12},{6,14},{8,0},{10,2},{12,4},{14,6},{16,24},{18,... | collective-permute-start | bytes 392 | tf_op jit(solution)/shard_map/ppermute | solution.py:585
  51.0 44.5 %collective-permute-start.19 = (bf16[512,1408]{1,0:T(8,128)(2,1)}, bf16[512,1408]{1,0:T(8,128)(2,1)}, u32[]{:S(2)}, u32[]{:S(2)}) collective-permute-start(bf16[512,1408]{1,0:T(8,128)(2,1)} %constant_dynamic-slice_fusion.27), channel_id=1, source_target_pairs={{0,1},{1,0},{2,3},{3,2},{4,5},{5,4},{6,7},{7,6},{8,9},{9,8},{10,11... | collective-permute-start | bytes 4325384 | tf_op jit(solution)/shard_map/ppermute | solution.py:585
  60.7 7.2 %collective-permute-start.8 = (bf16[4,2,128,128]{3,2,1,0:T(8,128)(2,1)}, bf16[4,2,128,128]{3,2,1,0:T(8,128)(2,1)S(1)}, u32[]{:S(2)}, u32[]{:S(2)}) collective-permute-start(bf16[4,2,128,128]{3,2,1,0:T(8,128)(2,1)} %dynamic-slice_bitcast_fusion.11), channel_id=1, source_target_pairs={{0,2},{2,0},{4,6},{6,4},{8,10},{10,8},{12,14},{14,12},{16,18},{18,... | collective-permute-start | bytes 786440 | tf_op jit(solution)/shard_map/ppermute | solution.py:585
  74.9 19.9 %collective-permute-start.15 = (bf16[512,256]{1,0:T(8,128)(2,1)}, bf16[512,256]{1,0:T(8,128)(2,1)}, u32[]{:S(2)}, u32[]{:S(2)}) collective-permute-start(bf16[512,256]{1,0:T(8,128)(2,1)} %constant_dynamic-slice_fusion.28), channel_id=1, source_target_pairs={{0,1},{1,0},{2,3},{3,2},{4,5},{5,4},{6,7},{7,6},{8,9},{9,8},{10,11... | collective-permute-start | bytes 786440 | tf_op jit(solution)/shard_map/ppermute | solution.py:585
  78.8 18.1 %collective-permute-start.10 = (bf16[2,2,128,128]{3,2,1,0:T(8,128)(2,1)}, bf16[2,2,128,128]{3,2,1,0:T(8,128)(2,1)S(1)}, u32[]{:S(2)}, u32[]{:S(2)}) collective-permute-start(bf16[2,2,128,128]{3,2,1,0:T(8,128)(2,1)} %fusion.35), channel_id=1, source_target_pairs={{0,8},{2,10},{4,12},{6,14},{8,0},{10,2},{12,4},{14,6},{16,24},{18,... | collective-permute-start | bytes 393224 | tf_op jit(solution)/shard_map/ppermute | solution.py:585
  94.8 41.7 %collective-permute-start.16 = (bf16[512,256]{1,0:T(8,128)(2,1)}, bf16[512,256]{1,0:T(8,128)(2,1)}, u32[]{:S(2)}, u32[]{:S(2)}) collective-permute-start(bf16[512,256]{1,0:T(8,128)(2,1)} %collective-permute-done.15.out_a), channel_id=1, source_target_pairs={{0,4},{2,6},{4,0},{6,2},{8,12},{10,14},{12,8},{14,10},{16,20},{18,... | collective-permute-start | bytes 786440 | tf_op jit(solution)/shard_map/ppermute | solution.py:585
  95.5 40.4 %collective-permute-start.20 = (bf16[512,1408]{1,0:T(8,128)(2,1)}, bf16[512,1408]{1,0:T(8,128)(2,1)S(1)}, u32[]{:S(2)}, u32[]{:S(2)}) collective-permute-start(bf16[512,1408]{1,0:T(8,128)(2,1)} %collective-permute-done.19.refs_4_), channel_id=1, source_target_pairs={{0,4},{2,6},{4,0},{6,2},{8,12},{10,14},{12,8},{14,10},{16,20},{18,... | collective-permute-start | bytes 4325384 | tf_op jit(solution)/shard_map/ppermute | solution.py:585
  97.8 7.2 %collective-permute-start.11 = (bf16[2,2,128,128]{3,2,1,0:T(8,128)(2,1)S(1)}, bf16[2,2,128,128]{3,2,1,0:T(8,128)(2,1)S(1)}, u32[]{:S(2)}, u32[]{:S(2)}) collective-permute-start(bf16[2,2,128,128]{3,2,1,0:T(8,128)(2,1)S(1)} %fusion.40), channel_id=1, source_target_pairs={{0,16},{2,18},{4,20},{6,22},{8,24},{10,26},{12,28},{14,30},{16,0},... | collective-permute-start | bytes 393224 | tf_op jit(solution)/shard_map/ppermute | solution.py:585
  100.8 34.4 %collective-permute-start.23 = (bf16[1408,256]{1,0:T(8,128)(2,1)S(1)}, bf16[1408,256]{1,0:T(8,128)(2,1)}, u32[]{:S(2)}, u32[]{:S(2)}) collective-permute-start(bf16[1408,256]{1,0:T(8,128)(2,1)S(1)} %constant_dynamic-slice_fusion.26), channel_id=1, source_target_pairs={{0,1},{1,0},{2,3},{3,2},{4,5},{5,4},{6,7},{7,6},{8,9},{9,8},{10,11... | collective-permute-start | bytes 2162696 | tf_op jit(solution)/shard_map/ppermute | solution.py:585
  105.3 29.7 %collective-permute-start.12 = (bf16[2,2,128,128]{3,2,1,0:T(8,128)(2,1)S(1)}, bf16[2,2,128,128]{3,2,1,0:T(8,128)(2,1)S(1)}, u32[]{:S(2)}, u32[]{:S(2)}) collective-permute-start(bf16[2,2,128,128]{3,2,1,0:T(8,128)(2,1)S(1)} %select_convert_fusion.3), channel_id=1, source_target_pairs={{0,4},{2,6},{4,0},{6,2},{8,12},{10,14},{12,8},{14,10},{16,20},{18,... | collective-permute-start | bytes 393224 | tf_op jit(solution)/shard_map/ppermute | solution.py:585
  106.3 30.7 %collective-permute-start.14 = (bf16[128,1024]{1,0:T(8,128)(2,1)S(1)}, bf16[128,1024]{1,0:T(8,128)(2,1)S(1)}, u32[]{:S(2)}, u32[]{:S(2)}) collective-permute-start(bf16[128,1024]{1,0:T(8,128)(2,1)S(1)} %convolution_convert_fusion.9), channel_id=1, source_target_pairs={{0,1},{1,0},{2,3},{3,2},{4,5},{5,4},{6,7},{7,6},{8,9},{9,8},{10,11... | collective-permute-start | bytes 786440 | tf_op jit(solution)/shard_map/ppermute | solution.py:585
  135.2 15.5 %collective-permute-start.24 = (bf16[1408,256]{1,0:T(8,128)(2,1)}, bf16[1408,256]{1,0:T(8,128)(2,1)}, u32[]{:S(2)}, u32[]{:S(2)}) collective-permute-start(bf16[1408,256]{1,0:T(8,128)(2,1)} %collective-permute-done.23.refs_9_), channel_id=1, source_target_pairs={{0,4},{2,6},{4,0},{6,2},{8,12},{10,14},{12,8},{14,10},{16,20},{18,... | collective-permute-start | bytes 2162696 | tf_op jit(solution)/shard_map/ppermute | solution.py:585
  135.7 37.7 %collective-permute-start.21 = (bf16[512,1408]{1,0:T(8,128)(2,1)}, bf16[512,1408]{1,0:T(8,128)(2,1)S(1)}, u32[]{:S(2)}, u32[]{:S(2)}) collective-permute-start(bf16[512,1408]{1,0:T(8,128)(2,1)} %collective-permute-done.19.refs_4_), channel_id=1, source_target_pairs={{0,2},{2,0},{4,6},{6,4},{8,10},{10,8},{12,14},{14,12},{16,18},{18,... | collective-permute-start | bytes 4325384 | tf_op jit(solution)/shard_map/ppermute | solution.py:585
  135.8 37.6 %collective-permute-start.22 = (bf16[512,1408]{1,0:T(8,128)(2,1)S(1)}, bf16[512,1408]{1,0:T(8,128)(2,1)S(1)}, u32[]{:S(2)}, u32[]{:S(2)}) collective-permute-start(bf16[512,1408]{1,0:T(8,128)(2,1)S(1)} %collective-permute-done.20.refs_5_), channel_id=1, source_target_pairs={{0,2},{2,0},{4,6},{6,4},{8,10},{10,8},{12,14},{14,12},{16,18},{18,... | collective-permute-start | bytes 4325384 | tf_op jit(solution)/shard_map/ppermute | solution.py:585
  137.0 14.8 %collective-permute-start.17 = (bf16[512,256]{1,0:T(8,128)(2,1)}, bf16[512,256]{1,0:T(8,128)(2,1)S(1)}, u32[]{:S(2)}, u32[]{:S(2)}) collective-permute-start(bf16[512,256]{1,0:T(8,128)(2,1)} %collective-permute-done.15.out_a), channel_id=1, source_target_pairs={{0,2},{2,0},{4,6},{6,4},{8,10},{10,8},{12,14},{14,12},{16,18},{18,... | collective-permute-start | bytes 786440 | tf_op jit(solution)/shard_map/ppermute | solution.py:585
  141.8 31.6 %collective-permute-start.25 = (bf16[1408,256]{1,0:T(8,128)(2,1)}, bf16[1408,256]{1,0:T(8,128)(2,1)}, u32[]{:S(2)}, u32[]{:S(2)}) collective-permute-start(bf16[1408,256]{1,0:T(8,128)(2,1)} %collective-permute-done.23.refs_9_), channel_id=1, source_target_pairs={{0,2},{2,0},{4,6},{6,4},{8,10},{10,8},{12,14},{14,12},{16,18},{18,... | collective-permute-start | bytes 2162696 | tf_op jit(solution)/shard_map/ppermute | solution.py:585
  150.7 22.8 %collective-permute-start.26 = (bf16[1408,256]{1,0:T(8,128)(2,1)}, bf16[1408,256]{1,0:T(8,128)(2,1)}, u32[]{:S(2)}, u32[]{:S(2)}) collective-permute-start(bf16[1408,256]{1,0:T(8,128)(2,1)} %collective-permute-done.24.refs_10_), channel_id=1, source_target_pairs={{0,2},{2,0},{4,6},{6,4},{8,10},{10,8},{12,14},{14,12},{16,18},{18,... | collective-permute-start | bytes 2162696 | tf_op jit(solution)/shard_map/ppermute | solution.py:585
  151.8 21.2 %collective-permute-start.18 = (bf16[512,256]{1,0:T(8,128)(2,1)}, bf16[512,256]{1,0:T(8,128)(2,1)S(1)}, u32[]{:S(2)}, u32[]{:S(2)}) collective-permute-start(bf16[512,256]{1,0:T(8,128)(2,1)} %collective-permute-done.16.out_b), channel_id=1, source_target_pairs={{0,2},{2,0},{4,6},{6,4},{8,10},{10,8},{12,14},{14,12},{16,18},{18,... | collective-permute-start | bytes 786440 | tf_op jit(solution)/shard_map/ppermute | solution.py:585
  173.0 110.4 %collective-permute-start.71 = (bf16[128,1024]{1,0:T(8,128)(2,1)}, bf16[128,1024]{1,0:T(8,128)(2,1)}, u32[]{:S(2)}, u32[]{:S(2)}) collective-permute-start(bf16[128,1024]{1,0:T(8,128)(2,1)} %bitcast_convert_fusion), channel_id=1, source_target_pairs={{0,1},{1,0},{2,3},{3,2},{4,5},{5,4},{6,7},{7,6},{8,9},{9,8},{10,11... | collective-permute-start | bytes 786440 | tf_op jit(solution)/shard_map/ppermute | solution.py:585
  219.6 18.5 %collective-permute-start.27 = (bf16[4,2,128,128]{3,2,1,0:T(8,128)(2,1)}, bf16[4,2,128,128]{3,2,1,0:T(8,128)(2,1)}, u32[]{:S(2)}, u32[]{:S(2)}) collective-permute-start(bf16[4,2,128,128]{3,2,1,0:T(8,128)(2,1)} %dynamic-slice_bitcast_fusion.10), channel_id=1, source_target_pairs={{0,2},{2,0},{4,6},{6,4},{8,10},{10,8},{12,14},{14,12},{16,18},{18,... | collective-permute-start | bytes 786440 | tf_op jit(solution)/shard_map/ppermute | solution.py:585
  219.9 20.1 %collective-permute-start.35 = (bf16[128,1024]{1,0:T(8,128)(2,1)}, bf16[128,1024]{1,0:T(8,128)(2,1)}, u32[]{:S(2)}, u32[]{:S(2)}) collective-permute-start(bf16[128,1024]{1,0:T(8,128)(2,1)} %get-tuple-element.74), channel_id=1, source_target_pairs={{0,1},{1,0},{2,3},{3,2},{4,5},{5,4},{6,7},{7,6},{8,9},{9,8},{10,11... | collective-permute-start | bytes 786440 | tf_op jit(solution)/shard_map/ppermute | solution.py:585
  223.4 10.6 %collective-permute-start.52 = (bf16[512,128]{1,0:T(8,128)(2,1)S(1)}, bf16[512,128]{1,0:T(8,128)(2,1)S(1)}, u32[]{:S(2)}, u32[]{:S(2)}) collective-permute-start(bf16[512,128]{1,0:T(8,128)(2,1)S(1)} %bitcast.428), channel_id=1, source_target_pairs={{0,1},{1,0},{2,3},{3,2},{4,5},{5,4},{6,7},{7,6},{8,9},{9,8},{10,11... | collective-permute-start | bytes 393224 | tf_op jit(solution)/shard_map/ppermute | solution.py:585
  224.8 10.9 %collective-permute-start.46 = (bf16[512,128]{1,0:T(8,128)(2,1)}, bf16[512,128]{1,0:T(8,128)(2,1)}, u32[]{:S(2)}, u32[]{:S(2)}) collective-permute-start(bf16[512,128]{1,0:T(8,128)(2,1)} %bitcast.55), channel_id=1, source_target_pairs={{0,1},{1,0},{2,3},{3,2},{4,5},{5,4},{6,7},{7,6},{8,9},{9,8},{10,11... | collective-permute-start | bytes 393224 | tf_op jit(solution)/shard_map/ppermute | solution.py:585
  234.0 92.0 %collective-permute-start.53 = (bf16[4,128,1408]{2,1,0:T(8,128)(2,1)}, bf16[4,128,1408]{2,1,0:T(8,128)(2,1)}, u32[]{:S(2)}, u32[]{:S(2)}) collective-permute-start(bf16[4,128,1408]{2,1,0:T(8,128)(2,1)} %get-tuple-element.78), channel_id=1, source_target_pairs={{0,1},{1,0},{2,3},{3,2},{4,5},{5,4},{6,7},{7,6},{8,9},{9,8},{10,11... | collective-permute-start | bytes 4325384 | tf_op jit(solution)/shard_map/ppermute | solution.py:585
  235.6 38.8 %collective-permute-start.47 = (bf16[128,1024]{1,0:T(8,128)(2,1)}, bf16[128,1024]{1,0:T(8,128)(2,1)S(1)}, u32[]{:S(2)}, u32[]{:S(2)}) collective-permute-start(bf16[128,1024]{1,0:T(8,128)(2,1)} %get-tuple-element.76), channel_id=1, source_target_pairs={{0,1},{1,0},{2,3},{3,2},{4,5},{5,4},{6,7},{7,6},{8,9},{9,8},{10,11... | collective-permute-start | bytes 786440 | tf_op jit(solution)/shard_map/ppermute | solution.py:585
  238.1 42.5 %collective-permute-start.70 = (bf16[1408,128]{1,0:T(8,128)(2,1)}, bf16[1408,128]{1,0:T(8,128)(2,1)S(1)}, u32[]{:S(2)}, u32[]{:S(2)}) collective-permute-start(bf16[1408,128]{1,0:T(8,128)(2,1)} %bitcast.422), channel_id=1, source_target_pairs={{0,1},{1,0},{2,3},{3,2},{4,5},{5,4},{6,7},{7,6},{8,9},{9,8},{10,11... | collective-permute-start | bytes 1081352 | tf_op jit(solution)/shard_map/ppermute | solution.py:585
  239.9 34.5 %collective-permute-start.28 = (bf16[2,2,128,128]{3,2,1,0:T(8,128)(2,1)S(1)}, bf16[2,2,128,128]{3,2,1,0:T(8,128)(2,1)S(1)}, u32[]{:S(2)}, u32[]{:S(2)}) collective-permute-start(bf16[2,2,128,128]{3,2,1,0:T(8,128)(2,1)S(1)} %dynamic-slice_bitcast_fusion.18), channel_id=1, source_target_pairs={{0,4},{2,6},{4,0},{6,2},{8,12},{10,14},{12,8},{14,10},{16,20},{18,... | collective-permute-start | bytes 393224 | tf_op jit(solution)/shard_map/ppermute | solution.py:585
  274.6 6.8 %collective-permute-start.29 = (bf16[2,2,128,128]{3,2,1,0:T(8,128)(2,1)S(1)}, bf16[2,2,128,128]{3,2,1,0:T(8,128)(2,1)S(1)}, u32[]{:S(2)}, u32[]{:S(2)}) collective-permute-start(bf16[2,2,128,128]{3,2,1,0:T(8,128)(2,1)S(1)} %fusion.37), channel_id=1, source_target_pairs={{0,8},{2,10},{4,12},{6,14},{8,0},{10,2},{12,4},{14,6},{16,24},{18,... | collective-permute-start | bytes 393224 | tf_op jit(solution)/shard_map/ppermute | solution.py:585
  276.3 13.9 %collective-permute-start.48 = (bf16[256,1024]{1,0:T(8,128)(2,1)S(1)}, bf16[256,1024]{1,0:T(8,128)(2,1)S(1)}, u32[]{:S(2)}, u32[]{:S(2)}) collective-permute-start(bf16[256,1024]{1,0:T(8,128)(2,1)S(1)} %convolution_convert_fusion.7), channel_id=1, source_target_pairs={{0,2},{2,0},{4,6},{6,4},{8,10},{10,8},{12,14},{14,12},{16,18},{18,... | collective-permute-start | bytes 1572872 | tf_op jit(solution)/shard_map/ppermute | solution.py:585
  281.5 7.7 %collective-permute-start.30 = (bf16[2,2,128,128]{3,2,1,0:T(8,128)(2,1)S(1)}, bf16[2,2,128,128]{3,2,1,0:T(8,128)(2,1)S(1)}, u32[]{:S(2)}, u32[]{:S(2)}) collective-permute-start(bf16[2,2,128,128]{3,2,1,0:T(8,128)(2,1)S(1)} %fusion.44), channel_id=1, source_target_pairs={{0,16},{2,18},{4,20},{6,22},{8,24},{10,26},{12,28},{14,30},{16,0},... | collective-permute-start | bytes 393224 | tf_op jit(solution)/shard_map/ppermute | solution.py:585
  286.0 67.1 %collective-permute-start.72 = (bf16[704,1024]{1,0:T(8,128)(2,1)}, bf16[704,1024]{1,0:T(8,128)(2,1)}, u32[]{:S(2)}, u32[]{:S(2)}) collective-permute-start(bf16[704,1024]{1,0:T(8,128)(2,1)} %convolution_convert_fusion.6), channel_id=1, source_target_pairs={{0,2},{2,0},{4,6},{6,4},{8,10},{10,8},{12,14},{14,12},{16,18},{18,... | collective-permute-start | bytes 4325384 | tf_op jit(solution)/shard_map/ppermute | solution.py:585
  290.6 7.5 %collective-permute-start.49 = (bf16[4,32,1024]{2,1,0:T(8,128)(2,1)S(1)}, bf16[4,32,1024]{2,1,0:T(8,128)(2,1)S(1)}, u32[]{:S(2)}, u32[]{:S(2)}) collective-permute-start(bf16[4,32,1024]{2,1,0:T(8,128)(2,1)S(1)} %dynamic-slice_bitcast_fusion.8), channel_id=1, source_target_pairs={{0,4},{2,6},{4,0},{6,2},{8,12},{10,14},{12,8},{14,10},{16,20},{18,... | collective-permute-start | bytes 786440 | tf_op jit(solution)/shard_map/ppermute | solution.py:585
  298.9 17.8 %collective-permute-start.50 = (bf16[2,32,1024]{2,1,0:T(8,128)(2,1)}, bf16[2,32,1024]{2,1,0:T(8,128)(2,1)}, u32[]{:S(2)}, u32[]{:S(2)}) collective-permute-start(bf16[2,32,1024]{2,1,0:T(8,128)(2,1)} %dynamic-slice_bitcast_fusion.16), channel_id=1, source_target_pairs={{0,8},{2,10},{4,12},{6,14},{8,0},{10,2},{12,4},{14,6},{16,24},{18,... | collective-permute-start | bytes 393224 | tf_op jit(solution)/shard_map/ppermute | solution.py:585
  317.7 7.7 %collective-permute-start.51 = (bf16[1,32,1024]{2,1,0:T(8,128)(2,1)S(1)}, bf16[1,32,1024]{2,1,0:T(8,128)(2,1)S(1)}, u32[]{:S(2)}, u32[]{:S(2)}) collective-permute-start(bf16[1,32,1024]{2,1,0:T(8,128)(2,1)S(1)} %constant_dynamic-slice_fusion.19), channel_id=1, source_target_pairs={{0,16},{2,18},{4,20},{6,22},{8,24},{10,26},{12,28},{14,30},{16,0},... | collective-permute-start | bytes 196616 | tf_op jit(solution)/shard_map/ppermute | solution.py:585
  323.2 19.7 %collective-permute-start.34 = (bf16[128,3072]{1,0:T(8,128)(2,1)S(1)}, bf16[128,3072]{1,0:T(8,128)(2,1)S(1)}, u32[]{:S(2)}, u32[]{:S(2)}) collective-permute-start(bf16[128,3072]{1,0:T(8,128)(2,1)S(1)} %fusion.5), channel_id=1, source_target_pairs={{0,1},{1,0},{2,3},{3,2},{4,5},{5,4},{6,7},{7,6},{8,9},{9,8},{10,11... | collective-permute-start | bytes 2359304 | tf_op jit(solution)/shard_map/ppermute | solution.py:585
  345.8 39.9 %collective-permute-start.54 = (bf16[256,1408]{1,0:T(8,128)(2,1)}, bf16[256,1408]{1,0:T(8,128)(2,1)}, u32[]{:S(2)}, u32[]{:S(2)}) collective-permute-start(bf16[256,1408]{1,0:T(8,128)(2,1)} %convolution_convert_fusion.5), channel_id=1, source_target_pairs={{0,2},{2,0},{4,6},{6,4},{8,10},{10,8},{12,14},{14,12},{16,18},{18,... | collective-permute-start | bytes 2162696 | tf_op jit(solution)/shard_map/ppermute | solution.py:585
  345.8 42.6 %collective-permute-start.58 = (bf16[256,1408]{1,0:T(8,128)(2,1)}, bf16[256,1408]{1,0:T(8,128)(2,1)}, u32[]{:S(2)}, u32[]{:S(2)}) collective-permute-start(bf16[256,1408]{1,0:T(8,128)(2,1)} %convolution_convert_fusion.4), channel_id=1, source_target_pairs={{0,2},{2,0},{4,6},{6,4},{8,10},{10,8},{12,14},{14,12},{16,18},{18,... | collective-permute-start | bytes 2162696 | tf_op jit(solution)/shard_map/ppermute | solution.py:585
  346.3 43.8 %collective-permute-start.62 = (bf16[256,1408]{1,0:T(8,128)(2,1)}, bf16[256,1408]{1,0:T(8,128)(2,1)}, u32[]{:S(2)}, u32[]{:S(2)}) collective-permute-start(bf16[256,1408]{1,0:T(8,128)(2,1)} %convolution_convert_fusion.3), channel_id=1, source_target_pairs={{0,2},{2,0},{4,6},{6,4},{8,10},{10,8},{12,14},{14,12},{16,18},{18,... | collective-permute-start | bytes 2162696 | tf_op jit(solution)/shard_map/ppermute | solution.py:585
  349.3 42.4 %collective-permute-start.66 = (bf16[256,1408]{1,0:T(8,128)(2,1)}, bf16[256,1408]{1,0:T(8,128)(2,1)}, u32[]{:S(2)}, u32[]{:S(2)}) collective-permute-start(bf16[256,1408]{1,0:T(8,128)(2,1)} %convolution_convert_fusion.2), channel_id=1, source_target_pairs={{0,2},{2,0},{4,6},{6,4},{8,10},{10,8},{12,14},{14,12},{16,18},{18,... | collective-permute-start | bytes 2162696 | tf_op jit(solution)/shard_map/ppermute | solution.py:585
  380.8 47.9 %collective-permute-start.73 = (bf16[4,88,1024]{2,1,0:T(8,128)(2,1)}, bf16[4,88,1024]{2,1,0:T(8,128)(2,1)S(1)}, u32[]{:S(2)}, u32[]{:S(2)}) collective-permute-start(bf16[4,88,1024]{2,1,0:T(8,128)(2,1)} %dynamic-slice_bitcast_fusion.1), channel_id=1, source_target_pairs={{0,4},{2,6},{4,0},{6,2},{8,12},{10,14},{12,8},{14,10},{16,20},{18,... | collective-permute-start | bytes 2162696 | tf_op jit(solution)/shard_map/ppermute | solution.py:585
  385.7 43.8 %collective-permute-start.42 = (bf16[256,1024]{1,0:T(8,128)(2,1)S(1)}, bf16[256,1024]{1,0:T(8,128)(2,1)S(1)}, u32[]{:S(2)}, u32[]{:S(2)}) collective-permute-start(bf16[256,1024]{1,0:T(8,128)(2,1)S(1)} %convolution_convert_fusion.8), channel_id=1, source_target_pairs={{0,2},{2,0},{4,6},{6,4},{8,10},{10,8},{12,14},{14,12},{16,18},{18,... | collective-permute-start | bytes 1572872 | tf_op jit(solution)/shard_map/ppermute | solution.py:585
  388.5 72.9 %collective-permute-start.38 = (bf16[256,3072]{1,0:T(8,128)(2,1)S(1)}, bf16[256,3072]{1,0:T(8,128)(2,1)S(1)}, u32[]{:S(2)}, u32[]{:S(2)}) collective-permute-start(bf16[256,3072]{1,0:T(8,128)(2,1)S(1)} %convolution_convert_fusion), channel_id=1, source_target_pairs={{0,2},{2,0},{4,6},{6,4},{8,10},{10,8},{12,14},{14,12},{16,18},{18,... | collective-permute-start | bytes 4718600 | tf_op jit(solution)/shard_map/ppermute | solution.py:585
  390.1 16.8 %collective-permute-start.55 = (bf16[4,32,1408]{2,1,0:T(8,128)(2,1)S(1)}, bf16[4,32,1408]{2,1,0:T(8,128)(2,1)S(1)}, u32[]{:S(2)}, u32[]{:S(2)}) collective-permute-start(bf16[4,32,1408]{2,1,0:T(8,128)(2,1)S(1)} %dynamic-slice_bitcast_fusion.7), channel_id=1, source_target_pairs={{0,4},{2,6},{4,0},{6,2},{8,12},{10,14},{12,8},{14,10},{16,20},{18,... | collective-permute-start | bytes 1081352 | tf_op jit(solution)/shard_map/ppermute | solution.py:585
  391.7 23.0 %collective-permute-start.59 = (bf16[4,32,1408]{2,1,0:T(8,128)(2,1)S(1)}, bf16[4,32,1408]{2,1,0:T(8,128)(2,1)S(1)}, u32[]{:S(2)}, u32[]{:S(2)}) collective-permute-start(bf16[4,32,1408]{2,1,0:T(8,128)(2,1)S(1)} %dynamic-slice_bitcast_fusion.6), channel_id=1, source_target_pairs={{0,4},{2,6},{4,0},{6,2},{8,12},{10,14},{12,8},{14,10},{16,20},{18,... | collective-permute-start | bytes 1081352 | tf_op jit(solution)/shard_map/ppermute | solution.py:585
  406.9 15.3 %collective-permute-start.63 = (bf16[4,32,1408]{2,1,0:T(8,128)(2,1)S(1)}, bf16[4,32,1408]{2,1,0:T(8,128)(2,1)S(1)}, u32[]{:S(2)}, u32[]{:S(2)}) collective-permute-start(bf16[4,32,1408]{2,1,0:T(8,128)(2,1)S(1)} %dynamic-slice_bitcast_fusion.5), channel_id=1, source_target_pairs={{0,4},{2,6},{4,0},{6,2},{8,12},{10,14},{12,8},{14,10},{16,20},{18,... | collective-permute-start | bytes 1081352 | tf_op jit(solution)/shard_map/ppermute | solution.py:585
  414.7 12.3 %collective-permute-start.67 = (bf16[4,32,1408]{2,1,0:T(8,128)(2,1)S(1)}, bf16[4,32,1408]{2,1,0:T(8,128)(2,1)S(1)}, u32[]{:S(2)}, u32[]{:S(2)}) collective-permute-start(bf16[4,32,1408]{2,1,0:T(8,128)(2,1)S(1)} %dynamic-slice_bitcast_fusion.4), channel_id=1, source_target_pairs={{0,4},{2,6},{4,0},{6,2},{8,12},{10,14},{12,8},{14,10},{16,20},{18,... | collective-permute-start | bytes 1081352 | tf_op jit(solution)/shard_map/ppermute | solution.py:585
  422.2 9.4 %collective-permute-start.56 = (bf16[2,32,1408]{2,1,0:T(8,128)(2,1)S(1)}, bf16[2,32,1408]{2,1,0:T(8,128)(2,1)S(1)}, u32[]{:S(2)}, u32[]{:S(2)}) collective-permute-start(bf16[2,32,1408]{2,1,0:T(8,128)(2,1)S(1)} %dynamic-slice_bitcast_fusion.15), channel_id=1, source_target_pairs={{0,8},{2,10},{4,12},{6,14},{8,0},{10,2},{12,4},{14,6},{16,24},{18,... | collective-permute-start | bytes 540680 | tf_op jit(solution)/shard_map/ppermute | solution.py:585
  427.0 7.5 %collective-permute-start.60 = (bf16[2,32,1408]{2,1,0:T(8,128)(2,1)S(1)}, bf16[2,32,1408]{2,1,0:T(8,128)(2,1)S(1)}, u32[]{:S(2)}, u32[]{:S(2)}) collective-permute-start(bf16[2,32,1408]{2,1,0:T(8,128)(2,1)S(1)} %dynamic-slice_bitcast_fusion.14), channel_id=1, source_target_pairs={{0,8},{2,10},{4,12},{6,14},{8,0},{10,2},{12,4},{14,6},{16,24},{18,... | collective-permute-start | bytes 540680 | tf_op jit(solution)/shard_map/ppermute | solution.py:585
  428.8 10.5 %collective-permute-start.64 = (bf16[2,32,1408]{2,1,0:T(8,128)(2,1)S(1)}, bf16[2,32,1408]{2,1,0:T(8,128)(2,1)S(1)}, u32[]{:S(2)}, u32[]{:S(2)}) collective-permute-start(bf16[2,32,1408]{2,1,0:T(8,128)(2,1)S(1)} %dynamic-slice_bitcast_fusion.13), channel_id=1, source_target_pairs={{0,8},{2,10},{4,12},{6,14},{8,0},{10,2},{12,4},{14,6},{16,24},{18,... | collective-permute-start | bytes 540680 | tf_op jit(solution)/shard_map/ppermute | solution.py:585
  429.5 15.6 %collective-permute-start.68 = (bf16[2,32,1408]{2,1,0:T(8,128)(2,1)S(1)}, bf16[2,32,1408]{2,1,0:T(8,128)(2,1)S(1)}, u32[]{:S(2)}, u32[]{:S(2)}) collective-permute-start(bf16[2,32,1408]{2,1,0:T(8,128)(2,1)S(1)} %dynamic-slice_bitcast_fusion.12), channel_id=1, source_target_pairs={{0,8},{2,10},{4,12},{6,14},{8,0},{10,2},{12,4},{14,6},{16,24},{18,... | collective-permute-start | bytes 540680 | tf_op jit(solution)/shard_map/ppermute | solution.py:585
  431.6 32.5 %collective-permute-start.74 = (bf16[2,88,1024]{2,1,0:T(8,128)(2,1)S(1)}, bf16[2,88,1024]{2,1,0:T(8,128)(2,1)S(1)}, u32[]{:S(2)}, u32[]{:S(2)}) collective-permute-start(bf16[2,88,1024]{2,1,0:T(8,128)(2,1)S(1)} %dynamic-slice_bitcast_fusion.3), channel_id=1, source_target_pairs={{0,8},{2,10},{4,12},{6,14},{8,0},{10,2},{12,4},{14,6},{16,24},{18,... | collective-permute-start | bytes 1081352 | tf_op jit(solution)/shard_map/ppermute | solution.py:585
  434.5 29.8 %collective-permute-start.43 = (bf16[4,32,1024]{2,1,0:T(8,128)(2,1)S(1)}, bf16[4,32,1024]{2,1,0:T(8,128)(2,1)S(1)}, u32[]{:S(2)}, u32[]{:S(2)}) collective-permute-start(bf16[4,32,1024]{2,1,0:T(8,128)(2,1)S(1)} %dynamic-slice_bitcast_fusion.9), channel_id=1, source_target_pairs={{0,4},{2,6},{4,0},{6,2},{8,12},{10,14},{12,8},{14,10},{16,20},{18,... | collective-permute-start | bytes 786440 | tf_op jit(solution)/shard_map/ppermute | solution.py:585
  439.3 10.2 %collective-permute-start.57 = (bf16[1,32,1408]{2,1,0:T(8,128)(2,1)S(1)}, bf16[1,32,1408]{2,1,0:T(8,128)(2,1)S(1)}, u32[]{:S(2)}, u32[]{:S(2)}) collective-permute-start(bf16[1,32,1408]{2,1,0:T(8,128)(2,1)S(1)} %constant_dynamic-slice_fusion.16), channel_id=1, source_target_pairs={{0,16},{2,18},{4,20},{6,22},{8,24},{10,26},{12,28},{14,30},{16,0},... | collective-permute-start | bytes 270344 | tf_op jit(solution)/shard_map/ppermute | solution.py:585
  445.1 9.8 %collective-permute-start.61 = (bf16[1,32,1408]{2,1,0:T(8,128)(2,1)S(1)}, bf16[1,32,1408]{2,1,0:T(8,128)(2,1)S(1)}, u32[]{:S(2)}, u32[]{:S(2)}) collective-permute-start(bf16[1,32,1408]{2,1,0:T(8,128)(2,1)S(1)} %constant_dynamic-slice_fusion.15), channel_id=1, source_target_pairs={{0,16},{2,18},{4,20},{6,22},{8,24},{10,26},{12,28},{14,30},{16,0},... | collective-permute-start | bytes 270344 | tf_op jit(solution)/shard_map/ppermute | solution.py:585
  449.5 8.3 %collective-permute-start.65 = (bf16[1,32,1408]{2,1,0:T(8,128)(2,1)S(1)}, bf16[1,32,1408]{2,1,0:T(8,128)(2,1)S(1)}, u32[]{:S(2)}, u32[]{:S(2)}) collective-permute-start(bf16[1,32,1408]{2,1,0:T(8,128)(2,1)S(1)} %constant_dynamic-slice_fusion.14), channel_id=1, source_target_pairs={{0,16},{2,18},{4,20},{6,22},{8,24},{10,26},{12,28},{14,30},{16,0},... | collective-permute-start | bytes 270344 | tf_op jit(solution)/shard_map/ppermute | solution.py:585
  462.0 16.3 %collective-permute-start.39 = (bf16[4,32,3072]{2,1,0:T(8,128)(2,1)S(1)}, bf16[4,32,3072]{2,1,0:T(8,128)(2,1)S(1)}, u32[]{:S(2)}, u32[]{:S(2)}) collective-permute-start(bf16[4,32,3072]{2,1,0:T(8,128)(2,1)S(1)} %dynamic-slice_bitcast_fusion), channel_id=1, source_target_pairs={{0,4},{2,6},{4,0},{6,2},{8,12},{10,14},{12,8},{14,10},{16,20},{18,... | collective-permute-start | bytes 2359304 | tf_op jit(solution)/shard_map/ppermute | solution.py:585
  464.2 16.8 %collective-permute-start.75 = (bf16[1,88,1024]{2,1,0:T(8,128)(2,1)S(1)}, bf16[1,88,1024]{2,1,0:T(8,128)(2,1)S(1)}, u32[]{:S(2)}, u32[]{:S(2)}) collective-permute-start(bf16[1,88,1024]{2,1,0:T(8,128)(2,1)S(1)} %constant_dynamic-slice_fusion.10), channel_id=1, source_target_pairs={{0,16},{2,18},{4,20},{6,22},{8,24},{10,26},{12,28},{14,30},{16,0},... | collective-permute-start | bytes 540680 | tf_op jit(solution)/shard_map/ppermute | solution.py:585
  464.4 14.2 %collective-permute-start.44 = (bf16[2,32,1024]{2,1,0:T(8,128)(2,1)S(1)}, bf16[2,32,1024]{2,1,0:T(8,128)(2,1)S(1)}, u32[]{:S(2)}, u32[]{:S(2)}) collective-permute-start(bf16[2,32,1024]{2,1,0:T(8,128)(2,1)S(1)} %dynamic-slice_bitcast_fusion.17), channel_id=1, source_target_pairs={{0,8},{2,10},{4,12},{6,14},{8,0},{10,2},{12,4},{14,6},{16,24},{18,... | collective-permute-start | bytes 393224 | tf_op jit(solution)/shard_map/ppermute | solution.py:585
  478.5 9.7 %collective-permute-start.40 = (bf16[2,32,3072]{2,1,0:T(8,128)(2,1)S(1)}, bf16[2,32,3072]{2,1,0:T(8,128)(2,1)S(1)}, u32[]{:S(2)}, u32[]{:S(2)}) collective-permute-start(bf16[2,32,3072]{2,1,0:T(8,128)(2,1)S(1)} %dynamic-slice_bitcast_fusion.2), channel_id=1, source_target_pairs={{0,8},{2,10},{4,12},{6,14},{8,0},{10,2},{12,4},{14,6},{16,24},{18,... | collective-permute-start | bytes 1179656 | tf_op jit(solution)/shard_map/ppermute | solution.py:585
  478.7 10.0 %collective-permute-start.45 = (bf16[1,32,1024]{2,1,0:T(8,128)(2,1)S(1)}, bf16[1,32,1024]{2,1,0:T(8,128)(2,1)S(1)}, u32[]{:S(2)}, u32[]{:S(2)}) collective-permute-start(bf16[1,32,1024]{2,1,0:T(8,128)(2,1)S(1)} %constant_dynamic-slice_fusion.22), channel_id=1, source_target_pairs={{0,16},{2,18},{4,20},{6,22},{8,24},{10,26},{12,28},{14,30},{16,0},... | collective-permute-start | bytes 196616 | tf_op jit(solution)/shard_map/ppermute | solution.py:585
  488.3 8.0 %collective-permute-start.41 = (bf16[1,32,3072]{2,1,0:T(8,128)(2,1)S(1)}, bf16[1,32,3072]{2,1,0:T(8,128)(2,1)S(1)}, u32[]{:S(2)}, u32[]{:S(2)}) collective-permute-start(bf16[1,32,3072]{2,1,0:T(8,128)(2,1)S(1)} %constant_dynamic-slice_fusion.23), channel_id=1, source_target_pairs={{0,16},{2,18},{4,20},{6,22},{8,24},{10,26},{12,28},{14,30},{16,0},... | collective-permute-start | bytes 589832 | tf_op jit(solution)/shard_map/ppermute | solution.py:585
  (83 other events, 841.7 us)

commit v3 on v0

v3 whole, which is shorter than its diff:
```python
import functools
import jax
import jax.numpy as jnp
from jax import lax
from jax.experimental import pallas as pl
from jax.experimental.pallas import tpu as pltpu
from jax.sharding import PartitionSpec as P

D = 1024
HEADS = 8
FF = 2816
KW = 4
ITERS = 8
HEAD_DIM = 128
QUARTERS = 4
SHARE = HEADS // QUARTERS
HALO = 16

f32 = jnp.float32
bf16 = jnp.bfloat16
VMEM_LIMIT = 56 * 1024 * 1024


def nn(a, b):
    return lax.dot_general(a, b, (((1,), (0,)), ((), ())), preferred_element_type=f32)


def nt(a, b):
    return lax.dot_general(a, b, (((1,), (1,)), ((), ())), preferred_element_type=f32)


def tn(a, b):
    return lax.dot_general(a, b, (((0,), (0,)), ((), ())), preferred_element_type=f32)


def column(row, like):
    return jnp.broadcast_to(row, like).T


def decay_mask(c, b, tokens):
    shape = (tokens, tokens)
    late = lax.broadcasted_iota(jnp.int32, shape, 1) >= lax.broadcasted_iota(jnp.int32, shape, 0)
    spread = jnp.broadcast_to(c, shape) - column(c, shape)
    return jnp.where(late, jnp.exp(jnp.where(late, spread, 0.0)), 0.0) * column(b, shape)


def like(shape, kind=f32):
    return jax.ShapeDtypeStruct(shape, kind)


def smem():
    return pl.BlockSpec(memory_space=pltpu.SMEM)


EXTRA = 16


def norm_kernel(place, tok_ref, taps_ref, lines_ref, mine_o, theirs_o):
    half = D // 2
    y = place[0]
    a = tok_ref[...]
    unit = a * lax.rsqrt(jnp.mean(a * a, axis=-1, keepdims=True) + 1e-05)
    left, right = unit[:, :half], unit[:, half:]
    rows = a.shape[0]
    gain = lines_ref[0:1].astype(f32)
    mine_o[...] = (jnp.where(y == 0, left, right) * gain).astype(bf16)
    theirs_o[:rows] = jnp.where(y == 0, right, left)
    taps = taps_ref[...].astype(f32)
    lines = [taps[t : t + 1, i * half : (i + 1) * half] for t in range(KW) for i in range(3)]
    theirs_o[rows:] = jnp.concatenate(lines + [lines_ref[...].astype(f32)], axis=0)


def norm(place, tokens, taps, lines):
    rows = tokens.shape[0]
    vmem = pl.BlockSpec(memory_space=pltpu.VMEM)
    return pl.pallas_call(
        norm_kernel,
        in_specs=[smem()] + [vmem] * 3,
        out_specs=[vmem, vmem],
        out_shape=[like((rows, D // 2), bf16), like((rows + EXTRA, D // 2))],
        name="norm",
    )(place, tokens, taps, lines)


def with_halo(own, lent, halo):
    before = halo[...].astype(f32)
    blank = jnp.zeros((HALO - before.shape[0], before.shape[1]), f32)
    return jnp.concatenate([blank, before, own[...] + lent[...].astype(f32)], axis=0)


def conv_parts(padded, taps):
    rows = padded.shape[0] - HALO
    shifted = [padded[HALO - KW + 1 + j : HALO - KW + 1 + j + rows] for j in range(KW)]
    total = taps[0:1] * shifted[0]
    for j in range(1, KW):
        total = total + taps[j : j + 1] * shifted[j]
    return total, shifted


def unit(a):
    return a * lax.rsqrt(jnp.sum(a * a, axis=-1, keepdims=True) + 1e-06)


def ending_of(c_ref, b_ref, head):
    c = c_ref[pl.ds(head, 1), :]
    b = b_ref[pl.ds(head, 1), :]
    return column(jnp.exp(c[:, c.shape[1] - 1 :] - c) * b, (HEAD_DIM, c.shape[1]))


def position(spot):
    return spot[0] % FOUR


FOUR = 4
PAIR = (2 * SHARE, HEAD_DIM, HEAD_DIM)
MESSAGE = (2 * SHARE, HEAD_DIM + 16, HEAD_DIM)


def decay_rows(decay):
    shape = (16, HEAD_DIM)
    at = lax.broadcasted_iota(jnp.int32, shape, 0)
    decay = jnp.broadcast_to(decay, shape)
    high = decay.astype(bf16).astype(f32)
    return jnp.where(at == 0, high, jnp.where(at == 1, decay - high, 0.0)).astype(bf16)


def decay_of(message, m):
    rows = message[m, HEAD_DIM:].astype(f32)
    return rows[0:1] + rows[1:2]


def block_decay(c_ref, head):
    c = c_ref[pl.ds(head, 1), :]
    return jnp.broadcast_to(jnp.exp(c[:, c.shape[1] - 1 :]), (1, HEAD_DIM))


def store_quarter(spot, quarter, outs, states, c_ref):
    rows = [decay_rows(block_decay(c_ref, quarter * SHARE + m)) for m in range(SHARE)]
    for i, out in enumerate(outs):

        @pl.when((position(spot) ^ i) == quarter)
        def _():
            for m in range(2 * SHARE):
                out[m, :HEAD_DIM] = states[m]
                out[m, HEAD_DIM:] = rows[m % SHARE]


def cut(h):
    return slice(h * HEAD_DIM, (h + 1) * HEAD_DIM)


def keys_kernel(oq, ok, lq, lk, hq, hk, tq, tk, c_ref, b_ref, q_o, k_o, state_o):
    quarter = pl.program_id(0)
    sums = []
    for own, lent, halo, taps in ((oq, lq, hq, tq), (ok, lk, hk, tk)):
        total, _ = conv_parts(with_halo(own, lent, halo), taps[...])
        sums.append(total * jax.nn.sigmoid(total))
    for m in range(SHARE):
        k = unit(sums[1][:, cut(m)])
        k_low = k.astype(bf16)
        k_o[m] = k_low
        ending = ending_of(c_ref, b_ref, quarter * SHARE + m)
        state_o[m] = tn((k * ending).astype(bf16), k_low).astype(bf16)
        q_o[m] = unit(sums[0][:, cut(m)]).T


def values_kernel(spot, ov, lv, hv, tv, k_ref, ks_ref, c_ref, b_ref, v_o, *outs):
    quarter = pl.program_id(0)
    total, _ = conv_parts(with_halo(ov, lv, hv), tv[...])
    values = total * jax.nn.sigmoid(total)
    states = [ks_ref[m] for m in range(SHARE)]
    for m in range(SHARE):
        v = values[:, cut(m)]
        v_o[m] = v.astype(bf16)
        ending = ending_of(c_ref, b_ref, quarter * SHARE + m)
        states.append(tn((v * ending).astype(bf16), k_ref[m]).astype(bf16))
    store_quarter(spot, quarter, outs, states, c_ref)


def whole(*shape):
    return pl.BlockSpec(shape, lambda *g: (0,) * len(shape))


def per_quarter(*shape):
    return pl.BlockSpec((SHARE,) + shape, lambda p: (p,) + (0,) * len(shape))


def quarter_columns(rows, third):
    return pl.BlockSpec((rows, SHARE * HEAD_DIM), lambda p: (0, third * QUARTERS + p))


def keys(own, lent, halo, taps, c, b):
    tokens = own.shape[0]
    square = (HEADS, HEAD_DIM, HEAD_DIM)
    return pl.pallas_call(
        keys_kernel,
        grid=(QUARTERS,),
        in_specs=[quarter_columns(rows, i) for rows in (tokens, tokens, halo.shape[0], KW) for i in (0, 1)]
        + [whole(HEADS, tokens)] * 2,
        out_specs=[per_quarter(HEAD_DIM, tokens), per_quarter(tokens, HEAD_DIM), per_quarter(HEAD_DIM, HEAD_DIM)],
        out_shape=[like((HEADS, HEAD_DIM, tokens)), like((HEADS, tokens, HEAD_DIM), bf16), like(square, bf16)],
        cost_estimate=pl.CostEstimate(flops=1, bytes_accessed=1, transcendentals=0),
        name="keys",
    )(own, own, lent, lent, halo, halo, taps, taps, c, b)


def values(spot, own, lent, halo, taps, k, key_states, c, b):
    tokens = own.shape[0]
    return pl.pallas_call(
        values_kernel,
        grid=(QUARTERS,),
        in_specs=[smem()] + [quarter_columns(rows, 0) for rows in (tokens, tokens, halo.shape[0])] + [quarter_columns(KW, 2)]
        + [per_quarter(tokens, HEAD_DIM), per_quarter(HEAD_DIM, HEAD_DIM)] + [whole(HEADS, tokens)] * 2,
        out_specs=[per_quarter(tokens, HEAD_DIM)] + [whole(*MESSAGE)] * QUARTERS,
        out_shape=[like((HEADS, tokens, HEAD_DIM), bf16)] + [like(MESSAGE, bf16)] * QUARTERS,
        cost_estimate=pl.CostEstimate(flops=1, bytes_accessed=1, transcendentals=0),
        name="values",
    )(spot, own, lent, halo, taps, k, key_states, c, b)


def decay_between(indices, decays, low, high):
    total = None
    for index, decay in zip(indices, decays):
        one = jnp.where((index > low) & (index < high), decay, 1.0)
        total = one if total is None else total * one
    return total


def summed(factors, arrays, m):
    total = factors[0] * arrays[0][m, :HEAD_DIM].astype(f32)
    for factor, array in zip(factors[1:], arrays[1:]):
        total = total + factor * array[m, :HEAD_DIM].astype(f32)
    return total


def members(spot, unit, count):
    place = (spot[0] // unit) % count
    return place, [place ^ i for i in range(count)]


def whole_group(indices, arrays, m):
    decays = [decay_of(a, m) for a in arrays]
    count = len(arrays)
    state = summed([decay_between(indices, decays, i, count) for i in indices], arrays, m)
    return state, decay_between(indices, decays, -1, count)


def earlier(place, indices, arrays, m, before):
    decays = [decay_of(a, m) for a in arrays]
    factors = [jnp.where(i < place, decay_between(indices, decays, i, place), 0.0) for i in indices[1:]]
    state = summed(factors, arrays[1:], m)
    decay = decay_between(indices, decays, -1, place)
    if before is None:
        return state, decay
    old = before[m, HEAD_DIM : HEAD_DIM + 1]
    return before[m, :HEAD_DIM] + old * state, old * decay


def group_kernel(spot, *refs):
    arrays, out = refs[:FOUR], refs[FOUR]
    _, indices = members(spot, 1, FOUR)
    for m in range(2 * SHARE):
        state, decay = whole_group(indices, arrays, m)
        out[m, :HEAD_DIM] = state.astype(bf16)
        out[m, HEAD_DIM:] = decay_rows(decay)


def upper_kernel(unit, count, has_before, spot, *refs):
    arrays = refs[:count]
    before = refs[count] if has_before else None
    before_o, total_o = refs[-2:]
    place, indices = members(spot, unit, count)
    for m in range(2 * SHARE):
        state, decay = earlier(place, indices, arrays, m, before)
        before_o[m, :HEAD_DIM] = state
        before_o[m, HEAD_DIM:] = jnp.broadcast_to(decay, (16, HEAD_DIM))
        state, decay = whole_group(indices, arrays, m)
        total_o[m, :HEAD_DIM] = state.astype(bf16)
        total_o[m, HEAD_DIM:] = decay_rows(decay)


def spread_kernel(unit, count, has_before, spot, *refs):
    arrays, near = refs[:count], refs[count : count + FOUR]
    before = refs[count + FOUR] if has_before else None
    outs = refs[-FOUR:]
    place, upper = members(spot, unit, count)
    _, indices = members(spot, 1, FOUR)
    for m in range(2 * SHARE):
        state, _ = earlier(place, upper, arrays, m, before)
        decays = [decay_of(x, m) for x in near]
        for j in range(FOUR):
            at = indices[j]
            factors = [jnp.where(i < at, decay_between(indices, decays, i, at), 0.0) for i in indices]
            total = decay_between(indices, decays, -1, at) * state + summed(factors, near, m)
            outs[j][m] = total.astype(bf16)


def small_call(kernel, name, shapes, spot, *args):
    vmem = pl.BlockSpec(memory_space=pltpu.VMEM)
    return pl.pallas_call(
        kernel,
        in_specs=[smem()] + [vmem] * len(args),
        out_specs=[vmem] * len(shapes),
        out_shape=shapes,
        cost_estimate=pl.CostEstimate(flops=1, bytes_accessed=1, transcendentals=0),
        name=name,
    )(spot, *args)


def neighbour(axis, bit):
    return [(i, i ^ bit) for i in range(lax.axis_size(axis))]


def partner(x, axis, bit=1):
    return lax.ppermute(x, axis, neighbour(axis, bit))


def radices(peers):
    sizes = []
    left = peers // FOUR
    while left > 1:
        sizes.append(min(FOUR, left))
        left //= sizes[-1]
    return sizes


def swapped(arrays, axis, unit_size=1):
    return [arrays[0]] + [partner(a, axis, unit_size * i) for i, a in enumerate(arrays) if i]


class Scan:
    def __init__(self, spot, near, axis):
        self.spot, self.axis, self.near = spot, axis, near
        self.sizes = radices(lax.axis_size(axis))

    def group(self):
        message = like(MESSAGE, bf16)
        (self.total,) = small_call(group_kernel, "group", [message], self.spot, *self.near)
        self.before = ()
        self.unit = FOUR
        for radix in self.sizes[:-1]:
            arrays = swapped([self.total] * radix, self.axis, self.unit)
            kernel = functools.partial(upper_kernel, self.unit, radix, bool(self.before))
            before, self.total = small_call(kernel, "upper", [like(MESSAGE), message], self.spot, *arrays, *self.before)
            self.before = (before,)
            self.unit *= radix
        self.far = swapped([self.total] * self.sizes[-1], self.axis, self.unit)

    def spread(self):
        kernel = functools.partial(spread_kernel, self.unit, self.sizes[-1], bool(self.before))
        self.parts = small_call(
            kernel, "spread", [like(PAIR, bf16)] * FOUR, self.spot, *self.far, *self.near, *self.before
        )
        self.entering = swapped(self.parts, self.axis)
        return self.entering


def prepare(k_ref, c_ref, b_ref, ridge_ref, state_refs, place, left, wide, mask, decay, ridge, pair):
    tokens = k_ref.shape[1]
    for i, state in enumerate(state_refs):
        for m in range(SHARE):
            left[(place ^ i) * SHARE + m, :, :HEAD_DIM] = state[m]
    pair[...] = jnp.zeros_like(pair)
    for h in range(HEADS):
        k = k_ref[h]
        left[h, :, HEAD_DIM:] = k.T
        wide[h // 2, :, cut(h % 2)] = k
        mask[h] = decay_mask(c_ref[h : h + 1, :], b_ref[h : h + 1, :], tokens)
        decay[h] = jnp.broadcast_to(jnp.exp(c_ref[h : h + 1, :]), (8, tokens))
        ridge[h] = column(ridge_ref[h : h + 1, :], (tokens, HEAD_DIM))


def key_products(columns, wide, pair):
    products = []
    for h in range(0, HEADS, 2):
        pair[h // 2, :HEAD_DIM, :HEAD_DIM] = columns(h)
        pair[h // 2, HEAD_DIM:, HEAD_DIM:] = columns(h + 1)
        both = nn(wide[h // 2], pair[h // 2])
        products += [both[:, :HEAD_DIM], both[:, HEAD_DIM:]]
    return products


def solve_kernel(
    place, q_ref, k_ref, s0, s1, s2, s3, c_ref, b_ref, ridge_ref,
    x_out, p_out, m_out, score_out, scal_out,
    left, wide, mask, decay, ridge, pair, x_s, r_s, p_s,
):
    i = pl.program_id(0)

    @pl.when(i == 0)
    def _():
        prepare(k_ref, c_ref, b_ref, ridge_ref, (s0, s1, s2, s3), place[0], left, wide, mask, decay, ridge, pair)
        for h in range(HEADS):
            q = q_ref[h]
            x_s[h] = jnp.zeros_like(q)
            r_s[h] = q
            p_s[h] = q
            scal_out[h, 0:1] = jnp.sum(q * q, axis=0, keepdims=True)

    products = key_products(lambda h: p_s[h].astype(bf16), wide, pair)
    for h in range(HEADS):
        p = p_s[h]
        scores = (products[h] * mask[h]).astype(bf16)
        score_out[0, h] = scores
        stacked = jnp.concatenate([(decay[h, 0:1] * p).astype(bf16), scores], axis=0)
        image = nn(left[h], stacked) + ridge[h] * p
        norm = scal_out[h, pl.ds(i, 1)]
        dot = jnp.sum(p * image, axis=0, keepdims=True)
        size = norm / dot
        p_out[0, h] = p
        m_out[0, h] = image
        scal_out[h, pl.ds(2 * ITERS + i, 1)] = dot
        x_s[h] = x_s[h] + size * p
        r = r_s[h] - size * image
        r_s[h] = r
        norm_next = jnp.sum(r * r, axis=0, keepdims=True)
        scal_out[h, pl.ds(i + 1, 1)] = norm_next
        p_s[h] = r + (norm_next / norm) * p

    @pl.when(i == ITERS - 1)
    def _():
        for h in range(HEADS):
            x_out[h] = x_s[h].astype(bf16)


def common_scratch(tokens):
    square = pltpu.VMEM((HEADS, HEAD_DIM, tokens), f32)
    return [
        pltpu.VMEM((HEADS, HEAD_DIM, HEAD_DIM + tokens), bf16),
        pltpu.VMEM((HEADS // 2, tokens, 2 * HEAD_DIM), bf16),
        pltpu.VMEM((HEADS, tokens, tokens), f32),
        pltpu.VMEM((HEADS, 8, tokens), f32),
        square,
        pltpu.VMEM((HEADS // 2, 2 * HEAD_DIM, 2 * tokens), bf16),
        square, square, square,
    ]


def solve(place, q, k, states, c, b, ridge):
    tokens = q.shape[2]
    step = pl.BlockSpec((1, HEADS, HEAD_DIM, tokens), lambda i: (i, 0, 0, 0))
    steps = (ITERS, HEADS, HEAD_DIM, tokens)
    return pl.pallas_call(
        solve_kernel,
        grid=(ITERS,),
        in_specs=[smem(), whole(HEADS, HEAD_DIM, tokens), whole(HEADS, tokens, HEAD_DIM)] + [whole(*PAIR)] * FOUR
        + [whole(HEADS, tokens)] * 2 + [whole(HEADS, HEAD_DIM)],
        out_specs=[whole(HEADS, HEAD_DIM, tokens), step, step, step, whole(HEADS, 3 * ITERS, tokens)],
        out_shape=[
            like((HEADS, HEAD_DIM, tokens), bf16), like(steps), like(steps), like(steps, bf16),
            like((HEADS, 3 * ITERS, tokens)),
        ],
        scratch_shapes=common_scratch(tokens),
        compiler_params=pltpu.CompilerParams(vmem_limit_bytes=VMEM_LIMIT),
        cost_estimate=pl.CostEstimate(flops=1, bytes_accessed=1, transcendentals=0),
        name="solve",
    )(place, q, k, *states, c, b, ridge)


def attend_back_kernel(place, ga_ref, k_ref, v_ref, x_ref, s0, s1, s2, s3, c_ref, b_ref, gx_o, dk_o, dv_o, state_o):
    quarter = pl.program_id(0)
    tokens = k_ref.shape[1]
    for m in range(SHARE):
        head = quarter * SHARE + m
        c = c_ref[pl.ds(head, 1), :]
        b = b_ref[pl.ds(head, 1), :]
        mask = decay_mask(c, b, tokens)
        e = jnp.exp(c)
        state = s0[SHARE + m]
        for i, other in ((1, s1), (2, s2), (3, s3)):
            state = jnp.where((place[0] ^ i) == quarter, other[SHARE + m], state)
        ga = ga_ref[:, cut(m)].T
        low = ga.astype(bf16)
        x = x_ref[m]
        k = k_ref[m]
        scores = (nn(k, x) * mask).astype(bf16)
        dscores = (nn(v_ref[m], low) * mask).astype(bf16)
        ega = (e * ga).astype(bf16)
        gx_o[m] = tn(state, ega) + tn(k, dscores)
        dv_o[m] = nt(scores, low)
        dk_o[m] = nt(dscores, x)
        state_o[m] = nt(ega, x).astype(bf16)


def attend_back(place, ga, k, v, x, states, c, b):
    tokens = k.shape[1]
    square = like((HEADS, HEAD_DIM, tokens))
    return pl.pallas_call(
        attend_back_kernel,
        grid=(QUARTERS,),
        in_specs=[smem(), quarter_columns(tokens, 0)] + [per_quarter(tokens, HEAD_DIM)] * 2
        + [per_quarter(HEAD_DIM, tokens)] + [whole(*PAIR)] * FOUR + [whole(HEADS, tokens)] * 2,
        out_specs=[per_quarter(HEAD_DIM, tokens)] * 4,
        out_shape=[square] * 3 + [like((HEADS, HEAD_DIM, HEAD_DIM), bf16)],
        cost_estimate=pl.CostEstimate(flops=1, bytes_accessed=1, transcendentals=0),
        name="attend_back",
    )(place, ga, k, v, x, *states, c, b)


def adjoint_kernel(
    spot, place, gx_ref, k_ref, s0, s1, s2, s3, c_ref, b_ref, ridge_ref, p_ref, m_ref, score_ref, scal_ref, values_ref,
    dq_ref, dk_ref, dridge_ref, o0, o1, o2, o3,
    left, wide, mask, decay, ridge, pair, gr_s, gp_s, acc_s, next_s, gnorm_s, low_s, steps_p, steps_g, steps_s, stack,
):
    s = pl.program_id(0)
    i = ITERS - 1 - s
    tokens = k_ref.shape[1]
    at = pl.ds(pl.multiple_of(i * tokens, tokens), tokens)

    @pl.when(s == 0)
    def _():
        prepare(k_ref, c_ref, b_ref, ridge_ref, (s0, s1, s2, s3), place[0], left, wide, mask, decay, ridge, pair)
        gr_s[...] = jnp.zeros_like(gr_s)
        gp_s[...] = jnp.zeros_like(gp_s)
        acc_s[...] = jnp.zeros_like(acc_s)
        next_s[...] = jnp.zeros_like(next_s)
        gnorm_s[...] = jnp.zeros_like(gnorm_s)

    for h in range(HEADS):
        p, m, gx = p_ref[0, h], m_ref[0, h], gx_ref[h]
        norm = scal_ref[h, pl.ds(i, 1)]
        dot = scal_ref[h, pl.ds(2 * ITERS + i, 1)]
        size = norm / dot
        ratio = jnp.where(s == 0, 0.0, scal_ref[h, pl.ds(i + 1, 1)] / norm)
        gp = gp_s[h]
        gratio = jnp.sum(gp * p, axis=0, keepdims=True)
        gnext = gnorm_s[h, 0:1] + gratio / norm
        gr = gr_s[h] + gp + (2.0 * gnext) * (next_s[h] - ratio * p)
        gsize = jnp.sum(gx * p - gr * m, axis=0, keepdims=True)
        gdot = -gsize * size / dot
        gm = gdot * p - size * gr
        gr_s[h] = gr
        gp_s[h] = ratio * gp + size * gx + gdot * m + ridge[h] * gm
        acc_s[h] = acc_s[h] + gm * p
        next_s[h] = p
        gnorm_s[h, 0:1] = gsize / dot - gratio * ratio / norm
        low = gm.astype(bf16)
        low_s[h] = low
        egm = (decay[h, 0:1] * gm).astype(bf16)
        steps_g[h, :, at] = low
        steps_p[h, :, at] = p.astype(bf16)
        steps_s[h, :, at] = score_ref[0, h]
        stack[h, HEAD_DIM:, at] = egm
    products = key_products(lambda h: low_s[h], wide, pair)
    for h in range(HEADS):
        dscores = (products[h] * mask[h]).astype(bf16)
        stack[h, :HEAD_DIM, at] = dscores
        stacked = jnp.concatenate([stack[h, HEAD_DIM:, at], dscores], axis=0)
        gp_s[h] = gp_s[h] + nn(left[h], stacked)

    @pl.when(s == ITERS - 1)
    def _():
        for h in range(HEADS):
            dq_ref[h] = gr_s[h] + gp_s[h] + 2.0 * gnorm_s[h, 0:1] * p_ref[0, h]
            both = nt(steps_p[h], stack[h])
            dk_ref[h] = (nt(steps_g[h], steps_s[h]) + both[:, :HEAD_DIM]).T
            left[h, :, :HEAD_DIM] = both[:, HEAD_DIM:].T.astype(bf16)
            dridge_ref[h] = jnp.sum(acc_s[h].T, axis=0, keepdims=True)
        for j, out in enumerate((o0, o1, o2, o3)):
            for m in range(SHARE):
                head = (position(spot) ^ j) * SHARE + m
                decay = decay_rows(block_decay(c_ref, head))
                out[m, :HEAD_DIM] = left[head, :, :HEAD_DIM]
                out[m, HEAD_DIM:] = decay
                out[SHARE + m, :HEAD_DIM] = values_ref[head]
                out[SHARE + m, HEAD_DIM:] = decay


def adjoint(spot, place, gx, k, states, c, b, ridge, p_all, m_all, scores, scal, value_states):
    tokens = k.shape[1]
    step = pl.BlockSpec((1, HEADS, HEAD_DIM, tokens), lambda s: (ITERS - 1 - s, 0, 0, 0))
    square = pltpu.VMEM((HEADS, HEAD_DIM, tokens), f32)
    line = pltpu.VMEM((HEADS, HEAD_DIM, ITERS * tokens), bf16)
    return pl.pallas_call(
        adjoint_kernel,
        grid=(ITERS,),
        in_specs=[smem(), smem(), whole(HEADS, HEAD_DIM, tokens), whole(HEADS, tokens, HEAD_DIM)] + [whole(*PAIR)] * FOUR
        + [whole(HEADS, tokens)] * 2 + [whole(HEADS, HEAD_DIM), step, step, step, whole(HEADS, 3 * ITERS, tokens), whole(HEADS, HEAD_DIM, HEAD_DIM)],
        out_specs=[whole(HEADS, HEAD_DIM, tokens), whole(HEADS, tokens, HEAD_DIM), whole(HEADS, 1, HEAD_DIM)]
        + [whole(*MESSAGE)] * FOUR,
        out_shape=[like((HEADS, HEAD_DIM, tokens)), like((HEADS, tokens, HEAD_DIM)), like((HEADS, 1, HEAD_DIM))]
        + [like(MESSAGE, bf16)] * FOUR,
        scratch_shapes=common_scratch(tokens) + [
            square,
            pltpu.VMEM((HEADS, 8, tokens), f32),
            pltpu.VMEM((HEADS, HEAD_DIM, tokens), bf16),
            line, line, line,
            pltpu.VMEM((HEADS, 2 * HEAD_DIM, ITERS * tokens), bf16),
        ],
        compiler_params=pltpu.CompilerParams(vmem_limit_bytes=VMEM_LIMIT),
        cost_estimate=pl.CostEstimate(flops=1, bytes_accessed=1, transcendentals=0),
        name="adjoint",
    )(spot, place, gx, k, *states, c, b, ridge, p_all, m_all, scores, scal, value_states)


def conv_forward(own, lent, halo, t):
    total, shifted = conv_parts(with_halo(own, lent, halo), t[...])
    sig = jax.nn.sigmoid(total)
    return shifted, sig * (1.0 + total * (1.0 - sig)), total * sig


def unit_back(act, grad):
    scale = lax.rsqrt(jnp.sum(act * act, axis=-1, keepdims=True) + 1e-06)
    rows = act * scale
    return scale * (grad - rows * jnp.sum(rows * grad, axis=-1, keepdims=True))


def conv_back(dconv, shifted, t, g, dt):
    taps = t[...]
    tokens = dconv.shape[0]
    blank = jnp.zeros((HALO, dconv.shape[1]), f32)
    padded = jnp.concatenate([blank, dconv, blank], axis=0)
    rows = tokens + HALO
    total = taps[KW - 1 : KW] * padded[:rows]
    for j in range(KW - 1):
        total = total + taps[j : j + 1] * padded[KW - 1 - j : KW - 1 - j + rows]
    g[...] = total.astype(bf16)
    dt[...] = jnp.concatenate(
        [jnp.sum(dconv * shifted[j], axis=0, keepdims=True) for j in range(KW)], axis=0
    )


def queries_back_kernel(own, lent, halo, t, dq_ref, g, dt):
    shifted, slope, act = conv_forward(own, lent, halo, t)
    grads = [unit_back(act[:, cut(m)], dq_ref[m].T) for m in range(SHARE)]
    conv_back(jnp.concatenate(grads, axis=1) * slope, shifted, t, g, dt)


def returned(place, quarter, refs, m):
    state = refs[0][m]
    for i in range(1, FOUR):
        state = jnp.where((place ^ i) == quarter, refs[i][m], state)
    return state


def values_back_kernel(spot, own, lent, halo, t, dv_ref, k_ref, r0, r1, r2, r3, c_ref, b_ref, g, dt):
    quarter = pl.program_id(0)
    shifted, slope, _ = conv_forward(own, lent, halo, t)
    grads = []
    for m in range(SHARE):
        rv = returned(position(spot), quarter, (r0, r1, r2, r3), SHARE + m)
        grads.append(dv_ref[m] + ending_of(c_ref, b_ref, quarter * SHARE + m) * nt(k_ref[m], rv))
    conv_back(jnp.concatenate(grads, axis=1) * slope, shifted, t, g, dt)


def keys_back_kernel(
    spot, own, lent, halo, t, dk1, dk2, k_ref, v_ref, r0, r1, r2, r3, c_ref, b_ref, g, dt
):
    quarter = pl.program_id(0)
    shifted, slope, act = conv_forward(own, lent, halo, t)
    grads = []
    for m in range(SHARE):
        rv = returned(position(spot), quarter, (r0, r1, r2, r3), SHARE + m)
        rk = returned(position(spot), quarter, (r0, r1, r2, r3), m).astype(f32)
        rk = (rk + rk.T).astype(bf16)
        ending = ending_of(c_ref, b_ref, quarter * SHARE + m)
        dk = dk1[m] + dk2[m] + ending * (nn(k_ref[m], rk) + nn(v_ref[m], rv))
        grads.append(unit_back(act[:, cut(m)], dk))
    conv_back(jnp.concatenate(grads, axis=1) * slope, shifted, t, g, dt)


def third_back(kernel, name, which, taps_third, projected, taps, before, others, specs):
    own, lent, halo = projected
    tokens = own.shape[0]
    return pl.pallas_call(
        kernel,
        grid=(QUARTERS,),
        in_specs=[smem()] * len(before) + [quarter_columns(rows, which) for rows in (tokens, tokens, halo.shape[0])]
        + [quarter_columns(KW, taps_third)] + specs,
        out_specs=[quarter_columns(tokens + HALO, 0), quarter_columns(KW, 0)],
        out_shape=[like((tokens + HALO, D), bf16), like((KW, D))],
        cost_estimate=pl.CostEstimate(flops=1, bytes_accessed=1, transcendentals=0),
        name=name,
    )(*before, own, lent, halo, taps, *others)


def queries_back(projected, taps, dq):
    return third_back(queries_back_kernel, "queries_back", 0, 0, projected, taps, (), (dq,), [per_quarter(HEAD_DIM, HEAD_DIM)])


def values_back(spot, projected, taps, dv, k, states, c, b):
    square = per_quarter(HEAD_DIM, HEAD_DIM)
    return third_back(
        values_back_kernel, "values_back", 0, 2, projected, taps, (spot,), (dv, k, *states, c, b),
        [square] * 2 + [whole(*PAIR)] * FOUR + [whole(*c.shape)] * 2,
    )


def keys_back(spot, projected, taps, dk1, dk2, k, v, states, c, b):
    square = per_quarter(HEAD_DIM, HEAD_DIM)
    return third_back(
        keys_back_kernel, "keys_back", 1, 1, projected, taps, (spot,), (dk1, dk2, k, v, *states, c, b),
        [square] * 4 + [whole(*PAIR)] * FOUR + [whole(*c.shape)] * 2,
    )


def completed(ref, extra):
    more = extra[...].astype(f32)
    more = jnp.concatenate([jnp.zeros_like(more), more], axis=0)
    last = ref.shape[0] - 16
    return [ref[HALO:last], (ref[last:].astype(f32) + more).astype(bf16)]


def products_kernel(plan, joined, cuts, spot, *refs):
    count = len(plan)
    odd = spot[0] % 2 == 1
    outs, scratch = refs[-count - (1 if joined else 1 + len(cuts)) : -count], refs[-count:]

    @pl.when(pl.program_id(0) == 0)
    def _():
        for (lefts, _, _), both in zip(plan, scratch):
            both[...] = jnp.concatenate([refs[at][...] if rows is None else refs[at][rows] for at, rows in lefts], axis=1)

    start = 0
    def right(at, stacked):
        if not stacked:
            return refs[at][...]
        return jnp.concatenate([refs[at][i : i + stacked] for i in range(0, refs[at].shape[0], stacked)], axis=1)

    for (_, rights, size), both in zip(plan, scratch):
        if len(rights) == 4:
            rows = [part for i in (0, 1) for part in completed(refs[rights[i][0]], refs[rights[2 + i][0]])]
        else:
            rows = [right(*at) for at in rights]
        product = nn(both[...], jnp.concatenate(rows, axis=0))
        at = slice(start, start + size)
        start += size
        if joined:
            outs[0][:, at, :] = product.reshape(product.shape[0] // size, size, product.shape[1]).astype(bf16)
            continue
        blocks = product.reshape(product.shape[0] // (2 * size), 2, size, product.shape[1])
        outs[0][:, at, :] = jnp.where(odd, blocks[:, 1], blocks[:, 0]).astype(bf16)
        other = jnp.where(odd, blocks[:, 0], blocks[:, 1]).astype(bf16)
        for out, cut_at in zip(outs[1:], cuts):
            first, last = max(at.start, cut_at.start), min(at.stop, cut_at.stop)
            if first < last:
                out[:, first - cut_at.start : last - cut_at.start, :] = other[:, first - at.start : last - at.start]


def unstacked(array, index):
    row, tokens = index
    return jnp.concatenate([array[row + i * tokens : row + (i + 1) * tokens] for i in range(D // HEAD_DIM)], axis=1)


def products(spot, peers, lefts, rights, tile, joined=False, messages=1):
    sizes = [(part[0][1].stop - part[0][1].start) // peers for part in lefts]
    width = rights[0][0][0].shape[1] if rights[0][0][1] is None else D
    count, number = (peers, 1) if joined else (peers // 2, 2)
    shape = (count, sum(sizes), width)
    cuts = [slice(i * shape[1] // messages, (i + 1) * shape[1] // messages) for i in range(messages)]
    if any(size % 8 for size in sizes):
        odd = spot[0] % 2
        sides = []
        for side in range(number):
            parts = []
            for left, right in zip(lefts, rights):
                if len(right) == 4:
                    rows = []
                    for i in (0, 1):
                        (array, third), (extra, _) = right[i], right[2 + i]
                        size = array.shape[0] // 3
                        rows += completed(array[third * size : (third + 1) * size], extra[:, third * D : (third + 1) * D])
                else:
                    rows = [unstacked(array, index) if index else array for array, index in right]
                blocks = nn(jnp.concatenate([array[at] for array, at in left], axis=1), jnp.concatenate(rows, axis=0))
                blocks = blocks.astype(bf16).reshape(count, number, -1, width)
                parts.append(lax.dynamic_index_in_dim(blocks, 0 if joined else odd ^ side, 1, keepdims=False))
            sides.append(jnp.concatenate(parts, axis=1))
        return sides if joined else sides[:1] + [sides[1][:, at] for at in cuts]
    arrays, specs, plan = [], [], []

    def place_of(array, spec):
        for at, other in enumerate(arrays):
            if other is array and specs[at] is None and spec is None:
                return at
        arrays.append(array)
        specs.append(spec)
        return len(arrays) - 1

    def columns(array, index):
        if index is None:
            return pl.BlockSpec((array.shape[0], tile), lambda j: (0, j))
        if isinstance(index, int) and array.shape[1] == D:
            return pl.BlockSpec((array.shape[0] // 3, tile), lambda j: (index, j))
        if isinstance(index, int):
            return pl.BlockSpec((array.shape[0], tile), lambda j: (0, index * (D // tile) + j))
        size = index[1] * tile // HEAD_DIM
        return pl.BlockSpec((size, HEAD_DIM), lambda j: (index[0] // size + j, 0))

    def left_part(array, rows):
        size = rows.stop - rows.start
        if rows.start % size:
            return place_of(array, None), rows
        at = rows.start // size
        return place_of(array, pl.BlockSpec((size, array.shape[1]), lambda j: (at, 0))), None

    for left, right, size in zip(lefts, rights, sizes):
        plan.append((
            [left_part(array, rows) for array, rows in left],
            [(place_of(array, columns(array, index)), index[1] if isinstance(index, tuple) else None) for array, index in right],
            size,
        ))
    heights = [shape[1]] + ([] if joined else [at.stop - at.start for at in cuts])
    return pl.pallas_call(
        functools.partial(products_kernel, plan, joined, cuts),
        grid=(width // tile,),
        in_specs=[smem()] + [spec or whole(*array.shape) for array, spec in zip(arrays, specs)],
        out_specs=[pl.BlockSpec((count, height, tile), lambda j: (0, 0, j)) for height in heights],
        out_shape=[like((count, height, width), bf16) for height in heights],
        scratch_shapes=[
            pltpu.VMEM((left[0][1].stop - left[0][1].start, sum(array.shape[1] for array, _ in left)), bf16) for left in lefts
        ],
        compiler_params=pltpu.CompilerParams(vmem_limit_bytes=VMEM_LIMIT),
        cost_estimate=pl.CostEstimate(flops=1, bytes_accessed=1, transcendentals=0),
        name="products",
    )(spot, *arrays)


def lent_kernel(own, peer, extra1, extra2, logit1, logit2, qkv_ref, gate_ref, own_o, theirs_o):
    rows = own_o.shape[0]
    logits = [unstacked(ref, (D // HEAD_DIM * rows, rows)) for ref in (logit1, logit2)]
    total = nt(jnp.concatenate(logits, axis=0), gate_ref[...])
    size = rows + HALO
    for third in range(3):
        at, columns = slice(third * size, (third + 1) * size), slice(third * D, (third + 1) * D)
        both = completed(own.at[at], extra1[:, columns]) + completed(peer.at[at], extra2[:, columns])
        total = total + nt(jnp.concatenate(both, axis=0), qkv_ref[:, columns])
    own_o[...] = total[:rows]
    theirs_o[...] = total[rows:].astype(bf16)


def lent_rows(own, peer, extras, logits, qkv_weight, gate_weight):
    rows = own.shape[0] // 3 - HALO
    half = qkv_weight.shape[0]
    vmem = pl.BlockSpec(memory_space=pltpu.VMEM)
    return pl.pallas_call(
        lent_kernel,
        in_specs=[vmem] * 8,
        out_specs=[vmem] * 2,
        out_shape=[like((rows, half)), like((rows, half), bf16)],
        compiler_params=pltpu.CompilerParams(vmem_limit_bytes=VMEM_LIMIT),
        cost_estimate=pl.CostEstimate(flops=1, bytes_accessed=1, transcendentals=0),
        name="lent_rows",
    )(own, peer, *extras, *logits, qkv_weight, gate_weight)


def norm_back_kernel(place, own, back, tok_ref, gain_ref, hid_ref, tq, tk, tv, second_ref, ridge_ref, tok_o, vec_o):
    mine, other = own[...], back[...].astype(f32)
    grad = jnp.where(
        place[0] == 0, jnp.concatenate([mine, other], axis=1), jnp.concatenate([other, mine], axis=1)
    )
    tokens = tok_ref[...]
    scale = lax.rsqrt(jnp.mean(tokens * tokens, axis=-1, keepdims=True) + 1e-05)
    rows = tokens * scale
    grows = grad * gain_ref[...]
    tok_o[...] = hid_ref[...] + scale * (grows - rows * jnp.mean(grows * rows, axis=-1, keepdims=True))
    vec_o[:KW] = jnp.concatenate([tq[...], tk[...], tv[...]], axis=1)
    ridge = jnp.concatenate([ridge_ref[h] for h in range(HEADS)], axis=1)
    first = jnp.sum(grad * rows, axis=0, keepdims=True)
    vec_o[KW : KW + 1] = jnp.concatenate([first, second_ref[...], ridge], axis=1)
    vec_o[KW + 1 :] = jnp.zeros((8 - KW - 1, 3 * D), f32)


def norm_back(place, own, back, tokens, gain, hidden, taps, second, ridge):
    vmem = pl.BlockSpec(memory_space=pltpu.VMEM)
    return pl.pallas_call(
        norm_back_kernel,
        in_specs=[smem()] + [vmem] * 10,
        out_specs=[vmem] * 2,
        out_shape=[like(tokens.shape), like((8, 3 * D))],
        cost_estimate=pl.CostEstimate(flops=1, bytes_accessed=1, transcendentals=0),
        name="norm_back",
    )(place, own, back, tokens, gain, hidden, *taps, second, ridge)


def step_kernel(bit, kept_mine, kept_other, *refs):
    mine_o, other_o = refs[-2:]
    start = 0
    for mine, other in zip(refs[0:-2:2], refs[1:-2:2]):
        at = slice(start, start + mine.shape[1])
        start += mine.shape[1]
        mine_o[0, at] = (kept_mine[0, at].astype(f32) + mine[0].astype(f32)).astype(bf16)
        other_o[0, at] = (kept_other[0, at].astype(f32) + other[0].astype(f32)).astype(bf16)


def halving_step(bit, below, kept, got):
    count, size, width = kept.shape

    def half(side, rows):
        def index(i, s):
            return ((i // below) * 2 * below + (s[0] if side == 0 else 1 - s[0]) * below + i % below, 0, 0)

        return pl.BlockSpec((1, rows, width), index)

    out = pl.BlockSpec((1, size, width), lambda i, s: (i, 0, 0))
    arrays = [kept] + list(got)
    return pl.pallas_call(
        step_kernel,
        grid_spec=pltpu.PrefetchScalarGridSpec(
            num_scalar_prefetch=1,
            grid=(count // 2,),
            in_specs=[half(side, x.shape[1]) for x in arrays for side in (0, 1)],
            out_specs=[out, out],
        ),
        out_shape=[like((count // 2, size, width), bf16)] * 2,
        cost_estimate=pl.CostEstimate(flops=1, bytes_accessed=1, transcendentals=0),
        name="halving",
    )(bit, *[x for x in arrays for _ in (0, 1)])


BLOCKS = D // HEAD_DIM


def middle_kernel(
    owners, place, x_ref, s0, s1, s2, s3, k_ref, v_ref, c_ref, b_ref, own_logit, lent_logit, tok_ref, cot_ref, gain_ref, first_ref,
    own_out, out_a, out_b, out_c, out_d, *refs,
):
    own_up = refs[:4]
    up_parts = (refs[4:8], refs[8:12])
    own_down = refs[12]
    down_parts = refs[13:17]
    (out_o, hid_o, gatt_o, own_o, sent_o, ggu_o, dgain_o) = refs[17:24]
    out_s, up_s, down_s, nf_s, gb_s, att_s, sig_s, hid_s, acc_s, gnf_s, inner_s = refs[24:]
    j = pl.program_id(0)
    y = place[0]
    half = D // 2

    def aligned(at, by):
        return pl.multiple_of(at, by)

    mine = pl.ds(aligned(y * half, half), half)
    theirs = pl.ds(aligned((1 - y) * half, half), half)

    def order(q):
        return [q, q ^ 2, q ^ 1, q ^ 3]

    tile = own_up[0].shape[1]
    tokens = tok_ref.shape[0]

    def spread_rows(rows, start):
        total = rows.shape[0]
        size = total // owners
        own_at = slice(start, start + total // 2)
        sent_at = slice(3 * BLOCKS * tokens + start, 3 * BLOCKS * tokens + start + total // 2)
        if size % 8:
            own_o[own_at], sent_o[sent_at] = rows[: total // 2].astype(bf16), rows[total // 2 :].astype(bf16)
            return
        blocks = rows.reshape(owners // 2, 2, size, rows.shape[1])
        for out, at, odd in ((own_o, own_at, y == 1), (sent_o, sent_at, y == 0)):
            out[at] = jnp.where(odd, blocks[:, 1], blocks[:, 0]).reshape(total // 2, rows.shape[1]).astype(bf16)

    def stack_right(value, index):
        for i in range(BLOCKS):
            sent_o[(index * BLOCKS + i) * tokens : (index * BLOCKS + i + 1) * tokens] = value[:, cut(i)]

    def scale_of(hidden):
        return lax.rsqrt(jnp.mean(hidden * hidden, axis=-1, keepdims=True) + 1e-05)

    @pl.when(j == 0)
    def _():
        for i, state in enumerate((s0, s1, s2, s3)):
            for m in range(SHARE):
                head = (place[1] ^ i) * SHARE + m
                c = c_ref[pl.ds(head, 1), :]
                b = b_ref[pl.ds(head, 1), :]
                x = x_ref[head]
                scores = (nn(k_ref[head], x) * decay_mask(c, b, tokens)).astype(bf16)
                part = jnp.exp(c) * nn(state[SHARE + m], x) + tn(v_ref[head], scores)
                att_s[:, pl.ds(aligned(head * HEAD_DIM, HEAD_DIM), HEAD_DIM)] = part.T
        out_s[mine, :] = own_out[...]
        wide = out_a.shape[1]
        for part, q in zip((out_a, out_b, out_c, out_d), order(place[1])):
            out_s[theirs, pl.ds(aligned(q * wide, wide), wide)] = part[...]
        sig = jax.nn.sigmoid(own_logit[...] + lent_logit[...].astype(f32))
        sig_s[...] = sig
        mix = (att_s[...] * sig).astype(bf16)
        spread_rows(mix.astype(f32).T, half)
        normed = tok_ref[...] * scale_of(tok_ref[...]) * first_ref[...]
        spread_rows(normed.astype(bf16).astype(f32).T, 2 * half)
        hidden = tok_ref[...] + nn(mix, out_s[...])
        hid_s[...] = hidden
        normed = (hidden * scale_of(hidden) * gain_ref[...]).astype(bf16)
        nf_s[...] = normed
        spread_rows(normed.astype(f32).T, 0)
        gb_s[...] = cot_ref[...].astype(bf16)
        stack_right(gb_s[...], 2)
        acc_s[...] = jnp.zeros_like(acc_s)
        gnf_s[...] = jnp.zeros_like(gnf_s)

    for i in range(4):
        up_s[mine, i * tile : (i + 1) * tile] = own_up[i][...]
    start = 0
    for parts, q0 in zip(up_parts, (place[2], place[1])):
        count = parts[0].shape[0]
        at = pl.ds(aligned((1 - y) * half + start, 16), count)
        for part, q in zip(parts, order(q0)):
            slot = (q >> 1) * 2 + ((q & 1) ^ y)
            up_s[at, pl.ds(aligned(slot * tile, tile), tile)] = part[...]
        start += count
    down_s[:tile, :] = own_down[...]
    wide = down_parts[0].shape[1]
    for part, q in zip(down_parts, order(place[1])):
        down_s[tile:, pl.ds(aligned(q * wide, wide), wide)] = part[...]
    product = nn(nf_s[...], up_s[...])
    gate, up = product[:, : 2 * tile], product[:, 2 * tile :]
    ginner = nt(gb_s[...], down_s[...])
    sig = jax.nn.sigmoid(gate)
    silu = gate * sig
    inner = (silu * up).astype(bf16)
    ggate = (ginner * up * (sig * (1.0 + gate * (1.0 - sig)))).astype(bf16)
    gup = (ginner * silu).astype(bf16)
    ggu = jnp.concatenate([ggate, gup], axis=1)
    acc_s[...] += nn(inner, down_s[...])
    gnf_s[...] += nt(ggu, up_s[...])
    inner_t = inner.astype(f32).T
    for slot, value in ((y, inner_t[:tile]), (1 - y, inner_t[tile:])):
        inner_s[pl.ds(aligned(slot * (FF // 2) + j * tile, tile), tile), :] = value
    share = FF // 2
    for i, (slot, value) in enumerate(((y, ggate), (1 - y, ggate), (2 + y, gup), (3 - y, gup))):
        at = pl.ds(aligned(slot * share + j * tile, tile), tile)
        ggu_o[:, at] = value[:, (i % 2) * tile : (i % 2 + 1) * tile]

    @pl.when(j == pl.num_programs(0) - 1)
    def _():
        spread_rows(inner_s[...], 3 * half)
        hidden = hid_s[...]
        out_o[...] = hidden + acc_s[...]
        scale = scale_of(hidden)
        rows = hidden * scale
        gnf = gnf_s[...]
        dgain_o[...] = jnp.sum(gnf * rows, axis=0, keepdims=True)
        grows = gnf * gain_ref[...]
        ghid = cot_ref[...] + scale * (grows - rows * jnp.mean(grows * rows, axis=-1, keepdims=True))
        hid_o[...] = ghid
        low = ghid.astype(bf16)
        stack_right(low, 0)
        gmix = nt(low, out_s[...])
        sig = sig_s[...]
        gatt = gmix * sig
        gatt_o[...] = gatt
        stack_right((gatt * att_s[...] * (1.0 - sig)).astype(bf16), 1)


def middle(owners, place, attention, own_logit, lent_logit, tok, cot, gain, gain_first, out_weight, up_weight, down_weight, up_parts, rest_parts):
    tokens = tok.shape[0]
    tile = 128
    share = FF // 2 // tile
    half = D // 2
    left_rows = 3 * half + FF // 2

    def full(*shape):
        return pl.BlockSpec(shape, lambda j, s: (0,) * len(shape))

    rows = full(tokens, D)
    own_up = [
        pl.BlockSpec((half, tile), lambda j, s: (0, s[0] * share + j)),
        pl.BlockSpec((half, tile), lambda j, s: (0, (1 - s[0]) * share + j)),
        pl.BlockSpec((half, tile), lambda j, s: (0, (2 + s[0]) * share + j)),
        pl.BlockSpec((half, tile), lambda j, s: (0, (3 - s[0]) * share + j)),
    ]
    up_specs = [pl.BlockSpec((p.shape[0], tile), lambda j, s: (0, j)) for p in up_parts]
    own_down = pl.BlockSpec((tile, D), lambda j, s: (j, 0))
    down_specs = [pl.BlockSpec((tile, D // 4), lambda j, s: (half // tile + j, 0))] * 4
    square = (HEAD_DIM, HEAD_DIM)
    return pl.pallas_call(
        functools.partial(middle_kernel, owners),
        grid_spec=pltpu.PrefetchScalarGridSpec(
            num_scalar_prefetch=1,
            grid=(share,),
            in_specs=[full(HEADS, HEAD_DIM, tokens)] + [full(*PAIR)] * FOUR + [full(HEADS, tokens, HEAD_DIM)] * 2
            + [full(HEADS, tokens)] * 2
            + [rows, pl.BlockSpec((tokens, D), lambda j, s: (0, 1))]
            + [rows] * 2 + [full(1, D), full(1, D), full(half, D)] + [full(half, D // 4)] * 4
            + own_up + up_specs + [own_down] + down_specs,
            out_specs=[
                rows, rows, rows, full(left_rows, tokens), full(3 * BLOCKS * tokens + left_rows, tokens),
                full(tokens, 2 * FF),
                full(1, D),
            ],
            scratch_shapes=[
                pltpu.VMEM((D, D), bf16),
                pltpu.VMEM((D, 4 * tile), bf16),
                pltpu.VMEM((2 * tile, D), bf16),
                pltpu.VMEM((tokens, D), bf16),
                pltpu.VMEM((tokens, D), bf16),
                pltpu.VMEM((tokens, D), f32),
                pltpu.VMEM((tokens, D), f32),
                pltpu.VMEM((tokens, D), f32),
                pltpu.VMEM((tokens, D), f32),
                pltpu.VMEM((tokens, D), f32),
                pltpu.VMEM((FF, tokens), f32),
            ],
        ),
        out_shape=[
            like((tokens, D)), like((tokens, D)), like((tokens, D)),
            like((left_rows, tokens), bf16), like((3 * BLOCKS * tokens + left_rows, tokens), bf16),
            like((tokens, 2 * FF), bf16),
            like((1, D)),
        ],
        compiler_params=pltpu.CompilerParams(vmem_limit_bytes=VMEM_LIMIT),
        cost_estimate=pl.CostEstimate(flops=1, bytes_accessed=1, transcendentals=0),
        name="middle",
    )(
        place, *attention, own_logit, lent_logit, tok, cot, gain, gain_first, out_weight, *rest_parts,
        *[up_weight] * 4, *up_parts, down_weight, *rest_parts,
    )


def shifted(x, axis, by):
    peers = lax.axis_size(axis)
    return lax.ppermute(x, axis, [(i, i + by) for i in range(peers) if 0 <= i + by < peers])


def crossed(x, by):
    peers, pair = lax.axis_size("ctx"), 2
    return lax.ppermute(
        x,
        ("ctx", "fsdp"),
        [(i * pair + s, (i + by) * pair + 1 - s) for i in range(peers) if 0 <= i + by < peers for s in range(pair)],
    )


def pick(x, index, axis=0):
    return lax.dynamic_index_in_dim(x, index, axis, keepdims=False)


def part(x, index, axis):
    size = x.shape[axis] // 2
    return lax.dynamic_slice_in_dim(x, index * size, size, axis)


def quarter(shard, q, start=0, count=None):
    wide = shard.shape[1] // 4
    return lax.dynamic_slice(shard, (start, q * wide), (count or shard.shape[0], wide))


class Reduction:
    def __init__(self, order, blocks):
        self.here = lax.axis_index("ctx")
        levels = lax.axis_size("ctx").bit_length() - 1
        self.order = list(order) + [level for level in range(levels) if level not in order]
        self.left = list(range(levels))
        self.kept, *sent = blocks
        self.send(sent)

    def bit(self):
        return (self.here >> self.order[0]) & 1

    def send(self, arrays):
        level = self.order.pop(0)
        self.left.remove(level)
        self.got = [partner(array, "ctx", 1 << level) for array in arrays]

    def step(self):
        below = 1 << self.left.index(self.order[0])
        self.kept, sent = halving_step(self.bit().astype(jnp.int32)[None], below, self.kept, self.got)
        self.send([sent])
        return sent

    def result(self, sizes):
        while self.order:
            self.step()
        total = (self.kept.astype(f32) + self.got[0].astype(f32))[0]
        ends = [sum(sizes[: i + 1]) for i in range(len(sizes))]
        return [total[end - size : end] for end, size in zip(ends, sizes)]


class Sequence:
    def __init__(self):
        self.last = ()

    def gate(self, *values):
        return lax.optimization_barrier(values + self.last)[: len(values)]

    def mark(self, *values):
        self.last = values


def added(value, axis):
    for level in range(lax.axis_size(axis).bit_length() - 1):
        value = value + partner(value, axis, 1 << level)
    return value


def rms_scale(values, gain):
    return values * lax.rsqrt(jnp.mean(values * values, axis=-1, keepdims=True) + 1e-05) * gain


def sided(mine, theirs, y, axis):
    return jnp.where(
        y == 0, jnp.concatenate([mine, theirs], axis=axis), jnp.concatenate([theirs, mine], axis=axis)
    )


UP_ROWS = (0, 320, 512)


def local(
    inputs,
    qkv_weight,
    gate_weight,
    out_weight,
    up_weight,
    down_weight,
    conv_taps,
    gain_attn,
    gain_ffn,
    ridge_terms,
    forget,
    cotangent,
):
    tokens = inputs[0]
    rows = tokens.shape[0]
    y = lax.axis_index("fsdp")
    here = lax.axis_index("ctx")
    peers = lax.axis_size("ctx")
    owners = peers * 2
    near_x = here % 4
    near_z = here % 2 + 2 * ((here // 4) % 2)
    place = jnp.stack([y, near_x, near_z]).astype(jnp.int32)
    spot = here.astype(jnp.int32)[None]
    spot_back = (peers - 1 - here).astype(jnp.int32)[None]
    ring = near_x.astype(jnp.int32)[None]
    seq = Sequence()

    lines = jnp.stack([gain_attn, gain_ffn, ridge_terms, ridge_terms])
    mine, theirs = norm(place, tokens, conv_taps, lines)
    theirs = partner(theirs, "fsdp")
    gain_mine = gain_attn.astype(f32)
    peer_extra, left_theirs = lax.optimization_barrier((theirs[rows:], (theirs[:rows] * gain_mine).astype(bf16)))
    lent_qk = nn(left_theirs, qkv_weight[:, : 2 * D]).astype(bf16)
    seq.mark(lent_qk)
    lent_qk = partner(lent_qk, "fsdp")
    (left,) = seq.gate(left_theirs)
    lent_v = jnp.concatenate([nn(left, qkv_weight[:, 2 * D :]).astype(bf16), nn(left, gate_weight).astype(bf16)], axis=1)
    seq.mark(lent_v)
    lent_v = partner(lent_v, "fsdp")
    (left,) = seq.gate(mine)
    own_qk = nn(left, qkv_weight[:, : 2 * D])
    own_v = nn(left, qkv_weight[:, 2 * D :])
    own_gate = nn(left, gate_weight)
    (peer_extra,) = seq.gate(peer_extra)
    taps_rows = KW * 3
    vectors = sided(lines[:3].astype(f32), peer_extra[taps_rows : taps_rows + 3], y, 1)
    taps = sided(conv_taps.astype(f32), peer_extra[:taps_rows].reshape(conv_taps.shape), y, 1)
    gain_first, gain_second = vectors[0], vectors[1:2]
    ridge = vectors[2].reshape(HEADS, HEAD_DIM)
    cumulative = jnp.cumsum(jnp.log(forget[0]).T, axis=-1)
    strength = (1.0 - forget[0]).T
    out_here, up_here, down_here = seq.gate(out_weight, up_weight, down_weight)
    rest_quarter = jnp.concatenate([quarter(out_here, near_x), quarter(down_here, near_x)], axis=0)
    seq.mark(own_qk, own_v, own_gate, rest_quarter, taps, cumulative, strength)
    rest_direct = partner(rest_quarter, "fsdp")
    (up_here,) = seq.gate(up_here)
    up_quarters = [
        quarter(up_here, near, start, stop - start)
        for near, start, stop in zip((near_z, near_x), UP_ROWS, UP_ROWS[1:])
    ]
    seq.mark(*up_quarters)

    own_qk, lent_qk = seq.gate(own_qk, lent_qk)

    def halo_of(own, lent):
        return shifted((own[rows - 8 :] + lent[rows - 8 :].astype(f32)).astype(bf16), "ctx", 1)

    halo_qk = halo_of(own_qk, lent_qk)
    queries, keys_low, key_states = keys(own_qk, lent_qk, halo_qk, taps, cumulative, strength)
    seq.mark(key_states)
    own_v, lent_v, up_first = seq.gate(own_v, lent_v, up_quarters[0])
    halo_v = halo_of(own_v, lent_v[:, :D])
    values_low, *own = values(spot, own_v, lent_v, halo_v, taps, keys_low, key_states, cumulative, strength)
    seq.mark(*own)
    scan = Scan(spot, swapped(own, "ctx"), "ctx")
    up_first = partner(up_first, "fsdp")

    def split(left):
        flat = left.reshape(peers, 2, left.shape[0] // owners, left.shape[1])
        return [pick(flat, side, 1).reshape(-1, left.shape[1]) for side in (y, 1 - y)]

    scan.near = list(seq.gate(*scan.near))
    scan.group()
    seq.mark(scan.total)
    (rest_direct,) = seq.gate(rest_direct)
    rest_across = partner(rest_direct, "ctx", 2)
    scan.far = list(seq.gate(*scan.far))
    states = scan.spread()
    seq.mark(scan.parts[0])
    up_first, up_second = seq.gate(up_first, up_quarters[1])
    up_second = partner(up_second, "fsdp")
    first_across = partner(up_first, "ctx", 4)
    *states, queries = seq.gate(*states, queries)
    seq.mark(states[1], states[2], states[3])
    rest_direct, rest_across, up_first, up_second = seq.gate(rest_direct, rest_across, up_first, up_second)
    second_across = partner(up_second, "ctx", 2)
    rest_core, rest_far, first_core = partner(rest_direct, "ctx", 1), partner(rest_across, "ctx", 1), partner(up_first, "ctx", 1)
    (queries,) = seq.gate(queries)
    x, p_all, m_all, scores, scal = solve(ring, queries, keys_low, states, cumulative, strength, ridge)
    seq.mark(x)

    def share(right):
        return right, partner(right, "fsdp")

    def below(pair):
        return jnp.concatenate(pair, axis=0)

    rest_core, rest_far, first_core, first_across, up_second, second_across = seq.gate(
        rest_core, rest_far, first_core, first_across, up_second, second_across
    )
    rest_parts = (rest_direct, rest_across, rest_core, rest_far)
    up_parts = (up_first, first_across, first_core, partner(first_across, "ctx", 1))
    up_parts += (up_second, second_across, partner(up_second, "ctx", 1), partner(second_across, "ctx", 1))

    output, grad_hidden, grad_attended, lefts, message, grad_gate_up, grad_second_gain = middle(
        owners, place, (x, *states, keys_low, values_low, cumulative, strength), own_gate, lent_v,
        tokens, cotangent[0], gain_second, gain_first[None], out_weight, up_weight, down_weight, up_parts, rest_parts
    )
    size = D // 2
    parts = [slice(0, size), slice(size, 2 * size), slice(2 * size, 3 * size), slice(3 * size, 3 * size + FF // 2)]
    start = 3 * BLOCKS * rows
    peer_parts = [slice(start + at.start, start + at.stop) for at in parts]
    if (D // owners) % 8 or (FF // owners) % 8:
        pairs = [split(jnp.concatenate([lefts[at], message[there]], axis=0)) for at, there in zip(parts, peer_parts)]
        lefts = jnp.concatenate([own for own, _ in pairs], axis=0)
        message = jnp.concatenate([message[:start]] + [sent for _, sent in pairs], axis=0)
    seq.mark(grad_second_gain)
    message_peer = partner(message, "fsdp")
    (grad_attended,) = seq.gate(grad_attended)
    gx, dk_attend, dv, value_states = attend_back(
        ring, grad_attended, keys_low, values_low, x, states, cumulative, strength
    )
    dq, dk_solve, grad_ridge, *own = adjoint(
        spot_back, ring, gx, keys_low, states, cumulative, strength, ridge, p_all, m_all, scores, scal, value_states
    )
    seq.mark(*own)
    back = Scan(spot_back, swapped(own, "ctx"), "ctx")
    (up_here,) = seq.gate(grad_gate_up)
    both_up = share(up_here)
    dq, back.near[1] = seq.gate(dq, back.near[1])
    low_q, taps_q = queries_back((own_qk, lent_qk, halo_qk), taps, dq)
    seq.mark(low_q)
    back.near = list(seq.gate(*back.near))
    back.group()
    seq.mark(back.total)
    lefts_here, message_peer, back.far[1] = seq.gate(lefts, message_peer, back.far[1])
    rights = [(i * BLOCKS * rows, rows) for i in range(3)]
    (early,) = products(
        spot, peers, [[(lefts_here, parts[i]), (message_peer, peer_parts[i])] for i in (1, 2, 3)],
        [[(message, at), (message_peer, at)] for at in rights], 256, joined=True
    )
    seq.mark(early)
    early = lax.psum_scatter(early.reshape(-1, D), "ctx", scatter_dimension=0, tiled=True)
    back.far = list(seq.gate(*back.far))
    states_back = back.spread()
    seq.mark(back.parts[0])
    dv, *states_back = seq.gate(dv, *states_back)
    low_v, taps_v = values_back(
        spot_back, (own_v, lent_v, halo_v), taps, dv, keys_low, states_back, cumulative, strength
    )
    seq.mark(low_v)
    (dk_attend,) = seq.gate(dk_attend)
    low_k, taps_k = keys_back(
        spot_back, (own_qk, lent_qk, halo_qk), taps, dk_attend, dk_solve, keys_low, values_low, states_back, cumulative, strength
    )
    seq.mark(low_k)
    ahead = jnp.concatenate([low[HALO - 8 : HALO] for low in (low_q, low_k, low_v)], axis=1)
    extra = shifted(ahead, "ctx", -1), crossed(ahead, -1)
    thirds = jnp.concatenate([low_q, low_k, low_v], axis=0)
    seq.mark(thirds)
    thirds_peer = partner(thirds, "fsdp")
    up_peer, *extra = seq.gate(both_up[1], *extra)
    blocks = products(
        spot, peers, [[(lefts, parts[0]), (message_peer, peer_parts[0])]], [[(both_up[0], None), (up_peer, None)]], 512
    )
    seq.mark(blocks[0])
    ups = Reduction((0, 1, 2), blocks)
    ups.got = seq.gate(*ups.got)
    seq.mark(ups.step())
    lefts_here, thirds_peer = seq.gate(lefts, thirds_peer)
    left = [(lefts_here, parts[2]), (message_peer, peer_parts[2])]
    rights = [[(thirds, i), (thirds_peer, i), (extra[0], i), (extra[1], i)] for i in range(3)]
    blocks = products(spot, peers, [left] * 3, rights, 256, messages=2)
    seq.mark(blocks[0])
    late = Reduction((0, 1, 2), blocks)
    late.got = seq.gate(*late.got)
    seq.mark(late.step())
    ups.got = seq.gate(*ups.got)
    seq.mark(ups.step())
    (thirds_here,) = seq.gate(thirds)
    kept, lent = lent_rows(thirds_here, thirds_peer, extra, (message, message_peer), qkv_weight, gate_weight)
    seq.mark(lent)
    arriving = partner(lent, "fsdp")
    late.got = seq.gate(*late.got)
    seq.mark(late.step())
    (arriving,) = seq.gate(arriving)
    grad_tokens, vector = norm_back(
        place, kept, arriving, tokens, gain_first[None], grad_hidden, (taps_q, taps_k, taps_v), grad_second_gain, grad_ridge
    )
    seq.mark(vector)
    size, width = D // owners, 3 * D // owners
    vector = jnp.concatenate(
        [vector[:KW].reshape(KW, owners, width).transpose(1, 0, 2).reshape(owners, KW * width),
         vector[KW].reshape(3, owners, size).transpose(1, 0, 2).reshape(owners, 3 * size)], axis=1
    ).reshape(peers, 2, KW * width + 3 * size)
    vector_kept, vector_sent = pick(vector, y, 1), pick(vector, 1 - y, 1)
    seq.mark(vector_sent)
    arriving = partner(vector_sent, "fsdp")
    *ups.got, early = seq.gate(*ups.got, early)
    seq.mark(ups.step())
    vector_kept, arriving = seq.gate(vector_kept, arriving)
    vector = vector_kept + arriving
    seq.mark(vector)
    vector = lax.all_to_all(vector, "ctx", 0, 0, tiled=True)
    late.got = seq.gate(*late.got)
    seq.mark(late.step())
    vector = jnp.sum(seq.gate(vector)[0], axis=0)
    size = D // owners
    grad_up = ups.result([size])[0]
    grad_q, grad_k, grad_v = late.result([size] * 3)
    grad_qkv = jnp.concatenate([grad_q, grad_k, grad_v], axis=1)
    early = early.astype(f32)
    grad_out, grad_gate, grad_down = early[:size], early[size : 2 * size], early[2 * size :]
    return (
        output[None],
        grad_tokens[None],
        grad_qkv,
        grad_gate,
        grad_out,
        grad_up,
        grad_down,
        vector[: KW * width].reshape(KW, width),
        vector[KW * width : KW * width + size],
        vector[KW * width + size : KW * width + 2 * size],
        vector[KW * width + 2 * size :],
    )


def solution(mesh):
    tokens = P("fsdp", "ctx", None)
    rows = P("fsdp", None)
    vector = P("fsdp")
    owned = P(("ctx", "fsdp"), None)
    owned_vector = P(("ctx", "fsdp"))
    return jax.shard_map(
        local,
        mesh=mesh,
        in_specs=(
            tokens, rows, rows, rows, rows, rows, P(None, "fsdp"), vector, vector, vector, tokens, tokens,
        ),
        out_specs=(
            tokens, tokens, owned, owned, owned, owned, owned, P(None, ("ctx", "fsdp")),
            owned_vector, owned_vector, owned_vector,
        ),
        check_vma=False,
    )
```

time: 2030 us -> 390 us (0.19)
  waiting for transfers between devices: 1580 us -> 120 us
  matrix products: 192 us -> 7.96 us
  Pallas kernels: 0 us -> 136 us
  blocking collectives: 92.9 us -> 0 us
  other arithmetic: 83.6 us -> 11.1 us
  starting transfers between devices: 3.89 us -> 65.3 us
    reduce_scatter x5 -> x1, waiting for transfers between devices: 1180 us -> 0.02 us  [local(): lax.psum_scatter(early.reshape(-1, D), 'ctx', scatter_dimension=0, tiled=...]
    all_gather x9 -> x0, waiting for transfers between devices: 394 us -> none  [the longest x1 137 us: local(): lax.all_gather(shards[3], 'fsdp', axis=0, tiled=True)]
    dot_general x102 -> x6, matrix products: 192 us -> 7.96 us  [nn(): lax.dot_general(a, b, (((1,), (0,)), ((), ())), preferred_element_type=f32)]
    pallas_call x0 -> x25, Pallas kernels: none -> 136 us  [the longest x1 24 us: middle(): pl.pallas_call(functools.partial(middle_kernel, owners), grid_spec=pltpu....]
    ppermute x2 -> x51, waiting for transfers between devices: 1.75 us -> 110 us  [the longest x47 105 us: partner(): return lax.ppermute(x, axis, neighbour(axis, bit))]
    unnamed x2 -> x0, blocking collectives: 74.6 us -> none
    ppermute x2 -> x51, starting transfers between devices: 3.29 us -> 60.4 us  [the longest x47 55.1 us: partner(): return lax.ppermute(x, axis, neighbour(axis, bit))]
    select_n x32 -> x2, other arithmetic: 43.8 us -> 0.64 us  [sided(): jnp.where(y == 0, jnp.concatenate([mine, theirs], axis=axis), jnp.concate...]
  transfers between devices with their start and end apart: 17 -> 53, of which waited for: 15 -> 30; matrix products, arithmetic and copies ran while one was open for 8% -> 6% of each run, Pallas kernels for 0% -> 27%
where the time goes in v3:
time: 390 us; the launch traced here: 388 us
  Pallas kernels  136 us (35%)
  waiting for transfers between devices  120 us (31%)
  starting transfers between devices  65.3 us (17%)
  local copies, waits for them, and re-layouts  32.4 us (8%)
  between operations  14.7 us (4%)
  other arithmetic  11.1 us (3%)
  matrix products  7.96 us (2%)
    ppermute x47, waiting for transfers between devices, partner(): return lax.ppermute(x, axis, neighbour(axis, bit))  105 us
    ppermute x47, starting transfers between devices, partner(): return lax.ppermute(x, axis, neighbour(axis, bit))  55.1 us
    pallas_call x1, Pallas kernels, middle(): pl.pallas_call(functools.partial(middle_kernel, owners), grid_spec=pltpu....  24 us
    pallas_call x3, Pallas kernels, products(): pl.pallas_call(functools.partial(products_kernel, plan, joined, cuts), gr...  21.9 us
    pallas_call x6, Pallas kernels, halving_step(): pl.pallas_call(step_kernel, grid_spec=pltpu.PrefetchScalarGridSpec(num_sc...  18 us
    unnamed x116, local copies, waits for them, and re-layouts  15.9 us
    pallas_call x1, Pallas kernels, adjoint(): pl.pallas_call(adjoint_kernel, grid=(ITERS,), in_specs=[smem(), smem(), w...  15.7 us
    pallas_call x3, Pallas kernels, third_back(): pl.pallas_call(kernel, grid=(QUARTERS,), in_specs=[smem()] * len(before)...  13.8 us
  transfers between devices with their start and end apart: 53, of which 30 were waited for; matrix products, arithmetic and copies ran while one was open for 6% of the time, Pallas kernels for 27%

profile of v3, /device:TPU:0, one launch (start us, length us, event | category | flops | bytes accessed | tf_op | source)
XLA Modules:
  0.0 387.9 jit_solution(271125670982379242)
XLA Ops:
  10.6 2.0 norm.1
  12.5 3.0 collective-permute-start
  19.0 3.7 collective-permute-done
  22.8 3.0 convolution_convert_fusion
  32.1 2.0 constant_dynamic-slice_fusion.3
  35.1 2.2 pad_maximum_fusion
  41.2 2.4 constant_dynamic-slice_fusion.2
  48.2 4.3 %keys.1 = (f32[8,128,128]{2,1,0:T(8,128)}, bf16[8,128,128]{2,1,0:T(8,128)(2,1)}, bf16[8,128,128]{2,1,0:T(8,128)(2,1)}) custom-call(f32[128,2048]{1,0:T(8,128)} %copy-done.1, f32[128,2048]{1,0:T(8,128)} %copy-done.1, bf16[128,2048]{1,0:T(8,128)(2,1)} %copy-done.6, bf16[128,2048]{1,0:T(8,128)(2,1)} %copy-done.6, bf16[8,2048]{1,0:T(8,128)(2,1)} %copy-done.40, ...), custom_call_target="tpu_custom_call" | custom-call | flops 1 | bytes 1 | tf_op jit(solution)/shard_map/keys/pallas_call | solution.py:195
  52.5 3.8 collective-permute-done.1.lv.lent_logit.lent
  60.8 4.3 %values.1 = (bf16[8,128,128]{2,1,0:T(8,128)(2,1)}, bf16[4,144,128]{2,1,0:T(8,128)(2,1)}, bf16[4,144,128]{2,1,0:T(8,128)(2,1)}, bf16[4,144,128]{2,1,0:T(8,128)(2,1)}, bf16[4,144,128]{2,1,0:T(8,128)(2,1)}) custom-call(s32[1]{0:T(128)} %bitcast.3.spot, f32[128,1024]{1,0:T(8,128)} %copy-done.8, bf16[128,2048]{1,0:T(8,128)(2,1)} %copy-done.9, ...), custom_call_target="tpu_custom_call" | custom-call | flops 1 | bytes 1 | tf_op jit(solution)/shard_map/values/pallas_call | solution.py:209
  65.2 2.3 collective-permute-start.5
  67.5 2.3 collective-permute-start.6
  69.9 4.8 %collective-permute-done.6.refs_2_.refs_6_ = bf16[4,144,128]{2,1,0:T(8,128)(2,1)S(1)} collective-permute-done((bf16[4,144,128]{2,1,0:T(8,128)(2,1)}, bf16[4,144,128]{2,1,0:T(8,128)(2,1)S(1)}, u32[]{:S(2)}, u32[]{:S(2)}) %collective-permute-start.6) | collective-permute-done | bytes 147488 | tf_op jit(solution)/shard_map/ppermute | solution.py:315
  74.7 2.6 collective-permute-done.7.refs_3_.refs_7_
  81.5 3.6 collective-permute-start.10
  85.9 4.3 %collective-permute-done.10.refs_3_ = bf16[4,144,128]{2,1,0:T(8,128)(2,1)S(1)} collective-permute-done((bf16[4,144,128]{2,1,0:T(8,128)(2,1)}, bf16[4,144,128]{2,1,0:T(8,128)(2,1)S(1)}, u32[]{:S(2)}, u32[]{:S(2)}) %collective-permute-start.10) | collective-permute-done | bytes 147488 | tf_op jit(solution)/shard_map/ppermute | solution.py:315
  90.2 3.7 collective-permute-done.8.refs_1_
  93.9 4.5 %collective-permute-done.9.refs_2_ = bf16[4,144,128]{2,1,0:T(8,128)(2,1)S(1)} collective-permute-done((bf16[4,144,128]{2,1,0:T(8,128)(2,1)}, bf16[4,144,128]{2,1,0:T(8,128)(2,1)S(1)}, u32[]{:S(2)}, u32[]{:S(2)}) %collective-permute-start.9) | collective-permute-done | bytes 147488 | tf_op jit(solution)/shard_map/ppermute | solution.py:315
  99.0 2.6 spread.2
  104.1 4.6 %collective-permute-done.12.s2 = bf16[4,128,128]{2,1,0:T(8,128)(2,1)S(1)} collective-permute-done((bf16[4,128,128]{2,1,0:T(8,128)(2,1)}, bf16[4,128,128]{2,1,0:T(8,128)(2,1)S(1)}, u32[]{:S(2)}, u32[]{:S(2)}) %collective-permute-start.12) | collective-permute-done | bytes 131104 | tf_op jit(solution)/shard_map/ppermute | solution.py:315
  108.7 2.0 collective-permute-done.13.s3
  110.7 5.0 %collective-permute-done.17.refs_8_ = bf16[192,1408]{1,0:T(8,128)(2,1)S(1)} collective-permute-done((bf16[192,1408]{1,0:T(8,128)(2,1)}, bf16[192,1408]{1,0:T(8,128)(2,1)S(1)}, u32[]{:S(2)}, u32[]{:S(2)}) %collective-permute-start.17) | collective-permute-done | bytes 540704 | tf_op jit(solution)/shard_map/ppermute | solution.py:315
  118.3 10.1 %solve.1 = (bf16[8,128,128]{2,1,0:T(8,128)(2,1)}, f32[8,8,128,128]{3,2,1,0:T(8,128)}, f32[8,8,128,128]{3,2,1,0:T(8,128)}, bf16[8,8,128,128]{3,2,1,0:T(8,128)(2,1)}, f32[8,24,128]{2,1,0:T(8,128)}) custom-call(s32[1]{0:T(128)} %bitcast.1.place, f32[8,128,128]{2,1,0:T(8,128)} %get-tuple-element.197.q_ref, bf16[8,128,128]{2,1,0:T(8,128)(2,1)} %get-tuple-element.175.k_ref, ...), custom_call_target="tpu_custom_call" | custom-call | flops 1 | bytes 1 | tf_op jit(solution)/shard_map/solve/pallas_call | solution.py:443
  128.4 9.9 %collective-permute-done.21.refs_5_ = bf16[320,1408]{1,0:T(8,128)(2,1)S(1)} collective-permute-done((bf16[320,1408]{1,0:T(8,128)(2,1)}, bf16[320,1408]{1,0:T(8,128)(2,1)S(1)}, u32[]{:S(2)}, u32[]{:S(2)}) %collective-permute-start.21) | collective-permute-done | bytes 901152 | tf_op jit(solution)/shard_map/ppermute | solution.py:315
  139.1 2.6 collective-permute-done.24.refs_10_
  143.6 24.0 %middle.1 = (f32[128,1024]{1,0:T(8,128)}, f32[128,1024]{1,0:T(8,128)}, f32[128,1024]{1,0:T(8,128)}, bf16[2944,128]{1,0:T(8,128)(2,1)}, bf16[6016,128]{1,0:T(8,12...) custom-call(s32[3]{0:T(128)} %pad_add_fusion.place, bf16[8,128,128]{2,1,0:T(8,128)(2,1)} %get-tuple-element.199.x_ref, ...), custom_call_target="tpu_custom_call" | custom-call | flops 1 | bytes 1 | tf_op jit(solution)/shard_map/middle/pallas_call | solution.py:1065
  168.3 4.8 %attend_back.1 = (f32[8,128,128]{2,1,0:T(8,128)}, f32[8,128,128]{2,1,0:T(8,128)}, f32[8,128,128]{2,1,0:T(8,128)}, bf16[8,128,128]{2,1,0:T(8,128)(2,1)}) custom-call(s32[1]{0:T(128)} %bitcast.1.place, f32[128,1024]{1,0:T(8,128)} %get-tuple-element.218.ga_ref, bf16[8,128,128]{2,1,0:T(8,128)(2,1)} %get-tuple-element.175.k_ref, ...), custom_call_target="tpu_custom_call" | custom-call | flops 1 | bytes 1 | tf_op jit(solution)/shard_map/attend_back/pallas_call | solution.py:488
  173.1 15.7 %adjoint.1 = (f32[8,128,128]{2,1,0:T(8,128)}, f32[8,128,128]{2,1,0:T(8,128)}, f32[8,1,128]{2,1,0:T(1,128)}, bf16[4,144,128]{2,1,0:T(8,128)(2,1)}, bf16[4,144,128...) custom-call(s32[1]{0:T(128)} %bitcast.13.spot, s32[1]{0:T(128)} %bitcast.1.place, ...), custom_call_target="tpu_custom_call" | custom-call | flops 1 | bytes 1 | tf_op jit(solution)/shard_map/adjoint/pallas_call | solution.py:574
  190.7 4.4 %queries_back.1 = (bf16[144,1024]{1,0:T(8,128)(2,1)}, f32[4,1024]{1,0:T(4,128)}) custom-call(f32[128,2048]{1,0:T(8,128)} %copy-done.1, bf16[128,2048]{1,0:T(8,128)(2,1)} %copy-done.6, bf16[8,2048]{1,0:T(8,128)(2,1)} %copy-done.40, f32[4,3072]{1,0:T(4,128)} %maximum_select_fusion.tq.tk.tv.t, f32[8,128,128]{2,1,0:T(8,128)} %get-tuple-element.230.dq_ref), custom_call_target="tpu_custom_call" | custom-call | flops 1 | bytes 1 | tf_op jit(solution)/shard_map/queries_back/pallas_call | solution.py:665
  195.8 2.3 collective-permute-done.28.refs_3_.refs_7_
  198.7 1.9 group.3.refs_0_
  200.9 6.3 %collective-permute-done.30.refs_1_ = bf16[4,144,128]{2,1,0:T(8,128)(2,1)S(1)} collective-permute-done((bf16[4,144,128]{2,1,0:T(8,128)(2,1)}, bf16[4,144,128]{2,1,0:T(8,128)(2,1)S(1)}, u32[]{:S(2)}, u32[]{:S(2)}) %collective-permute-start.30) | collective-permute-done | bytes 147488 | tf_op jit(solution)/shard_map/ppermute | solution.py:315
  208.3 6.4 %products.3 = bf16[16,152,1024]{2,1,0:T(8,128)(2,1)} custom-call(s32[1]{0:T(128)} %bitcast.3.spot, bf16[2944,128]{1,0:T(8,128)(2,1)} %get-tuple-element.269.refs_0_.refs_4_.refs_8_.refs_6_.refs_12_, bf16[6016,128]{1,0:T(8,128)(2,1)} %copy-done, bf16[6016,128]{1,0:T(8,128)(2,1)} %get-tuple-element.240.refs_2_.refs_6_.refs_10_.logit1, ...), custom_call_target="tpu_custom_call" | custom-call | flops 1 | bytes 1 | tf_op jit(solution)/shard_map/products/pallas_call | solution.py:804
  220.2 9.8 %collective-permute-done.31.refs_2_ = bf16[4,144,128]{2,1,0:T(8,128)(2,1)S(1)} collective-permute-done((bf16[4,144,128]{2,1,0:T(8,128)(2,1)S(1)}, bf16[4,144,128]{2,1,0:T(8,128)(2,1)S(1)}, u32[]{:S(2)}, u32[]{:S(2)}) %collective-permute-start.31) | collective-permute-done | bytes 147488 | tf_op jit(solution)/shard_map/ppermute | solution.py:315
  231.3 2.7 spread.3
  235.9 4.6 %collective-permute-done.34.r2 = bf16[4,128,128]{2,1,0:T(8,128)(2,1)S(1)} collective-permute-done((bf16[4,128,128]{2,1,0:T(8,128)(2,1)}, bf16[4,128,128]{2,1,0:T(8,128)(2,1)S(1)}, u32[]{:S(2)}, u32[]{:S(2)}) %collective-permute-start.34) | collective-permute-done | bytes 131104 | tf_op jit(solution)/shard_map/ppermute | solution.py:315
  240.6 2.0 collective-permute-done.35.r3
  243.2 4.3 %values_back.1 = (bf16[144,1024]{1,0:T(8,128)(2,1)}, f32[4,1024]{1,0:T(4,128)}) custom-call(s32[1]{0:T(128)} %bitcast.13.spot, f32[128,1024]{1,0:T(8,128)} %copy-done.8, bf16[128,2048]{1,0:T(8,128)(2,1)} %copy-done.9, bf16[8,1024]{1,0:T(8,128)(2,1)} %copy-done.54, f32[4,3072]{1,0:T(4,128)} %maximum_select_fusion.tq.tk.tv.t, ...), custom_call_target="tpu_custom_call" | custom-call | flops 1 | bytes 1 | tf_op jit(solution)/shard_map/values_back/pallas_call | solution.py:665
  247.5 5.1 %keys_back.1 = (bf16[144,1024]{1,0:T(8,128)(2,1)}, f32[4,1024]{1,0:T(4,128)}) custom-call(s32[1]{0:T(128)} %bitcast.13.spot, f32[128,2048]{1,0:T(8,128)} %copy-done.1, bf16[128,2048]{1,0:T(8,128)(2,1)} %copy-done.6, bf16[8,2048]{1,0:T(8,128)(2,1)} %copy-done.40, f32[4,3072]{1,0:T(4,128)} %maximum_select_fusion.tq.tk.tv.t, ...), custom_call_target="tpu_custom_call" | custom-call | flops 1 | bytes 1 | tf_op jit(solution)/shard_map/keys_back/pallas_call | solution.py:665
  257.0 3.0 collective-permute-done.38.refs_5_.refs_11_.refs_17_.extra2
  260.1 10.1 %products.4 = (bf16[8,32,5632]{2,1,0:T(8,128)(2,1)}, bf16[8,32,5632]{2,1,0:T(8,128)(2,1)}) custom-call(s32[1]{0:T(128)} %bitcast.3.spot, bf16[2944,128]{1,0:T(8,128)(2,1)} %get-tuple-element.269.refs_0_.refs_4_.refs_8_.refs_6_.refs_12_, bf16[6016,128]{1,0:T(8,128)(2,1)} %copy-done, bf16[128,5632]{1,0:T(8,128)(2,1)} %get-tuple-element.262.refs_2_, ...), custom_call_target="tpu_custom_call" | custom-call | flops 1 | bytes 1 | tf_op jit(solution)/shard_map/products/pallas_call | solution.py:804
  270.2 2.3 collective-permute-start.39
  273.5 4.3 %collective-permute-done.39.refs_0_.refs_1_ = bf16[8,32,5632]{2,1,0:T(8,128)(2,1)} collective-permute-done((bf16[8,32,5632]{2,1,0:T(8,128)(2,1)}, bf16[8,32,5632]{2,1,0:T(8,128)(2,1)}, u32[]{:S(2)}, u32[]{:S(2)}) %collective-permute-start.39) | collective-permute-done | bytes 2883616 | tf_op jit(solution)/shard_map/ppermute | solution.py:315
  277.8 4.7 %halving.6 = (bf16[4,32,5632]{2,1,0:T(8,128)(2,1)}, bf16[4,32,5632]{2,1,0:T(8,128)(2,1)}) custom-call(s32[1]{0:T(128)} %bitcast.15.bit, bf16[8,32,5632]{2,1,0:T(8,128)(2,1)} %get-tuple-element.264.kept_mine.kept_other, bf16[8,32,5632]{2,1,0:T(8,128)(2,1)} %get-tuple-element.264.kept_mine.kept_other, ...), custom_call_target="tpu_custom_call" | custom-call | flops 1 | bytes 1 | tf_op jit(solution)/shard_map/halving/pallas_call | solution.py:897
  282.5 2.5 collective-permute-start.40
  285.0 9.1 %collective-permute-done.41.refs_3_.refs_9_.refs_15_.peer = bf16[432,1024]{1,0:T(8,128)(2,1)S(1)} collective-permute-done((bf16[432,1024]{1,0:T(8,128)(2,1)S(1)}, bf16[432,1024]{1,0:T(8,128)(2,1)S(1)}, u32[]{:S(2)}, u32[]{:S(2)}) %collective-permute-start.41) | collective-permute-done | bytes 884768 | tf_op jit(solution)/shard_map/ppermute | solution.py:315
  295.1 5.4 %products.5 = (bf16[8,96,1024]{2,1,0:T(8,128)(2,1)}, bf16[8,48,1024]{2,1,0:T(8,128)(2,1)}, bf16[8,48,1024]{2,1,0:T(8,128)(2,1)}) custom-call(s32[1]{0:T(128)} %bitcast.3.spot, bf16[2944,128]{1,0:T(8,128)(2,1)} %get-tuple-element.269.refs_0_.refs_4_.refs_8_.refs_6_.refs_12_, bf16[6016,128]{1,0:T(8,128)(2,1)} %copy-done, bf16[432,1024]{1,0:T(8,128)(2,1)} %copy-done.2, ...), custom_call_target="tpu_custom_call" | custom-call | flops 1 | bytes 1 | tf_op jit(solution)/shard_map/products/pallas_call | solution.py:804
  301.1 2.0 collective-permute-done.42.refs_0_.refs_1_
  305.1 4.0 %halving.7 = (bf16[4,96,1024]{2,1,0:T(8,128)(2,1)}, bf16[4,96,1024]{2,1,0:T(8,128)(2,1)}) custom-call(s32[1]{0:T(128)} %bitcast.15.bit, bf16[8,96,1024]{2,1,0:T(8,128)(2,1)} %get-tuple-element.273.kept_mine.kept_other, bf16[8,96,1024]{2,1,0:T(8,128)(2,1)} %get-tuple-element.273.kept_mine.kept_other, bf16[8,48,1024]{2,1,0:T(8,128)(2,1)} %copy-done.13, ...), custom_call_target="tpu_custom_call" | custom-call | flops 1 | bytes 1 | tf_op jit(solution)/shard_map/halving/pallas_call | solution.py:897
  309.1 2.4 collective-permute-start.45
  311.6 6.1 %collective-permute-done.40.refs_0_.refs_1_ = bf16[4,32,5632]{2,1,0:T(8,128)(2,1)S(1)} collective-permute-done((bf16[4,32,5632]{2,1,0:T(8,128)(2,1)}, bf16[4,32,5632]{2,1,0:T(8,128)(2,1)S(1)}, u32[]{:S(2)}, u32[]{:S(2)}) %collective-permute-start.40) | collective-permute-done | bytes 1441824 | tf_op jit(solution)/shard_map/ppermute | solution.py:315
  318.8 2.7 halving.8
  321.5 4.0 %collective-permute-start.48 = (bf16[2,32,5632]{2,1,0:T(8,128)(2,1)}, bf16[2,32,5632]{2,1,0:T(8,128)(2,1)S(1)}, u32[]{:S(2)}, u32[]{:S(2)}) collective-permute-start(bf16[2,32,5632]{2,1,0:T(8,128)(2,1)} %get-tuple-element.280), channel_id=1, source_target_pairs={{0,8},{2,10},{4,12},{6,14},{8,0},{10,2},{12,4},{14,6},{16,24},{18,... | collective-permute-start | bytes 2162696 | tf_op jit(solution)/shard_map/ppermute | solution.py:315
  325.5 5.6 %lent_rows.1 = (f32[128,512]{1,0:T(8,128)}, bf16[128,512]{1,0:T(8,128)(2,1)}) custom-call(bf16[432,1024]{1,0:T(8,128)(2,1)} %copy-done.2, bf16[432,1024]{1,0:T(8,128)(2,1)} %copy-done.3, bf16[8,3072]{1,0:T(8,128)(2,1)} %copy-done.27, bf16[8,3072]{1,0:T(8,128)(2,1)} %copy-done.28, bf16[6016,128]{1,0:T(8,128)(2,1)} %get-tuple-element.240.refs_2_.refs_6_.refs_10_.logit1, ...), custom_call_target="tpu_custom_call" | custom-call | flops 1 | bytes 1 | tf_op jit(solution)/shard_map/lent_rows/pallas_call | solution.py:836
  332.1 2.1 collective-permute-done.45.refs_0_.refs_1_
  335.1 2.2 halving.9
  337.3 4.0 %collective-permute-start.46 = (bf16[2,96,1024]{2,1,0:T(8,128)(2,1)}, bf16[2,96,1024]{2,1,0:T(8,128)(2,1)S(1)}, u32[]{:S(2)}, u32[]{:S(2)}) collective-permute-start(bf16[2,96,1024]{2,1,0:T(8,128)(2,1)} %get-tuple-element.286), channel_id=1, source_target_pairs={{0,8},{2,10},{4,12},{6,14},{8,0},{10,2},{12,4},{14,6},{16,24},{18,... | collective-permute-start | bytes 1179656 | tf_op jit(solution)/shard_map/ppermute | solution.py:315
  342.0 2.5 norm_back.1
  348.8 2.3 halving.10
  352.4 4.9 %all-to-all-start = ((f32[16,1,480]{2,1,0:T(1,128)}), f32[16,1,480]{2,1,0:T(1,128)S(1)}, u32[]{:S(2)}, u32[]{:S(2)}) async-start(f32[16,1,480]{2,1,0:T(1,128)} %all_to_all.8), calls=%async_computation.1 | async-start | bytes 65536 | tf_op jit(solution)/shard_map/all_to_all | solution.py:1412
  358.7 2.0 halving.11
  361.5 2.8 collective-permute-start.49
  364.3 10.5 %all-to-all-done = f32[16,1,480]{2,1,0:T(1,128)S(1)} async-done(((f32[16,1,480]{2,1,0:T(1,128)}), f32[16,1,480]{2,1,0:T(1,128)S(1)}, u32[]{:S(2)}, u32[]{:S(2)}) %all-to-all-start) | async-done | bytes 30752 | tf_op jit(solution)/shard_map/all_to_all | solution.py:1412
  376.1 2.2 collective-permute-done.49
  (241 shorter events, 79.3 us)
Async XLA Ops:
  7.2 20.1 %copy-start.5 = (bf16[512,1024]{1,0:T(8,128)(2,1)S(1)}, bf16[512,1024]{1,0:T(8,128)(2,1)}, u32[]{:S(2)}) copy-start(bf16[512,1024]{1,0:T(8,128)(2,1)} %gate_ref.1) | copy-start | bytes 3145732
  7.2 340.8 %reduce-scatter.2.cloned.1.call-start = ((), (), s32[]{:S(2)}) async-start(), calls=%async_computation.2 | async-start | bytes 5292032 | tf_op jit(solution)/shard_map/reduce_scatter | solution.py:1351
  12.5 10.2 %collective-permute-start = (f32[144,512]{1,0:T(8,128)}, f32[144,512]{1,0:T(8,128)S(1)}, u32[]{:S(2)}, u32[]{:S(2)}) collective-permute-start(f32[144,512]{1,0:T(8,128)} %get-tuple-element.160), channel_id=1, source_target_pairs={{0,1},{1,0},{2,3},{3,2},{4,5},{5,4},{6,7},{7,6},{8,9},{9,8},{10,11... | collective-permute-start | bytes 884744 | tf_op jit(solution)/shard_map/ppermute | solution.py:315
  28.9 16.5 %copy-start.1 = (f32[128,2048]{1,0:T(8,128)}, f32[128,2048]{1,0:T(8,128)S(1)}, u32[]{:S(2)}) copy-start(f32[128,2048]{1,0:T(8,128)S(1)} %fusion.oq.ok.own) | copy-start | bytes 3145732
  30.1 15.3 %collective-permute-start.2 = (bf16[128,2048]{1,0:T(8,128)(2,1)}, bf16[128,2048]{1,0:T(8,128)(2,1)S(1)}, u32[]{:S(2)}, u32[]{:S(2)}) collective-permute-start(bf16[128,2048]{1,0:T(8,128)(2,1)} %convolution_convert_fusion), channel_id=1, source_target_pairs={{0,1},{1,0},{2,3},{3,2},{4,5},{5,4},{6,7},{7,6},{8,9},{9,8},{10,11... | collective-permute-start | bytes 1572872 | tf_op jit(solution)/shard_map/ppermute | solution.py:315
  31.8 24.6 %collective-permute-start.1 = (bf16[128,2048]{1,0:T(8,128)(2,1)}, bf16[128,2048]{1,0:T(8,128)(2,1)S(1)}, u32[]{:S(2)}, u32[]{:S(2)}) collective-permute-start(bf16[128,2048]{1,0:T(8,128)(2,1)} %pad_maximum_fusion.1), channel_id=1, source_target_pairs={{0,1},{1,0},{2,3},{3,2},{4,5},{5,4},{6,7},{7,6},{8,9},{9,8},{10,11... | collective-permute-start | bytes 1572872 | tf_op jit(solution)/shard_map/ppermute | solution.py:315
  37.3 42.6 %collective-permute-start.14 = (bf16[1920,256]{1,0:T(8,128)(2,1)}, bf16[1920,256]{1,0:T(8,128)(2,1)}, u32[]{:S(2)}, u32[]{:S(2)}) collective-permute-start(bf16[1920,256]{1,0:T(8,128)(2,1)} %pad_maximum_fusion), channel_id=1, source_target_pairs={{0,1},{1,0},{2,3},{3,2},{4,5},{5,4},{6,7},{7,6},{8,9},{9,8},{10,11... | collective-permute-start | bytes 2949128 | tf_op jit(solution)/shard_map/ppermute | solution.py:315
  41.2 17.0 %copy-start.8 = (f32[128,1024]{1,0:T(8,128)}, f32[128,1024]{1,0:T(8,128)S(1)}, u32[]{:S(2)}) copy-start(f32[128,1024]{1,0:T(8,128)S(1)} %fusion.3.ov.own) | copy-start | bytes 1572868
  45.4 2.1 collective-permute-start.3
  56.4 45.3 %collective-permute-start.16 = (bf16[320,1408]{1,0:T(8,128)(2,1)}, bf16[320,1408]{1,0:T(8,128)(2,1)}, u32[]{:S(2)}, u32[]{:S(2)}) collective-permute-start(bf16[320,1408]{1,0:T(8,128)(2,1)} %constant_dynamic-slice_fusion.2), channel_id=1, source_target_pairs={{0,1},{1,0},{2,3},{3,2},{4,5},{5,4},{6,7},{7,6},{8,9},{9,8},{10,11... | collective-permute-start | bytes 2703368 | tf_op jit(solution)/shard_map/ppermute | solution.py:315
  58.1 2.1 collective-permute-start.4
  65.2 4.7 %collective-permute-start.5 = (bf16[4,144,128]{2,1,0:T(8,128)(2,1)}, bf16[4,144,128]{2,1,0:T(8,128)(2,1)S(1)}, u32[]{:S(2)}, u32[]{:S(2)}) collective-permute-start(bf16[4,144,128]{2,1,0:T(8,128)(2,1)} %get-tuple-element.177), channel_id=1, source_target_pairs={{0,2},{2,0},{4,6},{6,4},{8,10},{10,8},{12,14},{14,12},{16,18},{18,... | collective-permute-start | bytes 442376 | tf_op jit(solution)/shard_map/ppermute | solution.py:315
  67.5 7.2 %collective-permute-start.6 = (bf16[4,144,128]{2,1,0:T(8,128)(2,1)}, bf16[4,144,128]{2,1,0:T(8,128)(2,1)S(1)}, u32[]{:S(2)}, u32[]{:S(2)}) collective-permute-start(bf16[4,144,128]{2,1,0:T(8,128)(2,1)} %get-tuple-element.178), channel_id=1, source_target_pairs={{0,4},{2,6},{4,0},{6,2},{8,12},{10,14},{12,8},{14,10},{16,20},{18,... | collective-permute-start | bytes 442376 | tf_op jit(solution)/shard_map/ppermute | solution.py:315
  69.8 7.5 %collective-permute-start.7 = (bf16[4,144,128]{2,1,0:T(8,128)(2,1)}, bf16[4,144,128]{2,1,0:T(8,128)(2,1)S(1)}, u32[]{:S(2)}, u32[]{:S(2)}) collective-permute-start(bf16[4,144,128]{2,1,0:T(8,128)(2,1)} %get-tuple-element.179), channel_id=1, source_target_pairs={{0,6},{2,4},{4,2},{6,0},{8,14},{10,12},{12,10},{14,8},{16,22},{18,... | collective-permute-start | bytes 442376 | tf_op jit(solution)/shard_map/ppermute | solution.py:315
  79.9 30.8 %collective-permute-start.15 = (bf16[1920,256]{1,0:T(8,128)(2,1)}, bf16[1920,256]{1,0:T(8,128)(2,1)S(1)}, u32[]{:S(2)}, u32[]{:S(2)}) collective-permute-start(bf16[1920,256]{1,0:T(8,128)(2,1)} %collective-permute-done.14.out_a.refs_13_), channel_id=1, source_target_pairs={{0,4},{2,6},{4,0},{6,2},{8,12},{10,14},{12,8},{14,10},{16,20},{18,... | collective-permute-start | bytes 2949128 | tf_op jit(solution)/shard_map/ppermute | solution.py:315
  81.5 8.7 %collective-permute-start.10 = (bf16[4,144,128]{2,1,0:T(8,128)(2,1)}, bf16[4,144,128]{2,1,0:T(8,128)(2,1)S(1)}, u32[]{:S(2)}, u32[]{:S(2)}) collective-permute-start(bf16[4,144,128]{2,1,0:T(8,128)(2,1)} %group.2.refs_0_), channel_id=1, source_target_pairs={{0,24},{2,26},{4,28},{6,30},{8,16},{10,18},{12,20},{14,22},{16,8},... | collective-permute-start | bytes 442376 | tf_op jit(solution)/shard_map/ppermute | solution.py:315
  85.1 8.8 %collective-permute-start.8 = (bf16[4,144,128]{2,1,0:T(8,128)(2,1)}, bf16[4,144,128]{2,1,0:T(8,128)(2,1)S(1)}, u32[]{:S(2)}, u32[]{:S(2)}) collective-permute-start(bf16[4,144,128]{2,1,0:T(8,128)(2,1)} %group.2.refs_0_), channel_id=1, source_target_pairs={{0,8},{2,10},{4,12},{6,14},{8,0},{10,2},{12,4},{14,6},{16,24},{18,... | collective-permute-start | bytes 442376 | tf_op jit(solution)/shard_map/ppermute | solution.py:315
  85.1 13.3 %collective-permute-start.9 = (bf16[4,144,128]{2,1,0:T(8,128)(2,1)}, bf16[4,144,128]{2,1,0:T(8,128)(2,1)S(1)}, u32[]{:S(2)}, u32[]{:S(2)}) collective-permute-start(bf16[4,144,128]{2,1,0:T(8,128)(2,1)} %group.2.refs_0_), channel_id=1, source_target_pairs={{0,16},{2,18},{4,20},{6,22},{8,24},{10,26},{12,28},{14,30},{16,0},... | collective-permute-start | bytes 442376 | tf_op jit(solution)/shard_map/ppermute | solution.py:315
  101.6 14.1 %collective-permute-start.17 = (bf16[192,1408]{1,0:T(8,128)(2,1)}, bf16[192,1408]{1,0:T(8,128)(2,1)S(1)}, u32[]{:S(2)}, u32[]{:S(2)}) collective-permute-start(bf16[192,1408]{1,0:T(8,128)(2,1)} %constant_dynamic-slice_fusion.5), channel_id=1, source_target_pairs={{0,1},{1,0},{2,3},{3,2},{4,5},{5,4},{6,7},{7,6},{8,9},{9,8},{10,11... | collective-permute-start | bytes 1622024 | tf_op jit(solution)/shard_map/ppermute | solution.py:315
  102.2 1.9 collective-permute-start.11
  102.2 6.5 %collective-permute-start.12 = (bf16[4,128,128]{2,1,0:T(8,128)(2,1)}, bf16[4,128,128]{2,1,0:T(8,128)(2,1)S(1)}, u32[]{:S(2)}, u32[]{:S(2)}) collective-permute-start(bf16[4,128,128]{2,1,0:T(8,128)(2,1)} %get-tuple-element.190), channel_id=1, source_target_pairs={{0,4},{2,6},{4,0},{6,2},{8,12},{10,14},{12,8},{14,10},{16,20},{18,... | collective-permute-start | bytes 393224 | tf_op jit(solution)/shard_map/ppermute | solution.py:315
  103.6 7.1 %collective-permute-start.13 = (bf16[4,128,128]{2,1,0:T(8,128)(2,1)}, bf16[4,128,128]{2,1,0:T(8,128)(2,1)S(1)}, u32[]{:S(2)}, u32[]{:S(2)}) collective-permute-start(bf16[4,128,128]{2,1,0:T(8,128)(2,1)} %get-tuple-element.191), channel_id=1, source_target_pairs={{0,6},{2,4},{4,2},{6,0},{8,14},{10,12},{12,10},{14,8},{16,22},{18,... | collective-permute-start | bytes 393224 | tf_op jit(solution)/shard_map/ppermute | solution.py:315
  104.1 14.3 %copy-start.17 = (bf16[4,128,128]{2,1,0:T(8,128)(2,1)}, bf16[4,128,128]{2,1,0:T(8,128)(2,1)S(1)}, u32[]{:S(2)}) copy-start(bf16[4,128,128]{2,1,0:T(8,128)(2,1)S(1)} %collective-permute-done.11.s1) | copy-start | bytes 393220
  110.7 31.8 %copy-start.10 = (bf16[1920,256]{1,0:T(8,128)(2,1)}, bf16[1920,256]{1,0:T(8,128)(2,1)S(1)}, u32[]{:S(2)}) copy-start(bf16[1920,256]{1,0:T(8,128)(2,1)S(1)} %collective-permute-done.15.out_b.refs_14_) | copy-start | bytes 2949124
  115.7 26.8 %copy-start.36 = (bf16[192,1408]{1,0:T(8,128)(2,1)}, bf16[192,1408]{1,0:T(8,128)(2,1)S(1)}, u32[]{:S(2)}) copy-start(bf16[192,1408]{1,0:T(8,128)(2,1)S(1)} %collective-permute-done.17.refs_8_) | copy-start | bytes 1622020
  115.7 22.7 %collective-permute-start.18 = (bf16[1920,256]{1,0:T(8,128)(2,1)}, bf16[1920,256]{1,0:T(8,128)(2,1)S(1)}, u32[]{:S(2)}, u32[]{:S(2)}) collective-permute-start(bf16[1920,256]{1,0:T(8,128)(2,1)} %collective-permute-done.14.out_a.refs_13_), channel_id=1, source_target_pairs={{0,2},{2,0},{4,6},{6,4},{8,10},{10,8},{12,14},{14,12},{16,18},{18,... | collective-permute-start | bytes 2949128 | tf_op jit(solution)/shard_map/ppermute | solution.py:315
  115.7 22.7 %collective-permute-start.19 = (bf16[1920,256]{1,0:T(8,128)(2,1)S(1)}, bf16[1920,256]{1,0:T(8,128)(2,1)S(1)}, u32[]{:S(2)}, u32[]{:S(2)}) collective-permute-start(bf16[1920,256]{1,0:T(8,128)(2,1)S(1)} %collective-permute-done.15.out_b.refs_14_), channel_id=1, source_target_pairs={{0,2},{2,0},{4,6},{6,4},{8,10},{10,8},{12,14},{14,12},{16,18},{18,... | collective-permute-start | bytes 2949128 | tf_op jit(solution)/shard_map/ppermute | solution.py:315
  116.2 22.1 %collective-permute-start.21 = (bf16[320,1408]{1,0:T(8,128)(2,1)}, bf16[320,1408]{1,0:T(8,128)(2,1)S(1)}, u32[]{:S(2)}, u32[]{:S(2)}) collective-permute-start(bf16[320,1408]{1,0:T(8,128)(2,1)} %collective-permute-done.16.refs_4_), channel_id=1, source_target_pairs={{0,8},{2,10},{4,12},{6,14},{8,0},{10,2},{12,4},{14,6},{16,24},{18,... | collective-permute-start | bytes 2703368 | tf_op jit(solution)/shard_map/ppermute | solution.py:315
  116.2 22.1 %collective-permute-start.20 = (bf16[320,1408]{1,0:T(8,128)(2,1)}, bf16[320,1408]{1,0:T(8,128)(2,1)S(1)}, u32[]{:S(2)}, u32[]{:S(2)}) collective-permute-start(bf16[320,1408]{1,0:T(8,128)(2,1)} %collective-permute-done.16.refs_4_), channel_id=1, source_target_pairs={{0,2},{2,0},{4,6},{6,4},{8,10},{10,8},{12,14},{14,12},{16,18},{18,... | collective-permute-start | bytes 2703368 | tf_op jit(solution)/shard_map/ppermute | solution.py:315
  116.2 22.1 %collective-permute-start.22 = (bf16[192,1408]{1,0:T(8,128)(2,1)S(1)}, bf16[192,1408]{1,0:T(8,128)(2,1)S(1)}, u32[]{:S(2)}, u32[]{:S(2)}) collective-permute-start(bf16[192,1408]{1,0:T(8,128)(2,1)S(1)} %collective-permute-done.17.refs_8_), channel_id=1, source_target_pairs={{0,4},{2,6},{4,0},{6,2},{8,12},{10,14},{12,8},{14,10},{16,20},{18,... | collective-permute-start | bytes 1622024 | tf_op jit(solution)/shard_map/ppermute | solution.py:315
  138.4 4.1 %collective-permute-start.23 = (bf16[320,1408]{1,0:T(8,128)(2,1)S(1)}, bf16[320,1408]{1,0:T(8,128)(2,1)S(1)}, u32[]{:S(2)}, u32[]{:S(2)}) collective-permute-start(bf16[320,1408]{1,0:T(8,128)(2,1)S(1)} %collective-permute-done.21.refs_5_), channel_id=1, source_target_pairs={{0,2},{2,0},{4,6},{6,4},{8,10},{10,8},{12,14},{14,12},{16,18},{18,... | collective-permute-start | bytes 2703368 | tf_op jit(solution)/shard_map/ppermute | solution.py:315
  138.5 3.2 collective-permute-start.24
  139.0 3.5 collective-permute-start.25
  167.6 39.5 %collective-permute-start.29 = (bf16[6016,128]{1,0:T(8,128)(2,1)}, bf16[6016,128]{1,0:T(8,128)(2,1)S(1)}, u32[]{:S(2)}, u32[]{:S(2)}) collective-permute-start(bf16[6016,128]{1,0:T(8,128)(2,1)} %get-tuple-element.240.refs_2_.refs_6_.refs_10_.logit1), channel_id=1, source_target_pairs={{0,1},{1,0},{2,3},{3,2},{4,5},{5,4},{6,7},{7,6},{8,9},{9,8},{10,11... | collective-permute-start | bytes 4620296 | tf_op jit(solution)/shard_map/ppermute | solution.py:315
  188.8 1.9 collective-permute-start.26
  188.9 6.9 %collective-permute-start.27 = (bf16[4,144,128]{2,1,0:T(8,128)(2,1)}, bf16[4,144,128]{2,1,0:T(8,128)(2,1)S(1)}, u32[]{:S(2)}, u32[]{:S(2)}) collective-permute-start(bf16[4,144,128]{2,1,0:T(8,128)(2,1)} %get-tuple-element.228), channel_id=1, source_target_pairs={{0,4},{2,6},{4,0},{6,2},{8,12},{10,14},{12,8},{14,10},{16,20},{18,... | collective-permute-start | bytes 442376 | tf_op jit(solution)/shard_map/ppermute | solution.py:315
  190.3 7.8 %collective-permute-start.28 = (bf16[4,144,128]{2,1,0:T(8,128)(2,1)}, bf16[4,144,128]{2,1,0:T(8,128)(2,1)S(1)}, u32[]{:S(2)}, u32[]{:S(2)}) collective-permute-start(bf16[4,144,128]{2,1,0:T(8,128)(2,1)} %get-tuple-element.229), channel_id=1, source_target_pairs={{0,6},{2,4},{4,2},{6,0},{8,14},{10,12},{12,10},{14,8},{16,22},{18,... | collective-permute-start | bytes 442376 | tf_op jit(solution)/shard_map/ppermute | solution.py:315
  200.6 6.5 %collective-permute-start.30 = (bf16[4,144,128]{2,1,0:T(8,128)(2,1)}, bf16[4,144,128]{2,1,0:T(8,128)(2,1)S(1)}, u32[]{:S(2)}, u32[]{:S(2)}) collective-permute-start(bf16[4,144,128]{2,1,0:T(8,128)(2,1)} %group.3.refs_0_), channel_id=1, source_target_pairs={{0,8},{2,10},{4,12},{6,14},{8,0},{10,2},{12,4},{14,6},{16,24},{18,... | collective-permute-start | bytes 442376 | tf_op jit(solution)/shard_map/ppermute | solution.py:315
  214.8 21.1 %copy-start.45 = (bf16[144,1024]{1,0:T(8,128)(2,1)S(1)}, bf16[144,1024]{1,0:T(8,128)(2,1)}, u32[]{:S(2)}) copy-start(bf16[144,1024]{1,0:T(8,128)(2,1)} %get-tuple-element.231) | copy-start | bytes 884740
  216.1 40.9 %collective-permute-start.36 = (bf16[128,5632]{1,0:T(8,128)(2,1)S(1)}, bf16[128,5632]{1,0:T(8,128)(2,1)}, u32[]{:S(2)}, u32[]{:S(2)}) collective-permute-start(bf16[128,5632]{1,0:T(8,128)(2,1)S(1)} %copy-done.21), channel_id=1, source_target_pairs={{0,1},{1,0},{2,3},{3,2},{4,5},{5,4},{6,7},{7,6},{8,9},{9,8},{10,11... | collective-permute-start | bytes 4325384 | tf_op jit(solution)/shard_map/ppermute | solution.py:315
  217.6 12.4 %collective-permute-start.31 = (bf16[4,144,128]{2,1,0:T(8,128)(2,1)S(1)}, bf16[4,144,128]{2,1,0:T(8,128)(2,1)S(1)}, u32[]{:S(2)}, u32[]{:S(2)}) collective-permute-start(bf16[4,144,128]{2,1,0:T(8,128)(2,1)S(1)} %copy-done.35), channel_id=1, source_target_pairs={{0,16},{2,18},{4,20},{6,22},{8,24},{10,26},{12,28},{14,30},{16,0},... | collective-permute-start | bytes 442376 | tf_op jit(solution)/shard_map/ppermute | solution.py:315
  218.8 11.1 %collective-permute-start.32 = (bf16[4,144,128]{2,1,0:T(8,128)(2,1)S(1)}, bf16[4,144,128]{2,1,0:T(8,128)(2,1)S(1)}, u32[]{:S(2)}, u32[]{:S(2)}) collective-permute-start(bf16[4,144,128]{2,1,0:T(8,128)(2,1)S(1)} %copy-done.35), channel_id=1, source_target_pairs={{0,24},{2,26},{4,28},{6,30},{8,16},{10,18},{12,20},{14,22},{16,8},... | collective-permute-start | bytes 442376 | tf_op jit(solution)/shard_map/ppermute | solution.py:315
  234.0 1.9 collective-permute-start.33
  234.0 6.5 %collective-permute-start.34 = (bf16[4,128,128]{2,1,0:T(8,128)(2,1)}, bf16[4,128,128]{2,1,0:T(8,128)(2,1)S(1)}, u32[]{:S(2)}, u32[]{:S(2)}) collective-permute-start(bf16[4,128,128]{2,1,0:T(8,128)(2,1)} %get-tuple-element.250), channel_id=1, source_target_pairs={{0,4},{2,6},{4,0},{6,2},{8,12},{10,14},{12,8},{14,10},{16,20},{18,... | collective-permute-start | bytes 393224 | tf_op jit(solution)/shard_map/ppermute | solution.py:315
  235.5 7.0 %collective-permute-start.35 = (bf16[4,128,128]{2,1,0:T(8,128)(2,1)}, bf16[4,128,128]{2,1,0:T(8,128)(2,1)S(1)}, u32[]{:S(2)}, u32[]{:S(2)}) collective-permute-start(bf16[4,128,128]{2,1,0:T(8,128)(2,1)} %get-tuple-element.251), channel_id=1, source_target_pairs={{0,6},{2,4},{4,2},{6,0},{8,14},{10,12},{12,10},{14,8},{16,22},{18,... | collective-permute-start | bytes 393224 | tf_op jit(solution)/shard_map/ppermute | solution.py:315
  253.4 3.6 collective-permute-start.37
  254.7 5.4 %collective-permute-start.38 = (bf16[8,3072]{1,0:T(8,128)(2,1)S(1)}, bf16[8,3072]{1,0:T(8,128)(2,1)S(1)}, u32[]{:S(2)}, u32[]{:S(2)}) collective-permute-start(bf16[8,3072]{1,0:T(8,128)(2,1)S(1)} %pad_maximum_fusion.3), channel_id=1, source_target_pairs={{2,1},{3,0},{4,3},{5,2},{6,5},{7,4},{8,7},{9,6},{10,9},{11,8},{12,... | collective-permute-start | bytes 147464 | tf_op jit(solution)/shard_map/ppermute | solution.py:1116
  257.0 25.5 %copy-start.2 = (bf16[432,1024]{1,0:T(8,128)(2,1)}, bf16[432,1024]{1,0:T(8,128)(2,1)S(1)}, u32[]{:S(2)}) copy-start(bf16[432,1024]{1,0:T(8,128)(2,1)S(1)} %constant_dynamic-update-slice_fusion.refs_2_.refs_8_.refs_14_.own) | copy-start | bytes 2654212
  257.0 25.5 %copy-start.27 = (bf16[8,3072]{1,0:T(8,128)(2,1)}, bf16[8,3072]{1,0:T(8,128)(2,1)S(1)}, u32[]{:S(2)}) copy-start(bf16[8,3072]{1,0:T(8,128)(2,1)S(1)} %collective-permute-done.37.refs_4_.refs_10_.refs_16_.extra1) | copy-start | bytes 147460
  260.1 22.4 %copy-start.28 = (bf16[8,3072]{1,0:T(8,128)(2,1)}, bf16[8,3072]{1,0:T(8,128)(2,1)S(1)}, u32[]{:S(2)}) copy-start(bf16[8,3072]{1,0:T(8,128)(2,1)S(1)} %collective-permute-done.38.refs_5_.refs_11_.refs_17_.extra2) | copy-start | bytes 147460
  270.2 7.6 %collective-permute-start.39 = (bf16[8,32,5632]{2,1,0:T(8,128)(2,1)}, bf16[8,32,5632]{2,1,0:T(8,128)(2,1)}, u32[]{:S(2)}, u32[]{:S(2)}) collective-permute-start(bf16[8,32,5632]{2,1,0:T(8,128)(2,1)} %get-tuple-element.265), channel_id=1, source_target_pairs={{0,2},{2,0},{4,6},{6,4},{8,10},{10,8},{12,14},{14,12},{16,18},{18,... | collective-permute-start | bytes 8650760 | tf_op jit(solution)/shard_map/ppermute | solution.py:315
  272.5 21.6 %collective-permute-start.41 = (bf16[432,1024]{1,0:T(8,128)(2,1)S(1)}, bf16[432,1024]{1,0:T(8,128)(2,1)S(1)}, u32[]{:S(2)}, u32[]{:S(2)}) collective-permute-start(bf16[432,1024]{1,0:T(8,128)(2,1)S(1)} %constant_dynamic-update-slice_fusion.refs_2_.refs_8_.refs_14_.own), channel_id=1, source_target_pairs={{0,1},{1,0},{2,3},{3,2},{4,5},{5,4},{6,7},{7,6},{8,9},{9,8},{10,11... | collective-permute-start | bytes 2654216 | tf_op jit(solution)/shard_map/ppermute | solution.py:315
  282.5 35.1 %collective-permute-start.40 = (bf16[4,32,5632]{2,1,0:T(8,128)(2,1)}, bf16[4,32,5632]{2,1,0:T(8,128)(2,1)S(1)}, u32[]{:S(2)}, u32[]{:S(2)}) collective-permute-start(bf16[4,32,5632]{2,1,0:T(8,128)(2,1)} %get-tuple-element.268), channel_id=1, source_target_pairs={{0,4},{2,6},{4,0},{6,2},{8,12},{10,14},{12,8},{14,10},{16,20},{18,... | collective-permute-start | bytes 4325384 | tf_op jit(solution)/shard_map/ppermute | solution.py:315
  300.5 2.6 collective-permute-start.42
  300.6 3.6 collective-permute-start.43
  309.1 25.1 %collective-permute-start.45 = (bf16[4,96,1024]{2,1,0:T(8,128)(2,1)}, bf16[4,96,1024]{2,1,0:T(8,128)(2,1)S(1)}, u32[]{:S(2)}, u32[]{:S(2)}) collective-permute-start(bf16[4,96,1024]{2,1,0:T(8,128)(2,1)} %get-tuple-element.278), channel_id=1, source_target_pairs={{0,4},{2,6},{4,0},{6,2},{8,12},{10,14},{12,8},{14,10},{16,20},{18,... | collective-permute-start | bytes 2359304 | tf_op jit(solution)/shard_map/ppermute | solution.py:315
  321.5 26.5 %collective-permute-start.48 = (bf16[2,32,5632]{2,1,0:T(8,128)(2,1)}, bf16[2,32,5632]{2,1,0:T(8,128)(2,1)S(1)}, u32[]{:S(2)}, u32[]{:S(2)}) collective-permute-start(bf16[2,32,5632]{2,1,0:T(8,128)(2,1)} %get-tuple-element.280), channel_id=1, source_target_pairs={{0,8},{2,10},{4,12},{6,14},{8,0},{10,2},{12,4},{14,6},{16,24},{18,... | collective-permute-start | bytes 2162696 | tf_op jit(solution)/shard_map/ppermute | solution.py:315
  331.1 10.2 %collective-permute-start.44 = (bf16[128,512]{1,0:T(8,128)(2,1)}, bf16[128,512]{1,0:T(8,128)(2,1)S(1)}, u32[]{:S(2)}, u32[]{:S(2)}) collective-permute-start(bf16[128,512]{1,0:T(8,128)(2,1)} %get-tuple-element.283), channel_id=1, source_target_pairs={{0,1},{1,0},{2,3},{3,2},{4,5},{5,4},{6,7},{7,6},{8,9},{9,8},{10,11... | collective-permute-start | bytes 393224 | tf_op jit(solution)/shard_map/ppermute | solution.py:315
  337.3 20.6 %collective-permute-start.46 = (bf16[2,96,1024]{2,1,0:T(8,128)(2,1)}, bf16[2,96,1024]{2,1,0:T(8,128)(2,1)S(1)}, u32[]{:S(2)}, u32[]{:S(2)}) collective-permute-start(bf16[2,96,1024]{2,1,0:T(8,128)(2,1)} %get-tuple-element.286), channel_id=1, source_target_pairs={{0,8},{2,10},{4,12},{6,14},{8,0},{10,2},{12,4},{14,6},{16,24},{18,... | collective-permute-start | bytes 1179656 | tf_op jit(solution)/shard_map/ppermute | solution.py:315
  346.9 4.8 %collective-permute-start.47 = (f32[16,480]{1,0:T(8,128)S(1)}, f32[16,480]{1,0:T(8,128)S(1)}, u32[]{:S(2)}, u32[]{:S(2)}) collective-permute-start(f32[16,480]{1,0:T(8,128)S(1)} %bitcast.67), channel_id=1, source_target_pairs={{0,1},{1,0},{2,3},{3,2},{4,5},{5,4},{6,7},{7,6},{8,9},{9,8},{10,11... | collective-permute-start | bytes 92168 | tf_op jit(solution)/shard_map/ppermute | solution.py:315
  351.1 29.0 %copy-start.44 = (bf16[1,32,5632]{2,1,0:T(8,128)(2,1)S(1)}, bf16[1,32,5632]{2,1,0:T(8,128)(2,1)}, u32[]{:S(2)}) copy-start(bf16[1,32,5632]{2,1,0:T(8,128)(2,1)} %get-tuple-element.305) | copy-start | bytes 1081348
  351.1 29.0 %collective-permute-start.50 = (bf16[1,32,5632]{2,1,0:T(8,128)(2,1)}, bf16[1,32,5632]{2,1,0:T(8,128)(2,1)S(1)}, u32[]{:S(2)}, u32[]{:S(2)}) collective-permute-start(bf16[1,32,5632]{2,1,0:T(8,128)(2,1)} %get-tuple-element.298), channel_id=1, source_target_pairs={{0,16},{2,18},{4,20},{6,22},{8,24},{10,26},{12,28},{14,30},{16,0},... | collective-permute-start | bytes 1081352 | tf_op jit(solution)/shard_map/ppermute | solution.py:315
  352.4 22.5 %all-to-all-start = ((f32[16,1,480]{2,1,0:T(1,128)}), f32[16,1,480]{2,1,0:T(1,128)S(1)}, u32[]{:S(2)}, u32[]{:S(2)}) async-start(f32[16,1,480]{2,1,0:T(1,128)} %all_to_all.8), calls=%async_computation.1 | async-start | bytes 65536 | tf_op jit(solution)/shard_map/all_to_all | solution.py:1412
  361.5 16.8 %collective-permute-start.49 = (bf16[1,96,1024]{2,1,0:T(8,128)(2,1)}, bf16[1,96,1024]{2,1,0:T(8,128)(2,1)S(1)}, u32[]{:S(2)}, u32[]{:S(2)}) collective-permute-start(bf16[1,96,1024]{2,1,0:T(8,128)(2,1)} %get-tuple-element.303), channel_id=1, source_target_pairs={{0,16},{2,18},{4,20},{6,22},{8,24},{10,26},{12,28},{14,30},{16,0},... | collective-permute-start | bytes 589832 | tf_op jit(solution)/shard_map/ppermute | solution.py:315
  (44 other events, 138.8 us)
Sparse Core Ops, SparseCore 0:
  214.9 78.1 reduce-scatter.1

commit v4 on v3

--- a/solution.py
+++ b/solution.py
@@ -82,6 +82,68 @@
     )(place, tokens, taps, lines)
 
 
+def weigh_kernel(scaled, left_ref, gain_ref, qkv_ref, gate_ref, out, left):
+    j = pl.program_id(0)
+
+    @pl.when(j == 0)
+    def _():
+        rows = left_ref[: left.shape[0]]
+        left[...] = (rows * gain_ref[...].astype(f32)).astype(bf16) if scaled else rows
+
+    steps = 3 * D // out.shape[1]
+
+    @pl.when(j < steps)
+    def _():
+        out[...] = nn(left[...], qkv_ref[...]).astype(out.dtype)
+
+    @pl.when(j >= steps)
+    def _():
+        out[...] = nn(left[...], gate_ref[...]).astype(out.dtype)
+
+
+def weigh(left, rows, gain, qkv_weight, gate_weight, kind):
+    half = left.shape[1]
+    tile = 1024
+    steps = 3 * D // tile
+    return pl.pallas_call(
+        functools.partial(weigh_kernel, left.dtype == f32),
+        grid=(4 * D // tile,),
+        in_specs=[
+            whole(*left.shape), whole(1, half),
+            pl.BlockSpec((half, tile), lambda j: (0, jnp.minimum(j, steps - 1))),
+            pl.BlockSpec((half, tile), lambda j: (0, jnp.maximum(j - steps, 0))),
+        ],
+        out_specs=pl.BlockSpec((rows, tile), lambda j: (0, j)),
+        out_shape=like((rows, 4 * D), kind),
+        scratch_shapes=[pltpu.VMEM((rows, half), bf16)],
+        cost_estimate=pl.CostEstimate(flops=1, bytes_accessed=1, transcendentals=0),
+        name="weigh",
+    )(left, gain, qkv_weight, gate_weight)
+
+
+def tables_kernel(c_ref, b_ref, ridge_ref, mask_o, ending_o, ridge_o):
+    tokens = c_ref.shape[1]
+    head = pl.program_id(0)
+    c, b = c_ref[pl.ds(head, 1), :], b_ref[pl.ds(head, 1), :]
+    mask_o[0] = decay_mask(c, b, tokens)
+    ending_o[0] = column(jnp.exp(c[:, tokens - 1 :] - c) * b, (HEAD_DIM, tokens))
+    ridge_o[0] = column(ridge_ref[pl.ds(head, 1), :], (tokens, HEAD_DIM))
+
+
+def tables(c, b, ridge):
+    tokens = c.shape[1]
+    shapes = [(tokens, tokens), (tokens, HEAD_DIM), (HEAD_DIM, tokens)]
+    return pl.pallas_call(
+        tables_kernel,
+        grid=(HEADS,),
+        in_specs=[whole(HEADS, tokens)] * 2 + [whole(HEADS, HEAD_DIM)],
+        out_specs=[pl.BlockSpec((1,) + shape, lambda h: (h, 0, 0)) for shape in shapes],
+        out_shape=[like((HEADS,) + shape) for shape in shapes],
+        cost_estimate=pl.CostEstimate(flops=1, bytes_accessed=1, transcendentals=0),
+        name="tables",
+    )(c, b, ridge)
+
+
 def with_halo(own, lent, halo):
     before = halo[...].astype(f32)
     blank = jnp.zeros((HALO - before.shape[0], before.shape[1]), f32)
@@ -101,12 +163,6 @@
     return a * lax.rsqrt(jnp.sum(a * a, axis=-1, keepdims=True) + 1e-06)
 
 
-def ending_of(c_ref, b_ref, head):
-    c = c_ref[pl.ds(head, 1), :]
-    b = b_ref[pl.ds(head, 1), :]
-    return column(jnp.exp(c[:, c.shape[1] - 1 :] - c) * b, (HEAD_DIM, c.shape[1]))
-
-
 def position(spot):
     return spot[0] % FOUR
 
@@ -149,32 +205,27 @@
     return slice(h * HEAD_DIM, (h + 1) * HEAD_DIM)
 
 
-def keys_kernel(oq, ok, lq, lk, hq, hk, tq, tk, c_ref, b_ref, q_o, k_o, state_o):
+def features_kernel(
+    spot, oq, ok, ov, lq, lk, lv, hq, hk, hv, tq, tk, tv, ending_ref, c_ref, q_o, k_o, v_o, *outs
+):
     quarter = pl.program_id(0)
-    sums = []
-    for own, lent, halo, taps in ((oq, lq, hq, tq), (ok, lk, hk, tk)):
+
+    def activated(own, lent, halo, taps):
         total, _ = conv_parts(with_halo(own, lent, halo), taps[...])
-        sums.append(total * jax.nn.sigmoid(total))
+        return total * jax.nn.sigmoid(total)
+
+    queries, keys, values = activated(oq, lq, hq, tq), activated(ok, lk, hk, tk), activated(ov, lv, hv, tv)
+    key_states, value_states = [], []
     for m in range(SHARE):
-        k = unit(sums[1][:, cut(m)])
+        k, v = unit(keys[:, cut(m)]), values[:, cut(m)]
         k_low = k.astype(bf16)
         k_o[m] = k_low
-        ending = ending_of(c_ref, b_ref, quarter * SHARE + m)
-        state_o[m] = tn((k * ending).astype(bf16), k_low).astype(bf16)
-        q_o[m] = unit(sums[0][:, cut(m)]).T
-
-
-def values_kernel(spot, ov, lv, hv, tv, k_ref, ks_ref, c_ref, b_ref, v_o, *outs):
-    quarter = pl.program_id(0)
-    total, _ = conv_parts(with_halo(ov, lv, hv), tv[...])
-    values = total * jax.nn.sigmoid(total)
-    states = [ks_ref[m] for m in range(SHARE)]
-    for m in range(SHARE):
-        v = values[:, cut(m)]
         v_o[m] = v.astype(bf16)
-        ending = ending_of(c_ref, b_ref, quarter * SHARE + m)
-        states.append(tn((v * ending).astype(bf16), k_ref[m]).astype(bf16))
-    store_quarter(spot, quarter, outs, states, c_ref)
+        q_o[m] = unit(queries[:, cut(m)]).T
+        ending = ending_ref[m]
+        key_states.append(tn((k * ending).astype(bf16), k_low).astype(bf16))
+        value_states.append(tn((v * ending).astype(bf16), k_low).astype(bf16))
+    store_quarter(spot, quarter, outs, key_states + value_states, c_ref)
 
 
 def whole(*shape):
@@ -189,33 +240,20 @@
     return pl.BlockSpec((rows, SHARE * HEAD_DIM), lambda p: (0, third * QUARTERS + p))
 
 
-def keys(own, lent, halo, taps, c, b):
-    tokens = own.shape[0]
-    square = (HEADS, HEAD_DIM, HEAD_DIM)
-    return pl.pallas_call(
-        keys_kernel,
-        grid=(QUARTERS,),
-        in_specs=[quarter_columns(rows, i) for rows in (tokens, tokens, halo.shape[0], KW) for i in (0, 1)]
-        + [whole(HEADS, tokens)] * 2,
-        out_specs=[per_quarter(HEAD_DIM, tokens), per_quarter(tokens, HEAD_DIM), per_quarter(HEAD_DIM, HEAD_DIM)],
-        out_shape=[like((HEADS, HEAD_DIM, tokens)), like((HEADS, tokens, HEAD_DIM), bf16), like(square, bf16)],
-        cost_estimate=pl.CostEstimate(flops=1, bytes_accessed=1, transcendentals=0),
-        name="keys",
-    )(own, own, lent, lent, halo, halo, taps, taps, c, b)
-
-
-def values(spot, own, lent, halo, taps, k, key_states, c, b):
+def features(spot, projected, taps, ending, c):
+    own, lent, halo = projected
     tokens = own.shape[0]
     return pl.pallas_call(
-        values_kernel,
+        features_kernel,
         grid=(QUARTERS,),
-        in_specs=[smem()] + [quarter_columns(rows, 0) for rows in (tokens, tokens, halo.shape[0])] + [quarter_columns(KW, 2)]
-        + [per_quarter(tokens, HEAD_DIM), per_quarter(HEAD_DIM, HEAD_DIM)] + [whole(HEADS, tokens)] * 2,
-        out_specs=[per_quarter(tokens, HEAD_DIM)] + [whole(*MESSAGE)] * QUARTERS,
-        out_shape=[like((HEADS, tokens, HEAD_DIM), bf16)] + [like(MESSAGE, bf16)] * QUARTERS,
+        in_specs=[smem()] + [quarter_columns(x, i) for x in (tokens, tokens, halo.shape[0], KW) for i in range(3)]
+        + [per_quarter(tokens, HEAD_DIM), whole(HEADS, tokens)],
+        out_specs=[per_quarter(HEAD_DIM, tokens)] + [per_quarter(tokens, HEAD_DIM)] * 2 + [whole(*MESSAGE)] * QUARTERS,
+        out_shape=[like((HEADS, HEAD_DIM, tokens))] + [like((HEADS, tokens, HEAD_DIM), bf16)] * 2
+        + [like(MESSAGE, bf16)] * QUARTERS,
         cost_estimate=pl.CostEstimate(flops=1, bytes_accessed=1, transcendentals=0),
-        name="values",
-    )(spot, own, lent, halo, taps, k, key_states, c, b)
+        name="features",
+    )(spot, own, own, own, lent, lent, lent, halo, halo, halo, taps, taps, taps, ending, c)
 
 
 def decay_between(indices, decays, low, high):
@@ -355,7 +393,7 @@
         return self.entering
 
 
-def prepare(k_ref, c_ref, b_ref, ridge_ref, state_refs, place, left, wide, mask, decay, ridge, pair):
+def prepare(k_ref, c_ref, state_refs, place, left, wide, decay, pair):
     tokens = k_ref.shape[1]
     for i, state in enumerate(state_refs):
         for m in range(SHARE):
@@ -365,9 +403,7 @@
         k = k_ref[h]
         left[h, :, HEAD_DIM:] = k.T
         wide[h // 2, :, cut(h % 2)] = k
-        mask[h] = decay_mask(c_ref[h : h + 1, :], b_ref[h : h + 1, :], tokens)
         decay[h] = jnp.broadcast_to(jnp.exp(c_ref[h : h + 1, :]), (8, tokens))
-        ridge[h] = column(ridge_ref[h : h + 1, :], (tokens, HEAD_DIM))
 
 
 def key_products(columns, wide, pair):
@@ -381,15 +417,15 @@
 
 
 def solve_kernel(
-    place, q_ref, k_ref, s0, s1, s2, s3, c_ref, b_ref, ridge_ref,
+    place, q_ref, k_ref, s0, s1, s2, s3, c_ref, mask, ridge,
     x_out, p_out, m_out, score_out, scal_out,
-    left, wide, mask, decay, ridge, pair, x_s, r_s, p_s,
+    left, wide, decay, pair, x_s, r_s, p_s,
 ):
     i = pl.program_id(0)
 
     @pl.when(i == 0)
     def _():
-        prepare(k_ref, c_ref, b_ref, ridge_ref, (s0, s1, s2, s3), place[0], left, wide, mask, decay, ridge, pair)
+        prepare(k_ref, c_ref, (s0, s1, s2, s3), place[0], left, wide, decay, pair)
         for h in range(HEADS):
             q = q_ref[h]
             x_s[h] = jnp.zeros_like(q)
@@ -428,15 +464,13 @@
     return [
         pltpu.VMEM((HEADS, HEAD_DIM, HEAD_DIM + tokens), bf16),
         pltpu.VMEM((HEADS // 2, tokens, 2 * HEAD_DIM), bf16),
-        pltpu.VMEM((HEADS, tokens, tokens), f32),
         pltpu.VMEM((HEADS, 8, tokens), f32),
-        square,
         pltpu.VMEM((HEADS // 2, 2 * HEAD_DIM, 2 * tokens), bf16),
         square, square, square,
     ]
 
 
-def solve(place, q, k, states, c, b, ridge):
+def solve(place, q, k, states, c, mask, ridge):
     tokens = q.shape[2]
     step = pl.BlockSpec((1, HEADS, HEAD_DIM, tokens), lambda i: (i, 0, 0, 0))
     steps = (ITERS, HEADS, HEAD_DIM, tokens)
@@ -444,7 +478,7 @@
         solve_kernel,
         grid=(ITERS,),
         in_specs=[smem(), whole(HEADS, HEAD_DIM, tokens), whole(HEADS, tokens, HEAD_DIM)] + [whole(*PAIR)] * FOUR
-        + [whole(HEADS, tokens)] * 2 + [whole(HEADS, HEAD_DIM)],
+        + [whole(HEADS, tokens), whole(HEADS, tokens, tokens), whole(HEADS, HEAD_DIM, tokens)],
         out_specs=[whole(HEADS, HEAD_DIM, tokens), step, step, step, whole(HEADS, 3 * ITERS, tokens)],
         out_shape=[
             like((HEADS, HEAD_DIM, tokens), bf16), like(steps), like(steps), like(steps, bf16),
@@ -454,17 +488,16 @@
         compiler_params=pltpu.CompilerParams(vmem_limit_bytes=VMEM_LIMIT),
         cost_estimate=pl.CostEstimate(flops=1, bytes_accessed=1, transcendentals=0),
         name="solve",
-    )(place, q, k, *states, c, b, ridge)
-
-
-def attend_back_kernel(place, ga_ref, k_ref, v_ref, x_ref, s0, s1, s2, s3, c_ref, b_ref, gx_o, dk_o, dv_o, state_o):
+    )(place, q, k, *states, c, mask, ridge)
+
+
+def attend_back_kernel(place, ga_ref, k_ref, v_ref, x_ref, s0, s1, s2, s3, c_ref, mask_ref, gx_o, dk_o, dv_o, state_o):
     quarter = pl.program_id(0)
     tokens = k_ref.shape[1]
     for m in range(SHARE):
         head = quarter * SHARE + m
         c = c_ref[pl.ds(head, 1), :]
-        b = b_ref[pl.ds(head, 1), :]
-        mask = decay_mask(c, b, tokens)
+        mask = mask_ref[m]
         e = jnp.exp(c)
         state = s0[SHARE + m]
         for i, other in ((1, s1), (2, s2), (3, s3)):
@@ -482,25 +515,25 @@
         state_o[m] = nt(ega, x).astype(bf16)
 
 
-def attend_back(place, ga, k, v, x, states, c, b):
+def attend_back(place, ga, k, v, x, states, c, mask):
     tokens = k.shape[1]
     square = like((HEADS, HEAD_DIM, tokens))
     return pl.pallas_call(
         attend_back_kernel,
         grid=(QUARTERS,),
         in_specs=[smem(), quarter_columns(tokens, 0)] + [per_quarter(tokens, HEAD_DIM)] * 2
-        + [per_quarter(HEAD_DIM, tokens)] + [whole(*PAIR)] * FOUR + [whole(HEADS, tokens)] * 2,
+        + [per_quarter(HEAD_DIM, tokens)] + [whole(*PAIR)] * FOUR + [whole(HEADS, tokens), per_quarter(tokens, tokens)],
         out_specs=[per_quarter(HEAD_DIM, tokens)] * 4,
         out_shape=[square] * 3 + [like((HEADS, HEAD_DIM, HEAD_DIM), bf16)],
         cost_estimate=pl.CostEstimate(flops=1, bytes_accessed=1, transcendentals=0),
         name="attend_back",
-    )(place, ga, k, v, x, *states, c, b)
+    )(place, ga, k, v, x, *states, c, mask)
 
 
 def adjoint_kernel(
-    spot, place, gx_ref, k_ref, s0, s1, s2, s3, c_ref, b_ref, ridge_ref, p_ref, m_ref, score_ref, scal_ref, values_ref,
+    spot, place, gx_ref, k_ref, s0, s1, s2, s3, c_ref, mask, ridge, p_ref, m_ref, score_ref, scal_ref, values_ref,
     dq_ref, dk_ref, dridge_ref, o0, o1, o2, o3,
-    left, wide, mask, decay, ridge, pair, gr_s, gp_s, acc_s, next_s, gnorm_s, low_s, steps_p, steps_g, steps_s, stack,
+    left, wide, decay, pair, gr_s, gp_s, acc_s, next_s, gnorm_s, low_s, steps_p, steps_g, steps_s, stack,
 ):
     s = pl.program_id(0)
     i = ITERS - 1 - s
@@ -509,7 +542,7 @@
 
     @pl.when(s == 0)
     def _():
-        prepare(k_ref, c_ref, b_ref, ridge_ref, (s0, s1, s2, s3), place[0], left, wide, mask, decay, ridge, pair)
+        prepare(k_ref, c_ref, (s0, s1, s2, s3), place[0], left, wide, decay, pair)
         gr_s[...] = jnp.zeros_like(gr_s)
         gp_s[...] = jnp.zeros_like(gp_s)
         acc_s[...] = jnp.zeros_like(acc_s)
@@ -566,7 +599,7 @@
                 out[SHARE + m, HEAD_DIM:] = decay
 
 
-def adjoint(spot, place, gx, k, states, c, b, ridge, p_all, m_all, scores, scal, value_states):
+def adjoint(spot, place, gx, k, states, c, mask, ridge, p_all, m_all, scores, scal, value_states):
     tokens = k.shape[1]
     step = pl.BlockSpec((1, HEADS, HEAD_DIM, tokens), lambda s: (ITERS - 1 - s, 0, 0, 0))
     square = pltpu.VMEM((HEADS, HEAD_DIM, tokens), f32)
@@ -575,7 +608,7 @@
         adjoint_kernel,
         grid=(ITERS,),
         in_specs=[smem(), smem(), whole(HEADS, HEAD_DIM, tokens), whole(HEADS, tokens, HEAD_DIM)] + [whole(*PAIR)] * FOUR
-        + [whole(HEADS, tokens)] * 2 + [whole(HEADS, HEAD_DIM), step, step, step, whole(HEADS, 3 * ITERS, tokens), whole(HEADS, HEAD_DIM, HEAD_DIM)],
+        + [whole(HEADS, tokens), whole(HEADS, tokens, tokens), whole(HEADS, HEAD_DIM, tokens), step, step, step, whole(HEADS, 3 * ITERS, tokens), whole(HEADS, HEAD_DIM, HEAD_DIM)],
         out_specs=[whole(HEADS, HEAD_DIM, tokens), whole(HEADS, tokens, HEAD_DIM), whole(HEADS, 1, HEAD_DIM)]
         + [whole(*MESSAGE)] * FOUR,
         out_shape=[like((HEADS, HEAD_DIM, tokens)), like((HEADS, tokens, HEAD_DIM)), like((HEADS, 1, HEAD_DIM))]
@@ -590,7 +623,7 @@
         compiler_params=pltpu.CompilerParams(vmem_limit_bytes=VMEM_LIMIT),
         cost_estimate=pl.CostEstimate(flops=1, bytes_accessed=1, transcendentals=0),
         name="adjoint",
-    )(spot, place, gx, k, *states, c, b, ridge, p_all, m_all, scores, scal, value_states)
+    )(spot, place, gx, k, *states, c, mask, ridge, p_all, m_all, scores, scal, value_states)
 
 
 def conv_forward(own, lent, halo, t):
@@ -633,18 +666,18 @@
     return state
 
 
-def values_back_kernel(spot, own, lent, halo, t, dv_ref, k_ref, r0, r1, r2, r3, c_ref, b_ref, g, dt):
+def values_back_kernel(spot, own, lent, halo, t, dv_ref, k_ref, r0, r1, r2, r3, ending_ref, g, dt):
     quarter = pl.program_id(0)
     shifted, slope, _ = conv_forward(own, lent, halo, t)
     grads = []
     for m in range(SHARE):
         rv = returned(position(spot), quarter, (r0, r1, r2, r3), SHARE + m)
-        grads.append(dv_ref[m] + ending_of(c_ref, b_ref, quarter * SHARE + m) * nt(k_ref[m], rv))
+        grads.append(dv_ref[m] + ending_ref[m] * nt(k_ref[m], rv))
     conv_back(jnp.concatenate(grads, axis=1) * slope, shifted, t, g, dt)
 
 
 def keys_back_kernel(
-    spot, own, lent, halo, t, dk1, dk2, k_ref, v_ref, r0, r1, r2, r3, c_ref, b_ref, g, dt
+    spot, own, lent, halo, t, dk1, dk2, k_ref, v_ref, r0, r1, r2, r3, ending_ref, g, dt
 ):
     quarter = pl.program_id(0)
     shifted, slope, act = conv_forward(own, lent, halo, t)
@@ -653,7 +686,7 @@
         rv = returned(position(spot), quarter, (r0, r1, r2, r3), SHARE + m)
         rk = returned(position(spot), quarter, (r0, r1, r2, r3), m).astype(f32)
         rk = (rk + rk.T).astype(bf16)
-        ending = ending_of(c_ref, b_ref, quarter * SHARE + m)
+        ending = ending_ref[m]
         dk = dk1[m] + dk2[m] + ending * (nn(k_ref[m], rk) + nn(v_ref[m], rv))
         grads.append(unit_back(act[:, cut(m)], dk))
     conv_back(jnp.concatenate(grads, axis=1) * slope, shifted, t, g, dt)
@@ -678,19 +711,19 @@
     return third_back(queries_back_kernel, "queries_back", 0, 0, projected, taps, (), (dq,), [per_quarter(HEAD_DIM, HEAD_DIM)])
 
 
-def values_back(spot, projected, taps, dv, k, states, c, b):
+def values_back(spot, projected, taps, dv, k, states, ending):
     square = per_quarter(HEAD_DIM, HEAD_DIM)
     return third_back(
-        values_back_kernel, "values_back", 0, 2, projected, taps, (spot,), (dv, k, *states, c, b),
-        [square] * 2 + [whole(*PAIR)] * FOUR + [whole(*c.shape)] * 2,
-    )
-
-
-def keys_back(spot, projected, taps, dk1, dk2, k, v, states, c, b):
+        values_back_kernel, "values_back", 2, 2, projected, taps, (spot,), (dv, k, *states, ending),
+        [square] * 2 + [whole(*PAIR)] * FOUR + [square],
+    )
+
+
+def keys_back(spot, projected, taps, dk1, dk2, k, v, states, ending):
     square = per_quarter(HEAD_DIM, HEAD_DIM)
     return third_back(
-        keys_back_kernel, "keys_back", 1, 1, projected, taps, (spot,), (dk1, dk2, k, v, *states, c, b),
-        [square] * 4 + [whole(*PAIR)] * FOUR + [whole(*c.shape)] * 2,
+        keys_back_kernel, "keys_back", 1, 1, projected, taps, (spot,), (dk1, dk2, k, v, *states, ending),
+        [square] * 4 + [whole(*PAIR)] * FOUR + [square],
     )
 
 
@@ -912,7 +945,7 @@
 
 
 def middle_kernel(
-    owners, place, x_ref, s0, s1, s2, s3, k_ref, v_ref, c_ref, b_ref, own_logit, lent_logit, tok_ref, cot_ref, gain_ref, first_ref,
+    owners, place, x_ref, s0, s1, s2, s3, k_ref, v_ref, c_ref, mask_ref, own_logit, lent_logit, tok_ref, cot_ref, gain_ref, first_ref,
     own_out, out_a, out_b, out_c, out_d, *refs,
 ):
     own_up = refs[:4]
@@ -962,9 +995,8 @@
             for m in range(SHARE):
                 head = (place[1] ^ i) * SHARE + m
                 c = c_ref[pl.ds(head, 1), :]
-                b = b_ref[pl.ds(head, 1), :]
                 x = x_ref[head]
-                scores = (nn(k_ref[head], x) * decay_mask(c, b, tokens)).astype(bf16)
+                scores = (nn(k_ref[head], x) * mask_ref[head]).astype(bf16)
                 part = jnp.exp(c) * nn(state[SHARE + m], x) + tn(v_ref[head], scores)
                 att_s[:, pl.ds(aligned(head * HEAD_DIM, HEAD_DIM), HEAD_DIM)] = part.T
         out_s[mine, :] = own_out[...]
@@ -989,14 +1021,15 @@
 
     for i in range(4):
         up_s[mine, i * tile : (i + 1) * tile] = own_up[i][...]
-    start = 0
-    for parts, q0 in zip(up_parts, (place[2], place[1])):
-        count = parts[0].shape[0]
-        at = pl.ds(aligned((1 - y) * half + start, 16), count)
-        for part, q in zip(parts, order(q0)):
-            slot = (q >> 1) * 2 + ((q & 1) ^ y)
-            up_s[at, pl.ds(aligned(slot * tile, tile), tile)] = part[...]
-        start += count
+    count = up_parts[0][0].shape[0]
+    at = pl.ds(aligned((1 - y) * half, 16), count)
+    for part, q in zip(up_parts[0], order(place[2])):
+        slot = (q >> 1) * 2 + ((q & 1) ^ y)
+        up_s[at, pl.ds(aligned(slot * tile, tile), tile)] = part[...]
+    at = pl.ds(aligned((1 - y) * half + count, 16), half - count)
+    for i, part in enumerate(up_parts[1]):
+        slot = ((place[1] ^ (i // 2)) & 1) * 2 + i % 2
+        up_s[at, pl.ds(aligned(slot * tile, tile), tile)] = part[...]
     down_s[:tile, :] = own_down[...]
     wide = down_parts[0].shape[1]
     for part, q in zip(down_parts, order(place[1])):
@@ -1058,7 +1091,13 @@
         pl.BlockSpec((half, tile), lambda j, s: (0, (2 + s[0]) * share + j)),
         pl.BlockSpec((half, tile), lambda j, s: (0, (3 - s[0]) * share + j)),
     ]
-    up_specs = [pl.BlockSpec((p.shape[0], tile), lambda j, s: (0, j)) for p in up_parts]
+    up_specs = [pl.BlockSpec((p.shape[0], tile), lambda j, s: (0, j)) for p in up_parts[:4]]
+    rest_rows = up_parts[4].shape[0]
+    up_specs += [
+        pl.BlockSpec((rest_rows, tile), lambda j, s: (0, s[0] * share + j)),
+        pl.BlockSpec((rest_rows, tile), lambda j, s: (0, (1 - s[0]) * share + j)),
+    ] * 2
+    up_parts = up_parts[:4] + (up_parts[4],) * 2 + (up_parts[5],) * 2
     own_down = pl.BlockSpec((tile, D), lambda j, s: (j, 0))
     down_specs = [pl.BlockSpec((tile, D // 4), lambda j, s: (half // tile + j, 0))] * 4
     square = (HEAD_DIM, HEAD_DIM)
@@ -1068,8 +1107,8 @@
             num_scalar_prefetch=1,
             grid=(share,),
             in_specs=[full(HEADS, HEAD_DIM, tokens)] + [full(*PAIR)] * FOUR + [full(HEADS, tokens, HEAD_DIM)] * 2
-            + [full(HEADS, tokens)] * 2
-            + [rows, pl.BlockSpec((tokens, D), lambda j, s: (0, 1))]
+            + [full(HEADS, tokens), full(HEADS, tokens, tokens)]
+            + [pl.BlockSpec((tokens, D), lambda j, s: (0, 3))] * 2
             + [rows] * 2 + [full(1, D), full(1, D), full(half, D)] + [full(half, D // 4)] * 4
             + own_up + up_specs + [own_down] + down_specs,
             out_specs=[
@@ -1192,7 +1231,7 @@
     )
 
 
-UP_ROWS = (0, 320, 512)
+UP_ROWS = 384
 
 
 def local(
@@ -1226,19 +1265,10 @@
     lines = jnp.stack([gain_attn, gain_ffn, ridge_terms, ridge_terms])
     mine, theirs = norm(place, tokens, conv_taps, lines)
     theirs = partner(theirs, "fsdp")
-    gain_mine = gain_attn.astype(f32)
-    peer_extra, left_theirs = lax.optimization_barrier((theirs[rows:], (theirs[:rows] * gain_mine).astype(bf16)))
-    lent_qk = nn(left_theirs, qkv_weight[:, : 2 * D]).astype(bf16)
-    seq.mark(lent_qk)
-    lent_qk = partner(lent_qk, "fsdp")
-    (left,) = seq.gate(left_theirs)
-    lent_v = jnp.concatenate([nn(left, qkv_weight[:, 2 * D :]).astype(bf16), nn(left, gate_weight).astype(bf16)], axis=1)
-    seq.mark(lent_v)
-    lent_v = partner(lent_v, "fsdp")
-    (left,) = seq.gate(mine)
-    own_qk = nn(left, qkv_weight[:, : 2 * D])
-    own_v = nn(left, qkv_weight[:, 2 * D :])
-    own_gate = nn(left, gate_weight)
+    lent = weigh(theirs, rows, gain_attn[None], qkv_weight, gate_weight, bf16)
+    seq.mark(lent)
+    lent = partner(lent, "fsdp")
+    peer_extra = theirs[rows:]
     (peer_extra,) = seq.gate(peer_extra)
     taps_rows = KW * 3
     vectors = sided(lines[:3].astype(f32), peer_extra[taps_rows : taps_rows + 3], y, 1)
@@ -1249,28 +1279,25 @@
     strength = (1.0 - forget[0]).T
     out_here, up_here, down_here = seq.gate(out_weight, up_weight, down_weight)
     rest_quarter = jnp.concatenate([quarter(out_here, near_x), quarter(down_here, near_x)], axis=0)
-    seq.mark(own_qk, own_v, own_gate, rest_quarter, taps, cumulative, strength)
+    seq.mark(rest_quarter)
     rest_direct = partner(rest_quarter, "fsdp")
     (up_here,) = seq.gate(up_here)
     up_quarters = [
-        quarter(up_here, near, start, stop - start)
-        for near, start, stop in zip((near_z, near_x), UP_ROWS, UP_ROWS[1:])
+        quarter(up_here, near_z, 0, UP_ROWS),
+        lax.dynamic_slice(up_here, (UP_ROWS, (here % 2) * FF), (D // 2 - UP_ROWS, FF)),
     ]
     seq.mark(*up_quarters)
-
-    own_qk, lent_qk = seq.gate(own_qk, lent_qk)
-
-    def halo_of(own, lent):
-        return shifted((own[rows - 8 :] + lent[rows - 8 :].astype(f32)).astype(bf16), "ctx", 1)
-
-    halo_qk = halo_of(own_qk, lent_qk)
-    queries, keys_low, key_states = keys(own_qk, lent_qk, halo_qk, taps, cumulative, strength)
-    seq.mark(key_states)
-    own_v, lent_v, up_first = seq.gate(own_v, lent_v, up_quarters[0])
-    halo_v = halo_of(own_v, lent_v[:, :D])
-    values_low, *own = values(spot, own_v, lent_v, halo_v, taps, keys_low, key_states, cumulative, strength)
-    seq.mark(*own)
-    scan = Scan(spot, swapped(own, "ctx"), "ctx")
+    cumulative, strength, ridge, taps, mine = seq.gate(cumulative, strength, ridge, taps, mine)
+    own = weigh(mine, rows, gain_attn[None], qkv_weight, gate_weight, f32)
+    mask, ending, ridge = tables(cumulative, strength, ridge)
+    seq.mark(mask, own)
+
+    own, lent, up_first = seq.gate(own, lent, up_quarters[0])
+    halo = shifted((own[rows - 8 :, : 3 * D] + lent[rows - 8 :, : 3 * D].astype(f32)).astype(bf16), "ctx", 1)
+    projected = own, lent, halo
+    queries, keys_low, values_low, *near = features(spot, projected, taps, ending, cumulative)
+    seq.mark(*near)
+    scan = Scan(spot, swapped(near, "ctx"), "ctx")
     up_first = partner(up_first, "fsdp")
 
     def split(left):
@@ -1290,28 +1317,28 @@
     first_across = partner(up_first, "ctx", 4)
     *states, queries = seq.gate(*states, queries)
     seq.mark(states[1], states[2], states[3])
-    rest_direct, rest_across, up_first, up_second = seq.gate(rest_direct, rest_across, up_first, up_second)
-    second_across = partner(up_second, "ctx", 2)
+    rest_direct, rest_across, up_first = seq.gate(rest_direct, rest_across, up_first)
     rest_core, rest_far, first_core = partner(rest_direct, "ctx", 1), partner(rest_across, "ctx", 1), partner(up_first, "ctx", 1)
     (queries,) = seq.gate(queries)
-    x, p_all, m_all, scores, scal = solve(ring, queries, keys_low, states, cumulative, strength, ridge)
+    x, p_all, m_all, scores, scal = solve(ring, queries, keys_low, states, cumulative, mask, ridge)
     seq.mark(x)
+
+    def split(left):
+        flat = left.reshape(peers, 2, left.shape[0] // owners, left.shape[1])
+        return [pick(flat, side, 1).reshape(-1, left.shape[1]) for side in (y, 1 - y)]
 
     def share(right):
         return right, partner(right, "fsdp")
 
-    def below(pair):
-        return jnp.concatenate(pair, axis=0)
-
-    rest_core, rest_far, first_core, first_across, up_second, second_across = seq.gate(
-        rest_core, rest_far, first_core, first_across, up_second, second_across
-    )
+    up_second, rest_core, rest_far = seq.gate(up_second, rest_core, rest_far)
+    second_core = partner(up_second, "ctx", 1)
+    (first_across,) = seq.gate(first_across)
     rest_parts = (rest_direct, rest_across, rest_core, rest_far)
     up_parts = (up_first, first_across, first_core, partner(first_across, "ctx", 1))
-    up_parts += (up_second, second_across, partner(up_second, "ctx", 1), partner(second_across, "ctx", 1))
+    up_parts += (up_second, second_core)
 
     output, grad_hidden, grad_attended, lefts, message, grad_gate_up, grad_second_gain = middle(
-        owners, place, (x, *states, keys_low, values_low, cumulative, strength), own_gate, lent_v,
+        owners, place, (x, *states, keys_low, values_low, cumulative, mask), own, lent,
         tokens, cotangent[0], gain_second, gain_first[None], out_weight, up_weight, down_weight, up_parts, rest_parts
     )
     size = D // 2
@@ -1326,17 +1353,17 @@
     message_peer = partner(message, "fsdp")
     (grad_attended,) = seq.gate(grad_attended)
     gx, dk_attend, dv, value_states = attend_back(
-        ring, grad_attended, keys_low, values_low, x, states, cumulative, strength
+        ring, grad_attended, keys_low, values_low, x, states, cumulative, mask
     )
     dq, dk_solve, grad_ridge, *own = adjoint(
-        spot_back, ring, gx, keys_low, states, cumulative, strength, ridge, p_all, m_all, scores, scal, value_states
+        spot_back, ring, gx, keys_low, states, cumulative, mask, ridge, p_all, m_all, scores, scal, value_states
     )
     seq.mark(*own)
     back = Scan(spot_back, swapped(own, "ctx"), "ctx")
     (up_here,) = seq.gate(grad_gate_up)
     both_up = share(up_here)
     dq, back.near[1] = seq.gate(dq, back.near[1])
-    low_q, taps_q = queries_back((own_qk, lent_qk, halo_qk), taps, dq)
+    low_q, taps_q = queries_back(projected, taps, dq)
     seq.mark(low_q)
     back.near = list(seq.gate(*back.near))
     back.group()
@@ -1345,7 +1372,7 @@
     rights = [(i * BLOCKS * rows, rows) for i in range(3)]
     (early,) = products(
         spot, peers, [[(lefts_here, parts[i]), (message_peer, peer_parts[i])] for i in (1, 2, 3)],
-        [[(message, at), (message_peer, at)] for at in rights], 256, joined=True
+        [[(message, at), (message_peer, at)] for at in rights], 512, joined=True
     )
     seq.mark(early)
     early = lax.psum_scatter(early.reshape(-1, D), "ctx", scatter_dimension=0, tiled=True)
@@ -1354,12 +1381,12 @@
     seq.mark(back.parts[0])
     dv, *states_back = seq.gate(dv, *states_back)
     low_v, taps_v = values_back(
-        spot_back, (own_v, lent_v, halo_v), taps, dv, keys_low, states_back, cumulative, strength
+        spot_back, projected, taps, dv, keys_low, states_back, ending
     )
     seq.mark(low_v)
     (dk_attend,) = seq.gate(dk_attend)
     low_k, taps_k = keys_back(
-        spot_back, (own_qk, lent_qk, halo_qk), taps, dk_attend, dk_solve, keys_low, values_low, states_back, cumulative, strength
+        spot_back, projected, taps, dk_attend, dk_solve, keys_low, values_low, states_back, ending
     )
     seq.mark(low_k)
     ahead = jnp.concatenate([low[HALO - 8 : HALO] for low in (low_q, low_k, low_v)], axis=1)
@@ -1369,7 +1396,7 @@
     thirds_peer = partner(thirds, "fsdp")
     up_peer, *extra = seq.gate(both_up[1], *extra)
     blocks = products(
-        spot, peers, [[(lefts, parts[0]), (message_peer, peer_parts[0])]], [[(both_up[0], None), (up_peer, None)]], 512
+        spot, peers, [[(lefts, parts[0]), (message_peer, peer_parts[0])]], [[(both_up[0], None), (up_peer, None)]], 1408
     )
     seq.mark(blocks[0])
     ups = Reduction((0, 1, 2), blocks)
@@ -1378,19 +1405,17 @@
     lefts_here, thirds_peer = seq.gate(lefts, thirds_peer)
     left = [(lefts_here, parts[2]), (message_peer, peer_parts[2])]
     rights = [[(thirds, i), (thirds_peer, i), (extra[0], i), (extra[1], i)] for i in range(3)]
-    blocks = products(spot, peers, [left] * 3, rights, 256, messages=2)
+    blocks = products(spot, peers, [left] * 3, rights, 512, messages=2)
     seq.mark(blocks[0])
     late = Reduction((0, 1, 2), blocks)
     late.got = seq.gate(*late.got)
     seq.mark(late.step())
-    ups.got = seq.gate(*ups.got)
-    seq.mark(ups.step())
     (thirds_here,) = seq.gate(thirds)
     kept, lent = lent_rows(thirds_here, thirds_peer, extra, (message, message_peer), qkv_weight, gate_weight)
     seq.mark(lent)
     arriving = partner(lent, "fsdp")
-    late.got = seq.gate(*late.got)
-    seq.mark(late.step())
+    ups.got = seq.gate(*ups.got)
+    seq.mark(ups.step())
     (arriving,) = seq.gate(arriving)
     grad_tokens, vector = norm_back(
         place, kept, arriving, tokens, gain_first[None], grad_hidden, (taps_q, taps_k, taps_v), grad_second_gain, grad_ridge
@@ -1404,6 +1429,8 @@
     vector_kept, vector_sent = pick(vector, y, 1), pick(vector, 1 - y, 1)
     seq.mark(vector_sent)
     arriving = partner(vector_sent, "fsdp")
+    late.got = seq.gate(*late.got)
+    seq.mark(late.step())
     *ups.got, early = seq.gate(*ups.got, early)
     seq.mark(ups.step())
     vector_kept, arriving = seq.gate(vector_kept, arriving)

time: 390 us -> 372 us (0.954)
  waiting for transfers between devices: 120 us -> 111 us
  matrix products: 7.96 us -> 0 us
  Pallas kernels: 136 us -> 142 us
  starting transfers between devices: 65.3 us -> 61 us
    ppermute x47 -> x44, waiting for transfers between devices: 105 us -> 94 us  [partner(): return lax.ppermute(x, axis, neighbour(axis, bit))]
    pallas_call x2 -> x4, Pallas kernels: 8.67 us -> 19.4 us  [the longest x2 9.74 us: weigh(): pl.pallas_call(functools.partial(weigh_kernel, left.dtype == f32), grid=(...]
    dot_general x6 -> x0, matrix products: 7.96 us -> none  [nn(): lax.dot_general(a, b, (((1,), (0,)), ((), ())), preferred_element_type=f32)]
    pallas_call x3, Pallas kernels: 21.9 us -> 15.8 us  [products(): pl.pallas_call(functools.partial(products_kernel, plan, joined, cuts), gr...]
    ppermute x47 -> x44, starting transfers between devices: 55.1 us -> 52.2 us  [partner(): return lax.ppermute(x, axis, neighbour(axis, bit))]
    unnamed x116 -> x104, local copies, waits for them, and re-layouts: 15.9 us -> 16.8 us
  transfers between devices with their start and end apart: 53 -> 49, of which waited for: 30 -> 28; matrix products, arithmetic and copies ran while one was open for 6% -> 6% of each run, Pallas kernels for 27% -> 28%
where the time goes in v4:
time: 372 us; the launch traced here: 370 us
  Pallas kernels  142 us (38%)
  waiting for transfers between devices  111 us (30%)
  starting transfers between devices  61 us (16%)
  local copies, waits for them, and re-layouts  32.3 us (9%)
  between operations  14.6 us (4%)
  other arithmetic  9.36 us (3%)
    ppermute x44, waiting for transfers between devices, partner(): return lax.ppermute(x, axis, neighbour(axis, bit))  94 us
    ppermute x44, starting transfers between devices, partner(): return lax.ppermute(x, axis, neighbour(axis, bit))  52.2 us
    pallas_call x1, Pallas kernels, middle(): pl.pallas_call(functools.partial(middle_kernel, owners), grid_spec=pltpu....  24.8 us
    pallas_call x6, Pallas kernels, halving_step(): pl.pallas_call(step_kernel, grid_spec=pltpu.PrefetchScalarGridSpec(num_sc...  18.2 us
    unnamed x104, local copies, waits for them, and re-layouts  16.8 us
    pallas_call x3, Pallas kernels, products(): pl.pallas_call(functools.partial(products_kernel, plan, joined, cuts), gr...  15.8 us
    pallas_call x1, Pallas kernels, adjoint(): pl.pallas_call(adjoint_kernel, grid=(ITERS,), in_specs=[smem(), smem(), w...  15.3 us
    pallas_call x3, Pallas kernels, third_back(): pl.pallas_call(kernel, grid=(QUARTERS,), in_specs=[smem()] * len(before)...  14.6 us
  transfers between devices with their start and end apart: 49, of which 28 were waited for; matrix products, arithmetic and copies ran while one was open for 6% of the time, Pallas kernels for 28%

profile of v4, /device:TPU:0, one launch (start us, length us, event | category | flops | bytes accessed | tf_op | source)
XLA Modules:
  0.0 370.0 jit_solution(14855232359107043865)
XLA Ops:
  10.5 2.0 norm.1
  12.5 3.0 collective-permute-start
  18.3 4.4 %collective-permute-done.left_ref = f32[144,512]{1,0:T(8,128)S(1)} collective-permute-done((f32[144,512]{1,0:T(8,128)}, f32[144,512]{1,0:T(8,128)S(1)}, u32[]{:S(2)}, u32[]{:S(2)}) %collective-permute-start) | collective-permute-done | bytes 294944 | tf_op jit(solution)/shard_map/ppermute | solution.py:353
  23.4 4.8 %weigh.2 = bf16[128,4096]{1,0:T(8,128)(2,1)} custom-call(f32[144,512]{1,0:T(8,128)} %copy-done.37, bf16[1,512]{1,0:T(2,128)(2,1)} %copy-done.48, bf16[512,3072]{1,0:T(8,128)(2,1)} %qkv_ref.5, bf16[512,1024]{1,0:T(8,128)(2,1)} %gate_ref.5), custom_call_target="tpu_custom_call" | custom-call | flops 1 | bytes 1 | tf_op jit(solution)/shard_map/weigh/pallas_call | solution.py:108
  28.2 1.7 collective-permute-start.1
  36.1 2.0 constant_dynamic-slice_fusion.5
  38.8 5.0 %weigh.3.oq.ok.ov.own_logit.own = f32[128,4096]{1,0:T(8,128)} custom-call(bf16[128,512]{1,0:T(8,128)(2,1)} %get-tuple-element.164.left_ref, bf16[1,512]{1,0:T(2,128)(2,1)} %copy-done.48, bf16[512,3072]{1,0:T(8,128)(2,1)} %qkv_ref.5, bf16[512,1024]{1,0:T(8,128)(2,1)} %gate_ref.5), custom_call_target="tpu_custom_call" | custom-call | flops 1 | bytes 1 | tf_op jit(solution)/shard_map/weigh/pallas_call | solution.py:108
  43.7 4.2 %tables.1 = (f32[8,128,128]{2,1,0:T(8,128)}, f32[8,128,128]{2,1,0:T(8,128)}, f32[8,128,128]{2,1,0:T(8,128)}) custom-call(f32[8,128]{1,0:T(8,128)} %reduce_window_sum.11.c_ref, f32[8,128]{1,0:T(8,128)} %get-tuple-element.166.b_ref, f32[8,128]{1,0:T(8,128)} %bitcast.58), custom_call_target="tpu_custom_call" | custom-call | flops 1 | bytes 1 | tf_op jit(solution)/shard_map/tables/pallas_call | solution.py:136
  47.9 6.6 %collective-permute-done.1.lq.lk.lv.lent_logit.lent = bf16[128,4096]{1,0:T(8,128)(2,1)S(1)} collective-permute-done((bf16[128,4096]{1,0:T(8,128)(2,1)}, bf16[128,4096]{1,0:T(8,128)(2,1)S(1)}, u32[]{:S(2)}, u32[]{:S(2)}) %collective-permute-start.1) | collective-permute-done | bytes 1048608 | tf_op jit(solution)/shard_map/ppermute | solution.py:353
  54.5 1.7 collective-permute-start.14
  59.9 5.5 %features.1 = (f32[8,128,128]{2,1,0:T(8,128)}, bf16[8,128,128]{2,1,0:T(8,128)(2,1)}, bf16[8,128,128]{2,1,0:T(8,128)(2,1)}, bf16[4,144,128]{2,1,0:T(8,128)(2,1)},...) custom-call(s32[1]{0:T(128)} %bitcast.3.spot, ...), custom_call_target="tpu_custom_call" | custom-call | flops 1 | bytes 1 | tf_op jit(solution)/shard_map/features/pallas_call | solution.py:246
  65.4 2.6 collective-permute-start.3
  68.0 2.3 collective-permute-start.4
  70.4 4.8 %collective-permute-done.4.refs_2_.refs_6_ = bf16[4,144,128]{2,1,0:T(8,128)(2,1)S(1)} collective-permute-done((bf16[4,144,128]{2,1,0:T(8,128)(2,1)}, bf16[4,144,128]{2,1,0:T(8,128)(2,1)S(1)}, u32[]{:S(2)}, u32[]{:S(2)}) %collective-permute-start.4) | collective-permute-done | bytes 147488 | tf_op jit(solution)/shard_map/ppermute | solution.py:353
  75.2 2.6 collective-permute-done.5.refs_3_.refs_7_
  78.5 1.9 group.2.refs_0_
  83.5 2.6 collective-permute-start.7
  86.4 4.7 %collective-permute-done.6.refs_1_ = bf16[4,144,128]{2,1,0:T(8,128)(2,1)S(1)} collective-permute-done((bf16[4,144,128]{2,1,0:T(8,128)(2,1)}, bf16[4,144,128]{2,1,0:T(8,128)(2,1)S(1)}, u32[]{:S(2)}, u32[]{:S(2)}) %collective-permute-start.6) | collective-permute-done | bytes 147488 | tf_op jit(solution)/shard_map/ppermute | solution.py:353
  91.1 6.6 %collective-permute-done.7.refs_2_ = bf16[4,144,128]{2,1,0:T(8,128)(2,1)S(1)} collective-permute-done((bf16[4,144,128]{2,1,0:T(8,128)(2,1)}, bf16[4,144,128]{2,1,0:T(8,128)(2,1)S(1)}, u32[]{:S(2)}, u32[]{:S(2)}) %collective-permute-start.7) | collective-permute-done | bytes 147488 | tf_op jit(solution)/shard_map/ppermute | solution.py:353
  99.0 2.6 spread.2
  101.7 2.3 collective-permute-start.18
  106.2 3.6 collective-permute-done.10.s2
  109.7 1.7 collective-permute-done.11.s3
  112.8 10.0 %solve.1 = (bf16[8,128,128]{2,1,0:T(8,128)(2,1)}, f32[8,8,128,128]{3,2,1,0:T(8,128)}, f32[8,8,128,128]{3,2,1,0:T(8,128)}, bf16[8,8,128,128]{3,2,1,0:T(8,128)(2,1)}, f32[8,24,128]{2,1,0:T(8,128)}) custom-call(s32[1]{0:T(128)} %bitcast.1.place, f32[8,128,128]{2,1,0:T(8,128)} %get-tuple-element.194.q_ref, bf16[8,128,128]{2,1,0:T(8,128)(2,1)} %get-tuple-element.195.k_ref, ...), custom_call_target="tpu_custom_call" | custom-call | flops 1 | bytes 1 | tf_op jit(solution)/shard_map/solve/pallas_call | solution.py:477
  123.0 4.6 %collective-permute-done.18.refs_5_ = bf16[384,1408]{1,0:T(8,128)(2,1)S(1)} collective-permute-done((bf16[384,1408]{1,0:T(8,128)(2,1)}, bf16[384,1408]{1,0:T(8,128)(2,1)S(1)}, u32[]{:S(2)}, u32[]{:S(2)}) %collective-permute-start.18) | collective-permute-done | bytes 1081376 | tf_op jit(solution)/shard_map/ppermute | solution.py:353
  127.6 3.4 collective-permute-done.15.refs_8_.refs_9_
  131.1 2.2 collective-permute-done.21.refs_10_.refs_11_
  134.5 24.8 %middle.1 = (f32[128,1024]{1,0:T(8,128)}, f32[128,1024]{1,0:T(8,128)}, f32[128,1024]{1,0:T(8,128)}, bf16[2944,128]{1,0:T(8,128)(2,1)}, bf16[6016,128]{1,0:T(8,12...) custom-call(s32[3]{0:T(128)} %pad_add_fusion.place, bf16[8,128,128]{2,1,0:T(8,128)(2,1)} %get-tuple-element.198.x_ref, ...), custom_call_target="tpu_custom_call" | custom-call | flops 1 | bytes 1 | tf_op jit(solution)/shard_map/middle/pallas_call | solution.py:1104
  159.9 5.0 %attend_back.1 = (f32[8,128,128]{2,1,0:T(8,128)}, f32[8,128,128]{2,1,0:T(8,128)}, f32[8,128,128]{2,1,0:T(8,128)}, bf16[8,128,128]{2,1,0:T(8,128)(2,1)}) custom-call(s32[1]{0:T(128)} %bitcast.1.place, f32[128,1024]{1,0:T(8,128)} %get-tuple-element.214.ga_ref, bf16[8,128,128]{2,1,0:T(8,128)(2,1)} %get-tuple-element.195.k_ref, ...), custom_call_target="tpu_custom_call" | custom-call | flops 1 | bytes 1 | tf_op jit(solution)/shard_map/attend_back/pallas_call | solution.py:521
  164.9 15.3 %adjoint.1 = (f32[8,128,128]{2,1,0:T(8,128)}, f32[8,128,128]{2,1,0:T(8,128)}, f32[8,1,128]{2,1,0:T(1,128)}, bf16[4,144,128]{2,1,0:T(8,128)(2,1)}, bf16[4,144,128...) custom-call(s32[1]{0:T(128)} %bitcast.12.spot, s32[1]{0:T(128)} %bitcast.1.place, ...), custom_call_target="tpu_custom_call" | custom-call | flops 1 | bytes 1 | tf_op jit(solution)/shard_map/adjoint/pallas_call | solution.py:607
  182.1 4.6 %queries_back.1 = (bf16[144,1024]{1,0:T(8,128)(2,1)}, f32[4,1024]{1,0:T(4,128)}) custom-call(f32[128,4096]{1,0:T(8,128)} %weigh.3.oq.ok.ov.own_logit.own, bf16[128,4096]{1,0:T(8,128)(2,1)} %copy-done.1, bf16[8,3072]{1,0:T(8,128)(2,1)} %copy-done.18, f32[4,3072]{1,0:T(4,128)} %maximum_select_fusion.tq.tk.tv.t, f32[8,128,128]{2,1,0:T(8,128)} %get-tuple-element.226.dq_ref), custom_call_target="tpu_custom_call" | custom-call | flops 1 | bytes 1 | tf_op jit(solution)/shard_map/queries_back/pallas_call | solution.py:698
  187.2 2.3 collective-permute-done.24.refs_3_.refs_7_
  190.1 1.9 group.3.refs_0_
  192.9 5.6 %collective-permute-done.26.refs_1_ = bf16[4,144,128]{2,1,0:T(8,128)(2,1)S(1)} collective-permute-done((bf16[4,144,128]{2,1,0:T(8,128)(2,1)}, bf16[4,144,128]{2,1,0:T(8,128)(2,1)S(1)}, u32[]{:S(2)}, u32[]{:S(2)}) %collective-permute-start.26) | collective-permute-done | bytes 147488 | tf_op jit(solution)/shard_map/ppermute | solution.py:353
  199.8 5.6 %products.3 = bf16[16,152,1024]{2,1,0:T(8,128)(2,1)} custom-call(s32[1]{0:T(128)} %bitcast.3.spot, bf16[2944,128]{1,0:T(8,128)(2,1)} %get-tuple-element.264.refs_0_.refs_4_.refs_8_.refs_6_.refs_12_, bf16[6016,128]{1,0:T(8,128)(2,1)} %copy-done, bf16[6016,128]{1,0:T(8,128)(2,1)} %get-tuple-element.236.refs_2_.refs_6_.refs_10_.logit1, ...), custom_call_target="tpu_custom_call" | custom-call | flops 1 | bytes 1 | tf_op jit(solution)/shard_map/products/pallas_call | solution.py:837
  208.2 1.9 collective-permute-start.27
  211.5 9.7 %collective-permute-done.27.refs_2_ = bf16[4,144,128]{2,1,0:T(8,128)(2,1)S(1)} collective-permute-done((bf16[4,144,128]{2,1,0:T(8,128)(2,1)S(1)}, bf16[4,144,128]{2,1,0:T(8,128)(2,1)S(1)}, u32[]{:S(2)}, u32[]{:S(2)}) %collective-permute-start.27) | collective-permute-done | bytes 147488 | tf_op jit(solution)/shard_map/ppermute | solution.py:353
  222.5 2.7 spread.3
  227.2 4.6 %collective-permute-done.30.r2 = bf16[4,128,128]{2,1,0:T(8,128)(2,1)S(1)} collective-permute-done((bf16[4,128,128]{2,1,0:T(8,128)(2,1)}, bf16[4,128,128]{2,1,0:T(8,128)(2,1)S(1)}, u32[]{:S(2)}, u32[]{:S(2)}) %collective-permute-start.30) | collective-permute-done | bytes 131104 | tf_op jit(solution)/shard_map/ppermute | solution.py:353
  231.8 2.0 collective-permute-done.31.r3
  234.4 4.8 %values_back.1 = (bf16[144,1024]{1,0:T(8,128)(2,1)}, f32[4,1024]{1,0:T(4,128)}) custom-call(s32[1]{0:T(128)} %bitcast.12.spot, f32[128,4096]{1,0:T(8,128)} %weigh.3.oq.ok.ov.own_logit.own, bf16[128,4096]{1,0:T(8,128)(2,1)} %copy-done.1, bf16[8,3072]{1,0:T(8,128)(2,1)} %copy-done.18, f32[4,3072]{1,0:T(4,128)} %maximum_select_fusion.tq.tk.tv.t, ...), custom_call_target="tpu_custom_call" | custom-call | flops 1 | bytes 1 | tf_op jit(solution)/shard_map/values_back/pallas_call | solution.py:698
  239.2 5.2 %keys_back.1 = (bf16[144,1024]{1,0:T(8,128)(2,1)}, f32[4,1024]{1,0:T(4,128)}) custom-call(s32[1]{0:T(128)} %bitcast.12.spot, f32[128,4096]{1,0:T(8,128)} %weigh.3.oq.ok.ov.own_logit.own, bf16[128,4096]{1,0:T(8,128)(2,1)} %copy-done.1, bf16[8,3072]{1,0:T(8,128)(2,1)} %copy-done.18, f32[4,3072]{1,0:T(4,128)} %maximum_select_fusion.tq.tk.tv.t, ...), custom_call_target="tpu_custom_call" | custom-call | flops 1 | bytes 1 | tf_op jit(solution)/shard_map/keys_back/pallas_call | solution.py:698
  248.8 3.0 collective-permute-done.35.refs_5_.refs_11_.refs_17_.extra2
  251.8 6.0 %products.4 = (bf16[8,32,5632]{2,1,0:T(8,128)(2,1)}, bf16[8,32,5632]{2,1,0:T(8,128)(2,1)}) custom-call(s32[1]{0:T(128)} %bitcast.3.spot, bf16[2944,128]{1,0:T(8,128)(2,1)} %get-tuple-element.264.refs_0_.refs_4_.refs_8_.refs_6_.refs_12_, bf16[6016,128]{1,0:T(8,128)(2,1)} %copy-done, bf16[128,5632]{1,0:T(8,128)(2,1)} %get-tuple-element.258.refs_2_, ...), custom_call_target="tpu_custom_call" | custom-call | flops 1 | bytes 1 | tf_op jit(solution)/shard_map/products/pallas_call | solution.py:837
  257.9 2.1 collective-permute-start.36
  260.8 4.5 %collective-permute-done.36.refs_0_.refs_1_ = bf16[8,32,5632]{2,1,0:T(8,128)(2,1)} collective-permute-done((bf16[8,32,5632]{2,1,0:T(8,128)(2,1)}, bf16[8,32,5632]{2,1,0:T(8,128)(2,1)}, u32[]{:S(2)}, u32[]{:S(2)}) %collective-permute-start.36) | collective-permute-done | bytes 2883616 | tf_op jit(solution)/shard_map/ppermute | solution.py:353
  265.3 4.9 %halving.6 = (bf16[4,32,5632]{2,1,0:T(8,128)(2,1)}, bf16[4,32,5632]{2,1,0:T(8,128)(2,1)}) custom-call(s32[1]{0:T(128)} %bitcast.13.bit, bf16[8,32,5632]{2,1,0:T(8,128)(2,1)} %get-tuple-element.260.kept_mine.kept_other, bf16[8,32,5632]{2,1,0:T(8,128)(2,1)} %get-tuple-element.260.kept_mine.kept_other, ...), custom_call_target="tpu_custom_call" | custom-call | flops 1 | bytes 1 | tf_op jit(solution)/shard_map/halving/pallas_call | solution.py:930
  271.7 9.9 %collective-permute-done.32.refs_3_.refs_9_.refs_15_.peer = bf16[432,1024]{1,0:T(8,128)(2,1)S(1)} collective-permute-done((bf16[432,1024]{1,0:T(8,128)(2,1)S(1)}, bf16[432,1024]{1,0:T(8,128)(2,1)S(1)}, u32[]{:S(2)}, u32[]{:S(2)}) %collective-permute-start.32) | collective-permute-done | bytes 884768 | tf_op jit(solution)/shard_map/ppermute | solution.py:353
  282.6 4.2 %products.5 = (bf16[8,96,1024]{2,1,0:T(8,128)(2,1)}, bf16[8,48,1024]{2,1,0:T(8,128)(2,1)}, bf16[8,48,1024]{2,1,0:T(8,128)(2,1)}) custom-call(s32[1]{0:T(128)} %bitcast.3.spot, bf16[2944,128]{1,0:T(8,128)(2,1)} %get-tuple-element.264.refs_0_.refs_4_.refs_8_.refs_6_.refs_12_, bf16[6016,128]{1,0:T(8,128)(2,1)} %copy-done, bf16[432,1024]{1,0:T(8,128)(2,1)} %copy-done.2, ...), custom_call_target="tpu_custom_call" | custom-call | flops 1 | bytes 1 | tf_op jit(solution)/shard_map/products/pallas_call | solution.py:837
  287.4 2.0 collective-permute-done.37.refs_0_.refs_1_
  291.4 4.0 %halving.7 = (bf16[4,96,1024]{2,1,0:T(8,128)(2,1)}, bf16[4,96,1024]{2,1,0:T(8,128)(2,1)}) custom-call(s32[1]{0:T(128)} %bitcast.13.bit, bf16[8,96,1024]{2,1,0:T(8,128)(2,1)} %get-tuple-element.268.kept_mine.kept_other, bf16[8,96,1024]{2,1,0:T(8,128)(2,1)} %get-tuple-element.268.kept_mine.kept_other, bf16[8,48,1024]{2,1,0:T(8,128)(2,1)} %copy-done.9, ...), custom_call_target="tpu_custom_call" | custom-call | flops 1 | bytes 1 | tf_op jit(solution)/shard_map/halving/pallas_call | solution.py:930
  297.0 5.6 %lent_rows.1 = (f32[128,512]{1,0:T(8,128)}, bf16[128,512]{1,0:T(8,128)(2,1)}) custom-call(bf16[432,1024]{1,0:T(8,128)(2,1)} %copy-done.2, bf16[432,1024]{1,0:T(8,128)(2,1)} %copy-done.3, bf16[8,3072]{1,0:T(8,128)(2,1)} %copy-done.25, bf16[8,3072]{1,0:T(8,128)(2,1)} %copy-done.26, bf16[6016,128]{1,0:T(8,128)(2,1)} %get-tuple-element.236.refs_2_.refs_6_.refs_10_.logit1, ...), custom_call_target="tpu_custom_call" | custom-call | flops 1 | bytes 1 | tf_op jit(solution)/shard_map/lent_rows/pallas_call | solution.py:869
  303.2 1.7 collective-permute-done.40.refs_0_.refs_1_
  306.0 2.7 halving.8
  308.7 3.7 %collective-permute-start.44 = (bf16[2,32,5632]{2,1,0:T(8,128)(2,1)}, bf16[2,32,5632]{2,1,0:T(8,128)(2,1)S(1)}, u32[]{:S(2)}, u32[]{:S(2)}) collective-permute-start(bf16[2,32,5632]{2,1,0:T(8,128)(2,1)} %get-tuple-element.279), channel_id=1, source_target_pairs={{0,8},{2,10},{4,12},{6,14},{8,0},{10,2},{12,4},{14,6},{16,24},{18,... | collective-permute-start | bytes 2162696 | tf_op jit(solution)/shard_map/ppermute | solution.py:353
  313.1 2.5 norm_back.1
  318.1 3.4 collective-permute-done.41.refs_0_.refs_1_
  322.4 2.2 halving.9
  324.6 3.6 collective-permute-start.42
  330.6 2.3 halving.10
  334.3 4.7 %all-to-all-start = ((f32[16,1,480]{2,1,0:T(1,128)}), f32[16,1,480]{2,1,0:T(1,128)S(1)}, u32[]{:S(2)}, u32[]{:S(2)}) async-start(f32[16,1,480]{2,1,0:T(1,128)} %all_to_all.8), calls=%async_computation.1 | async-start | bytes 65536 | tf_op jit(solution)/shard_map/all_to_all | solution.py:1439
  341.6 2.0 halving.11
  344.4 1.7 collective-permute-start.45
  346.1 12.7 %all-to-all-done = f32[16,1,480]{2,1,0:T(1,128)S(1)} async-done(((f32[16,1,480]{2,1,0:T(1,128)}), f32[16,1,480]{2,1,0:T(1,128)S(1)}, u32[]{:S(2)}, u32[]{:S(2)}) %all-to-all-start) | async-done | bytes 30752 | tf_op jit(solution)/shard_map/all_to_all | solution.py:1439
  (213 shorter events, 70.5 us)
Async XLA Ops:
  7.2 322.6 %reduce-scatter.2.cloned.1.call-start = ((), (), s32[]{:S(2)}) async-start(), calls=%async_computation.2 | async-start | bytes 5292032 | tf_op jit(solution)/shard_map/reduce_scatter | solution.py:1378
  7.9 14.7 %copy-start.48 = (bf16[1,512]{1,0:T(2,128)(2,1)}, bf16[1,512]{1,0:T(2,128)(2,1)S(1)}, u32[]{:S(2)}) copy-start(bf16[1,512]{1,0:T(2,128)(2,1)S(1)} %stack.31.gain_ref) | copy-start | bytes 3076
  12.5 10.2 %collective-permute-start = (f32[144,512]{1,0:T(8,128)}, f32[144,512]{1,0:T(8,128)S(1)}, u32[]{:S(2)}, u32[]{:S(2)}) collective-permute-start(f32[144,512]{1,0:T(8,128)} %get-tuple-element.157), channel_id=1, source_target_pairs={{0,1},{1,0},{2,3},{3,2},{4,5},{5,4},{6,7},{7,6},{8,9},{9,8},{10,11... | collective-permute-start | bytes 884744 | tf_op jit(solution)/shard_map/ppermute | solution.py:353
  28.2 26.3 %collective-permute-start.1 = (bf16[128,4096]{1,0:T(8,128)(2,1)}, bf16[128,4096]{1,0:T(8,128)(2,1)S(1)}, u32[]{:S(2)}, u32[]{:S(2)}) collective-permute-start(bf16[128,4096]{1,0:T(8,128)(2,1)} %weigh.2), channel_id=1, source_target_pairs={{0,1},{1,0},{2,3},{3,2},{4,5},{5,4},{6,7},{7,6},{8,9},{9,8},{10,11... | collective-permute-start | bytes 3145736 | tf_op jit(solution)/shard_map/ppermute | solution.py:353
  33.1 47.3 %collective-permute-start.12 = (bf16[1920,256]{1,0:T(8,128)(2,1)}, bf16[1920,256]{1,0:T(8,128)(2,1)S(1)}, u32[]{:S(2)}, u32[]{:S(2)}) collective-permute-start(bf16[1920,256]{1,0:T(8,128)(2,1)} %pad_maximum_fusion), channel_id=1, source_target_pairs={{0,1},{1,0},{2,3},{3,2},{4,5},{5,4},{6,7},{7,6},{8,9},{9,8},{10,11... | collective-permute-start | bytes 2949128 | tf_op jit(solution)/shard_map/ppermute | solution.py:353
  54.5 47.2 %collective-permute-start.14 = (bf16[384,1408]{1,0:T(8,128)(2,1)S(1)}, bf16[384,1408]{1,0:T(8,128)(2,1)}, u32[]{:S(2)}, u32[]{:S(2)}) collective-permute-start(bf16[384,1408]{1,0:T(8,128)(2,1)S(1)} %constant_dynamic-slice_fusion.2), channel_id=1, source_target_pairs={{0,1},{1,0},{2,3},{3,2},{4,5},{5,4},{6,7},{7,6},{8,9},{9,8},{10,11... | collective-permute-start | bytes 3244040 | tf_op jit(solution)/shard_map/ppermute | solution.py:353
  57.1 2.2 collective-permute-start.2
  65.4 5.0 %collective-permute-start.3 = (bf16[4,144,128]{2,1,0:T(8,128)(2,1)}, bf16[4,144,128]{2,1,0:T(8,128)(2,1)S(1)}, u32[]{:S(2)}, u32[]{:S(2)}) collective-permute-start(bf16[4,144,128]{2,1,0:T(8,128)(2,1)} %get-tuple-element.174), channel_id=1, source_target_pairs={{0,2},{2,0},{4,6},{6,4},{8,10},{10,8},{12,14},{14,12},{16,18},{18,... | collective-permute-start | bytes 442376 | tf_op jit(solution)/shard_map/ppermute | solution.py:353
  68.0 7.2 %collective-permute-start.4 = (bf16[4,144,128]{2,1,0:T(8,128)(2,1)}, bf16[4,144,128]{2,1,0:T(8,128)(2,1)S(1)}, u32[]{:S(2)}, u32[]{:S(2)}) collective-permute-start(bf16[4,144,128]{2,1,0:T(8,128)(2,1)} %get-tuple-element.175), channel_id=1, source_target_pairs={{0,4},{2,6},{4,0},{6,2},{8,12},{10,14},{12,8},{14,10},{16,20},{18,... | collective-permute-start | bytes 442376 | tf_op jit(solution)/shard_map/ppermute | solution.py:353
  70.3 7.5 %collective-permute-start.5 = (bf16[4,144,128]{2,1,0:T(8,128)(2,1)}, bf16[4,144,128]{2,1,0:T(8,128)(2,1)S(1)}, u32[]{:S(2)}, u32[]{:S(2)}) collective-permute-start(bf16[4,144,128]{2,1,0:T(8,128)(2,1)} %get-tuple-element.176), channel_id=1, source_target_pairs={{0,6},{2,4},{4,2},{6,0},{8,14},{10,12},{12,10},{14,8},{16,22},{18,... | collective-permute-start | bytes 442376 | tf_op jit(solution)/shard_map/ppermute | solution.py:353
  70.4 7.5 %copy-start.30 = (bf16[4,144,128]{2,1,0:T(8,128)(2,1)}, bf16[4,144,128]{2,1,0:T(8,128)(2,1)S(1)}, u32[]{:S(2)}) copy-start(bf16[4,144,128]{2,1,0:T(8,128)(2,1)S(1)} %collective-permute-done.3.refs_1_.refs_5_) | copy-start | bytes 442372
  80.4 53.9 %copy-start.5 = (bf16[1920,256]{1,0:T(8,128)(2,1)}, bf16[1920,256]{1,0:T(8,128)(2,1)S(1)}, u32[]{:S(2)}) copy-start(bf16[1920,256]{1,0:T(8,128)(2,1)S(1)} %collective-permute-done.12.out_a.refs_13_) | copy-start | bytes 2949124
  80.4 31.0 %collective-permute-start.13 = (bf16[1920,256]{1,0:T(8,128)(2,1)S(1)}, bf16[1920,256]{1,0:T(8,128)(2,1)S(1)}, u32[]{:S(2)}, u32[]{:S(2)}) collective-permute-start(bf16[1920,256]{1,0:T(8,128)(2,1)S(1)} %collective-permute-done.12.out_a.refs_13_), channel_id=1, source_target_pairs={{0,4},{2,6},{4,0},{6,2},{8,12},{10,14},{12,8},{14,10},{16,20},{18,... | collective-permute-start | bytes 2949128 | tf_op jit(solution)/shard_map/ppermute | solution.py:353
  82.0 9.1 %collective-permute-start.6 = (bf16[4,144,128]{2,1,0:T(8,128)(2,1)}, bf16[4,144,128]{2,1,0:T(8,128)(2,1)S(1)}, u32[]{:S(2)}, u32[]{:S(2)}) collective-permute-start(bf16[4,144,128]{2,1,0:T(8,128)(2,1)} %group.2.refs_0_), channel_id=1, source_target_pairs={{0,8},{2,10},{4,12},{6,14},{8,0},{10,2},{12,4},{14,6},{16,24},{18,... | collective-permute-start | bytes 442376 | tf_op jit(solution)/shard_map/ppermute | solution.py:353
  83.5 14.2 %collective-permute-start.7 = (bf16[4,144,128]{2,1,0:T(8,128)(2,1)}, bf16[4,144,128]{2,1,0:T(8,128)(2,1)S(1)}, u32[]{:S(2)}, u32[]{:S(2)}) collective-permute-start(bf16[4,144,128]{2,1,0:T(8,128)(2,1)} %group.2.refs_0_), channel_id=1, source_target_pairs={{0,16},{2,18},{4,20},{6,22},{8,24},{10,26},{12,28},{14,30},{16,0},... | collective-permute-start | bytes 442376 | tf_op jit(solution)/shard_map/ppermute | solution.py:353
  86.1 11.6 %collective-permute-start.8 = (bf16[4,144,128]{2,1,0:T(8,128)(2,1)}, bf16[4,144,128]{2,1,0:T(8,128)(2,1)S(1)}, u32[]{:S(2)}, u32[]{:S(2)}) collective-permute-start(bf16[4,144,128]{2,1,0:T(8,128)(2,1)} %group.2.refs_0_), channel_id=1, source_target_pairs={{0,24},{2,26},{4,28},{6,30},{8,16},{10,18},{12,20},{14,22},{16,8},... | collective-permute-start | bytes 442376 | tf_op jit(solution)/shard_map/ppermute | solution.py:353
  91.1 6.7 %copy-start.42 = (bf16[4,144,128]{2,1,0:T(8,128)(2,1)}, bf16[4,144,128]{2,1,0:T(8,128)(2,1)S(1)}, u32[]{:S(2)}) copy-start(bf16[4,144,128]{2,1,0:T(8,128)(2,1)S(1)} %collective-permute-done.6.refs_1_) | copy-start | bytes 442372
  101.7 25.9 %collective-permute-start.18 = (bf16[384,1408]{1,0:T(8,128)(2,1)}, bf16[384,1408]{1,0:T(8,128)(2,1)S(1)}, u32[]{:S(2)}, u32[]{:S(2)}) collective-permute-start(bf16[384,1408]{1,0:T(8,128)(2,1)} %collective-permute-done.14.refs_4_), channel_id=1, source_target_pairs={{0,8},{2,10},{4,12},{6,14},{8,0},{10,2},{12,4},{14,6},{16,24},{18,... | collective-permute-start | bytes 3244040 | tf_op jit(solution)/shard_map/ppermute | solution.py:353
  104.0 5.7 %collective-permute-start.10 = (bf16[4,128,128]{2,1,0:T(8,128)(2,1)}, bf16[4,128,128]{2,1,0:T(8,128)(2,1)S(1)}, u32[]{:S(2)}, u32[]{:S(2)}) collective-permute-start(bf16[4,128,128]{2,1,0:T(8,128)(2,1)} %get-tuple-element.187), channel_id=1, source_target_pairs={{0,4},{2,6},{4,0},{6,2},{8,12},{10,14},{12,8},{14,10},{16,20},{18,... | collective-permute-start | bytes 393224 | tf_op jit(solution)/shard_map/ppermute | solution.py:353
  105.4 6.0 %collective-permute-start.11 = (bf16[4,128,128]{2,1,0:T(8,128)(2,1)}, bf16[4,128,128]{2,1,0:T(8,128)(2,1)S(1)}, u32[]{:S(2)}, u32[]{:S(2)}) collective-permute-start(bf16[4,128,128]{2,1,0:T(8,128)(2,1)} %get-tuple-element.188), channel_id=1, source_target_pairs={{0,6},{2,4},{4,2},{6,0},{8,14},{10,12},{12,10},{14,8},{16,22},{18,... | collective-permute-start | bytes 393224 | tf_op jit(solution)/shard_map/ppermute | solution.py:353
  105.4 6.0 %collective-permute-start.9 = (bf16[4,128,128]{2,1,0:T(8,128)(2,1)}, bf16[4,128,128]{2,1,0:T(8,128)(2,1)S(1)}, u32[]{:S(2)}, u32[]{:S(2)}) collective-permute-start(bf16[4,128,128]{2,1,0:T(8,128)(2,1)} %get-tuple-element.186), channel_id=1, source_target_pairs={{0,2},{2,0},{4,6},{6,4},{8,10},{10,8},{12,14},{14,12},{16,18},{18,... | collective-permute-start | bytes 393224 | tf_op jit(solution)/shard_map/ppermute | solution.py:353
  111.4 22.9 %copy-start.6 = (bf16[1920,256]{1,0:T(8,128)(2,1)}, bf16[1920,256]{1,0:T(8,128)(2,1)S(1)}, u32[]{:S(2)}) copy-start(bf16[1920,256]{1,0:T(8,128)(2,1)S(1)} %collective-permute-done.13.out_b.refs_14_) | copy-start | bytes 2949124
  111.5 19.5 %collective-permute-start.16 = (bf16[1920,256]{1,0:T(8,128)(2,1)S(1)}, bf16[1920,256]{1,0:T(8,128)(2,1)S(1)}, u32[]{:S(2)}, u32[]{:S(2)}) collective-permute-start(bf16[1920,256]{1,0:T(8,128)(2,1)S(1)} %collective-permute-done.12.out_a.refs_13_), channel_id=1, source_target_pairs={{0,2},{2,0},{4,6},{6,4},{8,10},{10,8},{12,14},{14,12},{16,18},{18,... | collective-permute-start | bytes 2949128 | tf_op jit(solution)/shard_map/ppermute | solution.py:353
  112.2 18.8 %collective-permute-start.17 = (bf16[1920,256]{1,0:T(8,128)(2,1)S(1)}, bf16[1920,256]{1,0:T(8,128)(2,1)S(1)}, u32[]{:S(2)}, u32[]{:S(2)}) collective-permute-start(bf16[1920,256]{1,0:T(8,128)(2,1)S(1)} %collective-permute-done.13.out_b.refs_14_), channel_id=1, source_target_pairs={{0,2},{2,0},{4,6},{6,4},{8,10},{10,8},{12,14},{14,12},{16,18},{18,... | collective-permute-start | bytes 2949128 | tf_op jit(solution)/shard_map/ppermute | solution.py:353
  112.3 18.7 %collective-permute-start.15 = (bf16[128,2816]{1,0:T(8,128)(2,1)}, bf16[128,2816]{1,0:T(8,128)(2,1)S(1)}, u32[]{:S(2)}, u32[]{:S(2)}) collective-permute-start(bf16[128,2816]{1,0:T(8,128)(2,1)} %constant_dynamic-slice_fusion.5), channel_id=1, source_target_pairs={{0,1},{1,0},{2,3},{3,2},{4,5},{5,4},{6,7},{7,6},{8,9},{9,8},{10,11... | collective-permute-start | bytes 2162696 | tf_op jit(solution)/shard_map/ppermute | solution.py:353
  122.8 8.3 %collective-permute-start.19 = (bf16[384,1408]{1,0:T(8,128)(2,1)}, bf16[384,1408]{1,0:T(8,128)(2,1)S(1)}, u32[]{:S(2)}, u32[]{:S(2)}) collective-permute-start(bf16[384,1408]{1,0:T(8,128)(2,1)} %collective-permute-done.14.refs_4_), channel_id=1, source_target_pairs={{0,2},{2,0},{4,6},{6,4},{8,10},{10,8},{12,14},{14,12},{16,18},{18,... | collective-permute-start | bytes 3244040 | tf_op jit(solution)/shard_map/ppermute | solution.py:353
  127.6 6.7 %copy-start.22 = (bf16[384,1408]{1,0:T(8,128)(2,1)}, bf16[384,1408]{1,0:T(8,128)(2,1)S(1)}, u32[]{:S(2)}) copy-start(bf16[384,1408]{1,0:T(8,128)(2,1)S(1)} %collective-permute-done.18.refs_5_) | copy-start | bytes 3244036
  127.6 5.7 %collective-permute-start.20 = (bf16[384,1408]{1,0:T(8,128)(2,1)S(1)}, bf16[384,1408]{1,0:T(8,128)(2,1)S(1)}, u32[]{:S(2)}, u32[]{:S(2)}) collective-permute-start(bf16[384,1408]{1,0:T(8,128)(2,1)S(1)} %collective-permute-done.18.refs_5_), channel_id=1, source_target_pairs={{0,2},{2,0},{4,6},{6,4},{8,10},{10,8},{12,14},{14,12},{16,18},{18,... | collective-permute-start | bytes 3244040 | tf_op jit(solution)/shard_map/ppermute | solution.py:353
  131.0 2.3 collective-permute-start.21
  159.3 39.2 %collective-permute-start.25 = (bf16[6016,128]{1,0:T(8,128)(2,1)}, bf16[6016,128]{1,0:T(8,128)(2,1)S(1)}, u32[]{:S(2)}, u32[]{:S(2)}) collective-permute-start(bf16[6016,128]{1,0:T(8,128)(2,1)} %get-tuple-element.236.refs_2_.refs_6_.refs_10_.logit1), channel_id=1, source_target_pairs={{0,1},{1,0},{2,3},{3,2},{4,5},{5,4},{6,7},{7,6},{8,9},{9,8},{10,11... | collective-permute-start | bytes 4620296 | tf_op jit(solution)/shard_map/ppermute | solution.py:353
  180.2 1.9 collective-permute-start.22
  180.2 6.9 %collective-permute-start.23 = (bf16[4,144,128]{2,1,0:T(8,128)(2,1)}, bf16[4,144,128]{2,1,0:T(8,128)(2,1)S(1)}, u32[]{:S(2)}, u32[]{:S(2)}) collective-permute-start(bf16[4,144,128]{2,1,0:T(8,128)(2,1)} %get-tuple-element.224), channel_id=1, source_target_pairs={{0,4},{2,6},{4,0},{6,2},{8,12},{10,14},{12,8},{14,10},{16,20},{18,... | collective-permute-start | bytes 442376 | tf_op jit(solution)/shard_map/ppermute | solution.py:353
  181.7 7.7 %collective-permute-start.24 = (bf16[4,144,128]{2,1,0:T(8,128)(2,1)}, bf16[4,144,128]{2,1,0:T(8,128)(2,1)S(1)}, u32[]{:S(2)}, u32[]{:S(2)}) collective-permute-start(bf16[4,144,128]{2,1,0:T(8,128)(2,1)} %get-tuple-element.225), channel_id=1, source_target_pairs={{0,6},{2,4},{4,2},{6,0},{8,14},{10,12},{12,10},{14,8},{16,22},{18,... | collective-permute-start | bytes 442376 | tf_op jit(solution)/shard_map/ppermute | solution.py:353
  182.1 7.3 %copy-start.27 = (bf16[4,144,128]{2,1,0:T(8,128)(2,1)}, bf16[4,144,128]{2,1,0:T(8,128)(2,1)S(1)}, u32[]{:S(2)}) copy-start(bf16[4,144,128]{2,1,0:T(8,128)(2,1)S(1)} %collective-permute-done.22.refs_1_.refs_5_) | copy-start | bytes 442372
  192.0 6.5 %collective-permute-start.26 = (bf16[4,144,128]{2,1,0:T(8,128)(2,1)}, bf16[4,144,128]{2,1,0:T(8,128)(2,1)S(1)}, u32[]{:S(2)}, u32[]{:S(2)}) collective-permute-start(bf16[4,144,128]{2,1,0:T(8,128)(2,1)} %group.3.refs_0_), channel_id=1, source_target_pairs={{0,8},{2,10},{4,12},{6,14},{8,0},{10,2},{12,4},{14,6},{16,24},{18,... | collective-permute-start | bytes 442376 | tf_op jit(solution)/shard_map/ppermute | solution.py:353
  198.6 6.8 %copy-start.41 = (bf16[4,144,128]{2,1,0:T(8,128)(2,1)}, bf16[4,144,128]{2,1,0:T(8,128)(2,1)S(1)}, u32[]{:S(2)}) copy-start(bf16[4,144,128]{2,1,0:T(8,128)(2,1)S(1)} %collective-permute-done.26.refs_1_) | copy-start | bytes 442372
  205.3 21.8 %copy-start.39 = (bf16[144,1024]{1,0:T(8,128)(2,1)S(1)}, bf16[144,1024]{1,0:T(8,128)(2,1)}, u32[]{:S(2)}) copy-start(bf16[144,1024]{1,0:T(8,128)(2,1)} %get-tuple-element.227) | copy-start | bytes 884740
  206.7 42.1 %collective-permute-start.33 = (bf16[128,5632]{1,0:T(8,128)(2,1)S(1)}, bf16[128,5632]{1,0:T(8,128)(2,1)}, u32[]{:S(2)}, u32[]{:S(2)}) collective-permute-start(bf16[128,5632]{1,0:T(8,128)(2,1)S(1)} %copy-done.20), channel_id=1, source_target_pairs={{0,1},{1,0},{2,3},{3,2},{4,5},{5,4},{6,7},{7,6},{8,9},{9,8},{10,11... | collective-permute-start | bytes 4325384 | tf_op jit(solution)/shard_map/ppermute | solution.py:353
  208.2 13.0 %collective-permute-start.27 = (bf16[4,144,128]{2,1,0:T(8,128)(2,1)S(1)}, bf16[4,144,128]{2,1,0:T(8,128)(2,1)S(1)}, u32[]{:S(2)}, u32[]{:S(2)}) collective-permute-start(bf16[4,144,128]{2,1,0:T(8,128)(2,1)S(1)} %copy-done.33), channel_id=1, source_target_pairs={{0,16},{2,18},{4,20},{6,22},{8,24},{10,26},{12,28},{14,30},{16,0},... | collective-permute-start | bytes 442376 | tf_op jit(solution)/shard_map/ppermute | solution.py:353
  210.1 11.1 %collective-permute-start.28 = (bf16[4,144,128]{2,1,0:T(8,128)(2,1)S(1)}, bf16[4,144,128]{2,1,0:T(8,128)(2,1)S(1)}, u32[]{:S(2)}, u32[]{:S(2)}) collective-permute-start(bf16[4,144,128]{2,1,0:T(8,128)(2,1)S(1)} %copy-done.33), channel_id=1, source_target_pairs={{0,24},{2,26},{4,28},{6,30},{8,16},{10,18},{12,20},{14,22},{16,8},... | collective-permute-start | bytes 442376 | tf_op jit(solution)/shard_map/ppermute | solution.py:353
  225.3 1.9 collective-permute-start.29
  225.3 6.5 %collective-permute-start.30 = (bf16[4,128,128]{2,1,0:T(8,128)(2,1)}, bf16[4,128,128]{2,1,0:T(8,128)(2,1)S(1)}, u32[]{:S(2)}, u32[]{:S(2)}) collective-permute-start(bf16[4,128,128]{2,1,0:T(8,128)(2,1)} %get-tuple-element.246), channel_id=1, source_target_pairs={{0,4},{2,6},{4,0},{6,2},{8,12},{10,14},{12,8},{14,10},{16,20},{18,... | collective-permute-start | bytes 393224 | tf_op jit(solution)/shard_map/ppermute | solution.py:353
  226.1 7.6 %collective-permute-start.31 = (bf16[4,128,128]{2,1,0:T(8,128)(2,1)}, bf16[4,128,128]{2,1,0:T(8,128)(2,1)S(1)}, u32[]{:S(2)}, u32[]{:S(2)}) collective-permute-start(bf16[4,128,128]{2,1,0:T(8,128)(2,1)} %get-tuple-element.247), channel_id=1, source_target_pairs={{0,6},{2,4},{4,2},{6,0},{8,14},{10,12},{12,10},{14,8},{16,22},{18,... | collective-permute-start | bytes 393224 | tf_op jit(solution)/shard_map/ppermute | solution.py:353
  227.2 6.6 %copy-start.34 = (bf16[4,128,128]{2,1,0:T(8,128)(2,1)}, bf16[4,128,128]{2,1,0:T(8,128)(2,1)S(1)}, u32[]{:S(2)}) copy-start(bf16[4,128,128]{2,1,0:T(8,128)(2,1)S(1)} %collective-permute-done.29.r1) | copy-start | bytes 393220
  245.2 3.6 collective-permute-start.34
  246.4 5.4 %collective-permute-start.35 = (bf16[8,3072]{1,0:T(8,128)(2,1)S(1)}, bf16[8,3072]{1,0:T(8,128)(2,1)S(1)}, u32[]{:S(2)}, u32[]{:S(2)}) collective-permute-start(bf16[8,3072]{1,0:T(8,128)(2,1)S(1)} %pad_maximum_fusion.2), channel_id=1, source_target_pairs={{2,1},{3,0},{4,3},{5,2},{6,5},{7,4},{8,7},{9,6},{10,9},{11,8},{12,... | collective-permute-start | bytes 147464 | tf_op jit(solution)/shard_map/ppermute | solution.py:1155
  248.8 11.2 %copy-start.2 = (bf16[432,1024]{1,0:T(8,128)(2,1)}, bf16[432,1024]{1,0:T(8,128)(2,1)S(1)}, u32[]{:S(2)}) copy-start(bf16[432,1024]{1,0:T(8,128)(2,1)S(1)} %constant_dynamic-update-slice_fusion.refs_2_.refs_8_.refs_14_.own) | copy-start | bytes 2654212
  248.8 9.1 %copy-start.25 = (bf16[8,3072]{1,0:T(8,128)(2,1)}, bf16[8,3072]{1,0:T(8,128)(2,1)S(1)}, u32[]{:S(2)}) copy-start(bf16[8,3072]{1,0:T(8,128)(2,1)S(1)} %collective-permute-done.34.refs_4_.refs_10_.refs_16_.extra1) | copy-start | bytes 147460
  251.8 6.0 %copy-start.26 = (bf16[8,3072]{1,0:T(8,128)(2,1)}, bf16[8,3072]{1,0:T(8,128)(2,1)S(1)}, u32[]{:S(2)}) copy-start(bf16[8,3072]{1,0:T(8,128)(2,1)S(1)} %collective-permute-done.35.refs_5_.refs_11_.refs_17_.extra2) | copy-start | bytes 147460
  257.9 7.4 %collective-permute-start.36 = (bf16[8,32,5632]{2,1,0:T(8,128)(2,1)}, bf16[8,32,5632]{2,1,0:T(8,128)(2,1)}, u32[]{:S(2)}, u32[]{:S(2)}) collective-permute-start(bf16[8,32,5632]{2,1,0:T(8,128)(2,1)} %get-tuple-element.261), channel_id=1, source_target_pairs={{0,2},{2,0},{4,6},{6,4},{8,10},{10,8},{12,14},{14,12},{16,18},{18,... | collective-permute-start | bytes 8650760 | tf_op jit(solution)/shard_map/ppermute | solution.py:353
  260.0 21.6 %collective-permute-start.32 = (bf16[432,1024]{1,0:T(8,128)(2,1)S(1)}, bf16[432,1024]{1,0:T(8,128)(2,1)S(1)}, u32[]{:S(2)}, u32[]{:S(2)}) collective-permute-start(bf16[432,1024]{1,0:T(8,128)(2,1)S(1)} %constant_dynamic-update-slice_fusion.refs_2_.refs_8_.refs_14_.own), channel_id=1, source_target_pairs={{0,1},{1,0},{2,3},{3,2},{4,5},{5,4},{6,7},{7,6},{8,9},{9,8},{10,11... | collective-permute-start | bytes 2654216 | tf_op jit(solution)/shard_map/ppermute | solution.py:353
  270.2 34.7 %collective-permute-start.40 = (bf16[4,32,5632]{2,1,0:T(8,128)(2,1)}, bf16[4,32,5632]{2,1,0:T(8,128)(2,1)S(1)}, u32[]{:S(2)}, u32[]{:S(2)}) collective-permute-start(bf16[4,32,5632]{2,1,0:T(8,128)(2,1)} %get-tuple-element.263), channel_id=1, source_target_pairs={{0,4},{2,6},{4,0},{6,2},{8,12},{10,14},{12,8},{14,10},{16,20},{18,... | collective-permute-start | bytes 4325384 | tf_op jit(solution)/shard_map/ppermute | solution.py:353
  286.8 2.6 collective-permute-start.37
  286.9 3.6 collective-permute-start.38
  295.5 26.0 %collective-permute-start.41 = (bf16[4,96,1024]{2,1,0:T(8,128)(2,1)}, bf16[4,96,1024]{2,1,0:T(8,128)(2,1)S(1)}, u32[]{:S(2)}, u32[]{:S(2)}) collective-permute-start(bf16[4,96,1024]{2,1,0:T(8,128)(2,1)} %get-tuple-element.273), channel_id=1, source_target_pairs={{0,4},{2,6},{4,0},{6,2},{8,12},{10,14},{12,8},{14,10},{16,20},{18,... | collective-permute-start | bytes 2359304 | tf_op jit(solution)/shard_map/ppermute | solution.py:353
  302.6 9.8 %collective-permute-start.39 = (bf16[128,512]{1,0:T(8,128)(2,1)}, bf16[128,512]{1,0:T(8,128)(2,1)S(1)}, u32[]{:S(2)}, u32[]{:S(2)}) collective-permute-start(bf16[128,512]{1,0:T(8,128)(2,1)} %get-tuple-element.276), channel_id=1, source_target_pairs={{0,1},{1,0},{2,3},{3,2},{4,5},{5,4},{6,7},{7,6},{8,9},{9,8},{10,11... | collective-permute-start | bytes 393224 | tf_op jit(solution)/shard_map/ppermute | solution.py:353
  308.7 21.0 %collective-permute-start.44 = (bf16[2,32,5632]{2,1,0:T(8,128)(2,1)}, bf16[2,32,5632]{2,1,0:T(8,128)(2,1)S(1)}, u32[]{:S(2)}, u32[]{:S(2)}) collective-permute-start(bf16[2,32,5632]{2,1,0:T(8,128)(2,1)} %get-tuple-element.279), channel_id=1, source_target_pairs={{0,8},{2,10},{4,12},{6,14},{8,0},{10,2},{12,4},{14,6},{16,24},{18,... | collective-permute-start | bytes 2162696 | tf_op jit(solution)/shard_map/ppermute | solution.py:353
  324.6 16.2 %collective-permute-start.42 = (bf16[2,96,1024]{2,1,0:T(8,128)(2,1)}, bf16[2,96,1024]{2,1,0:T(8,128)(2,1)S(1)}, u32[]{:S(2)}, u32[]{:S(2)}) collective-permute-start(bf16[2,96,1024]{2,1,0:T(8,128)(2,1)} %get-tuple-element.291), channel_id=1, source_target_pairs={{0,8},{2,10},{4,12},{6,14},{8,0},{10,2},{12,4},{14,6},{16,24},{18,... | collective-permute-start | bytes 1179656 | tf_op jit(solution)/shard_map/ppermute | solution.py:353
  328.3 5.4 %collective-permute-start.43 = (f32[16,480]{1,0:T(8,128)S(1)}, f32[16,480]{1,0:T(8,128)S(1)}, u32[]{:S(2)}, u32[]{:S(2)}) collective-permute-start(f32[16,480]{1,0:T(8,128)S(1)} %bitcast.57), channel_id=1, source_target_pairs={{0,1},{1,0},{2,3},{3,2},{4,5},{5,4},{6,7},{7,6},{8,9},{9,8},{10,11... | collective-permute-start | bytes 92168 | tf_op jit(solution)/shard_map/ppermute | solution.py:353
  329.7 9.2 %copy-start.21 = (bf16[152,1024]{1,0:T(8,128)(2,1)S(1)}, bf16[152,1024]{1,0:T(8,128)(2,1)}, u32[]{:S(2)}) copy-start(bf16[152,1024]{1,0:T(8,128)(2,1)} %reduce-scatter.2.cloned.1.call-done) | copy-start | bytes 933892
  332.8 29.4 %collective-permute-start.46 = (bf16[1,32,5632]{2,1,0:T(8,128)(2,1)}, bf16[1,32,5632]{2,1,0:T(8,128)(2,1)S(1)}, u32[]{:S(2)}, u32[]{:S(2)}) collective-permute-start(bf16[1,32,5632]{2,1,0:T(8,128)(2,1)} %get-tuple-element.294), channel_id=1, source_target_pairs={{0,16},{2,18},{4,20},{6,22},{8,24},{10,26},{12,28},{14,30},{16,0},... | collective-permute-start | bytes 1081352 | tf_op jit(solution)/shard_map/ppermute | solution.py:353
  334.3 24.5 %all-to-all-start = ((f32[16,1,480]{2,1,0:T(1,128)}), f32[16,1,480]{2,1,0:T(1,128)S(1)}, u32[]{:S(2)}, u32[]{:S(2)}) async-start(f32[16,1,480]{2,1,0:T(1,128)} %all_to_all.8), calls=%async_computation.1 | async-start | bytes 65536 | tf_op jit(solution)/shard_map/all_to_all | solution.py:1439
  343.6 18.6 %copy-start.38 = (bf16[1,32,5632]{2,1,0:T(8,128)(2,1)S(1)}, bf16[1,32,5632]{2,1,0:T(8,128)(2,1)}, u32[]{:S(2)}) copy-start(bf16[1,32,5632]{2,1,0:T(8,128)(2,1)} %get-tuple-element.301) | copy-start | bytes 1081348
  344.4 16.1 %collective-permute-start.45 = (bf16[1,96,1024]{2,1,0:T(8,128)(2,1)}, bf16[1,96,1024]{2,1,0:T(8,128)(2,1)S(1)}, u32[]{:S(2)}, u32[]{:S(2)}) collective-permute-start(bf16[1,96,1024]{2,1,0:T(8,128)(2,1)} %get-tuple-element.299), channel_id=1, source_target_pairs={{0,16},{2,18},{4,20},{6,22},{8,24},{10,26},{12,28},{14,30},{16,0},... | collective-permute-start | bytes 589832 | tf_op jit(solution)/shard_map/ppermute | solution.py:353
  (34 other events, 56.9 us)
Sparse Core Ops, SparseCore 0:
  205.5 78.0 reduce-scatter.1

commit v5 on v4

--- a/solution.py
+++ b/solution.py
@@ -64,10 +64,10 @@
     rows = a.shape[0]
     gain = lines_ref[0:1].astype(f32)
     mine_o[...] = (jnp.where(y == 0, left, right) * gain).astype(bf16)
-    theirs_o[:rows] = jnp.where(y == 0, right, left)
-    taps = taps_ref[...].astype(f32)
+    theirs_o[:rows] = jnp.where(y == 0, right, left).astype(bf16)
+    taps = taps_ref[...]
     lines = [taps[t : t + 1, i * half : (i + 1) * half] for t in range(KW) for i in range(3)]
-    theirs_o[rows:] = jnp.concatenate(lines + [lines_ref[...].astype(f32)], axis=0)
+    theirs_o[rows:] = jnp.concatenate(lines + [lines_ref[...]], axis=0)
 
 
 def norm(place, tokens, taps, lines):
@@ -77,7 +77,7 @@
         norm_kernel,
         in_specs=[smem()] + [vmem] * 3,
         out_specs=[vmem, vmem],
-        out_shape=[like((rows, D // 2), bf16), like((rows + EXTRA, D // 2))],
+        out_shape=[like((rows, D // 2), bf16), like((rows + EXTRA, D // 2), bf16)],
         name="norm",
     )(place, tokens, taps, lines)
 
@@ -88,7 +88,7 @@
     @pl.when(j == 0)
     def _():
         rows = left_ref[: left.shape[0]]
-        left[...] = (rows * gain_ref[...].astype(f32)).astype(bf16) if scaled else rows
+        left[...] = (rows.astype(f32) * gain_ref[...].astype(f32)).astype(bf16) if scaled else rows
 
     steps = 3 * D // out.shape[1]
 
@@ -106,7 +106,7 @@
     tile = 1024
     steps = 3 * D // tile
     return pl.pallas_call(
-        functools.partial(weigh_kernel, left.dtype == f32),
+        functools.partial(weigh_kernel, left.shape[0] > rows),
         grid=(4 * D // tile,),
         in_specs=[
             whole(*left.shape), whole(1, half),
@@ -1268,7 +1268,7 @@
     lent = weigh(theirs, rows, gain_attn[None], qkv_weight, gate_weight, bf16)
     seq.mark(lent)
     lent = partner(lent, "fsdp")
-    peer_extra = theirs[rows:]
+    peer_extra = theirs[rows:].astype(f32)
     (peer_extra,) = seq.gate(peer_extra)
     taps_rows = KW * 3
     vectors = sided(lines[:3].astype(f32), peer_extra[taps_rows : taps_rows + 3], y, 1)
@@ -1389,18 +1389,20 @@
         spot_back, projected, taps, dk_attend, dk_solve, keys_low, values_low, states_back, ending
     )
     seq.mark(low_k)
+    (up_peer,) = seq.gate(both_up[1])
+    blocks = products(
+        spot, peers, [[(lefts, parts[0]), (message_peer, peer_parts[0])]], [[(both_up[0], None), (up_peer, None)]], 1408
+    )
+    seq.mark(blocks[0])
+    ups = Reduction((0, 1, 2), blocks)
+    low_q, low_k, low_v = seq.gate(low_q, low_k, low_v)
     ahead = jnp.concatenate([low[HALO - 8 : HALO] for low in (low_q, low_k, low_v)], axis=1)
     extra = shifted(ahead, "ctx", -1), crossed(ahead, -1)
     thirds = jnp.concatenate([low_q, low_k, low_v], axis=0)
-    seq.mark(thirds)
+    thirds, *extra = lax.optimization_barrier((thirds, *extra))
     thirds_peer = partner(thirds, "fsdp")
-    up_peer, *extra = seq.gate(both_up[1], *extra)
-    blocks = products(
-        spot, peers, [[(lefts, parts[0]), (message_peer, peer_parts[0])]], [[(both_up[0], None), (up_peer, None)]], 1408
-    )
-    seq.mark(blocks[0])
-    ups = Reduction((0, 1, 2), blocks)
-    ups.got = seq.gate(*ups.got)
+    *ups.got, extra1, extra2 = seq.gate(*ups.got, *extra)
+    extra = extra1, extra2
     seq.mark(ups.step())
     lefts_here, thirds_peer = seq.gate(lefts, thirds_peer)
     left = [(lefts_here, parts[2]), (message_peer, peer_parts[2])]

time: 372 us -> 367 us (0.987)
    unnamed x104 -> x106, local copies, waits for them, and re-layouts: 16.8 us -> 16.9 us
  transfers between devices with their start and end apart: 49 -> 49, of which waited for: 28 -> 28; matrix products, arithmetic and copies ran while one was open for 6% -> 5% of each run, Pallas kernels for 28% -> 29%
where the time goes in v5:
time: 367 us; the launch traced here: 365 us
  Pallas kernels  142 us (39%)
  waiting for transfers between devices  108 us (29%)
  starting transfers between devices  59.3 us (16%)
  local copies, waits for them, and re-layouts  30.9 us (8%)
  between operations  14.5 us (4%)
  other arithmetic  10.2 us (3%)
    ppermute x44, waiting for transfers between devices, partner(): return lax.ppermute(x, axis, neighbour(axis, bit))  91.4 us
    ppermute x44, starting transfers between devices, partner(): return lax.ppermute(x, axis, neighbour(axis, bit))  51.8 us
    pallas_call x1, Pallas kernels, middle(): pl.pallas_call(functools.partial(middle_kernel, owners), grid_spec=pltpu....  24.8 us
    pallas_call x6, Pallas kernels, halving_step(): pl.pallas_call(step_kernel, grid_spec=pltpu.PrefetchScalarGridSpec(num_sc...  18 us
    unnamed x106, local copies, waits for them, and re-layouts  16.9 us
    pallas_call x3, Pallas kernels, products(): pl.pallas_call(functools.partial(products_kernel, plan, joined, cuts), gr...  15.8 us
    pallas_call x1, Pallas kernels, adjoint(): pl.pallas_call(adjoint_kernel, grid=(ITERS,), in_specs=[smem(), smem(), w...  15.3 us
    pallas_call x3, Pallas kernels, third_back(): pl.pallas_call(kernel, grid=(QUARTERS,), in_specs=[smem()] * len(before)...  14.5 us
  transfers between devices with their start and end apart: 49, of which 28 were waited for; matrix products, arithmetic and copies ran while one was open for 5% of the time, Pallas kernels for 29%

profile of v5, /device:TPU:0, one launch (start us, length us, event | category | flops | bytes accessed | tf_op | source)
XLA Modules:
  0.0 364.6 jit_solution(14172424682785415148)
XLA Ops:
  10.6 1.9 norm.1
  12.5 3.0 collective-permute-start
  20.2 4.7 %weigh.2 = bf16[128,4096]{1,0:T(8,128)(2,1)} custom-call(bf16[144,512]{1,0:T(8,128)(2,1)} %copy-done.42, bf16[1,512]{1,0:T(2,128)(2,1)} %copy-done.50, bf16[512,3072]{1,0:T(8,128)(2,1)} %qkv_ref.5, bf16[512,1024]{1,0:T(8,128)(2,1)} %gate_ref.5), custom_call_target="tpu_custom_call" | custom-call | flops 1 | bytes 1 | tf_op jit(solution)/shard_map/weigh/pallas_call | solution.py:108
  24.9 1.7 collective-permute-start.1
  32.9 2.0 constant_dynamic-slice_fusion.5
  35.5 5.0 %weigh.3.oq.ok.ov.own_logit.own = f32[128,4096]{1,0:T(8,128)} custom-call(bf16[128,512]{1,0:T(8,128)(2,1)} %get-tuple-element.170.left_ref, bf16[1,512]{1,0:T(2,128)(2,1)} %copy-done.50, bf16[512,3072]{1,0:T(8,128)(2,1)} %qkv_ref.5, bf16[512,1024]{1,0:T(8,128)(2,1)} %gate_ref.5), custom_call_target="tpu_custom_call" | custom-call | flops 1 | bytes 1 | tf_op jit(solution)/shard_map/weigh/pallas_call | solution.py:108
  40.4 4.2 %tables.1 = (f32[8,128,128]{2,1,0:T(8,128)}, f32[8,128,128]{2,1,0:T(8,128)}, f32[8,128,128]{2,1,0:T(8,128)}) custom-call(f32[8,128]{1,0:T(8,128)} %reduce_window_sum.11.c_ref, f32[8,128]{1,0:T(8,128)} %get-tuple-element.172.b_ref, f32[8,128]{1,0:T(8,128)} %bitcast.58), custom_call_target="tpu_custom_call" | custom-call | flops 1 | bytes 1 | tf_op jit(solution)/shard_map/tables/pallas_call | solution.py:136
  44.6 6.6 %collective-permute-done.1.lq.lk.lv.lent_logit.lent = bf16[128,4096]{1,0:T(8,128)(2,1)S(1)} collective-permute-done((bf16[128,4096]{1,0:T(8,128)(2,1)}, bf16[128,4096]{1,0:T(8,128)(2,1)S(1)}, u32[]{:S(2)}, u32[]{:S(2)}) %collective-permute-start.1) | collective-permute-done | bytes 1048608 | tf_op jit(solution)/shard_map/ppermute | solution.py:353
  51.2 1.7 collective-permute-start.14
  56.7 5.5 %features.1 = (f32[8,128,128]{2,1,0:T(8,128)}, bf16[8,128,128]{2,1,0:T(8,128)(2,1)}, bf16[8,128,128]{2,1,0:T(8,128)(2,1)}, bf16[4,144,128]{2,1,0:T(8,128)(2,1)},...) custom-call(s32[1]{0:T(128)} %bitcast.3.spot, ...), custom_call_target="tpu_custom_call" | custom-call | flops 1 | bytes 1 | tf_op jit(solution)/shard_map/features/pallas_call | solution.py:246
  62.2 2.6 collective-permute-start.3
  64.7 2.3 collective-permute-start.4
  67.1 4.8 %collective-permute-done.4.refs_2_.refs_6_ = bf16[4,144,128]{2,1,0:T(8,128)(2,1)S(1)} collective-permute-done((bf16[4,144,128]{2,1,0:T(8,128)(2,1)}, bf16[4,144,128]{2,1,0:T(8,128)(2,1)S(1)}, u32[]{:S(2)}, u32[]{:S(2)}) %collective-permute-start.4) | collective-permute-done | bytes 147488 | tf_op jit(solution)/shard_map/ppermute | solution.py:353
  72.0 2.6 collective-permute-done.5.refs_3_.refs_7_
  75.2 1.9 group.2.refs_0_
  80.3 2.6 collective-permute-start.7
  83.1 4.7 %collective-permute-done.6.refs_1_ = bf16[4,144,128]{2,1,0:T(8,128)(2,1)S(1)} collective-permute-done((bf16[4,144,128]{2,1,0:T(8,128)(2,1)}, bf16[4,144,128]{2,1,0:T(8,128)(2,1)S(1)}, u32[]{:S(2)}, u32[]{:S(2)}) %collective-permute-start.6) | collective-permute-done | bytes 147488 | tf_op jit(solution)/shard_map/ppermute | solution.py:353
  87.8 6.6 %collective-permute-done.7.refs_2_ = bf16[4,144,128]{2,1,0:T(8,128)(2,1)S(1)} collective-permute-done((bf16[4,144,128]{2,1,0:T(8,128)(2,1)}, bf16[4,144,128]{2,1,0:T(8,128)(2,1)S(1)}, u32[]{:S(2)}, u32[]{:S(2)}) %collective-permute-start.7) | collective-permute-done | bytes 147488 | tf_op jit(solution)/shard_map/ppermute | solution.py:353
  95.8 2.6 spread.2
  98.4 2.3 collective-permute-start.18
  102.9 3.6 collective-permute-done.10.s2
  109.6 9.9 %solve.1 = (bf16[8,128,128]{2,1,0:T(8,128)(2,1)}, f32[8,8,128,128]{3,2,1,0:T(8,128)}, f32[8,8,128,128]{3,2,1,0:T(8,128)}, bf16[8,8,128,128]{3,2,1,0:T(8,128)(2,1)}, f32[8,24,128]{2,1,0:T(8,128)}) custom-call(s32[1]{0:T(128)} %bitcast.1.place, f32[8,128,128]{2,1,0:T(8,128)} %get-tuple-element.200.q_ref, bf16[8,128,128]{2,1,0:T(8,128)(2,1)} %get-tuple-element.201.k_ref, ...), custom_call_target="tpu_custom_call" | custom-call | flops 1 | bytes 1 | tf_op jit(solution)/shard_map/solve/pallas_call | solution.py:477
  119.7 4.6 %collective-permute-done.18.refs_5_ = bf16[384,1408]{1,0:T(8,128)(2,1)S(1)} collective-permute-done((bf16[384,1408]{1,0:T(8,128)(2,1)}, bf16[384,1408]{1,0:T(8,128)(2,1)S(1)}, u32[]{:S(2)}, u32[]{:S(2)}) %collective-permute-start.18) | collective-permute-done | bytes 1081376 | tf_op jit(solution)/shard_map/ppermute | solution.py:353
  124.3 3.4 collective-permute-done.15.refs_8_.refs_9_
  127.9 2.2 collective-permute-done.21.refs_10_.refs_11_
  131.3 24.8 %middle.1 = (f32[128,1024]{1,0:T(8,128)}, f32[128,1024]{1,0:T(8,128)}, f32[128,1024]{1,0:T(8,128)}, bf16[2944,128]{1,0:T(8,128)(2,1)}, bf16[6016,128]{1,0:T(8,12...) custom-call(s32[3]{0:T(128)} %pad_add_fusion.place, bf16[8,128,128]{2,1,0:T(8,128)(2,1)} %get-tuple-element.204.x_ref, ...), custom_call_target="tpu_custom_call" | custom-call | flops 1 | bytes 1 | tf_op jit(solution)/shard_map/middle/pallas_call | solution.py:1104
  156.7 5.0 %attend_back.1 = (f32[8,128,128]{2,1,0:T(8,128)}, f32[8,128,128]{2,1,0:T(8,128)}, f32[8,128,128]{2,1,0:T(8,128)}, bf16[8,128,128]{2,1,0:T(8,128)(2,1)}) custom-call(s32[1]{0:T(128)} %bitcast.1.place, f32[128,1024]{1,0:T(8,128)} %get-tuple-element.220.ga_ref, bf16[8,128,128]{2,1,0:T(8,128)(2,1)} %get-tuple-element.201.k_ref, ...), custom_call_target="tpu_custom_call" | custom-call | flops 1 | bytes 1 | tf_op jit(solution)/shard_map/attend_back/pallas_call | solution.py:521
  161.6 15.3 %adjoint.1 = (f32[8,128,128]{2,1,0:T(8,128)}, f32[8,128,128]{2,1,0:T(8,128)}, f32[8,1,128]{2,1,0:T(1,128)}, bf16[4,144,128]{2,1,0:T(8,128)(2,1)}, bf16[4,144,128...) custom-call(s32[1]{0:T(128)} %bitcast.12.spot, s32[1]{0:T(128)} %bitcast.1.place, ...), custom_call_target="tpu_custom_call" | custom-call | flops 1 | bytes 1 | tf_op jit(solution)/shard_map/adjoint/pallas_call | solution.py:607
  178.9 4.6 %queries_back.1 = (bf16[144,1024]{1,0:T(8,128)(2,1)}, f32[4,1024]{1,0:T(4,128)}) custom-call(f32[128,4096]{1,0:T(8,128)} %weigh.3.oq.ok.ov.own_logit.own, bf16[128,4096]{1,0:T(8,128)(2,1)} %copy-done.1, bf16[8,3072]{1,0:T(8,128)(2,1)} %copy-done.18, f32[4,3072]{1,0:T(4,128)} %maximum_select_fusion.tq.tk.tv.t, f32[8,128,128]{2,1,0:T(8,128)} %get-tuple-element.232.dq_ref), custom_call_target="tpu_custom_call" | custom-call | flops 1 | bytes 1 | tf_op jit(solution)/shard_map/queries_back/pallas_call | solution.py:698
  183.9 2.3 collective-permute-done.24.refs_3_.refs_7_
  186.8 1.9 group.3.refs_0_
  189.7 5.6 %collective-permute-done.26.refs_1_ = bf16[4,144,128]{2,1,0:T(8,128)(2,1)S(1)} collective-permute-done((bf16[4,144,128]{2,1,0:T(8,128)(2,1)}, bf16[4,144,128]{2,1,0:T(8,128)(2,1)S(1)}, u32[]{:S(2)}, u32[]{:S(2)}) %collective-permute-start.26) | collective-permute-done | bytes 147488 | tf_op jit(solution)/shard_map/ppermute | solution.py:353
  196.5 5.6 %products.3 = bf16[16,152,1024]{2,1,0:T(8,128)(2,1)} custom-call(s32[1]{0:T(128)} %bitcast.3.spot, bf16[2944,128]{1,0:T(8,128)(2,1)} %get-tuple-element.276.refs_0_.refs_4_.refs_8_.refs_6_.refs_12_, bf16[6016,128]{1,0:T(8,128)(2,1)} %copy-done, bf16[6016,128]{1,0:T(8,128)(2,1)} %get-tuple-element.242.refs_2_.refs_6_.refs_10_.logit1, ...), custom_call_target="tpu_custom_call" | custom-call | flops 1 | bytes 1 | tf_op jit(solution)/shard_map/products/pallas_call | solution.py:837
  205.0 1.9 collective-permute-start.27
  208.3 9.7 %collective-permute-done.27.refs_2_ = bf16[4,144,128]{2,1,0:T(8,128)(2,1)S(1)} collective-permute-done((bf16[4,144,128]{2,1,0:T(8,128)(2,1)S(1)}, bf16[4,144,128]{2,1,0:T(8,128)(2,1)S(1)}, u32[]{:S(2)}, u32[]{:S(2)}) %collective-permute-start.27) | collective-permute-done | bytes 147488 | tf_op jit(solution)/shard_map/ppermute | solution.py:353
  219.3 2.7 spread.3
  223.9 4.7 %collective-permute-done.30.r2 = bf16[4,128,128]{2,1,0:T(8,128)(2,1)S(1)} collective-permute-done((bf16[4,128,128]{2,1,0:T(8,128)(2,1)}, bf16[4,128,128]{2,1,0:T(8,128)(2,1)S(1)}, u32[]{:S(2)}, u32[]{:S(2)}) %collective-permute-start.30) | collective-permute-done | bytes 131104 | tf_op jit(solution)/shard_map/ppermute | solution.py:353
  228.6 1.9 collective-permute-done.31.r3
  231.2 4.8 %values_back.1 = (bf16[144,1024]{1,0:T(8,128)(2,1)}, f32[4,1024]{1,0:T(4,128)}) custom-call(s32[1]{0:T(128)} %bitcast.12.spot, f32[128,4096]{1,0:T(8,128)} %weigh.3.oq.ok.ov.own_logit.own, bf16[128,4096]{1,0:T(8,128)(2,1)} %copy-done.1, bf16[8,3072]{1,0:T(8,128)(2,1)} %copy-done.18, f32[4,3072]{1,0:T(4,128)} %maximum_select_fusion.tq.tk.tv.t, ...), custom_call_target="tpu_custom_call" | custom-call | flops 1 | bytes 1 | tf_op jit(solution)/shard_map/values_back/pallas_call | solution.py:698
  236.0 5.2 %keys_back.1 = (bf16[144,1024]{1,0:T(8,128)(2,1)}, f32[4,1024]{1,0:T(4,128)}) custom-call(s32[1]{0:T(128)} %bitcast.12.spot, f32[128,4096]{1,0:T(8,128)} %weigh.3.oq.ok.ov.own_logit.own, bf16[128,4096]{1,0:T(8,128)(2,1)} %copy-done.1, bf16[8,3072]{1,0:T(8,128)(2,1)} %copy-done.18, f32[4,3072]{1,0:T(4,128)} %maximum_select_fusion.tq.tk.tv.t, ...), custom_call_target="tpu_custom_call" | custom-call | flops 1 | bytes 1 | tf_op jit(solution)/shard_map/keys_back/pallas_call | solution.py:698
  242.3 6.1 %products.4 = (bf16[8,32,5632]{2,1,0:T(8,128)(2,1)}, bf16[8,32,5632]{2,1,0:T(8,128)(2,1)}) custom-call(s32[1]{0:T(128)} %bitcast.3.spot, bf16[2944,128]{1,0:T(8,128)(2,1)} %get-tuple-element.276.refs_0_.refs_4_.refs_8_.refs_6_.refs_12_, bf16[6016,128]{1,0:T(8,128)(2,1)} %copy-done, bf16[128,5632]{1,0:T(8,128)(2,1)} %get-tuple-element.264.refs_2_, ...), custom_call_target="tpu_custom_call" | custom-call | flops 1 | bytes 1 | tf_op jit(solution)/shard_map/products/pallas_call | solution.py:837
  251.6 2.1 collective-permute-done.33.refs_4_.refs_10_.refs_16_.extra1
  253.7 1.9 collective-permute-done.34.refs_5_.refs_11_.refs_17_.extra2
  256.7 4.7 %halving.6 = (bf16[4,32,5632]{2,1,0:T(8,128)(2,1)}, bf16[4,32,5632]{2,1,0:T(8,128)(2,1)}) custom-call(s32[1]{0:T(128)} %bitcast.13.bit, bf16[8,32,5632]{2,1,0:T(8,128)(2,1)} %get-tuple-element.266.kept_mine.kept_other, bf16[8,32,5632]{2,1,0:T(8,128)(2,1)} %get-tuple-element.266.kept_mine.kept_other, ...), custom_call_target="tpu_custom_call" | custom-call | flops 1 | bytes 1 | tf_op jit(solution)/shard_map/halving/pallas_call | solution.py:930
  263.0 13.7 %collective-permute-done.35.refs_3_.refs_9_.refs_15_.peer = bf16[432,1024]{1,0:T(8,128)(2,1)S(1)} collective-permute-done((bf16[432,1024]{1,0:T(8,128)(2,1)S(1)}, bf16[432,1024]{1,0:T(8,128)(2,1)S(1)}, u32[]{:S(2)}, u32[]{:S(2)}) %collective-permute-start.35) | collective-permute-done | bytes 884768 | tf_op jit(solution)/shard_map/ppermute | solution.py:353
  277.7 4.2 %products.5 = (bf16[8,96,1024]{2,1,0:T(8,128)(2,1)}, bf16[8,48,1024]{2,1,0:T(8,128)(2,1)}, bf16[8,48,1024]{2,1,0:T(8,128)(2,1)}) custom-call(s32[1]{0:T(128)} %bitcast.3.spot, bf16[2944,128]{1,0:T(8,128)(2,1)} %get-tuple-element.276.refs_0_.refs_4_.refs_8_.refs_6_.refs_12_, bf16[6016,128]{1,0:T(8,128)(2,1)} %copy-done, bf16[432,1024]{1,0:T(8,128)(2,1)} %copy-done.2, ...), custom_call_target="tpu_custom_call" | custom-call | flops 1 | bytes 1 | tf_op jit(solution)/shard_map/products/pallas_call | solution.py:837
  281.9 1.8 collective-permute-start.37
  283.8 2.0 collective-permute-done.37.refs_0_.refs_1_
  287.8 4.0 %halving.7 = (bf16[4,96,1024]{2,1,0:T(8,128)(2,1)}, bf16[4,96,1024]{2,1,0:T(8,128)(2,1)}) custom-call(s32[1]{0:T(128)} %bitcast.13.bit, bf16[8,96,1024]{2,1,0:T(8,128)(2,1)} %get-tuple-element.280.kept_mine.kept_other, bf16[8,96,1024]{2,1,0:T(8,128)(2,1)} %get-tuple-element.280.kept_mine.kept_other, bf16[8,48,1024]{2,1,0:T(8,128)(2,1)} %copy-done.9, ...), custom_call_target="tpu_custom_call" | custom-call | flops 1 | bytes 1 | tf_op jit(solution)/shard_map/halving/pallas_call | solution.py:930
  291.9 2.2 collective-permute-start.41
  294.0 5.6 %lent_rows.1 = (f32[128,512]{1,0:T(8,128)}, bf16[128,512]{1,0:T(8,128)(2,1)}) custom-call(bf16[432,1024]{1,0:T(8,128)(2,1)} %copy-done.2, bf16[432,1024]{1,0:T(8,128)(2,1)} %copy-done.3, bf16[8,3072]{1,0:T(8,128)(2,1)} %copy-done.26, bf16[8,3072]{1,0:T(8,128)(2,1)} %copy-done.27, bf16[6016,128]{1,0:T(8,128)(2,1)} %get-tuple-element.242.refs_2_.refs_6_.refs_10_.logit1, ...), custom_call_target="tpu_custom_call" | custom-call | flops 1 | bytes 1 | tf_op jit(solution)/shard_map/lent_rows/pallas_call | solution.py:869
  301.2 2.7 halving.8
  303.9 2.7 collective-permute-start.44
  307.3 2.5 norm_back.1
  312.3 2.2 collective-permute-done.41.refs_0_.refs_1_
  315.3 2.3 halving.9
  317.5 5.3 %collective-permute-start.42 = (bf16[2,96,1024]{2,1,0:T(8,128)(2,1)}, bf16[2,96,1024]{2,1,0:T(8,128)(2,1)S(1)}, u32[]{:S(2)}, u32[]{:S(2)}) collective-permute-start(bf16[2,96,1024]{2,1,0:T(8,128)(2,1)} %get-tuple-element.303), channel_id=1, source_target_pairs={{0,8},{2,10},{4,12},{6,14},{8,0},{10,2},{12,4},{14,6},{16,24},{18,... | collective-permute-start | bytes 1179656 | tf_op jit(solution)/shard_map/ppermute | solution.py:353
  324.5 2.3 halving.10
  326.8 2.4 collective-permute-start.46
  329.8 3.5 all-to-all-start
  334.0 2.8 collective-permute-done.42.refs_0_.refs_1_
  337.5 2.0 halving.11
  340.3 11.4 %all-to-all-done = f32[16,1,480]{2,1,0:T(1,128)S(1)} async-done(((f32[16,1,480]{2,1,0:T(1,128)}), f32[16,1,480]{2,1,0:T(1,128)S(1)}, u32[]{:S(2)}, u32[]{:S(2)}) %all-to-all-start) | async-done | bytes 30752 | tf_op jit(solution)/shard_map/all_to_all | solution.py:1441
  353.0 2.0 collective-permute-done.45
  (215 shorter events, 68.4 us)
Async XLA Ops:
  7.2 316.5 %reduce-scatter.2.cloned.1.call-start = ((), (), s32[]{:S(2)}) async-start(), calls=%async_computation.2 | async-start | bytes 5292032 | tf_op jit(solution)/shard_map/reduce_scatter | solution.py:1378
  7.9 11.6 %copy-start.50 = (bf16[1,512]{1,0:T(2,128)(2,1)}, bf16[1,512]{1,0:T(2,128)(2,1)S(1)}, u32[]{:S(2)}) copy-start(bf16[1,512]{1,0:T(2,128)(2,1)S(1)} %stack.31.gain_ref) | copy-start | bytes 3076
  12.5 7.0 %collective-permute-start = (bf16[144,512]{1,0:T(8,128)(2,1)}, bf16[144,512]{1,0:T(8,128)(2,1)S(1)}, u32[]{:S(2)}, u32[]{:S(2)}) collective-permute-start(bf16[144,512]{1,0:T(8,128)(2,1)} %get-tuple-element.163), channel_id=1, source_target_pairs={{0,1},{1,0},{2,3},{3,2},{4,5},{5,4},{6,7},{7,6},{8,9},{9,8},{10,11... | collective-permute-start | bytes 442376 | tf_op jit(solution)/shard_map/ppermute | solution.py:353
  24.9 26.3 %collective-permute-start.1 = (bf16[128,4096]{1,0:T(8,128)(2,1)}, bf16[128,4096]{1,0:T(8,128)(2,1)S(1)}, u32[]{:S(2)}, u32[]{:S(2)}) collective-permute-start(bf16[128,4096]{1,0:T(8,128)(2,1)} %weigh.2), channel_id=1, source_target_pairs={{0,1},{1,0},{2,3},{3,2},{4,5},{5,4},{6,7},{7,6},{8,9},{9,8},{10,11... | collective-permute-start | bytes 3145736 | tf_op jit(solution)/shard_map/ppermute | solution.py:353
  29.9 47.3 %collective-permute-start.12 = (bf16[1920,256]{1,0:T(8,128)(2,1)}, bf16[1920,256]{1,0:T(8,128)(2,1)S(1)}, u32[]{:S(2)}, u32[]{:S(2)}) collective-permute-start(bf16[1920,256]{1,0:T(8,128)(2,1)} %pad_maximum_fusion), channel_id=1, source_target_pairs={{0,1},{1,0},{2,3},{3,2},{4,5},{5,4},{6,7},{7,6},{8,9},{9,8},{10,11... | collective-permute-start | bytes 2949128 | tf_op jit(solution)/shard_map/ppermute | solution.py:353
  51.2 47.2 %collective-permute-start.14 = (bf16[384,1408]{1,0:T(8,128)(2,1)S(1)}, bf16[384,1408]{1,0:T(8,128)(2,1)}, u32[]{:S(2)}, u32[]{:S(2)}) collective-permute-start(bf16[384,1408]{1,0:T(8,128)(2,1)S(1)} %constant_dynamic-slice_fusion.2), channel_id=1, source_target_pairs={{0,1},{1,0},{2,3},{3,2},{4,5},{5,4},{6,7},{7,6},{8,9},{9,8},{10,11... | collective-permute-start | bytes 3244040 | tf_op jit(solution)/shard_map/ppermute | solution.py:353
  53.9 2.2 collective-permute-start.2
  62.2 5.0 %collective-permute-start.3 = (bf16[4,144,128]{2,1,0:T(8,128)(2,1)}, bf16[4,144,128]{2,1,0:T(8,128)(2,1)S(1)}, u32[]{:S(2)}, u32[]{:S(2)}) collective-permute-start(bf16[4,144,128]{2,1,0:T(8,128)(2,1)} %get-tuple-element.180), channel_id=1, source_target_pairs={{0,2},{2,0},{4,6},{6,4},{8,10},{10,8},{12,14},{14,12},{16,18},{18,... | collective-permute-start | bytes 442376 | tf_op jit(solution)/shard_map/ppermute | solution.py:353
  64.7 7.2 %collective-permute-start.4 = (bf16[4,144,128]{2,1,0:T(8,128)(2,1)}, bf16[4,144,128]{2,1,0:T(8,128)(2,1)S(1)}, u32[]{:S(2)}, u32[]{:S(2)}) collective-permute-start(bf16[4,144,128]{2,1,0:T(8,128)(2,1)} %get-tuple-element.181), channel_id=1, source_target_pairs={{0,4},{2,6},{4,0},{6,2},{8,12},{10,14},{12,8},{14,10},{16,20},{18,... | collective-permute-start | bytes 442376 | tf_op jit(solution)/shard_map/ppermute | solution.py:353
  67.0 7.5 %collective-permute-start.5 = (bf16[4,144,128]{2,1,0:T(8,128)(2,1)}, bf16[4,144,128]{2,1,0:T(8,128)(2,1)S(1)}, u32[]{:S(2)}, u32[]{:S(2)}) collective-permute-start(bf16[4,144,128]{2,1,0:T(8,128)(2,1)} %get-tuple-element.182), channel_id=1, source_target_pairs={{0,6},{2,4},{4,2},{6,0},{8,14},{10,12},{12,10},{14,8},{16,22},{18,... | collective-permute-start | bytes 442376 | tf_op jit(solution)/shard_map/ppermute | solution.py:353
  67.1 7.5 %copy-start.31 = (bf16[4,144,128]{2,1,0:T(8,128)(2,1)}, bf16[4,144,128]{2,1,0:T(8,128)(2,1)S(1)}, u32[]{:S(2)}) copy-start(bf16[4,144,128]{2,1,0:T(8,128)(2,1)S(1)} %collective-permute-done.3.refs_1_.refs_5_) | copy-start | bytes 442372
  77.2 42.3 %copy-start.5 = (bf16[1920,256]{1,0:T(8,128)(2,1)}, bf16[1920,256]{1,0:T(8,128)(2,1)S(1)}, u32[]{:S(2)}) copy-start(bf16[1920,256]{1,0:T(8,128)(2,1)S(1)} %collective-permute-done.12.out_a.refs_13_) | copy-start | bytes 2949124
  77.2 31.0 %collective-permute-start.13 = (bf16[1920,256]{1,0:T(8,128)(2,1)S(1)}, bf16[1920,256]{1,0:T(8,128)(2,1)S(1)}, u32[]{:S(2)}, u32[]{:S(2)}) collective-permute-start(bf16[1920,256]{1,0:T(8,128)(2,1)S(1)} %collective-permute-done.12.out_a.refs_13_), channel_id=1, source_target_pairs={{0,4},{2,6},{4,0},{6,2},{8,12},{10,14},{12,8},{14,10},{16,20},{18,... | collective-permute-start | bytes 2949128 | tf_op jit(solution)/shard_map/ppermute | solution.py:353
  78.7 9.1 %collective-permute-start.6 = (bf16[4,144,128]{2,1,0:T(8,128)(2,1)}, bf16[4,144,128]{2,1,0:T(8,128)(2,1)S(1)}, u32[]{:S(2)}, u32[]{:S(2)}) collective-permute-start(bf16[4,144,128]{2,1,0:T(8,128)(2,1)} %group.2.refs_0_), channel_id=1, source_target_pairs={{0,8},{2,10},{4,12},{6,14},{8,0},{10,2},{12,4},{14,6},{16,24},{18,... | collective-permute-start | bytes 442376 | tf_op jit(solution)/shard_map/ppermute | solution.py:353
  80.3 14.2 %collective-permute-start.7 = (bf16[4,144,128]{2,1,0:T(8,128)(2,1)}, bf16[4,144,128]{2,1,0:T(8,128)(2,1)S(1)}, u32[]{:S(2)}, u32[]{:S(2)}) collective-permute-start(bf16[4,144,128]{2,1,0:T(8,128)(2,1)} %group.2.refs_0_), channel_id=1, source_target_pairs={{0,16},{2,18},{4,20},{6,22},{8,24},{10,26},{12,28},{14,30},{16,0},... | collective-permute-start | bytes 442376 | tf_op jit(solution)/shard_map/ppermute | solution.py:353
  82.9 11.6 %collective-permute-start.8 = (bf16[4,144,128]{2,1,0:T(8,128)(2,1)}, bf16[4,144,128]{2,1,0:T(8,128)(2,1)S(1)}, u32[]{:S(2)}, u32[]{:S(2)}) collective-permute-start(bf16[4,144,128]{2,1,0:T(8,128)(2,1)} %group.2.refs_0_), channel_id=1, source_target_pairs={{0,24},{2,26},{4,28},{6,30},{8,16},{10,18},{12,20},{14,22},{16,8},... | collective-permute-start | bytes 442376 | tf_op jit(solution)/shard_map/ppermute | solution.py:353
  87.8 6.7 %copy-start.44 = (bf16[4,144,128]{2,1,0:T(8,128)(2,1)}, bf16[4,144,128]{2,1,0:T(8,128)(2,1)S(1)}, u32[]{:S(2)}) copy-start(bf16[4,144,128]{2,1,0:T(8,128)(2,1)S(1)} %collective-permute-done.6.refs_1_) | copy-start | bytes 442372
  98.4 25.9 %collective-permute-start.18 = (bf16[384,1408]{1,0:T(8,128)(2,1)}, bf16[384,1408]{1,0:T(8,128)(2,1)S(1)}, u32[]{:S(2)}, u32[]{:S(2)}) collective-permute-start(bf16[384,1408]{1,0:T(8,128)(2,1)} %collective-permute-done.14.refs_4_), channel_id=1, source_target_pairs={{0,8},{2,10},{4,12},{6,14},{8,0},{10,2},{12,4},{14,6},{16,24},{18,... | collective-permute-start | bytes 3244040 | tf_op jit(solution)/shard_map/ppermute | solution.py:353
  100.8 5.7 %collective-permute-start.10 = (bf16[4,128,128]{2,1,0:T(8,128)(2,1)}, bf16[4,128,128]{2,1,0:T(8,128)(2,1)S(1)}, u32[]{:S(2)}, u32[]{:S(2)}) collective-permute-start(bf16[4,128,128]{2,1,0:T(8,128)(2,1)} %get-tuple-element.193), channel_id=1, source_target_pairs={{0,4},{2,6},{4,0},{6,2},{8,12},{10,14},{12,8},{14,10},{16,20},{18,... | collective-permute-start | bytes 393224 | tf_op jit(solution)/shard_map/ppermute | solution.py:353
  102.2 6.0 %collective-permute-start.11 = (bf16[4,128,128]{2,1,0:T(8,128)(2,1)}, bf16[4,128,128]{2,1,0:T(8,128)(2,1)S(1)}, u32[]{:S(2)}, u32[]{:S(2)}) collective-permute-start(bf16[4,128,128]{2,1,0:T(8,128)(2,1)} %get-tuple-element.194), channel_id=1, source_target_pairs={{0,6},{2,4},{4,2},{6,0},{8,14},{10,12},{12,10},{14,8},{16,22},{18,... | collective-permute-start | bytes 393224 | tf_op jit(solution)/shard_map/ppermute | solution.py:353
  102.2 6.0 %collective-permute-start.9 = (bf16[4,128,128]{2,1,0:T(8,128)(2,1)}, bf16[4,128,128]{2,1,0:T(8,128)(2,1)S(1)}, u32[]{:S(2)}, u32[]{:S(2)}) collective-permute-start(bf16[4,128,128]{2,1,0:T(8,128)(2,1)} %get-tuple-element.192), channel_id=1, source_target_pairs={{0,2},{2,0},{4,6},{6,4},{8,10},{10,8},{12,14},{14,12},{16,18},{18,... | collective-permute-start | bytes 393224 | tf_op jit(solution)/shard_map/ppermute | solution.py:353
  108.2 22.9 %copy-start.6 = (bf16[1920,256]{1,0:T(8,128)(2,1)}, bf16[1920,256]{1,0:T(8,128)(2,1)S(1)}, u32[]{:S(2)}) copy-start(bf16[1920,256]{1,0:T(8,128)(2,1)S(1)} %collective-permute-done.13.out_b.refs_14_) | copy-start | bytes 2949124
  108.2 19.5 %collective-permute-start.16 = (bf16[1920,256]{1,0:T(8,128)(2,1)S(1)}, bf16[1920,256]{1,0:T(8,128)(2,1)S(1)}, u32[]{:S(2)}, u32[]{:S(2)}) collective-permute-start(bf16[1920,256]{1,0:T(8,128)(2,1)S(1)} %collective-permute-done.12.out_a.refs_13_), channel_id=1, source_target_pairs={{0,2},{2,0},{4,6},{6,4},{8,10},{10,8},{12,14},{14,12},{16,18},{18,... | collective-permute-start | bytes 2949128 | tf_op jit(solution)/shard_map/ppermute | solution.py:353
  109.0 18.8 %collective-permute-start.17 = (bf16[1920,256]{1,0:T(8,128)(2,1)S(1)}, bf16[1920,256]{1,0:T(8,128)(2,1)S(1)}, u32[]{:S(2)}, u32[]{:S(2)}) collective-permute-start(bf16[1920,256]{1,0:T(8,128)(2,1)S(1)} %collective-permute-done.13.out_b.refs_14_), channel_id=1, source_target_pairs={{0,2},{2,0},{4,6},{6,4},{8,10},{10,8},{12,14},{14,12},{16,18},{18,... | collective-permute-start | bytes 2949128 | tf_op jit(solution)/shard_map/ppermute | solution.py:353
  109.0 18.7 %collective-permute-start.15 = (bf16[128,2816]{1,0:T(8,128)(2,1)}, bf16[128,2816]{1,0:T(8,128)(2,1)S(1)}, u32[]{:S(2)}, u32[]{:S(2)}) collective-permute-start(bf16[128,2816]{1,0:T(8,128)(2,1)} %constant_dynamic-slice_fusion.5), channel_id=1, source_target_pairs={{0,1},{1,0},{2,3},{3,2},{4,5},{5,4},{6,7},{7,6},{8,9},{9,8},{10,11... | collective-permute-start | bytes 2162696 | tf_op jit(solution)/shard_map/ppermute | solution.py:353
  119.5 8.3 %collective-permute-start.19 = (bf16[384,1408]{1,0:T(8,128)(2,1)}, bf16[384,1408]{1,0:T(8,128)(2,1)S(1)}, u32[]{:S(2)}, u32[]{:S(2)}) collective-permute-start(bf16[384,1408]{1,0:T(8,128)(2,1)} %collective-permute-done.14.refs_4_), channel_id=1, source_target_pairs={{0,2},{2,0},{4,6},{6,4},{8,10},{10,8},{12,14},{14,12},{16,18},{18,... | collective-permute-start | bytes 3244040 | tf_op jit(solution)/shard_map/ppermute | solution.py:353
  124.3 6.7 %copy-start.23 = (bf16[384,1408]{1,0:T(8,128)(2,1)}, bf16[384,1408]{1,0:T(8,128)(2,1)S(1)}, u32[]{:S(2)}) copy-start(bf16[384,1408]{1,0:T(8,128)(2,1)S(1)} %collective-permute-done.18.refs_5_) | copy-start | bytes 3244036
  124.3 5.7 %collective-permute-start.20 = (bf16[384,1408]{1,0:T(8,128)(2,1)S(1)}, bf16[384,1408]{1,0:T(8,128)(2,1)S(1)}, u32[]{:S(2)}, u32[]{:S(2)}) collective-permute-start(bf16[384,1408]{1,0:T(8,128)(2,1)S(1)} %collective-permute-done.18.refs_5_), channel_id=1, source_target_pairs={{0,2},{2,0},{4,6},{6,4},{8,10},{10,8},{12,14},{14,12},{16,18},{18,... | collective-permute-start | bytes 3244040 | tf_op jit(solution)/shard_map/ppermute | solution.py:353
  127.8 2.3 collective-permute-start.21
  156.1 39.2 %collective-permute-start.25 = (bf16[6016,128]{1,0:T(8,128)(2,1)}, bf16[6016,128]{1,0:T(8,128)(2,1)S(1)}, u32[]{:S(2)}, u32[]{:S(2)}) collective-permute-start(bf16[6016,128]{1,0:T(8,128)(2,1)} %get-tuple-element.242.refs_2_.refs_6_.refs_10_.logit1), channel_id=1, source_target_pairs={{0,1},{1,0},{2,3},{3,2},{4,5},{5,4},{6,7},{7,6},{8,9},{9,8},{10,11... | collective-permute-start | bytes 4620296 | tf_op jit(solution)/shard_map/ppermute | solution.py:353
  176.9 1.9 collective-permute-start.22
  177.0 6.9 %collective-permute-start.23 = (bf16[4,144,128]{2,1,0:T(8,128)(2,1)}, bf16[4,144,128]{2,1,0:T(8,128)(2,1)S(1)}, u32[]{:S(2)}, u32[]{:S(2)}) collective-permute-start(bf16[4,144,128]{2,1,0:T(8,128)(2,1)} %get-tuple-element.230), channel_id=1, source_target_pairs={{0,4},{2,6},{4,0},{6,2},{8,12},{10,14},{12,8},{14,10},{16,20},{18,... | collective-permute-start | bytes 442376 | tf_op jit(solution)/shard_map/ppermute | solution.py:353
  178.5 7.7 %collective-permute-start.24 = (bf16[4,144,128]{2,1,0:T(8,128)(2,1)}, bf16[4,144,128]{2,1,0:T(8,128)(2,1)S(1)}, u32[]{:S(2)}, u32[]{:S(2)}) collective-permute-start(bf16[4,144,128]{2,1,0:T(8,128)(2,1)} %get-tuple-element.231), channel_id=1, source_target_pairs={{0,6},{2,4},{4,2},{6,0},{8,14},{10,12},{12,10},{14,8},{16,22},{18,... | collective-permute-start | bytes 442376 | tf_op jit(solution)/shard_map/ppermute | solution.py:353
  188.8 6.5 %collective-permute-start.26 = (bf16[4,144,128]{2,1,0:T(8,128)(2,1)}, bf16[4,144,128]{2,1,0:T(8,128)(2,1)S(1)}, u32[]{:S(2)}, u32[]{:S(2)}) collective-permute-start(bf16[4,144,128]{2,1,0:T(8,128)(2,1)} %group.3.refs_0_), channel_id=1, source_target_pairs={{0,8},{2,10},{4,12},{6,14},{8,0},{10,2},{12,4},{14,6},{16,24},{18,... | collective-permute-start | bytes 442376 | tf_op jit(solution)/shard_map/ppermute | solution.py:353
  195.3 6.8 %copy-start.43 = (bf16[4,144,128]{2,1,0:T(8,128)(2,1)}, bf16[4,144,128]{2,1,0:T(8,128)(2,1)S(1)}, u32[]{:S(2)}) copy-start(bf16[4,144,128]{2,1,0:T(8,128)(2,1)S(1)} %collective-permute-done.26.refs_1_) | copy-start | bytes 442372
  203.4 37.7 %collective-permute-start.32 = (bf16[128,5632]{1,0:T(8,128)(2,1)S(1)}, bf16[128,5632]{1,0:T(8,128)(2,1)S(1)}, u32[]{:S(2)}, u32[]{:S(2)}) collective-permute-start(bf16[128,5632]{1,0:T(8,128)(2,1)S(1)} %copy-done.20), channel_id=1, source_target_pairs={{0,1},{1,0},{2,3},{3,2},{4,5},{5,4},{6,7},{7,6},{8,9},{9,8},{10,11... | collective-permute-start | bytes 4325384 | tf_op jit(solution)/shard_map/ppermute | solution.py:353
  205.0 13.0 %collective-permute-start.27 = (bf16[4,144,128]{2,1,0:T(8,128)(2,1)S(1)}, bf16[4,144,128]{2,1,0:T(8,128)(2,1)S(1)}, u32[]{:S(2)}, u32[]{:S(2)}) collective-permute-start(bf16[4,144,128]{2,1,0:T(8,128)(2,1)S(1)} %copy-done.34), channel_id=1, source_target_pairs={{0,16},{2,18},{4,20},{6,22},{8,24},{10,26},{12,28},{14,30},{16,0},... | collective-permute-start | bytes 442376 | tf_op jit(solution)/shard_map/ppermute | solution.py:353
  206.9 11.1 %collective-permute-start.28 = (bf16[4,144,128]{2,1,0:T(8,128)(2,1)S(1)}, bf16[4,144,128]{2,1,0:T(8,128)(2,1)S(1)}, u32[]{:S(2)}, u32[]{:S(2)}) collective-permute-start(bf16[4,144,128]{2,1,0:T(8,128)(2,1)S(1)} %copy-done.34), channel_id=1, source_target_pairs={{0,24},{2,26},{4,28},{6,30},{8,16},{10,18},{12,20},{14,22},{16,8},... | collective-permute-start | bytes 442376 | tf_op jit(solution)/shard_map/ppermute | solution.py:353
  222.0 1.9 collective-permute-start.29
  222.0 6.5 %collective-permute-start.30 = (bf16[4,128,128]{2,1,0:T(8,128)(2,1)}, bf16[4,128,128]{2,1,0:T(8,128)(2,1)S(1)}, u32[]{:S(2)}, u32[]{:S(2)}) collective-permute-start(bf16[4,128,128]{2,1,0:T(8,128)(2,1)} %get-tuple-element.252), channel_id=1, source_target_pairs={{0,4},{2,6},{4,0},{6,2},{8,12},{10,14},{12,8},{14,10},{16,20},{18,... | collective-permute-start | bytes 393224 | tf_op jit(solution)/shard_map/ppermute | solution.py:353
  222.9 7.6 %collective-permute-start.31 = (bf16[4,128,128]{2,1,0:T(8,128)(2,1)}, bf16[4,128,128]{2,1,0:T(8,128)(2,1)S(1)}, u32[]{:S(2)}, u32[]{:S(2)}) collective-permute-start(bf16[4,128,128]{2,1,0:T(8,128)(2,1)} %get-tuple-element.253), channel_id=1, source_target_pairs={{0,6},{2,4},{4,2},{6,0},{8,14},{10,12},{12,10},{14,8},{16,22},{18,... | collective-permute-start | bytes 393224 | tf_op jit(solution)/shard_map/ppermute | solution.py:353
  223.9 6.6 %copy-start.35 = (bf16[4,128,128]{2,1,0:T(8,128)(2,1)}, bf16[4,128,128]{2,1,0:T(8,128)(2,1)S(1)}, u32[]{:S(2)}) copy-start(bf16[4,128,128]{2,1,0:T(8,128)(2,1)S(1)} %collective-permute-done.29.r1) | copy-start | bytes 393220
  242.3 6.6 %copy-start.39 = (bf16[144,1024]{1,0:T(8,128)(2,1)S(1)}, bf16[144,1024]{1,0:T(8,128)(2,1)}, u32[]{:S(2)}) copy-start(bf16[144,1024]{1,0:T(8,128)(2,1)} %get-tuple-element.267) | copy-start | bytes 884740
  242.3 6.6 %copy-start.41 = (bf16[144,1024]{1,0:T(8,128)(2,1)S(1)}, bf16[144,1024]{1,0:T(8,128)(2,1)}, u32[]{:S(2)}) copy-start(bf16[144,1024]{1,0:T(8,128)(2,1)} %get-tuple-element.268) | copy-start | bytes 884740
  242.3 6.6 %copy-start.40 = (bf16[144,1024]{1,0:T(8,128)(2,1)S(1)}, bf16[144,1024]{1,0:T(8,128)(2,1)}, u32[]{:S(2)}) copy-start(bf16[144,1024]{1,0:T(8,128)(2,1)} %get-tuple-element.269) | copy-start | bytes 884740
  248.4 8.3 %collective-permute-start.36 = (bf16[8,32,5632]{2,1,0:T(8,128)(2,1)}, bf16[8,32,5632]{2,1,0:T(8,128)(2,1)}, u32[]{:S(2)}, u32[]{:S(2)}) collective-permute-start(bf16[8,32,5632]{2,1,0:T(8,128)(2,1)} %get-tuple-element.271), channel_id=1, source_target_pairs={{0,2},{2,0},{4,6},{6,4},{8,10},{10,8},{12,14},{14,12},{16,18},{18,... | collective-permute-start | bytes 8650760 | tf_op jit(solution)/shard_map/ppermute | solution.py:353
  248.9 4.8 %collective-permute-start.33 = (bf16[8,3072]{1,0:T(8,128)(2,1)S(1)}, bf16[8,3072]{1,0:T(8,128)(2,1)S(1)}, u32[]{:S(2)}, u32[]{:S(2)}) collective-permute-start(bf16[8,3072]{1,0:T(8,128)(2,1)S(1)} %pad_maximum_fusion.3), channel_id=1, source_target_pairs={{2,0},{4,2},{6,4},{8,6},{10,8},{12,10},{14,12},{16,14},{18,16},{20... | collective-permute-start | bytes 147464 | tf_op jit(solution)/shard_map/ppermute | solution.py:1150
  250.2 5.4 %collective-permute-start.34 = (bf16[8,3072]{1,0:T(8,128)(2,1)S(1)}, bf16[8,3072]{1,0:T(8,128)(2,1)S(1)}, u32[]{:S(2)}, u32[]{:S(2)}) collective-permute-start(bf16[8,3072]{1,0:T(8,128)(2,1)S(1)} %pad_maximum_fusion.3), channel_id=1, source_target_pairs={{2,1},{3,0},{4,3},{5,2},{6,5},{7,4},{8,7},{9,6},{10,9},{11,8},{12,... | collective-permute-start | bytes 147464 | tf_op jit(solution)/shard_map/ppermute | solution.py:1155
  251.6 9.8 %copy-start.2 = (bf16[432,1024]{1,0:T(8,128)(2,1)}, bf16[432,1024]{1,0:T(8,128)(2,1)S(1)}, u32[]{:S(2)}) copy-start(bf16[432,1024]{1,0:T(8,128)(2,1)S(1)} %pad_maximum_fusion.1.refs_2_.refs_8_.refs_14_.own) | copy-start | bytes 2654212
  253.7 7.7 %copy-start.26 = (bf16[8,3072]{1,0:T(8,128)(2,1)}, bf16[8,3072]{1,0:T(8,128)(2,1)S(1)}, u32[]{:S(2)}) copy-start(bf16[8,3072]{1,0:T(8,128)(2,1)S(1)} %collective-permute-done.33.refs_4_.refs_10_.refs_16_.extra1) | copy-start | bytes 147460
  255.7 21.0 %collective-permute-start.35 = (bf16[432,1024]{1,0:T(8,128)(2,1)S(1)}, bf16[432,1024]{1,0:T(8,128)(2,1)S(1)}, u32[]{:S(2)}, u32[]{:S(2)}) collective-permute-start(bf16[432,1024]{1,0:T(8,128)(2,1)S(1)} %pad_maximum_fusion.1.refs_2_.refs_8_.refs_14_.own), channel_id=1, source_target_pairs={{0,1},{1,0},{2,3},{3,2},{4,5},{5,4},{6,7},{7,6},{8,9},{9,8},{10,11... | collective-permute-start | bytes 2654216 | tf_op jit(solution)/shard_map/ppermute | solution.py:353
  261.4 38.6 %collective-permute-start.40 = (bf16[4,32,5632]{2,1,0:T(8,128)(2,1)}, bf16[4,32,5632]{2,1,0:T(8,128)(2,1)S(1)}, u32[]{:S(2)}, u32[]{:S(2)}) collective-permute-start(bf16[4,32,5632]{2,1,0:T(8,128)(2,1)} %get-tuple-element.275), channel_id=1, source_target_pairs={{0,4},{2,6},{4,0},{6,2},{8,12},{10,14},{12,8},{14,10},{16,20},{18,... | collective-permute-start | bytes 4325384 | tf_op jit(solution)/shard_map/ppermute | solution.py:353
  281.9 3.9 %collective-permute-start.37 = (bf16[8,48,1024]{2,1,0:T(8,128)(2,1)}, bf16[8,48,1024]{2,1,0:T(8,128)(2,1)S(1)}, u32[]{:S(2)}, u32[]{:S(2)}) collective-permute-start(bf16[8,48,1024]{2,1,0:T(8,128)(2,1)} %get-tuple-element.281), channel_id=1, source_target_pairs={{0,2},{2,0},{4,6},{6,4},{8,10},{10,8},{12,14},{14,12},{16,18},{18,... | collective-permute-start | bytes 2359304 | tf_op jit(solution)/shard_map/ppermute | solution.py:353
  283.7 3.2 collective-permute-start.38
  291.9 22.6 %collective-permute-start.41 = (bf16[4,96,1024]{2,1,0:T(8,128)(2,1)}, bf16[4,96,1024]{2,1,0:T(8,128)(2,1)S(1)}, u32[]{:S(2)}, u32[]{:S(2)}) collective-permute-start(bf16[4,96,1024]{2,1,0:T(8,128)(2,1)} %get-tuple-element.285), channel_id=1, source_target_pairs={{0,4},{2,6},{4,0},{6,2},{8,12},{10,14},{12,8},{14,10},{16,20},{18,... | collective-permute-start | bytes 2359304 | tf_op jit(solution)/shard_map/ppermute | solution.py:353
  299.7 7.0 %collective-permute-start.39 = (bf16[128,512]{1,0:T(8,128)(2,1)}, bf16[128,512]{1,0:T(8,128)(2,1)S(1)}, u32[]{:S(2)}, u32[]{:S(2)}) collective-permute-start(bf16[128,512]{1,0:T(8,128)(2,1)} %get-tuple-element.288), channel_id=1, source_target_pairs={{0,1},{1,0},{2,3},{3,2},{4,5},{5,4},{6,7},{7,6},{8,9},{9,8},{10,11... | collective-permute-start | bytes 393224 | tf_op jit(solution)/shard_map/ppermute | solution.py:353
  303.9 19.8 %collective-permute-start.44 = (bf16[2,32,5632]{2,1,0:T(8,128)(2,1)}, bf16[2,32,5632]{2,1,0:T(8,128)(2,1)S(1)}, u32[]{:S(2)}, u32[]{:S(2)}) collective-permute-start(bf16[2,32,5632]{2,1,0:T(8,128)(2,1)} %get-tuple-element.291), channel_id=1, source_target_pairs={{0,8},{2,10},{4,12},{6,14},{8,0},{10,2},{12,4},{14,6},{16,24},{18,... | collective-permute-start | bytes 2162696 | tf_op jit(solution)/shard_map/ppermute | solution.py:353
  317.5 19.2 %collective-permute-start.42 = (bf16[2,96,1024]{2,1,0:T(8,128)(2,1)}, bf16[2,96,1024]{2,1,0:T(8,128)(2,1)S(1)}, u32[]{:S(2)}, u32[]{:S(2)}) collective-permute-start(bf16[2,96,1024]{2,1,0:T(8,128)(2,1)} %get-tuple-element.303), channel_id=1, source_target_pairs={{0,8},{2,10},{4,12},{6,14},{8,0},{10,2},{12,4},{14,6},{16,24},{18,... | collective-permute-start | bytes 1179656 | tf_op jit(solution)/shard_map/ppermute | solution.py:353
  322.8 6.3 %collective-permute-start.43 = (f32[16,480]{1,0:T(8,128)S(1)}, f32[16,480]{1,0:T(8,128)S(1)}, u32[]{:S(2)}, u32[]{:S(2)}) collective-permute-start(f32[16,480]{1,0:T(8,128)S(1)} %bitcast.57), channel_id=1, source_target_pairs={{0,1},{1,0},{2,3},{3,2},{4,5},{5,4},{6,7},{7,6},{8,9},{9,8},{10,11... | collective-permute-start | bytes 92168 | tf_op jit(solution)/shard_map/ppermute | solution.py:353
  323.7 9.6 %copy-start.22 = (bf16[152,1024]{1,0:T(8,128)(2,1)S(1)}, bf16[152,1024]{1,0:T(8,128)(2,1)}, u32[]{:S(2)}) copy-start(bf16[152,1024]{1,0:T(8,128)(2,1)} %reduce-scatter.2.cloned.1.call-done) | copy-start | bytes 933892
  326.8 30.0 %collective-permute-start.46 = (bf16[1,32,5632]{2,1,0:T(8,128)(2,1)}, bf16[1,32,5632]{2,1,0:T(8,128)(2,1)S(1)}, u32[]{:S(2)}, u32[]{:S(2)}) collective-permute-start(bf16[1,32,5632]{2,1,0:T(8,128)(2,1)} %get-tuple-element.306), channel_id=1, source_target_pairs={{0,16},{2,18},{4,20},{6,22},{8,24},{10,26},{12,28},{14,30},{16,0},... | collective-permute-start | bytes 1081352 | tf_op jit(solution)/shard_map/ppermute | solution.py:353
  329.8 22.0 %all-to-all-start = ((f32[16,1,480]{2,1,0:T(1,128)}), f32[16,1,480]{2,1,0:T(1,128)S(1)}, u32[]{:S(2)}, u32[]{:S(2)}) async-start(f32[16,1,480]{2,1,0:T(1,128)} %all_to_all.8), calls=%async_computation.1 | async-start | bytes 65536 | tf_op jit(solution)/shard_map/all_to_all | solution.py:1441
  339.5 17.3 %copy-start.38 = (bf16[1,32,5632]{2,1,0:T(8,128)(2,1)S(1)}, bf16[1,32,5632]{2,1,0:T(8,128)(2,1)}, u32[]{:S(2)}) copy-start(bf16[1,32,5632]{2,1,0:T(8,128)(2,1)} %get-tuple-element.313) | copy-start | bytes 1081348
  340.3 14.7 %collective-permute-start.45 = (bf16[1,96,1024]{2,1,0:T(8,128)(2,1)}, bf16[1,96,1024]{2,1,0:T(8,128)(2,1)S(1)}, u32[]{:S(2)}, u32[]{:S(2)}) collective-permute-start(bf16[1,96,1024]{2,1,0:T(8,128)(2,1)} %get-tuple-element.311), channel_id=1, source_target_pairs={{0,16},{2,18},{4,20},{6,22},{8,24},{10,26},{12,28},{14,30},{16,0},... | collective-permute-start | bytes 589832 | tf_op jit(solution)/shard_map/ppermute | solution.py:353
  (36 other events, 63.1 us)
Sparse Core Ops, SparseCore 0:
  202.2 81.2 reduce-scatter.1

commit v6 on v5

--- a/solution.py
+++ b/solution.py
@@ -11,6 +11,7 @@
 FF = 2816
 KW = 4
 ITERS = 8
+AT_ONCE = 2
 HEAD_DIM = 128
 QUARTERS = 4
 SHARE = HEADS // QUARTERS
@@ -421,9 +422,7 @@
     x_out, p_out, m_out, score_out, scal_out,
     left, wide, decay, pair, x_s, r_s, p_s,
 ):
-    i = pl.program_id(0)
-
-    @pl.when(i == 0)
+    @pl.when(pl.program_id(0) == 0)
     def _():
         prepare(k_ref, c_ref, (s0, s1, s2, s3), place[0], left, wide, decay, pair)
         for h in range(HEADS):
@@ -433,25 +432,27 @@
             p_s[h] = q
             scal_out[h, 0:1] = jnp.sum(q * q, axis=0, keepdims=True)
 
-    products = key_products(lambda h: p_s[h].astype(bf16), wide, pair)
-    for h in range(HEADS):
-        p = p_s[h]
-        scores = (products[h] * mask[h]).astype(bf16)
-        score_out[0, h] = scores
-        stacked = jnp.concatenate([(decay[h, 0:1] * p).astype(bf16), scores], axis=0)
-        image = nn(left[h], stacked) + ridge[h] * p
-        norm = scal_out[h, pl.ds(i, 1)]
-        dot = jnp.sum(p * image, axis=0, keepdims=True)
-        size = norm / dot
-        p_out[0, h] = p
-        m_out[0, h] = image
-        scal_out[h, pl.ds(2 * ITERS + i, 1)] = dot
-        x_s[h] = x_s[h] + size * p
-        r = r_s[h] - size * image
-        r_s[h] = r
-        norm_next = jnp.sum(r * r, axis=0, keepdims=True)
-        scal_out[h, pl.ds(i + 1, 1)] = norm_next
-        p_s[h] = r + (norm_next / norm) * p
+    for t in range(AT_ONCE):
+        i = pl.program_id(0) * AT_ONCE + t
+        products = key_products(lambda h: p_s[h].astype(bf16), wide, pair)
+        for h in range(HEADS):
+            p = p_s[h]
+            scores = (products[h] * mask[h]).astype(bf16)
+            score_out[t, h] = scores
+            stacked = jnp.concatenate([(decay[h, 0:1] * p).astype(bf16), scores], axis=0)
+            image = nn(left[h], stacked) + ridge[h] * p
+            norm = scal_out[h, pl.ds(i, 1)]
+            dot = jnp.sum(p * image, axis=0, keepdims=True)
+            size = norm / dot
+            p_out[t, h] = p
+            m_out[t, h] = image
+            scal_out[h, pl.ds(2 * ITERS + i, 1)] = dot
+            x_s[h] = x_s[h] + size * p
+            r = r_s[h] - size * image
+            r_s[h] = r
+            norm_next = jnp.sum(r * r, axis=0, keepdims=True)
+            scal_out[h, pl.ds(i + 1, 1)] = norm_next
+            p_s[h] = r + (norm_next / norm) * p
 
     @pl.when(i == ITERS - 1)
     def _():
@@ -472,11 +473,11 @@
 
 def solve(place, q, k, states, c, mask, ridge):
     tokens = q.shape[2]
-    step = pl.BlockSpec((1, HEADS, HEAD_DIM, tokens), lambda i: (i, 0, 0, 0))
+    step = pl.BlockSpec((AT_ONCE, HEADS, HEAD_DIM, tokens), lambda i: (i, 0, 0, 0))
     steps = (ITERS, HEADS, HEAD_DIM, tokens)
     return pl.pallas_call(
         solve_kernel,
-        grid=(ITERS,),
+        grid=(ITERS // AT_ONCE,),
         in_specs=[smem(), whole(HEADS, HEAD_DIM, tokens), whole(HEADS, tokens, HEAD_DIM)] + [whole(*PAIR)] * FOUR
         + [whole(HEADS, tokens), whole(HEADS, tokens, tokens), whole(HEADS, HEAD_DIM, tokens)],
         out_specs=[whole(HEADS, HEAD_DIM, tokens), step, step, step, whole(HEADS, 3 * ITERS, tokens)],
@@ -536,9 +537,7 @@
     left, wide, decay, pair, gr_s, gp_s, acc_s, next_s, gnorm_s, low_s, steps_p, steps_g, steps_s, stack,
 ):
     s = pl.program_id(0)
-    i = ITERS - 1 - s
     tokens = k_ref.shape[1]
-    at = pl.ds(pl.multiple_of(i * tokens, tokens), tokens)
 
     @pl.when(s == 0)
     def _():
@@ -549,39 +548,42 @@
         next_s[...] = jnp.zeros_like(next_s)
         gnorm_s[...] = jnp.zeros_like(gnorm_s)
 
-    for h in range(HEADS):
-        p, m, gx = p_ref[0, h], m_ref[0, h], gx_ref[h]
-        norm = scal_ref[h, pl.ds(i, 1)]
-        dot = scal_ref[h, pl.ds(2 * ITERS + i, 1)]
-        size = norm / dot
-        ratio = jnp.where(s == 0, 0.0, scal_ref[h, pl.ds(i + 1, 1)] / norm)
-        gp = gp_s[h]
-        gratio = jnp.sum(gp * p, axis=0, keepdims=True)
-        gnext = gnorm_s[h, 0:1] + gratio / norm
-        gr = gr_s[h] + gp + (2.0 * gnext) * (next_s[h] - ratio * p)
-        gsize = jnp.sum(gx * p - gr * m, axis=0, keepdims=True)
-        gdot = -gsize * size / dot
-        gm = gdot * p - size * gr
-        gr_s[h] = gr
-        gp_s[h] = ratio * gp + size * gx + gdot * m + ridge[h] * gm
-        acc_s[h] = acc_s[h] + gm * p
-        next_s[h] = p
-        gnorm_s[h, 0:1] = gsize / dot - gratio * ratio / norm
-        low = gm.astype(bf16)
-        low_s[h] = low
-        egm = (decay[h, 0:1] * gm).astype(bf16)
-        steps_g[h, :, at] = low
-        steps_p[h, :, at] = p.astype(bf16)
-        steps_s[h, :, at] = score_ref[0, h]
-        stack[h, HEAD_DIM:, at] = egm
-    products = key_products(lambda h: low_s[h], wide, pair)
-    for h in range(HEADS):
-        dscores = (products[h] * mask[h]).astype(bf16)
-        stack[h, :HEAD_DIM, at] = dscores
-        stacked = jnp.concatenate([stack[h, HEAD_DIM:, at], dscores], axis=0)
-        gp_s[h] = gp_s[h] + nn(left[h], stacked)
-
-    @pl.when(s == ITERS - 1)
+    for t in reversed(range(AT_ONCE)):
+        i = ITERS - AT_ONCE * (s + 1) + t
+        at = pl.ds(pl.multiple_of(i * tokens, tokens), tokens)
+        for h in range(HEADS):
+            p, m, gx = p_ref[t, h], m_ref[t, h], gx_ref[h]
+            norm = scal_ref[h, pl.ds(i, 1)]
+            dot = scal_ref[h, pl.ds(2 * ITERS + i, 1)]
+            size = norm / dot
+            ratio = jnp.where(i == ITERS - 1, 0.0, scal_ref[h, pl.ds(i + 1, 1)] / norm)
+            gp = gp_s[h]
+            gratio = jnp.sum(gp * p, axis=0, keepdims=True)
+            gnext = gnorm_s[h, 0:1] + gratio / norm
+            gr = gr_s[h] + gp + (2.0 * gnext) * (next_s[h] - ratio * p)
+            gsize = jnp.sum(gx * p - gr * m, axis=0, keepdims=True)
+            gdot = -gsize * size / dot
+            gm = gdot * p - size * gr
+            gr_s[h] = gr
+            gp_s[h] = ratio * gp + size * gx + gdot * m + ridge[h] * gm
+            acc_s[h] = acc_s[h] + gm * p
+            next_s[h] = p
+            gnorm_s[h, 0:1] = gsize / dot - gratio * ratio / norm
+            low = gm.astype(bf16)
+            low_s[h] = low
+            egm = (decay[h, 0:1] * gm).astype(bf16)
+            steps_g[h, :, at] = low
+            steps_p[h, :, at] = p.astype(bf16)
+            steps_s[h, :, at] = score_ref[t, h]
+            stack[h, HEAD_DIM:, at] = egm
+        products = key_products(lambda h: low_s[h], wide, pair)
+        for h in range(HEADS):
+            dscores = (products[h] * mask[h]).astype(bf16)
+            stack[h, :HEAD_DIM, at] = dscores
+            stacked = jnp.concatenate([stack[h, HEAD_DIM:, at], dscores], axis=0)
+            gp_s[h] = gp_s[h] + nn(left[h], stacked)
+
+    @pl.when(s == ITERS // AT_ONCE - 1)
     def _():
         for h in range(HEADS):
             dq_ref[h] = gr_s[h] + gp_s[h] + 2.0 * gnorm_s[h, 0:1] * p_ref[0, h]
@@ -601,12 +603,12 @@
 
 def adjoint(spot, place, gx, k, states, c, mask, ridge, p_all, m_all, scores, scal, value_states):
     tokens = k.shape[1]
-    step = pl.BlockSpec((1, HEADS, HEAD_DIM, tokens), lambda s: (ITERS - 1 - s, 0, 0, 0))
+    step = pl.BlockSpec((AT_ONCE, HEADS, HEAD_DIM, tokens), lambda s: (ITERS // AT_ONCE - 1 - s, 0, 0, 0))
     square = pltpu.VMEM((HEADS, HEAD_DIM, tokens), f32)
     line = pltpu.VMEM((HEADS, HEAD_DIM, ITERS * tokens), bf16)
     return pl.pallas_call(
         adjoint_kernel,
-        grid=(ITERS,),
+        grid=(ITERS // AT_ONCE,),
         in_specs=[smem(), smem(), whole(HEADS, HEAD_DIM, tokens), whole(HEADS, tokens, HEAD_DIM)] + [whole(*PAIR)] * FOUR
         + [whole(HEADS, tokens), whole(HEADS, tokens, tokens), whole(HEADS, HEAD_DIM, tokens), step, step, step, whole(HEADS, 3 * ITERS, tokens), whole(HEADS, HEAD_DIM, HEAD_DIM)],
         out_specs=[whole(HEADS, HEAD_DIM, tokens), whole(HEADS, tokens, HEAD_DIM), whole(HEADS, 1, HEAD_DIM)]
@@ -725,6 +727,31 @@
         keys_back_kernel, "keys_back", 1, 1, projected, taps, (spot,), (dk1, dk2, k, v, *states, ending),
         [square] * 4 + [whole(*PAIR)] * FOUR + [square],
     )
+
+
+def keys_values_back_kernel(
+    spot, ok, lk, hk, tk, ov, lv, hv, tv, dk1, dk2, dv_ref, k_ref, v_ref, r0, r1, r2, r3, ending_ref, gk, dtk, gv, dtv
+):
+    values_back_kernel(spot, ov, lv, hv, tv, dv_ref, k_ref, r0, r1, r2, r3, ending_ref, gv, dtv)
+    keys_back_kernel(spot, ok, lk, hk, tk, dk1, dk2, k_ref, v_ref, r0, r1, r2, r3, ending_ref, gk, dtk)
+
+
+def keys_values_back(spot, projected, taps, dk1, dk2, dv, k, v, states, ending):
+    own, lent, halo = projected
+    tokens = own.shape[0]
+    square = per_quarter(HEAD_DIM, HEAD_DIM)
+    out = [quarter_columns(tokens + HALO, 0), quarter_columns(KW, 0)]
+    return pl.pallas_call(
+        keys_values_back_kernel,
+        grid=(QUARTERS,),
+        in_specs=[smem()]
+        + [quarter_columns(rows, third) for third in (1, 2) for rows in (tokens, tokens, halo.shape[0], KW)]
+        + [square] * 5 + [whole(*PAIR)] * FOUR + [square],
+        out_specs=out * 2,
+        out_shape=[like((tokens + HALO, D), bf16), like((KW, D))] * 2,
+        cost_estimate=pl.CostEstimate(flops=1, bytes_accessed=1, transcendentals=0),
+        name="keys_values_back",
+    )(spot, own, lent, halo, taps, own, lent, halo, taps, dk1, dk2, dv, k, v, *states, ending)
 
 
 def completed(ref, extra):
@@ -1231,7 +1258,7 @@
     )
 
 
-UP_ROWS = 384
+UP_ROWS = 400
 
 
 def local(
@@ -1380,13 +1407,8 @@
     states_back = back.spread()
     seq.mark(back.parts[0])
     dv, *states_back = seq.gate(dv, *states_back)
-    low_v, taps_v = values_back(
-        spot_back, projected, taps, dv, keys_low, states_back, ending
-    )
-    seq.mark(low_v)
-    (dk_attend,) = seq.gate(dk_attend)
-    low_k, taps_k = keys_back(
-        spot_back, projected, taps, dk_attend, dk_solve, keys_low, values_low, states_back, ending
+    low_k, taps_k, low_v, taps_v = keys_values_back(
+        spot_back, projected, taps, dk_attend, dk_solve, dv, keys_low, values_low, states_back, ending
     )
     seq.mark(low_k)
     (up_peer,) = seq.gate(both_up[1])

time: 367 us -> 364 us (level)
  starting transfers between devices: 59.3 us -> 66.1 us
  Pallas kernels: 142 us -> 137 us
  waiting for transfers between devices: 108 us -> 103 us
    pallas_call x3 -> x1, Pallas kernels: 14.5 us -> 4.41 us  [third_back(): pl.pallas_call(kernel, grid=(QUARTERS,), in_specs=[smem()] * len(before)...]
    ppermute x44, starting transfers between devices: 51.8 us -> 57.8 us  [partner(): return lax.ppermute(x, axis, neighbour(axis, bit))]
    pallas_call x2 -> x3, Pallas kernels: 25.3 us -> 30.6 us  [the longest x1 15.5 us: adjoint(): pl.pallas_call(adjoint_kernel, grid=(ITERS // AT_ONCE,), in_specs=[smem()...]
    ppermute x44, waiting for transfers between devices: 91.4 us -> 87 us  [partner(): return lax.ppermute(x, axis, neighbour(axis, bit))]
  transfers between devices with their start and end apart: 49 -> 49, of which waited for: 28 -> 27; matrix products, arithmetic and copies ran while one was open for 5% -> 5% of each run, Pallas kernels for 29% -> 28%
where the time goes in v6:
time: 364 us; the launch traced here: 362 us
  Pallas kernels  137 us (38%)
  waiting for transfers between devices  103 us (28%)
  starting transfers between devices  66.1 us (18%)
  local copies, waits for them, and re-layouts  31.9 us (9%)
  between operations  14.5 us (4%)
  other arithmetic  9.22 us (3%)
    ppermute x44, waiting for transfers between devices, partner(): return lax.ppermute(x, axis, neighbour(axis, bit))  87 us
    ppermute x44, starting transfers between devices, partner(): return lax.ppermute(x, axis, neighbour(axis, bit))  57.8 us
    pallas_call x1, Pallas kernels, middle(): pl.pallas_call(functools.partial(middle_kernel, owners), grid_spec=pltpu....  24.8 us
    pallas_call x6, Pallas kernels, halving_step(): pl.pallas_call(step_kernel, grid_spec=pltpu.PrefetchScalarGridSpec(num_sc...  18.2 us
    unnamed x106, local copies, waits for them, and re-layouts  16.9 us
    pallas_call x3, Pallas kernels, products(): pl.pallas_call(functools.partial(products_kernel, plan, joined, cuts), gr...  15.7 us
    pallas_call x1, Pallas kernels, adjoint(): pl.pallas_call(adjoint_kernel, grid=(ITERS // AT_ONCE,), in_specs=[smem()...  15.5 us
    all_to_all x1, waiting for transfers between devices, local(): vector = lax.all_to_all(vector, 'ctx', 0, 0, tiled=True)  11.1 us
  transfers between devices with their start and end apart: 49, of which 27 were waited for; matrix products, arithmetic and copies ran while one was open for 5% of the time, Pallas kernels for 28%

profile of v6, /device:TPU:0, one launch (start us, length us, event | category | flops | bytes accessed | tf_op | source)
XLA Modules:
  0.0 362.2 jit_solution(17362787059005155203)
XLA Ops:
  10.6 1.9 norm.1
  12.5 3.0 collective-permute-start
  20.2 4.8 %weigh.2 = bf16[128,4096]{1,0:T(8,128)(2,1)} custom-call(bf16[144,512]{1,0:T(8,128)(2,1)} %copy-done.39, bf16[1,512]{1,0:T(2,128)(2,1)} %copy-done.50, bf16[512,3072]{1,0:T(8,128)(2,1)} %qkv_ref.5, bf16[512,1024]{1,0:T(8,128)(2,1)} %gate_ref.5), custom_call_target="tpu_custom_call" | custom-call | flops 1 | bytes 1 | tf_op jit(solution)/shard_map/weigh/pallas_call | solution.py:109
  24.9 1.7 collective-permute-start.1
  29.3 2.4 constant_dynamic-slice_fusion.2
  33.0 1.9 constant_dynamic-slice_fusion.5
  35.6 5.0 %weigh.3.oq.ok.ov.own_logit.own = f32[128,4096]{1,0:T(8,128)} custom-call(bf16[128,512]{1,0:T(8,128)(2,1)} %get-tuple-element.169.left_ref, bf16[1,512]{1,0:T(2,128)(2,1)} %copy-done.50, bf16[512,3072]{1,0:T(8,128)(2,1)} %qkv_ref.5, bf16[512,1024]{1,0:T(8,128)(2,1)} %gate_ref.5), custom_call_target="tpu_custom_call" | custom-call | flops 1 | bytes 1 | tf_op jit(solution)/shard_map/weigh/pallas_call | solution.py:109
  40.6 4.2 %tables.1 = (f32[8,128,128]{2,1,0:T(8,128)}, f32[8,128,128]{2,1,0:T(8,128)}, f32[8,128,128]{2,1,0:T(8,128)}) custom-call(f32[8,128]{1,0:T(8,128)} %reduce_window_sum.11.c_ref, f32[8,128]{1,0:T(8,128)} %get-tuple-element.171.b_ref, f32[8,128]{1,0:T(8,128)} %bitcast.58), custom_call_target="tpu_custom_call" | custom-call | flops 1 | bytes 1 | tf_op jit(solution)/shard_map/tables/pallas_call | solution.py:137
  44.8 6.4 %collective-permute-done.1.lq.lk.lv.lent_logit.lent = bf16[128,4096]{1,0:T(8,128)(2,1)S(1)} collective-permute-done((bf16[128,4096]{1,0:T(8,128)(2,1)}, bf16[128,4096]{1,0:T(8,128)(2,1)S(1)}, u32[]{:S(2)}, u32[]{:S(2)}) %collective-permute-start.1) | collective-permute-done | bytes 1048608 | tf_op jit(solution)/shard_map/ppermute | solution.py:354
  51.3 1.7 collective-permute-start.14
  56.7 5.5 %features.1 = (f32[8,128,128]{2,1,0:T(8,128)}, bf16[8,128,128]{2,1,0:T(8,128)(2,1)}, bf16[8,128,128]{2,1,0:T(8,128)(2,1)}, bf16[4,144,128]{2,1,0:T(8,128)(2,1)},...) custom-call(s32[1]{0:T(128)} %bitcast.3.spot, ...), custom_call_target="tpu_custom_call" | custom-call | flops 1 | bytes 1 | tf_op jit(solution)/shard_map/features/pallas_call | solution.py:247
  62.2 2.6 collective-permute-start.3
  64.8 2.3 collective-permute-start.4
  67.2 4.8 %collective-permute-done.4.refs_2_.refs_6_ = bf16[4,144,128]{2,1,0:T(8,128)(2,1)S(1)} collective-permute-done((bf16[4,144,128]{2,1,0:T(8,128)(2,1)}, bf16[4,144,128]{2,1,0:T(8,128)(2,1)S(1)}, u32[]{:S(2)}, u32[]{:S(2)}) %collective-permute-start.4) | collective-permute-done | bytes 147488 | tf_op jit(solution)/shard_map/ppermute | solution.py:354
  72.0 2.6 collective-permute-done.5.refs_3_.refs_7_
  75.3 1.9 group.2.refs_0_
  80.3 2.6 collective-permute-start.7
  83.2 4.7 %collective-permute-done.6.refs_1_ = bf16[4,144,128]{2,1,0:T(8,128)(2,1)S(1)} collective-permute-done((bf16[4,144,128]{2,1,0:T(8,128)(2,1)}, bf16[4,144,128]{2,1,0:T(8,128)(2,1)S(1)}, u32[]{:S(2)}, u32[]{:S(2)}) %collective-permute-start.6) | collective-permute-done | bytes 147488 | tf_op jit(solution)/shard_map/ppermute | solution.py:354
  87.9 6.6 %collective-permute-done.7.refs_2_ = bf16[4,144,128]{2,1,0:T(8,128)(2,1)S(1)} collective-permute-done((bf16[4,144,128]{2,1,0:T(8,128)(2,1)}, bf16[4,144,128]{2,1,0:T(8,128)(2,1)S(1)}, u32[]{:S(2)}, u32[]{:S(2)}) %collective-permute-start.7) | collective-permute-done | bytes 147488 | tf_op jit(solution)/shard_map/ppermute | solution.py:354
  95.8 2.6 spread.2
  98.5 2.3 collective-permute-start.18
  102.9 3.6 collective-permute-done.10.s2
  106.5 1.7 collective-permute-done.11.s3
  109.6 9.0 %solve.1 = (bf16[8,128,128]{2,1,0:T(8,128)(2,1)}, f32[8,8,128,128]{3,2,1,0:T(8,128)}, f32[8,8,128,128]{3,2,1,0:T(8,128)}, bf16[8,8,128,128]{3,2,1,0:T(8,128)(2,1)}, f32[8,24,128]{2,1,0:T(8,128)}) custom-call(s32[1]{0:T(128)} %bitcast.1.place, f32[8,128,128]{2,1,0:T(8,128)} %get-tuple-element.199.q_ref, bf16[8,128,128]{2,1,0:T(8,128)(2,1)} %get-tuple-element.200.k_ref, ...), custom_call_target="tpu_custom_call" | custom-call | flops 1 | bytes 1 | tf_op jit(solution)/shard_map/solve/pallas_call | solution.py:478
  118.8 6.5 %collective-permute-done.18.refs_5_ = bf16[400,1408]{1,0:T(8,128)(2,1)S(1)} collective-permute-done((bf16[400,1408]{1,0:T(8,128)(2,1)}, bf16[400,1408]{1,0:T(8,128)(2,1)S(1)}, u32[]{:S(2)}, u32[]{:S(2)}) %collective-permute-start.18) | collective-permute-done | bytes 1126432 | tf_op jit(solution)/shard_map/ppermute | solution.py:354
  126.0 3.1 collective-permute-done.21.refs_10_.refs_11_
  130.2 24.8 %middle.1 = (f32[128,1024]{1,0:T(8,128)}, f32[128,1024]{1,0:T(8,128)}, f32[128,1024]{1,0:T(8,128)}, bf16[2944,128]{1,0:T(8,128)(2,1)}, bf16[6016,128]{1,0:T(8,12...) custom-call(s32[3]{0:T(128)} %pad_add_fusion.place, bf16[8,128,128]{2,1,0:T(8,128)(2,1)} %get-tuple-element.203.x_ref, ...), custom_call_target="tpu_custom_call" | custom-call | flops 1 | bytes 1 | tf_op jit(solution)/shard_map/middle/pallas_call | solution.py:1131
  155.7 5.0 %attend_back.1 = (f32[8,128,128]{2,1,0:T(8,128)}, f32[8,128,128]{2,1,0:T(8,128)}, f32[8,128,128]{2,1,0:T(8,128)}, bf16[8,128,128]{2,1,0:T(8,128)(2,1)}) custom-call(s32[1]{0:T(128)} %bitcast.1.place, f32[128,1024]{1,0:T(8,128)} %get-tuple-element.219.ga_ref, bf16[8,128,128]{2,1,0:T(8,128)(2,1)} %get-tuple-element.200.k_ref, ...), custom_call_target="tpu_custom_call" | custom-call | flops 1 | bytes 1 | tf_op jit(solution)/shard_map/attend_back/pallas_call | solution.py:522
  160.7 15.5 %adjoint.1 = (f32[8,128,128]{2,1,0:T(8,128)}, f32[8,128,128]{2,1,0:T(8,128)}, f32[8,1,128]{2,1,0:T(1,128)}, bf16[4,144,128]{2,1,0:T(8,128)(2,1)}, bf16[4,144,128...) custom-call(s32[1]{0:T(128)} %bitcast.12.spot, s32[1]{0:T(128)} %bitcast.1.place, ...), custom_call_target="tpu_custom_call" | custom-call | flops 1 | bytes 1 | tf_op jit(solution)/shard_map/adjoint/pallas_call | solution.py:609
  178.1 4.4 %queries_back.1 = (bf16[144,1024]{1,0:T(8,128)(2,1)}, f32[4,1024]{1,0:T(4,128)}) custom-call(f32[128,4096]{1,0:T(8,128)} %weigh.3.oq.ok.ov.own_logit.own, bf16[128,4096]{1,0:T(8,128)(2,1)} %copy-done.1, bf16[8,3072]{1,0:T(8,128)(2,1)} %copy-done.18, f32[4,3072]{1,0:T(4,128)} %maximum_select_fusion.tq.tk.tv.t, f32[8,128,128]{2,1,0:T(8,128)} %get-tuple-element.231.dq_ref), custom_call_target="tpu_custom_call" | custom-call | flops 1 | bytes 1 | tf_op jit(solution)/shard_map/queries_back/pallas_call | solution.py:700
  183.1 2.3 collective-permute-done.24.refs_3_.refs_7_
  186.0 1.9 group.3.refs_0_
  188.0 1.7 collective-permute-start.26
  189.7 4.8 %collective-permute-done.26.refs_1_ = bf16[4,144,128]{2,1,0:T(8,128)(2,1)S(1)} collective-permute-done((bf16[4,144,128]{2,1,0:T(8,128)(2,1)}, bf16[4,144,128]{2,1,0:T(8,128)(2,1)S(1)}, u32[]{:S(2)}, u32[]{:S(2)}) %collective-permute-start.26) | collective-permute-done | bytes 147488 | tf_op jit(solution)/shard_map/ppermute | solution.py:354
  195.7 5.6 %products.3 = bf16[16,152,1024]{2,1,0:T(8,128)(2,1)} custom-call(s32[1]{0:T(128)} %bitcast.3.spot, bf16[2944,128]{1,0:T(8,128)(2,1)} %get-tuple-element.274.refs_0_.refs_4_.refs_8_.refs_6_.refs_12_, bf16[6016,128]{1,0:T(8,128)(2,1)} %copy-done, bf16[6016,128]{1,0:T(8,128)(2,1)} %get-tuple-element.242.refs_2_.refs_6_.refs_10_.logit1, ...), custom_call_target="tpu_custom_call" | custom-call | flops 1 | bytes 1 | tf_op jit(solution)/shard_map/products/pallas_call | solution.py:864
  204.0 2.7 collective-permute-start.27
  208.2 9.7 %collective-permute-done.27.refs_2_ = bf16[4,144,128]{2,1,0:T(8,128)(2,1)S(1)} collective-permute-done((bf16[4,144,128]{2,1,0:T(8,128)(2,1)S(1)}, bf16[4,144,128]{2,1,0:T(8,128)(2,1)S(1)}, u32[]{:S(2)}, u32[]{:S(2)}) %collective-permute-start.27) | collective-permute-done | bytes 147488 | tf_op jit(solution)/shard_map/ppermute | solution.py:354
  219.2 2.7 spread.3
  223.8 4.7 %collective-permute-done.30.r2 = bf16[4,128,128]{2,1,0:T(8,128)(2,1)S(1)} collective-permute-done((bf16[4,128,128]{2,1,0:T(8,128)(2,1)}, bf16[4,128,128]{2,1,0:T(8,128)(2,1)S(1)}, u32[]{:S(2)}, u32[]{:S(2)}) %collective-permute-start.30) | collective-permute-done | bytes 131104 | tf_op jit(solution)/shard_map/ppermute | solution.py:354
  228.5 1.9 collective-permute-done.31.r3
  231.1 6.2 %keys_values_back.1 = (bf16[144,1024]{1,0:T(8,128)(2,1)}, f32[4,1024]{1,0:T(4,128)}, bf16[144,1024]{1,0:T(8,128)(2,1)}, f32[4,1024]{1,0:T(4,128)}) custom-call(s32[1]{0:T(128)} %bitcast.12.spot, f32[128,4096]{1,0:T(8,128)} %weigh.3.oq.ok.ov.own_logit.own, bf16[128,4096]{1,0:T(8,128)(2,1)} %copy-done.1, bf16[8,3072]{1,0:T(8,128)(2,1)} %copy-done.18, ...), custom_call_target="tpu_custom_call" | custom-call | flops 1 | bytes 1 | tf_op jit(solution)/shard_map/keys_values_back/pallas_call | solution.py:744
  238.4 6.0 %products.4 = (bf16[8,32,5632]{2,1,0:T(8,128)(2,1)}, bf16[8,32,5632]{2,1,0:T(8,128)(2,1)}) custom-call(s32[1]{0:T(128)} %bitcast.3.spot, bf16[2944,128]{1,0:T(8,128)(2,1)} %get-tuple-element.274.refs_0_.refs_4_.refs_8_.refs_6_.refs_12_, bf16[6016,128]{1,0:T(8,128)(2,1)} %copy-done, bf16[128,5632]{1,0:T(8,128)(2,1)} %get-tuple-element.262.refs_2_, ...), custom_call_target="tpu_custom_call" | custom-call | flops 1 | bytes 1 | tf_op jit(solution)/shard_map/products/pallas_call | solution.py:864
  247.6 2.2 collective-permute-done.33.refs_4_.refs_10_.refs_16_.extra1
  249.8 1.8 collective-permute-done.34.refs_5_.refs_11_.refs_17_.extra2
  252.6 4.9 %halving.6 = (bf16[4,32,5632]{2,1,0:T(8,128)(2,1)}, bf16[4,32,5632]{2,1,0:T(8,128)(2,1)}) custom-call(s32[1]{0:T(128)} %bitcast.13.bit, bf16[8,32,5632]{2,1,0:T(8,128)(2,1)} %get-tuple-element.264.kept_mine.kept_other, bf16[8,32,5632]{2,1,0:T(8,128)(2,1)} %get-tuple-element.264.kept_mine.kept_other, ...), custom_call_target="tpu_custom_call" | custom-call | flops 1 | bytes 1 | tf_op jit(solution)/shard_map/halving/pallas_call | solution.py:957
  257.6 2.2 collective-permute-start.40
  259.8 12.8 %collective-permute-done.35.refs_3_.refs_9_.refs_15_.peer = bf16[432,1024]{1,0:T(8,128)(2,1)S(1)} collective-permute-done((bf16[432,1024]{1,0:T(8,128)(2,1)S(1)}, bf16[432,1024]{1,0:T(8,128)(2,1)S(1)}, u32[]{:S(2)}, u32[]{:S(2)}) %collective-permute-start.35) | collective-permute-done | bytes 884768 | tf_op jit(solution)/shard_map/ppermute | solution.py:354
  273.6 4.2 %products.5 = (bf16[8,96,1024]{2,1,0:T(8,128)(2,1)}, bf16[8,48,1024]{2,1,0:T(8,128)(2,1)}, bf16[8,48,1024]{2,1,0:T(8,128)(2,1)}) custom-call(s32[1]{0:T(128)} %bitcast.3.spot, bf16[2944,128]{1,0:T(8,128)(2,1)} %get-tuple-element.274.refs_0_.refs_4_.refs_8_.refs_6_.refs_12_, bf16[6016,128]{1,0:T(8,128)(2,1)} %copy-done, bf16[432,1024]{1,0:T(8,128)(2,1)} %copy-done.2, ...), custom_call_target="tpu_custom_call" | custom-call | flops 1 | bytes 1 | tf_op jit(solution)/shard_map/products/pallas_call | solution.py:864
  277.8 1.8 collective-permute-start.37
  279.7 2.0 collective-permute-done.37.refs_0_.refs_1_
  283.8 4.0 %halving.7 = (bf16[4,96,1024]{2,1,0:T(8,128)(2,1)}, bf16[4,96,1024]{2,1,0:T(8,128)(2,1)}) custom-call(s32[1]{0:T(128)} %bitcast.13.bit, bf16[8,96,1024]{2,1,0:T(8,128)(2,1)} %get-tuple-element.278.kept_mine.kept_other, bf16[8,96,1024]{2,1,0:T(8,128)(2,1)} %get-tuple-element.278.kept_mine.kept_other, bf16[8,48,1024]{2,1,0:T(8,128)(2,1)} %copy-done.9, ...), custom_call_target="tpu_custom_call" | custom-call | flops 1 | bytes 1 | tf_op jit(solution)/shard_map/halving/pallas_call | solution.py:957
  287.8 2.5 collective-permute-start.41
  290.3 5.6 %lent_rows.1 = (f32[128,512]{1,0:T(8,128)}, bf16[128,512]{1,0:T(8,128)(2,1)}) custom-call(bf16[432,1024]{1,0:T(8,128)(2,1)} %copy-done.2, bf16[432,1024]{1,0:T(8,128)(2,1)} %copy-done.3, bf16[8,3072]{1,0:T(8,128)(2,1)} %copy-done.26, bf16[8,3072]{1,0:T(8,128)(2,1)} %copy-done.27, bf16[6016,128]{1,0:T(8,128)(2,1)} %get-tuple-element.242.refs_2_.refs_6_.refs_10_.logit1, ...), custom_call_target="tpu_custom_call" | custom-call | flops 1 | bytes 1 | tf_op jit(solution)/shard_map/lent_rows/pallas_call | solution.py:896
  297.7 2.7 halving.8
  300.4 3.7 %collective-permute-start.44 = (bf16[2,32,5632]{2,1,0:T(8,128)(2,1)}, bf16[2,32,5632]{2,1,0:T(8,128)(2,1)S(1)}, u32[]{:S(2)}, u32[]{:S(2)}) collective-permute-start(bf16[2,32,5632]{2,1,0:T(8,128)(2,1)} %get-tuple-element.289), channel_id=1, source_target_pairs={{0,8},{2,10},{4,12},{6,14},{8,0},{10,2},{12,4},{14,6},{16,24},{18,... | collective-permute-start | bytes 2162696 | tf_op jit(solution)/shard_map/ppermute | solution.py:354
  304.8 2.5 norm_back.1
  310.7 2.3 halving.9
  312.9 7.4 %collective-permute-start.42 = (bf16[2,96,1024]{2,1,0:T(8,128)(2,1)}, bf16[2,96,1024]{2,1,0:T(8,128)(2,1)S(1)}, u32[]{:S(2)}, u32[]{:S(2)}) collective-permute-start(bf16[2,96,1024]{2,1,0:T(8,128)(2,1)} %get-tuple-element.301), channel_id=1, source_target_pairs={{0,8},{2,10},{4,12},{6,14},{8,0},{10,2},{12,4},{14,6},{16,24},{18,... | collective-permute-start | bytes 1179656 | tf_op jit(solution)/shard_map/ppermute | solution.py:354
  322.0 2.2 halving.10
  326.3 4.4 %all-to-all-start = ((f32[16,1,480]{2,1,0:T(1,128)}), f32[16,1,480]{2,1,0:T(1,128)S(1)}, u32[]{:S(2)}, u32[]{:S(2)}) async-start(f32[16,1,480]{2,1,0:T(1,128)} %all_to_all.8), calls=%async_computation.1 | async-start | bytes 65536 | tf_op jit(solution)/shard_map/all_to_all | solution.py:1463
  331.5 1.9 collective-permute-done.42.refs_0_.refs_1_
  334.1 2.0 halving.11
  337.8 11.1 %all-to-all-done = f32[16,1,480]{2,1,0:T(1,128)S(1)} async-done(((f32[16,1,480]{2,1,0:T(1,128)}), f32[16,1,480]{2,1,0:T(1,128)S(1)}, u32[]{:S(2)}, u32[]{:S(2)}) %all-to-all-start) | async-done | bytes 30752 | tf_op jit(solution)/shard_map/all_to_all | solution.py:1463
  350.3 2.4 collective-permute-done.45
  (214 shorter events, 65.3 us)
Async XLA Ops:
  7.2 314.0 %reduce-scatter.2.cloned.1.call-start = ((), (), s32[]{:S(2)}) async-start(), calls=%async_computation.2 | async-start | bytes 5292032 | tf_op jit(solution)/shard_map/reduce_scatter | solution.py:1405
  7.9 11.6 %copy-start.50 = (bf16[1,512]{1,0:T(2,128)(2,1)}, bf16[1,512]{1,0:T(2,128)(2,1)S(1)}, u32[]{:S(2)}) copy-start(bf16[1,512]{1,0:T(2,128)(2,1)S(1)} %stack.31.gain_ref) | copy-start | bytes 3076
  12.5 7.0 %collective-permute-start = (bf16[144,512]{1,0:T(8,128)(2,1)}, bf16[144,512]{1,0:T(8,128)(2,1)S(1)}, u32[]{:S(2)}, u32[]{:S(2)}) collective-permute-start(bf16[144,512]{1,0:T(8,128)(2,1)} %get-tuple-element.162), channel_id=1, source_target_pairs={{0,1},{1,0},{2,3},{3,2},{4,5},{5,4},{6,7},{7,6},{8,9},{9,8},{10,11... | collective-permute-start | bytes 442376 | tf_op jit(solution)/shard_map/ppermute | solution.py:354
  24.9 26.3 %collective-permute-start.1 = (bf16[128,4096]{1,0:T(8,128)(2,1)}, bf16[128,4096]{1,0:T(8,128)(2,1)S(1)}, u32[]{:S(2)}, u32[]{:S(2)}) collective-permute-start(bf16[128,4096]{1,0:T(8,128)(2,1)} %weigh.2), channel_id=1, source_target_pairs={{0,1},{1,0},{2,3},{3,2},{4,5},{5,4},{6,7},{7,6},{8,9},{9,8},{10,11... | collective-permute-start | bytes 3145736 | tf_op jit(solution)/shard_map/ppermute | solution.py:354
  28.9 48.3 %collective-permute-start.12 = (bf16[1920,256]{1,0:T(8,128)(2,1)S(1)}, bf16[1920,256]{1,0:T(8,128)(2,1)S(1)}, u32[]{:S(2)}, u32[]{:S(2)}) collective-permute-start(bf16[1920,256]{1,0:T(8,128)(2,1)S(1)} %pad_maximum_fusion), channel_id=1, source_target_pairs={{0,1},{1,0},{2,3},{3,2},{4,5},{5,4},{6,7},{7,6},{8,9},{9,8},{10,11... | collective-permute-start | bytes 2949128 | tf_op jit(solution)/shard_map/ppermute | solution.py:354
  51.3 47.2 %collective-permute-start.14 = (bf16[400,1408]{1,0:T(8,128)(2,1)}, bf16[400,1408]{1,0:T(8,128)(2,1)}, u32[]{:S(2)}, u32[]{:S(2)}) collective-permute-start(bf16[400,1408]{1,0:T(8,128)(2,1)} %constant_dynamic-slice_fusion.2), channel_id=1, source_target_pairs={{0,1},{1,0},{2,3},{3,2},{4,5},{5,4},{6,7},{7,6},{8,9},{9,8},{10,11... | collective-permute-start | bytes 3379208 | tf_op jit(solution)/shard_map/ppermute | solution.py:354
  53.9 2.2 collective-permute-start.2
  62.2 5.0 %collective-permute-start.3 = (bf16[4,144,128]{2,1,0:T(8,128)(2,1)}, bf16[4,144,128]{2,1,0:T(8,128)(2,1)S(1)}, u32[]{:S(2)}, u32[]{:S(2)}) collective-permute-start(bf16[4,144,128]{2,1,0:T(8,128)(2,1)} %get-tuple-element.179), channel_id=1, source_target_pairs={{0,2},{2,0},{4,6},{6,4},{8,10},{10,8},{12,14},{14,12},{16,18},{18,... | collective-permute-start | bytes 442376 | tf_op jit(solution)/shard_map/ppermute | solution.py:354
  64.8 7.2 %collective-permute-start.4 = (bf16[4,144,128]{2,1,0:T(8,128)(2,1)}, bf16[4,144,128]{2,1,0:T(8,128)(2,1)S(1)}, u32[]{:S(2)}, u32[]{:S(2)}) collective-permute-start(bf16[4,144,128]{2,1,0:T(8,128)(2,1)} %get-tuple-element.180), channel_id=1, source_target_pairs={{0,4},{2,6},{4,0},{6,2},{8,12},{10,14},{12,8},{14,10},{16,20},{18,... | collective-permute-start | bytes 442376 | tf_op jit(solution)/shard_map/ppermute | solution.py:354
  67.1 7.5 %collective-permute-start.5 = (bf16[4,144,128]{2,1,0:T(8,128)(2,1)}, bf16[4,144,128]{2,1,0:T(8,128)(2,1)S(1)}, u32[]{:S(2)}, u32[]{:S(2)}) collective-permute-start(bf16[4,144,128]{2,1,0:T(8,128)(2,1)} %get-tuple-element.181), channel_id=1, source_target_pairs={{0,6},{2,4},{4,2},{6,0},{8,14},{10,12},{12,10},{14,8},{16,22},{18,... | collective-permute-start | bytes 442376 | tf_op jit(solution)/shard_map/ppermute | solution.py:354
  67.2 7.5 %copy-start.31 = (bf16[4,144,128]{2,1,0:T(8,128)(2,1)}, bf16[4,144,128]{2,1,0:T(8,128)(2,1)S(1)}, u32[]{:S(2)}) copy-start(bf16[4,144,128]{2,1,0:T(8,128)(2,1)S(1)} %collective-permute-done.3.refs_1_.refs_5_) | copy-start | bytes 442372
  77.2 41.3 %copy-start.5 = (bf16[1920,256]{1,0:T(8,128)(2,1)}, bf16[1920,256]{1,0:T(8,128)(2,1)S(1)}, u32[]{:S(2)}) copy-start(bf16[1920,256]{1,0:T(8,128)(2,1)S(1)} %collective-permute-done.12.out_a.refs_13_) | copy-start | bytes 2949124
  77.2 31.0 %collective-permute-start.13 = (bf16[1920,256]{1,0:T(8,128)(2,1)S(1)}, bf16[1920,256]{1,0:T(8,128)(2,1)S(1)}, u32[]{:S(2)}, u32[]{:S(2)}) collective-permute-start(bf16[1920,256]{1,0:T(8,128)(2,1)S(1)} %collective-permute-done.12.out_a.refs_13_), channel_id=1, source_target_pairs={{0,4},{2,6},{4,0},{6,2},{8,12},{10,14},{12,8},{14,10},{16,20},{18,... | collective-permute-start | bytes 2949128 | tf_op jit(solution)/shard_map/ppermute | solution.py:354
  78.8 9.1 %collective-permute-start.6 = (bf16[4,144,128]{2,1,0:T(8,128)(2,1)}, bf16[4,144,128]{2,1,0:T(8,128)(2,1)S(1)}, u32[]{:S(2)}, u32[]{:S(2)}) collective-permute-start(bf16[4,144,128]{2,1,0:T(8,128)(2,1)} %group.2.refs_0_), channel_id=1, source_target_pairs={{0,8},{2,10},{4,12},{6,14},{8,0},{10,2},{12,4},{14,6},{16,24},{18,... | collective-permute-start | bytes 442376 | tf_op jit(solution)/shard_map/ppermute | solution.py:354
  80.3 14.2 %collective-permute-start.7 = (bf16[4,144,128]{2,1,0:T(8,128)(2,1)}, bf16[4,144,128]{2,1,0:T(8,128)(2,1)S(1)}, u32[]{:S(2)}, u32[]{:S(2)}) collective-permute-start(bf16[4,144,128]{2,1,0:T(8,128)(2,1)} %group.2.refs_0_), channel_id=1, source_target_pairs={{0,16},{2,18},{4,20},{6,22},{8,24},{10,26},{12,28},{14,30},{16,0},... | collective-permute-start | bytes 442376 | tf_op jit(solution)/shard_map/ppermute | solution.py:354
  82.9 11.6 %collective-permute-start.8 = (bf16[4,144,128]{2,1,0:T(8,128)(2,1)}, bf16[4,144,128]{2,1,0:T(8,128)(2,1)S(1)}, u32[]{:S(2)}, u32[]{:S(2)}) collective-permute-start(bf16[4,144,128]{2,1,0:T(8,128)(2,1)} %group.2.refs_0_), channel_id=1, source_target_pairs={{0,24},{2,26},{4,28},{6,30},{8,16},{10,18},{12,20},{14,22},{16,8},... | collective-permute-start | bytes 442376 | tf_op jit(solution)/shard_map/ppermute | solution.py:354
  87.9 6.7 %copy-start.41 = (bf16[4,144,128]{2,1,0:T(8,128)(2,1)}, bf16[4,144,128]{2,1,0:T(8,128)(2,1)S(1)}, u32[]{:S(2)}) copy-start(bf16[4,144,128]{2,1,0:T(8,128)(2,1)S(1)} %collective-permute-done.6.refs_1_) | copy-start | bytes 442372
  98.5 26.9 %collective-permute-start.18 = (bf16[400,1408]{1,0:T(8,128)(2,1)}, bf16[400,1408]{1,0:T(8,128)(2,1)S(1)}, u32[]{:S(2)}, u32[]{:S(2)}) collective-permute-start(bf16[400,1408]{1,0:T(8,128)(2,1)} %collective-permute-done.14.refs_4_), channel_id=1, source_target_pairs={{0,8},{2,10},{4,12},{6,14},{8,0},{10,2},{12,4},{14,6},{16,24},{18,... | collective-permute-start | bytes 3379208 | tf_op jit(solution)/shard_map/ppermute | solution.py:354
  100.8 5.7 %collective-permute-start.10 = (bf16[4,128,128]{2,1,0:T(8,128)(2,1)}, bf16[4,128,128]{2,1,0:T(8,128)(2,1)S(1)}, u32[]{:S(2)}, u32[]{:S(2)}) collective-permute-start(bf16[4,128,128]{2,1,0:T(8,128)(2,1)} %get-tuple-element.192), channel_id=1, source_target_pairs={{0,4},{2,6},{4,0},{6,2},{8,12},{10,14},{12,8},{14,10},{16,20},{18,... | collective-permute-start | bytes 393224 | tf_op jit(solution)/shard_map/ppermute | solution.py:354
  102.2 6.0 %collective-permute-start.11 = (bf16[4,128,128]{2,1,0:T(8,128)(2,1)}, bf16[4,128,128]{2,1,0:T(8,128)(2,1)S(1)}, u32[]{:S(2)}, u32[]{:S(2)}) collective-permute-start(bf16[4,128,128]{2,1,0:T(8,128)(2,1)} %get-tuple-element.193), channel_id=1, source_target_pairs={{0,6},{2,4},{4,2},{6,0},{8,14},{10,12},{12,10},{14,8},{16,22},{18,... | collective-permute-start | bytes 393224 | tf_op jit(solution)/shard_map/ppermute | solution.py:354
  102.2 6.0 %collective-permute-start.9 = (bf16[4,128,128]{2,1,0:T(8,128)(2,1)}, bf16[4,128,128]{2,1,0:T(8,128)(2,1)S(1)}, u32[]{:S(2)}, u32[]{:S(2)}) collective-permute-start(bf16[4,128,128]{2,1,0:T(8,128)(2,1)} %get-tuple-element.191), channel_id=1, source_target_pairs={{0,2},{2,0},{4,6},{6,4},{8,10},{10,8},{12,14},{14,12},{16,18},{18,... | collective-permute-start | bytes 393224 | tf_op jit(solution)/shard_map/ppermute | solution.py:354
  108.2 21.8 %copy-start.6 = (bf16[1920,256]{1,0:T(8,128)(2,1)}, bf16[1920,256]{1,0:T(8,128)(2,1)S(1)}, u32[]{:S(2)}) copy-start(bf16[1920,256]{1,0:T(8,128)(2,1)S(1)} %collective-permute-done.13.out_b.refs_14_) | copy-start | bytes 2949124
  108.2 17.6 %collective-permute-start.16 = (bf16[1920,256]{1,0:T(8,128)(2,1)S(1)}, bf16[1920,256]{1,0:T(8,128)(2,1)S(1)}, u32[]{:S(2)}, u32[]{:S(2)}) collective-permute-start(bf16[1920,256]{1,0:T(8,128)(2,1)S(1)} %collective-permute-done.12.out_a.refs_13_), channel_id=1, source_target_pairs={{0,2},{2,0},{4,6},{6,4},{8,10},{10,8},{12,14},{14,12},{16,18},{18,... | collective-permute-start | bytes 2949128 | tf_op jit(solution)/shard_map/ppermute | solution.py:354
  109.0 16.9 %collective-permute-start.17 = (bf16[1920,256]{1,0:T(8,128)(2,1)S(1)}, bf16[1920,256]{1,0:T(8,128)(2,1)S(1)}, u32[]{:S(2)}, u32[]{:S(2)}) collective-permute-start(bf16[1920,256]{1,0:T(8,128)(2,1)S(1)} %collective-permute-done.13.out_b.refs_14_), channel_id=1, source_target_pairs={{0,2},{2,0},{4,6},{6,4},{8,10},{10,8},{12,14},{14,12},{16,18},{18,... | collective-permute-start | bytes 2949128 | tf_op jit(solution)/shard_map/ppermute | solution.py:354
  109.1 16.8 %collective-permute-start.15 = (bf16[112,2816]{1,0:T(8,128)(2,1)}, bf16[112,2816]{1,0:T(8,128)(2,1)S(1)}, u32[]{:S(2)}, u32[]{:S(2)}) collective-permute-start(bf16[112,2816]{1,0:T(8,128)(2,1)} %constant_dynamic-slice_fusion.5), channel_id=1, source_target_pairs={{0,1},{1,0},{2,3},{3,2},{4,5},{5,4},{6,7},{7,6},{8,9},{9,8},{10,11... | collective-permute-start | bytes 1892360 | tf_op jit(solution)/shard_map/ppermute | solution.py:354
  118.5 7.4 %collective-permute-start.19 = (bf16[400,1408]{1,0:T(8,128)(2,1)}, bf16[400,1408]{1,0:T(8,128)(2,1)S(1)}, u32[]{:S(2)}, u32[]{:S(2)}) collective-permute-start(bf16[400,1408]{1,0:T(8,128)(2,1)} %collective-permute-done.14.refs_4_), channel_id=1, source_target_pairs={{0,2},{2,0},{4,6},{6,4},{8,10},{10,8},{12,14},{14,12},{16,18},{18,... | collective-permute-start | bytes 3379208 | tf_op jit(solution)/shard_map/ppermute | solution.py:354
  125.3 3.7 %collective-permute-start.20 = (bf16[400,1408]{1,0:T(8,128)(2,1)S(1)}, bf16[400,1408]{1,0:T(8,128)(2,1)S(1)}, u32[]{:S(2)}, u32[]{:S(2)}) collective-permute-start(bf16[400,1408]{1,0:T(8,128)(2,1)S(1)} %collective-permute-done.18.refs_5_), channel_id=1, source_target_pairs={{0,2},{2,0},{4,6},{6,4},{8,10},{10,8},{12,14},{14,12},{16,18},{18,... | collective-permute-start | bytes 3379208 | tf_op jit(solution)/shard_map/ppermute | solution.py:354
  125.9 3.2 collective-permute-start.21
  155.0 39.5 %collective-permute-start.25 = (bf16[6016,128]{1,0:T(8,128)(2,1)}, bf16[6016,128]{1,0:T(8,128)(2,1)S(1)}, u32[]{:S(2)}, u32[]{:S(2)}) collective-permute-start(bf16[6016,128]{1,0:T(8,128)(2,1)} %get-tuple-element.242.refs_2_.refs_6_.refs_10_.logit1), channel_id=1, source_target_pairs={{0,1},{1,0},{2,3},{3,2},{4,5},{5,4},{6,7},{7,6},{8,9},{9,8},{10,11... | collective-permute-start | bytes 4620296 | tf_op jit(solution)/shard_map/ppermute | solution.py:354
  176.1 1.9 collective-permute-start.22
  176.2 6.9 %collective-permute-start.23 = (bf16[4,144,128]{2,1,0:T(8,128)(2,1)}, bf16[4,144,128]{2,1,0:T(8,128)(2,1)S(1)}, u32[]{:S(2)}, u32[]{:S(2)}) collective-permute-start(bf16[4,144,128]{2,1,0:T(8,128)(2,1)} %get-tuple-element.229), channel_id=1, source_target_pairs={{0,4},{2,6},{4,0},{6,2},{8,12},{10,14},{12,8},{14,10},{16,20},{18,... | collective-permute-start | bytes 442376 | tf_op jit(solution)/shard_map/ppermute | solution.py:354
  177.7 7.7 %collective-permute-start.24 = (bf16[4,144,128]{2,1,0:T(8,128)(2,1)}, bf16[4,144,128]{2,1,0:T(8,128)(2,1)S(1)}, u32[]{:S(2)}, u32[]{:S(2)}) collective-permute-start(bf16[4,144,128]{2,1,0:T(8,128)(2,1)} %get-tuple-element.230), channel_id=1, source_target_pairs={{0,6},{2,4},{4,2},{6,0},{8,14},{10,12},{12,10},{14,8},{16,22},{18,... | collective-permute-start | bytes 442376 | tf_op jit(solution)/shard_map/ppermute | solution.py:354
  188.0 6.5 %collective-permute-start.26 = (bf16[4,144,128]{2,1,0:T(8,128)(2,1)}, bf16[4,144,128]{2,1,0:T(8,128)(2,1)S(1)}, u32[]{:S(2)}, u32[]{:S(2)}) collective-permute-start(bf16[4,144,128]{2,1,0:T(8,128)(2,1)} %group.3.refs_0_), channel_id=1, source_target_pairs={{0,8},{2,10},{4,12},{6,14},{8,0},{10,2},{12,4},{14,6},{16,24},{18,... | collective-permute-start | bytes 442376 | tf_op jit(solution)/shard_map/ppermute | solution.py:354
  194.5 6.8 %copy-start.40 = (bf16[4,144,128]{2,1,0:T(8,128)(2,1)}, bf16[4,144,128]{2,1,0:T(8,128)(2,1)S(1)}, u32[]{:S(2)}) copy-start(bf16[4,144,128]{2,1,0:T(8,128)(2,1)S(1)} %collective-permute-done.26.refs_1_) | copy-start | bytes 442372
  202.6 34.6 %collective-permute-start.32 = (bf16[128,5632]{1,0:T(8,128)(2,1)S(1)}, bf16[128,5632]{1,0:T(8,128)(2,1)S(1)}, u32[]{:S(2)}, u32[]{:S(2)}) collective-permute-start(bf16[128,5632]{1,0:T(8,128)(2,1)S(1)} %copy-done.20), channel_id=1, source_target_pairs={{0,1},{1,0},{2,3},{3,2},{4,5},{5,4},{6,7},{7,6},{8,9},{9,8},{10,11... | collective-permute-start | bytes 4325384 | tf_op jit(solution)/shard_map/ppermute | solution.py:354
  204.0 13.8 %collective-permute-start.27 = (bf16[4,144,128]{2,1,0:T(8,128)(2,1)S(1)}, bf16[4,144,128]{2,1,0:T(8,128)(2,1)S(1)}, u32[]{:S(2)}, u32[]{:S(2)}) collective-permute-start(bf16[4,144,128]{2,1,0:T(8,128)(2,1)S(1)} %copy-done.34), channel_id=1, source_target_pairs={{0,16},{2,18},{4,20},{6,22},{8,24},{10,26},{12,28},{14,30},{16,0},... | collective-permute-start | bytes 442376 | tf_op jit(solution)/shard_map/ppermute | solution.py:354
  206.8 11.1 %collective-permute-start.28 = (bf16[4,144,128]{2,1,0:T(8,128)(2,1)S(1)}, bf16[4,144,128]{2,1,0:T(8,128)(2,1)S(1)}, u32[]{:S(2)}, u32[]{:S(2)}) collective-permute-start(bf16[4,144,128]{2,1,0:T(8,128)(2,1)S(1)} %copy-done.34), channel_id=1, source_target_pairs={{0,24},{2,26},{4,28},{6,30},{8,16},{10,18},{12,20},{14,22},{16,8},... | collective-permute-start | bytes 442376 | tf_op jit(solution)/shard_map/ppermute | solution.py:354
  221.9 1.9 collective-permute-start.29
  221.9 6.6 %collective-permute-start.30 = (bf16[4,128,128]{2,1,0:T(8,128)(2,1)}, bf16[4,128,128]{2,1,0:T(8,128)(2,1)S(1)}, u32[]{:S(2)}, u32[]{:S(2)}) collective-permute-start(bf16[4,128,128]{2,1,0:T(8,128)(2,1)} %get-tuple-element.252), channel_id=1, source_target_pairs={{0,4},{2,6},{4,0},{6,2},{8,12},{10,14},{12,8},{14,10},{16,20},{18,... | collective-permute-start | bytes 393224 | tf_op jit(solution)/shard_map/ppermute | solution.py:354
  223.4 7.0 %collective-permute-start.31 = (bf16[4,128,128]{2,1,0:T(8,128)(2,1)}, bf16[4,128,128]{2,1,0:T(8,128)(2,1)S(1)}, u32[]{:S(2)}, u32[]{:S(2)}) collective-permute-start(bf16[4,128,128]{2,1,0:T(8,128)(2,1)} %get-tuple-element.253), channel_id=1, source_target_pairs={{0,6},{2,4},{4,2},{6,0},{8,14},{10,12},{12,10},{14,8},{16,22},{18,... | collective-permute-start | bytes 393224 | tf_op jit(solution)/shard_map/ppermute | solution.py:354
  223.8 6.6 %copy-start.46 = (bf16[4,128,128]{2,1,0:T(8,128)(2,1)}, bf16[4,128,128]{2,1,0:T(8,128)(2,1)S(1)}, u32[]{:S(2)}) copy-start(bf16[4,128,128]{2,1,0:T(8,128)(2,1)S(1)} %collective-permute-done.29.r1) | copy-start | bytes 393220
  238.4 6.4 %copy-start.36 = (bf16[144,1024]{1,0:T(8,128)(2,1)S(1)}, bf16[144,1024]{1,0:T(8,128)(2,1)}, u32[]{:S(2)}) copy-start(bf16[144,1024]{1,0:T(8,128)(2,1)} %get-tuple-element.265) | copy-start | bytes 884740
  238.4 6.4 %copy-start.37 = (bf16[144,1024]{1,0:T(8,128)(2,1)S(1)}, bf16[144,1024]{1,0:T(8,128)(2,1)}, u32[]{:S(2)}) copy-start(bf16[144,1024]{1,0:T(8,128)(2,1)} %get-tuple-element.266) | copy-start | bytes 884740
  238.4 6.4 %copy-start.38 = (bf16[144,1024]{1,0:T(8,128)(2,1)S(1)}, bf16[144,1024]{1,0:T(8,128)(2,1)}, u32[]{:S(2)}) copy-start(bf16[144,1024]{1,0:T(8,128)(2,1)} %get-tuple-element.267) | copy-start | bytes 884740
  244.4 8.2 %collective-permute-start.36 = (bf16[8,32,5632]{2,1,0:T(8,128)(2,1)}, bf16[8,32,5632]{2,1,0:T(8,128)(2,1)}, u32[]{:S(2)}, u32[]{:S(2)}) collective-permute-start(bf16[8,32,5632]{2,1,0:T(8,128)(2,1)} %get-tuple-element.269), channel_id=1, source_target_pairs={{0,2},{2,0},{4,6},{6,4},{8,10},{10,8},{12,14},{14,12},{16,18},{18,... | collective-permute-start | bytes 8650760 | tf_op jit(solution)/shard_map/ppermute | solution.py:354
  244.9 4.9 %collective-permute-start.33 = (bf16[8,3072]{1,0:T(8,128)(2,1)S(1)}, bf16[8,3072]{1,0:T(8,128)(2,1)S(1)}, u32[]{:S(2)}, u32[]{:S(2)}) collective-permute-start(bf16[8,3072]{1,0:T(8,128)(2,1)S(1)} %pad_maximum_fusion.3), channel_id=1, source_target_pairs={{2,0},{4,2},{6,4},{8,6},{10,8},{12,10},{14,12},{16,14},{18,16},{20... | collective-permute-start | bytes 147464 | tf_op jit(solution)/shard_map/ppermute | solution.py:1177
  246.2 5.4 %collective-permute-start.34 = (bf16[8,3072]{1,0:T(8,128)(2,1)S(1)}, bf16[8,3072]{1,0:T(8,128)(2,1)S(1)}, u32[]{:S(2)}, u32[]{:S(2)}) collective-permute-start(bf16[8,3072]{1,0:T(8,128)(2,1)S(1)} %pad_maximum_fusion.3), channel_id=1, source_target_pairs={{2,1},{3,0},{4,3},{5,2},{6,5},{7,4},{8,7},{9,6},{10,9},{11,8},{12,... | collective-permute-start | bytes 147464 | tf_op jit(solution)/shard_map/ppermute | solution.py:1182
  247.6 10.0 %copy-start.2 = (bf16[432,1024]{1,0:T(8,128)(2,1)}, bf16[432,1024]{1,0:T(8,128)(2,1)S(1)}, u32[]{:S(2)}) copy-start(bf16[432,1024]{1,0:T(8,128)(2,1)S(1)} %pad_maximum_fusion.1.refs_2_.refs_8_.refs_14_.own) | copy-start | bytes 2654212
  249.8 7.8 %copy-start.26 = (bf16[8,3072]{1,0:T(8,128)(2,1)}, bf16[8,3072]{1,0:T(8,128)(2,1)S(1)}, u32[]{:S(2)}) copy-start(bf16[8,3072]{1,0:T(8,128)(2,1)S(1)} %collective-permute-done.33.refs_4_.refs_10_.refs_16_.extra1) | copy-start | bytes 147460
  251.6 6.0 %copy-start.27 = (bf16[8,3072]{1,0:T(8,128)(2,1)}, bf16[8,3072]{1,0:T(8,128)(2,1)S(1)}, u32[]{:S(2)}) copy-start(bf16[8,3072]{1,0:T(8,128)(2,1)S(1)} %collective-permute-done.34.refs_5_.refs_11_.refs_17_.extra2) | copy-start | bytes 147460
  251.6 21.0 %collective-permute-start.35 = (bf16[432,1024]{1,0:T(8,128)(2,1)S(1)}, bf16[432,1024]{1,0:T(8,128)(2,1)S(1)}, u32[]{:S(2)}, u32[]{:S(2)}) collective-permute-start(bf16[432,1024]{1,0:T(8,128)(2,1)S(1)} %pad_maximum_fusion.1.refs_2_.refs_8_.refs_14_.own), channel_id=1, source_target_pairs={{0,1},{1,0},{2,3},{3,2},{4,5},{5,4},{6,7},{7,6},{8,9},{9,8},{10,11... | collective-permute-start | bytes 2654216 | tf_op jit(solution)/shard_map/ppermute | solution.py:354
  257.6 39.0 %collective-permute-start.40 = (bf16[4,32,5632]{2,1,0:T(8,128)(2,1)}, bf16[4,32,5632]{2,1,0:T(8,128)(2,1)S(1)}, u32[]{:S(2)}, u32[]{:S(2)}) collective-permute-start(bf16[4,32,5632]{2,1,0:T(8,128)(2,1)} %get-tuple-element.273), channel_id=1, source_target_pairs={{0,4},{2,6},{4,0},{6,2},{8,12},{10,14},{12,8},{14,10},{16,20},{18,... | collective-permute-start | bytes 4325384 | tf_op jit(solution)/shard_map/ppermute | solution.py:354
  277.8 3.9 %collective-permute-start.37 = (bf16[8,48,1024]{2,1,0:T(8,128)(2,1)}, bf16[8,48,1024]{2,1,0:T(8,128)(2,1)S(1)}, u32[]{:S(2)}, u32[]{:S(2)}) collective-permute-start(bf16[8,48,1024]{2,1,0:T(8,128)(2,1)} %get-tuple-element.279), channel_id=1, source_target_pairs={{0,2},{2,0},{4,6},{6,4},{8,10},{10,8},{12,14},{14,12},{16,18},{18,... | collective-permute-start | bytes 2359304 | tf_op jit(solution)/shard_map/ppermute | solution.py:354
  279.6 3.2 collective-permute-start.38
  287.8 22.0 %collective-permute-start.41 = (bf16[4,96,1024]{2,1,0:T(8,128)(2,1)}, bf16[4,96,1024]{2,1,0:T(8,128)(2,1)S(1)}, u32[]{:S(2)}, u32[]{:S(2)}) collective-permute-start(bf16[4,96,1024]{2,1,0:T(8,128)(2,1)} %get-tuple-element.283), channel_id=1, source_target_pairs={{0,4},{2,6},{4,0},{6,2},{8,12},{10,14},{12,8},{14,10},{16,20},{18,... | collective-permute-start | bytes 2359304 | tf_op jit(solution)/shard_map/ppermute | solution.py:354
  295.9 8.2 %collective-permute-start.39 = (bf16[128,512]{1,0:T(8,128)(2,1)}, bf16[128,512]{1,0:T(8,128)(2,1)S(1)}, u32[]{:S(2)}, u32[]{:S(2)}) collective-permute-start(bf16[128,512]{1,0:T(8,128)(2,1)} %get-tuple-element.286), channel_id=1, source_target_pairs={{0,1},{1,0},{2,3},{3,2},{4,5},{5,4},{6,7},{7,6},{8,9},{9,8},{10,11... | collective-permute-start | bytes 393224 | tf_op jit(solution)/shard_map/ppermute | solution.py:354
  300.4 20.7 %collective-permute-start.44 = (bf16[2,32,5632]{2,1,0:T(8,128)(2,1)}, bf16[2,32,5632]{2,1,0:T(8,128)(2,1)S(1)}, u32[]{:S(2)}, u32[]{:S(2)}) collective-permute-start(bf16[2,32,5632]{2,1,0:T(8,128)(2,1)} %get-tuple-element.289), channel_id=1, source_target_pairs={{0,8},{2,10},{4,12},{6,14},{8,0},{10,2},{12,4},{14,6},{16,24},{18,... | collective-permute-start | bytes 2162696 | tf_op jit(solution)/shard_map/ppermute | solution.py:354
  312.9 20.5 %collective-permute-start.42 = (bf16[2,96,1024]{2,1,0:T(8,128)(2,1)}, bf16[2,96,1024]{2,1,0:T(8,128)(2,1)S(1)}, u32[]{:S(2)}, u32[]{:S(2)}) collective-permute-start(bf16[2,96,1024]{2,1,0:T(8,128)(2,1)} %get-tuple-element.301), channel_id=1, source_target_pairs={{0,8},{2,10},{4,12},{6,14},{8,0},{10,2},{12,4},{14,6},{16,24},{18,... | collective-permute-start | bytes 1179656 | tf_op jit(solution)/shard_map/ppermute | solution.py:354
  320.3 5.3 %collective-permute-start.43 = (f32[16,480]{1,0:T(8,128)S(1)}, f32[16,480]{1,0:T(8,128)S(1)}, u32[]{:S(2)}, u32[]{:S(2)}) collective-permute-start(f32[16,480]{1,0:T(8,128)S(1)} %bitcast.57), channel_id=1, source_target_pairs={{0,1},{1,0},{2,3},{3,2},{4,5},{5,4},{6,7},{7,6},{8,9},{9,8},{10,11... | collective-permute-start | bytes 92168 | tf_op jit(solution)/shard_map/ppermute | solution.py:354
  321.1 9.6 %copy-start.22 = (bf16[152,1024]{1,0:T(8,128)(2,1)S(1)}, bf16[152,1024]{1,0:T(8,128)(2,1)}, u32[]{:S(2)}) copy-start(bf16[152,1024]{1,0:T(8,128)(2,1)} %reduce-scatter.2.cloned.1.call-done) | copy-start | bytes 933892
  324.2 30.2 %collective-permute-start.46 = (bf16[1,32,5632]{2,1,0:T(8,128)(2,1)}, bf16[1,32,5632]{2,1,0:T(8,128)(2,1)S(1)}, u32[]{:S(2)}, u32[]{:S(2)}) collective-permute-start(bf16[1,32,5632]{2,1,0:T(8,128)(2,1)} %get-tuple-element.304), channel_id=1, source_target_pairs={{0,16},{2,18},{4,20},{6,22},{8,24},{10,26},{12,28},{14,30},{16,0},... | collective-permute-start | bytes 1081352 | tf_op jit(solution)/shard_map/ppermute | solution.py:354
  326.3 22.7 %all-to-all-start = ((f32[16,1,480]{2,1,0:T(1,128)}), f32[16,1,480]{2,1,0:T(1,128)S(1)}, u32[]{:S(2)}, u32[]{:S(2)}) async-start(f32[16,1,480]{2,1,0:T(1,128)} %all_to_all.8), calls=%async_computation.1 | async-start | bytes 65536 | tf_op jit(solution)/shard_map/all_to_all | solution.py:1463
  336.2 18.3 %copy-start.35 = (bf16[1,32,5632]{2,1,0:T(8,128)(2,1)S(1)}, bf16[1,32,5632]{2,1,0:T(8,128)(2,1)}, u32[]{:S(2)}) copy-start(bf16[1,32,5632]{2,1,0:T(8,128)(2,1)} %get-tuple-element.311) | copy-start | bytes 1081348
  336.9 15.7 %collective-permute-start.45 = (bf16[1,96,1024]{2,1,0:T(8,128)(2,1)}, bf16[1,96,1024]{2,1,0:T(8,128)(2,1)S(1)}, u32[]{:S(2)}, u32[]{:S(2)}) collective-permute-start(bf16[1,96,1024]{2,1,0:T(8,128)(2,1)} %get-tuple-element.309), channel_id=1, source_target_pairs={{0,16},{2,18},{4,20},{6,22},{8,24},{10,26},{12,28},{14,30},{16,0},... | collective-permute-start | bytes 589832 | tf_op jit(solution)/shard_map/ppermute | solution.py:354
  (36 other events, 65.3 us)
Sparse Core Ops, SparseCore 0:
  201.4 81.5 reduce-scatter.1

commit v7 on v6

--- a/solution.py
+++ b/solution.py
@@ -1399,7 +1399,7 @@
     rights = [(i * BLOCKS * rows, rows) for i in range(3)]
     (early,) = products(
         spot, peers, [[(lefts_here, parts[i]), (message_peer, peer_parts[i])] for i in (1, 2, 3)],
-        [[(message, at), (message_peer, at)] for at in rights], 512, joined=True
+        [[(message, at), (message_peer, at)] for at in rights], 1024, joined=True
     )
     seq.mark(early)
     early = lax.psum_scatter(early.reshape(-1, D), "ctx", scatter_dimension=0, tiled=True)
@@ -1413,7 +1413,7 @@
     seq.mark(low_k)
     (up_peer,) = seq.gate(both_up[1])
     blocks = products(
-        spot, peers, [[(lefts, parts[0]), (message_peer, peer_parts[0])]], [[(both_up[0], None), (up_peer, None)]], 1408
+        spot, peers, [[(lefts, parts[0]), (message_peer, peer_parts[0])]], [[(both_up[0], None), (up_peer, None)]], 2816
     )
     seq.mark(blocks[0])
     ups = Reduction((0, 1, 2), blocks)
@@ -1429,7 +1429,7 @@
     lefts_here, thirds_peer = seq.gate(lefts, thirds_peer)
     left = [(lefts_here, parts[2]), (message_peer, peer_parts[2])]
     rights = [[(thirds, i), (thirds_peer, i), (extra[0], i), (extra[1], i)] for i in range(3)]
-    blocks = products(spot, peers, [left] * 3, rights, 512, messages=2)
+    blocks = products(spot, peers, [left] * 3, rights, 1024, messages=2)
     seq.mark(blocks[0])
     late = Reduction((0, 1, 2), blocks)
     late.got = seq.gate(*late.got)

time: 364 us -> 362 us (level)
  no operation moved by 1% of the time
where the time goes in v7:
time: 362 us; the launch traced here: 361 us
  Pallas kernels  137 us (38%)
  waiting for transfers between devices  103 us (28%)
  starting transfers between devices  65.2 us (18%)
  local copies, waits for them, and re-layouts  31.9 us (9%)
  between operations  14.5 us (4%)
  other arithmetic  9.22 us (3%)
    ppermute x44, waiting for transfers between devices, partner(): return lax.ppermute(x, axis, neighbour(axis, bit))  87.3 us
    ppermute x44, starting transfers between devices, partner(): return lax.ppermute(x, axis, neighbour(axis, bit))  57.8 us
    pallas_call x1, Pallas kernels, middle(): pl.pallas_call(functools.partial(middle_kernel, owners), grid_spec=pltpu....  24.8 us
    pallas_call x6, Pallas kernels, halving_step(): pl.pallas_call(step_kernel, grid_spec=pltpu.PrefetchScalarGridSpec(num_sc...  18.2 us
    unnamed x106, local copies, waits for them, and re-layouts  16.9 us
    pallas_call x1, Pallas kernels, adjoint(): pl.pallas_call(adjoint_kernel, grid=(ITERS // AT_ONCE,), in_specs=[smem()...  15.5 us
    pallas_call x3, Pallas kernels, products(): pl.pallas_call(functools.partial(products_kernel, plan, joined, cuts), gr...  15.1 us
    all_to_all x1, waiting for transfers between devices, local(): vector = lax.all_to_all(vector, 'ctx', 0, 0, tiled=True)  10.6 us
  transfers between devices with their start and end apart: 49, of which 27 were waited for; matrix products, arithmetic and copies ran while one was open for 5% of the time, Pallas kernels for 28%

profile of v7, /device:TPU:0, one launch (start us, length us, event | category | flops | bytes accessed | tf_op | source)
XLA Modules:
  0.0 360.5 jit_solution(2886962097975854123)
XLA Ops:
  10.6 1.9 norm.1
  12.5 3.0 collective-permute-start
  20.2 4.8 %weigh.2 = bf16[128,4096]{1,0:T(8,128)(2,1)} custom-call(bf16[144,512]{1,0:T(8,128)(2,1)} %copy-done.39, bf16[1,512]{1,0:T(2,128)(2,1)} %copy-done.50, bf16[512,3072]{1,0:T(8,128)(2,1)} %qkv_ref.5, bf16[512,1024]{1,0:T(8,128)(2,1)} %gate_ref.5), custom_call_target="tpu_custom_call" | custom-call | flops 1 | bytes 1 | tf_op jit(solution)/shard_map/weigh/pallas_call | solution.py:109
  24.9 1.7 collective-permute-start.1
  29.3 2.4 constant_dynamic-slice_fusion.2
  33.0 1.9 constant_dynamic-slice_fusion.5
  35.6 5.0 %weigh.3.oq.ok.ov.own_logit.own = f32[128,4096]{1,0:T(8,128)} custom-call(bf16[128,512]{1,0:T(8,128)(2,1)} %get-tuple-element.169.left_ref, bf16[1,512]{1,0:T(2,128)(2,1)} %copy-done.50, bf16[512,3072]{1,0:T(8,128)(2,1)} %qkv_ref.5, bf16[512,1024]{1,0:T(8,128)(2,1)} %gate_ref.5), custom_call_target="tpu_custom_call" | custom-call | flops 1 | bytes 1 | tf_op jit(solution)/shard_map/weigh/pallas_call | solution.py:109
  40.6 4.2 %tables.1 = (f32[8,128,128]{2,1,0:T(8,128)}, f32[8,128,128]{2,1,0:T(8,128)}, f32[8,128,128]{2,1,0:T(8,128)}) custom-call(f32[8,128]{1,0:T(8,128)} %reduce_window_sum.11.c_ref, f32[8,128]{1,0:T(8,128)} %get-tuple-element.171.b_ref, f32[8,128]{1,0:T(8,128)} %bitcast.58), custom_call_target="tpu_custom_call" | custom-call | flops 1 | bytes 1 | tf_op jit(solution)/shard_map/tables/pallas_call | solution.py:137
  44.8 6.4 %collective-permute-done.1.lq.lk.lv.lent_logit.lent = bf16[128,4096]{1,0:T(8,128)(2,1)S(1)} collective-permute-done((bf16[128,4096]{1,0:T(8,128)(2,1)}, bf16[128,4096]{1,0:T(8,128)(2,1)S(1)}, u32[]{:S(2)}, u32[]{:S(2)}) %collective-permute-start.1) | collective-permute-done | bytes 1048608 | tf_op jit(solution)/shard_map/ppermute | solution.py:354
  51.3 1.7 collective-permute-start.14
  56.7 5.5 %features.1 = (f32[8,128,128]{2,1,0:T(8,128)}, bf16[8,128,128]{2,1,0:T(8,128)(2,1)}, bf16[8,128,128]{2,1,0:T(8,128)(2,1)}, bf16[4,144,128]{2,1,0:T(8,128)(2,1)},...) custom-call(s32[1]{0:T(128)} %bitcast.3.spot, ...), custom_call_target="tpu_custom_call" | custom-call | flops 1 | bytes 1 | tf_op jit(solution)/shard_map/features/pallas_call | solution.py:247
  62.2 2.6 collective-permute-start.3
  64.8 2.3 collective-permute-start.4
  67.2 4.8 %collective-permute-done.4.refs_2_.refs_6_ = bf16[4,144,128]{2,1,0:T(8,128)(2,1)S(1)} collective-permute-done((bf16[4,144,128]{2,1,0:T(8,128)(2,1)}, bf16[4,144,128]{2,1,0:T(8,128)(2,1)S(1)}, u32[]{:S(2)}, u32[]{:S(2)}) %collective-permute-start.4) | collective-permute-done | bytes 147488 | tf_op jit(solution)/shard_map/ppermute | solution.py:354
  72.0 2.6 collective-permute-done.5.refs_3_.refs_7_
  75.3 1.9 group.2.refs_0_
  80.3 2.6 collective-permute-start.7
  83.2 4.7 %collective-permute-done.6.refs_1_ = bf16[4,144,128]{2,1,0:T(8,128)(2,1)S(1)} collective-permute-done((bf16[4,144,128]{2,1,0:T(8,128)(2,1)}, bf16[4,144,128]{2,1,0:T(8,128)(2,1)S(1)}, u32[]{:S(2)}, u32[]{:S(2)}) %collective-permute-start.6) | collective-permute-done | bytes 147488 | tf_op jit(solution)/shard_map/ppermute | solution.py:354
  87.9 6.6 %collective-permute-done.7.refs_2_ = bf16[4,144,128]{2,1,0:T(8,128)(2,1)S(1)} collective-permute-done((bf16[4,144,128]{2,1,0:T(8,128)(2,1)}, bf16[4,144,128]{2,1,0:T(8,128)(2,1)S(1)}, u32[]{:S(2)}, u32[]{:S(2)}) %collective-permute-start.7) | collective-permute-done | bytes 147488 | tf_op jit(solution)/shard_map/ppermute | solution.py:354
  95.8 2.6 spread.2
  98.5 2.3 collective-permute-start.18
  102.9 3.6 collective-permute-done.10.s2
  109.6 9.0 %solve.1 = (bf16[8,128,128]{2,1,0:T(8,128)(2,1)}, f32[8,8,128,128]{3,2,1,0:T(8,128)}, f32[8,8,128,128]{3,2,1,0:T(8,128)}, bf16[8,8,128,128]{3,2,1,0:T(8,128)(2,1)}, f32[8,24,128]{2,1,0:T(8,128)}) custom-call(s32[1]{0:T(128)} %bitcast.1.place, f32[8,128,128]{2,1,0:T(8,128)} %get-tuple-element.199.q_ref, bf16[8,128,128]{2,1,0:T(8,128)(2,1)} %get-tuple-element.200.k_ref, ...), custom_call_target="tpu_custom_call" | custom-call | flops 1 | bytes 1 | tf_op jit(solution)/shard_map/solve/pallas_call | solution.py:478
  118.8 6.5 %collective-permute-done.18.refs_5_ = bf16[400,1408]{1,0:T(8,128)(2,1)S(1)} collective-permute-done((bf16[400,1408]{1,0:T(8,128)(2,1)}, bf16[400,1408]{1,0:T(8,128)(2,1)S(1)}, u32[]{:S(2)}, u32[]{:S(2)}) %collective-permute-start.18) | collective-permute-done | bytes 1126432 | tf_op jit(solution)/shard_map/ppermute | solution.py:354
  126.0 3.1 collective-permute-done.21.refs_10_.refs_11_
  130.2 24.8 %middle.1 = (f32[128,1024]{1,0:T(8,128)}, f32[128,1024]{1,0:T(8,128)}, f32[128,1024]{1,0:T(8,128)}, bf16[2944,128]{1,0:T(8,128)(2,1)}, bf16[6016,128]{1,0:T(8,12...) custom-call(s32[3]{0:T(128)} %pad_add_fusion.place, bf16[8,128,128]{2,1,0:T(8,128)(2,1)} %get-tuple-element.203.x_ref, ...), custom_call_target="tpu_custom_call" | custom-call | flops 1 | bytes 1 | tf_op jit(solution)/shard_map/middle/pallas_call | solution.py:1131
  155.7 5.0 %attend_back.1 = (f32[8,128,128]{2,1,0:T(8,128)}, f32[8,128,128]{2,1,0:T(8,128)}, f32[8,128,128]{2,1,0:T(8,128)}, bf16[8,128,128]{2,1,0:T(8,128)(2,1)}) custom-call(s32[1]{0:T(128)} %bitcast.1.place, f32[128,1024]{1,0:T(8,128)} %get-tuple-element.219.ga_ref, bf16[8,128,128]{2,1,0:T(8,128)(2,1)} %get-tuple-element.200.k_ref, ...), custom_call_target="tpu_custom_call" | custom-call | flops 1 | bytes 1 | tf_op jit(solution)/shard_map/attend_back/pallas_call | solution.py:522
  160.7 15.5 %adjoint.1 = (f32[8,128,128]{2,1,0:T(8,128)}, f32[8,128,128]{2,1,0:T(8,128)}, f32[8,1,128]{2,1,0:T(1,128)}, bf16[4,144,128]{2,1,0:T(8,128)(2,1)}, bf16[4,144,128...) custom-call(s32[1]{0:T(128)} %bitcast.12.spot, s32[1]{0:T(128)} %bitcast.1.place, ...), custom_call_target="tpu_custom_call" | custom-call | flops 1 | bytes 1 | tf_op jit(solution)/shard_map/adjoint/pallas_call | solution.py:609
  178.1 4.4 %queries_back.1 = (bf16[144,1024]{1,0:T(8,128)(2,1)}, f32[4,1024]{1,0:T(4,128)}) custom-call(f32[128,4096]{1,0:T(8,128)} %weigh.3.oq.ok.ov.own_logit.own, bf16[128,4096]{1,0:T(8,128)(2,1)} %copy-done.1, bf16[8,3072]{1,0:T(8,128)(2,1)} %copy-done.18, f32[4,3072]{1,0:T(4,128)} %maximum_select_fusion.tq.tk.tv.t, f32[8,128,128]{2,1,0:T(8,128)} %get-tuple-element.231.dq_ref), custom_call_target="tpu_custom_call" | custom-call | flops 1 | bytes 1 | tf_op jit(solution)/shard_map/queries_back/pallas_call | solution.py:700
  183.1 2.3 collective-permute-done.24.refs_3_.refs_7_
  186.0 1.9 group.3.refs_0_
  188.0 1.7 collective-permute-start.26
  189.7 4.8 %collective-permute-done.26.refs_1_ = bf16[4,144,128]{2,1,0:T(8,128)(2,1)S(1)} collective-permute-done((bf16[4,144,128]{2,1,0:T(8,128)(2,1)}, bf16[4,144,128]{2,1,0:T(8,128)(2,1)S(1)}, u32[]{:S(2)}, u32[]{:S(2)}) %collective-permute-start.26) | collective-permute-done | bytes 147488 | tf_op jit(solution)/shard_map/ppermute | solution.py:354
  195.7 6.0 %products.3 = bf16[16,152,1024]{2,1,0:T(8,128)(2,1)} custom-call(s32[1]{0:T(128)} %bitcast.3.spot, bf16[2944,128]{1,0:T(8,128)(2,1)} %get-tuple-element.274.refs_0_.refs_4_.refs_8_.refs_6_.refs_12_, bf16[6016,128]{1,0:T(8,128)(2,1)} %copy-done, bf16[6016,128]{1,0:T(8,128)(2,1)} %get-tuple-element.242.refs_2_.refs_6_.refs_10_.logit1, ...), custom_call_target="tpu_custom_call" | custom-call | flops 1 | bytes 1 | tf_op jit(solution)/shard_map/products/pallas_call | solution.py:864
  204.4 2.7 collective-permute-start.27
  208.5 9.7 %collective-permute-done.27.refs_2_ = bf16[4,144,128]{2,1,0:T(8,128)(2,1)S(1)} collective-permute-done((bf16[4,144,128]{2,1,0:T(8,128)(2,1)S(1)}, bf16[4,144,128]{2,1,0:T(8,128)(2,1)S(1)}, u32[]{:S(2)}, u32[]{:S(2)}) %collective-permute-start.27) | collective-permute-done | bytes 147488 | tf_op jit(solution)/shard_map/ppermute | solution.py:354
  219.6 2.7 spread.3
  224.2 4.7 %collective-permute-done.30.r2 = bf16[4,128,128]{2,1,0:T(8,128)(2,1)S(1)} collective-permute-done((bf16[4,128,128]{2,1,0:T(8,128)(2,1)}, bf16[4,128,128]{2,1,0:T(8,128)(2,1)S(1)}, u32[]{:S(2)}, u32[]{:S(2)}) %collective-permute-start.30) | collective-permute-done | bytes 131104 | tf_op jit(solution)/shard_map/ppermute | solution.py:354
  228.8 1.9 collective-permute-done.31.r3
  231.5 6.2 %keys_values_back.1 = (bf16[144,1024]{1,0:T(8,128)(2,1)}, f32[4,1024]{1,0:T(4,128)}, bf16[144,1024]{1,0:T(8,128)(2,1)}, f32[4,1024]{1,0:T(4,128)}) custom-call(s32[1]{0:T(128)} %bitcast.12.spot, f32[128,4096]{1,0:T(8,128)} %weigh.3.oq.ok.ov.own_logit.own, bf16[128,4096]{1,0:T(8,128)(2,1)} %copy-done.1, bf16[8,3072]{1,0:T(8,128)(2,1)} %copy-done.18, ...), custom_call_target="tpu_custom_call" | custom-call | flops 1 | bytes 1 | tf_op jit(solution)/shard_map/keys_values_back/pallas_call | solution.py:744
  238.8 5.0 %products.4 = (bf16[8,32,5632]{2,1,0:T(8,128)(2,1)}, bf16[8,32,5632]{2,1,0:T(8,128)(2,1)}) custom-call(s32[1]{0:T(128)} %bitcast.3.spot, bf16[2944,128]{1,0:T(8,128)(2,1)} %get-tuple-element.274.refs_0_.refs_4_.refs_8_.refs_6_.refs_12_, bf16[6016,128]{1,0:T(8,128)(2,1)} %copy-done, bf16[128,5632]{1,0:T(8,128)(2,1)} %get-tuple-element.262.refs_2_, ...), custom_call_target="tpu_custom_call" | custom-call | flops 1 | bytes 1 | tf_op jit(solution)/shard_map/products/pallas_call | solution.py:864
  247.0 2.2 collective-permute-done.33.refs_4_.refs_10_.refs_16_.extra1
  249.1 1.9 collective-permute-done.34.refs_5_.refs_11_.refs_17_.extra2
  252.0 5.0 %halving.6 = (bf16[4,32,5632]{2,1,0:T(8,128)(2,1)}, bf16[4,32,5632]{2,1,0:T(8,128)(2,1)}) custom-call(s32[1]{0:T(128)} %bitcast.13.bit, bf16[8,32,5632]{2,1,0:T(8,128)(2,1)} %get-tuple-element.264.kept_mine.kept_other, bf16[8,32,5632]{2,1,0:T(8,128)(2,1)} %get-tuple-element.264.kept_mine.kept_other, ...), custom_call_target="tpu_custom_call" | custom-call | flops 1 | bytes 1 | tf_op jit(solution)/shard_map/halving/pallas_call | solution.py:957
  257.0 2.2 collective-permute-start.40
  259.2 12.8 %collective-permute-done.35.refs_3_.refs_9_.refs_15_.peer = bf16[432,1024]{1,0:T(8,128)(2,1)S(1)} collective-permute-done((bf16[432,1024]{1,0:T(8,128)(2,1)S(1)}, bf16[432,1024]{1,0:T(8,128)(2,1)S(1)}, u32[]{:S(2)}, u32[]{:S(2)}) %collective-permute-start.35) | collective-permute-done | bytes 884768 | tf_op jit(solution)/shard_map/ppermute | solution.py:354
  273.0 4.2 %products.5 = (bf16[8,96,1024]{2,1,0:T(8,128)(2,1)}, bf16[8,48,1024]{2,1,0:T(8,128)(2,1)}, bf16[8,48,1024]{2,1,0:T(8,128)(2,1)}) custom-call(s32[1]{0:T(128)} %bitcast.3.spot, bf16[2944,128]{1,0:T(8,128)(2,1)} %get-tuple-element.274.refs_0_.refs_4_.refs_8_.refs_6_.refs_12_, bf16[6016,128]{1,0:T(8,128)(2,1)} %copy-done, bf16[432,1024]{1,0:T(8,128)(2,1)} %copy-done.2, ...), custom_call_target="tpu_custom_call" | custom-call | flops 1 | bytes 1 | tf_op jit(solution)/shard_map/products/pallas_call | solution.py:864
  277.2 1.8 collective-permute-start.37
  279.0 2.1 collective-permute-done.37.refs_0_.refs_1_
  283.1 4.0 %halving.7 = (bf16[4,96,1024]{2,1,0:T(8,128)(2,1)}, bf16[4,96,1024]{2,1,0:T(8,128)(2,1)}) custom-call(s32[1]{0:T(128)} %bitcast.13.bit, bf16[8,96,1024]{2,1,0:T(8,128)(2,1)} %get-tuple-element.278.kept_mine.kept_other, bf16[8,96,1024]{2,1,0:T(8,128)(2,1)} %get-tuple-element.278.kept_mine.kept_other, bf16[8,48,1024]{2,1,0:T(8,128)(2,1)} %copy-done.9, ...), custom_call_target="tpu_custom_call" | custom-call | flops 1 | bytes 1 | tf_op jit(solution)/shard_map/halving/pallas_call | solution.py:957
  287.2 2.5 collective-permute-start.41
  289.7 5.6 %lent_rows.1 = (f32[128,512]{1,0:T(8,128)}, bf16[128,512]{1,0:T(8,128)(2,1)}) custom-call(bf16[432,1024]{1,0:T(8,128)(2,1)} %copy-done.2, bf16[432,1024]{1,0:T(8,128)(2,1)} %copy-done.3, bf16[8,3072]{1,0:T(8,128)(2,1)} %copy-done.26, bf16[8,3072]{1,0:T(8,128)(2,1)} %copy-done.27, bf16[6016,128]{1,0:T(8,128)(2,1)} %get-tuple-element.242.refs_2_.refs_6_.refs_10_.logit1, ...), custom_call_target="tpu_custom_call" | custom-call | flops 1 | bytes 1 | tf_op jit(solution)/shard_map/lent_rows/pallas_call | solution.py:896
  297.2 2.7 halving.8
  300.0 2.5 collective-permute-start.44
  303.2 2.5 norm_back.1
  309.6 2.3 halving.9
  311.9 6.8 %collective-permute-start.42 = (bf16[2,96,1024]{2,1,0:T(8,128)(2,1)}, bf16[2,96,1024]{2,1,0:T(8,128)(2,1)S(1)}, u32[]{:S(2)}, u32[]{:S(2)}) collective-permute-start(bf16[2,96,1024]{2,1,0:T(8,128)(2,1)} %get-tuple-element.301), channel_id=1, source_target_pairs={{0,8},{2,10},{4,12},{6,14},{8,0},{10,2},{12,4},{14,6},{16,24},{18,... | collective-permute-start | bytes 1179656 | tf_op jit(solution)/shard_map/ppermute | solution.py:354
  319.5 2.2 halving.10
  321.8 3.9 %collective-permute-start.46 = (bf16[1,32,5632]{2,1,0:T(8,128)(2,1)}, bf16[1,32,5632]{2,1,0:T(8,128)(2,1)S(1)}, u32[]{:S(2)}, u32[]{:S(2)}) collective-permute-start(bf16[1,32,5632]{2,1,0:T(8,128)(2,1)} %get-tuple-element.304), channel_id=1, source_target_pairs={{0,16},{2,18},{4,20},{6,22},{8,24},{10,26},{12,28},{14,30},{16,0},... | collective-permute-start | bytes 1081352 | tf_op jit(solution)/shard_map/ppermute | solution.py:354
  326.4 3.5 all-to-all-start
  330.6 2.7 collective-permute-done.42.refs_0_.refs_1_
  334.1 2.0 halving.11
  336.9 10.6 %all-to-all-done = f32[16,1,480]{2,1,0:T(1,128)S(1)} async-done(((f32[16,1,480]{2,1,0:T(1,128)}), f32[16,1,480]{2,1,0:T(1,128)S(1)}, u32[]{:S(2)}, u32[]{:S(2)}) %all-to-all-start) | async-done | bytes 30752 | tf_op jit(solution)/shard_map/all_to_all | solution.py:1463
  348.8 2.1 collective-permute-done.45
  (214 shorter events, 64.6 us)
Async XLA Ops:
  7.2 311.5 %reduce-scatter.2.cloned.1.call-start = ((), (), s32[]{:S(2)}) async-start(), calls=%async_computation.2 | async-start | bytes 5292032 | tf_op jit(solution)/shard_map/reduce_scatter | solution.py:1405
  7.9 11.6 %copy-start.50 = (bf16[1,512]{1,0:T(2,128)(2,1)}, bf16[1,512]{1,0:T(2,128)(2,1)S(1)}, u32[]{:S(2)}) copy-start(bf16[1,512]{1,0:T(2,128)(2,1)S(1)} %stack.31.gain_ref) | copy-start | bytes 3076
  12.5 7.0 %collective-permute-start = (bf16[144,512]{1,0:T(8,128)(2,1)}, bf16[144,512]{1,0:T(8,128)(2,1)S(1)}, u32[]{:S(2)}, u32[]{:S(2)}) collective-permute-start(bf16[144,512]{1,0:T(8,128)(2,1)} %get-tuple-element.162), channel_id=1, source_target_pairs={{0,1},{1,0},{2,3},{3,2},{4,5},{5,4},{6,7},{7,6},{8,9},{9,8},{10,11... | collective-permute-start | bytes 442376 | tf_op jit(solution)/shard_map/ppermute | solution.py:354
  24.9 26.3 %collective-permute-start.1 = (bf16[128,4096]{1,0:T(8,128)(2,1)}, bf16[128,4096]{1,0:T(8,128)(2,1)S(1)}, u32[]{:S(2)}, u32[]{:S(2)}) collective-permute-start(bf16[128,4096]{1,0:T(8,128)(2,1)} %weigh.2), channel_id=1, source_target_pairs={{0,1},{1,0},{2,3},{3,2},{4,5},{5,4},{6,7},{7,6},{8,9},{9,8},{10,11... | collective-permute-start | bytes 3145736 | tf_op jit(solution)/shard_map/ppermute | solution.py:354
  28.9 48.3 %collective-permute-start.12 = (bf16[1920,256]{1,0:T(8,128)(2,1)S(1)}, bf16[1920,256]{1,0:T(8,128)(2,1)S(1)}, u32[]{:S(2)}, u32[]{:S(2)}) collective-permute-start(bf16[1920,256]{1,0:T(8,128)(2,1)S(1)} %pad_maximum_fusion), channel_id=1, source_target_pairs={{0,1},{1,0},{2,3},{3,2},{4,5},{5,4},{6,7},{7,6},{8,9},{9,8},{10,11... | collective-permute-start | bytes 2949128 | tf_op jit(solution)/shard_map/ppermute | solution.py:354
  51.3 47.2 %collective-permute-start.14 = (bf16[400,1408]{1,0:T(8,128)(2,1)}, bf16[400,1408]{1,0:T(8,128)(2,1)}, u32[]{:S(2)}, u32[]{:S(2)}) collective-permute-start(bf16[400,1408]{1,0:T(8,128)(2,1)} %constant_dynamic-slice_fusion.2), channel_id=1, source_target_pairs={{0,1},{1,0},{2,3},{3,2},{4,5},{5,4},{6,7},{7,6},{8,9},{9,8},{10,11... | collective-permute-start | bytes 3379208 | tf_op jit(solution)/shard_map/ppermute | solution.py:354
  53.9 2.2 collective-permute-start.2
  62.2 5.0 %collective-permute-start.3 = (bf16[4,144,128]{2,1,0:T(8,128)(2,1)}, bf16[4,144,128]{2,1,0:T(8,128)(2,1)S(1)}, u32[]{:S(2)}, u32[]{:S(2)}) collective-permute-start(bf16[4,144,128]{2,1,0:T(8,128)(2,1)} %get-tuple-element.179), channel_id=1, source_target_pairs={{0,2},{2,0},{4,6},{6,4},{8,10},{10,8},{12,14},{14,12},{16,18},{18,... | collective-permute-start | bytes 442376 | tf_op jit(solution)/shard_map/ppermute | solution.py:354
  64.8 7.2 %collective-permute-start.4 = (bf16[4,144,128]{2,1,0:T(8,128)(2,1)}, bf16[4,144,128]{2,1,0:T(8,128)(2,1)S(1)}, u32[]{:S(2)}, u32[]{:S(2)}) collective-permute-start(bf16[4,144,128]{2,1,0:T(8,128)(2,1)} %get-tuple-element.180), channel_id=1, source_target_pairs={{0,4},{2,6},{4,0},{6,2},{8,12},{10,14},{12,8},{14,10},{16,20},{18,... | collective-permute-start | bytes 442376 | tf_op jit(solution)/shard_map/ppermute | solution.py:354
  67.1 7.5 %collective-permute-start.5 = (bf16[4,144,128]{2,1,0:T(8,128)(2,1)}, bf16[4,144,128]{2,1,0:T(8,128)(2,1)S(1)}, u32[]{:S(2)}, u32[]{:S(2)}) collective-permute-start(bf16[4,144,128]{2,1,0:T(8,128)(2,1)} %get-tuple-element.181), channel_id=1, source_target_pairs={{0,6},{2,4},{4,2},{6,0},{8,14},{10,12},{12,10},{14,8},{16,22},{18,... | collective-permute-start | bytes 442376 | tf_op jit(solution)/shard_map/ppermute | solution.py:354
  67.2 7.5 %copy-start.31 = (bf16[4,144,128]{2,1,0:T(8,128)(2,1)}, bf16[4,144,128]{2,1,0:T(8,128)(2,1)S(1)}, u32[]{:S(2)}) copy-start(bf16[4,144,128]{2,1,0:T(8,128)(2,1)S(1)} %collective-permute-done.3.refs_1_.refs_5_) | copy-start | bytes 442372
  77.2 41.3 %copy-start.5 = (bf16[1920,256]{1,0:T(8,128)(2,1)}, bf16[1920,256]{1,0:T(8,128)(2,1)S(1)}, u32[]{:S(2)}) copy-start(bf16[1920,256]{1,0:T(8,128)(2,1)S(1)} %collective-permute-done.12.out_a.refs_13_) | copy-start | bytes 2949124
  77.2 31.0 %collective-permute-start.13 = (bf16[1920,256]{1,0:T(8,128)(2,1)S(1)}, bf16[1920,256]{1,0:T(8,128)(2,1)S(1)}, u32[]{:S(2)}, u32[]{:S(2)}) collective-permute-start(bf16[1920,256]{1,0:T(8,128)(2,1)S(1)} %collective-permute-done.12.out_a.refs_13_), channel_id=1, source_target_pairs={{0,4},{2,6},{4,0},{6,2},{8,12},{10,14},{12,8},{14,10},{16,20},{18,... | collective-permute-start | bytes 2949128 | tf_op jit(solution)/shard_map/ppermute | solution.py:354
  78.8 9.1 %collective-permute-start.6 = (bf16[4,144,128]{2,1,0:T(8,128)(2,1)}, bf16[4,144,128]{2,1,0:T(8,128)(2,1)S(1)}, u32[]{:S(2)}, u32[]{:S(2)}) collective-permute-start(bf16[4,144,128]{2,1,0:T(8,128)(2,1)} %group.2.refs_0_), channel_id=1, source_target_pairs={{0,8},{2,10},{4,12},{6,14},{8,0},{10,2},{12,4},{14,6},{16,24},{18,... | collective-permute-start | bytes 442376 | tf_op jit(solution)/shard_map/ppermute | solution.py:354
  80.3 14.2 %collective-permute-start.7 = (bf16[4,144,128]{2,1,0:T(8,128)(2,1)}, bf16[4,144,128]{2,1,0:T(8,128)(2,1)S(1)}, u32[]{:S(2)}, u32[]{:S(2)}) collective-permute-start(bf16[4,144,128]{2,1,0:T(8,128)(2,1)} %group.2.refs_0_), channel_id=1, source_target_pairs={{0,16},{2,18},{4,20},{6,22},{8,24},{10,26},{12,28},{14,30},{16,0},... | collective-permute-start | bytes 442376 | tf_op jit(solution)/shard_map/ppermute | solution.py:354
  82.9 11.6 %collective-permute-start.8 = (bf16[4,144,128]{2,1,0:T(8,128)(2,1)}, bf16[4,144,128]{2,1,0:T(8,128)(2,1)S(1)}, u32[]{:S(2)}, u32[]{:S(2)}) collective-permute-start(bf16[4,144,128]{2,1,0:T(8,128)(2,1)} %group.2.refs_0_), channel_id=1, source_target_pairs={{0,24},{2,26},{4,28},{6,30},{8,16},{10,18},{12,20},{14,22},{16,8},... | collective-permute-start | bytes 442376 | tf_op jit(solution)/shard_map/ppermute | solution.py:354
  87.9 6.7 %copy-start.41 = (bf16[4,144,128]{2,1,0:T(8,128)(2,1)}, bf16[4,144,128]{2,1,0:T(8,128)(2,1)S(1)}, u32[]{:S(2)}) copy-start(bf16[4,144,128]{2,1,0:T(8,128)(2,1)S(1)} %collective-permute-done.6.refs_1_) | copy-start | bytes 442372
  98.5 26.9 %collective-permute-start.18 = (bf16[400,1408]{1,0:T(8,128)(2,1)}, bf16[400,1408]{1,0:T(8,128)(2,1)S(1)}, u32[]{:S(2)}, u32[]{:S(2)}) collective-permute-start(bf16[400,1408]{1,0:T(8,128)(2,1)} %collective-permute-done.14.refs_4_), channel_id=1, source_target_pairs={{0,8},{2,10},{4,12},{6,14},{8,0},{10,2},{12,4},{14,6},{16,24},{18,... | collective-permute-start | bytes 3379208 | tf_op jit(solution)/shard_map/ppermute | solution.py:354
  100.8 5.7 %collective-permute-start.10 = (bf16[4,128,128]{2,1,0:T(8,128)(2,1)}, bf16[4,128,128]{2,1,0:T(8,128)(2,1)S(1)}, u32[]{:S(2)}, u32[]{:S(2)}) collective-permute-start(bf16[4,128,128]{2,1,0:T(8,128)(2,1)} %get-tuple-element.192), channel_id=1, source_target_pairs={{0,4},{2,6},{4,0},{6,2},{8,12},{10,14},{12,8},{14,10},{16,20},{18,... | collective-permute-start | bytes 393224 | tf_op jit(solution)/shard_map/ppermute | solution.py:354
  102.2 6.0 %collective-permute-start.11 = (bf16[4,128,128]{2,1,0:T(8,128)(2,1)}, bf16[4,128,128]{2,1,0:T(8,128)(2,1)S(1)}, u32[]{:S(2)}, u32[]{:S(2)}) collective-permute-start(bf16[4,128,128]{2,1,0:T(8,128)(2,1)} %get-tuple-element.193), channel_id=1, source_target_pairs={{0,6},{2,4},{4,2},{6,0},{8,14},{10,12},{12,10},{14,8},{16,22},{18,... | collective-permute-start | bytes 393224 | tf_op jit(solution)/shard_map/ppermute | solution.py:354
  102.2 6.0 %collective-permute-start.9 = (bf16[4,128,128]{2,1,0:T(8,128)(2,1)}, bf16[4,128,128]{2,1,0:T(8,128)(2,1)S(1)}, u32[]{:S(2)}, u32[]{:S(2)}) collective-permute-start(bf16[4,128,128]{2,1,0:T(8,128)(2,1)} %get-tuple-element.191), channel_id=1, source_target_pairs={{0,2},{2,0},{4,6},{6,4},{8,10},{10,8},{12,14},{14,12},{16,18},{18,... | collective-permute-start | bytes 393224 | tf_op jit(solution)/shard_map/ppermute | solution.py:354
  108.2 21.8 %copy-start.6 = (bf16[1920,256]{1,0:T(8,128)(2,1)}, bf16[1920,256]{1,0:T(8,128)(2,1)S(1)}, u32[]{:S(2)}) copy-start(bf16[1920,256]{1,0:T(8,128)(2,1)S(1)} %collective-permute-done.13.out_b.refs_14_) | copy-start | bytes 2949124
  108.2 17.6 %collective-permute-start.16 = (bf16[1920,256]{1,0:T(8,128)(2,1)S(1)}, bf16[1920,256]{1,0:T(8,128)(2,1)S(1)}, u32[]{:S(2)}, u32[]{:S(2)}) collective-permute-start(bf16[1920,256]{1,0:T(8,128)(2,1)S(1)} %collective-permute-done.12.out_a.refs_13_), channel_id=1, source_target_pairs={{0,2},{2,0},{4,6},{6,4},{8,10},{10,8},{12,14},{14,12},{16,18},{18,... | collective-permute-start | bytes 2949128 | tf_op jit(solution)/shard_map/ppermute | solution.py:354
  109.0 16.9 %collective-permute-start.17 = (bf16[1920,256]{1,0:T(8,128)(2,1)S(1)}, bf16[1920,256]{1,0:T(8,128)(2,1)S(1)}, u32[]{:S(2)}, u32[]{:S(2)}) collective-permute-start(bf16[1920,256]{1,0:T(8,128)(2,1)S(1)} %collective-permute-done.13.out_b.refs_14_), channel_id=1, source_target_pairs={{0,2},{2,0},{4,6},{6,4},{8,10},{10,8},{12,14},{14,12},{16,18},{18,... | collective-permute-start | bytes 2949128 | tf_op jit(solution)/shard_map/ppermute | solution.py:354
  109.1 16.8 %collective-permute-start.15 = (bf16[112,2816]{1,0:T(8,128)(2,1)}, bf16[112,2816]{1,0:T(8,128)(2,1)S(1)}, u32[]{:S(2)}, u32[]{:S(2)}) collective-permute-start(bf16[112,2816]{1,0:T(8,128)(2,1)} %constant_dynamic-slice_fusion.5), channel_id=1, source_target_pairs={{0,1},{1,0},{2,3},{3,2},{4,5},{5,4},{6,7},{7,6},{8,9},{9,8},{10,11... | collective-permute-start | bytes 1892360 | tf_op jit(solution)/shard_map/ppermute | solution.py:354
  118.5 7.4 %collective-permute-start.19 = (bf16[400,1408]{1,0:T(8,128)(2,1)}, bf16[400,1408]{1,0:T(8,128)(2,1)S(1)}, u32[]{:S(2)}, u32[]{:S(2)}) collective-permute-start(bf16[400,1408]{1,0:T(8,128)(2,1)} %collective-permute-done.14.refs_4_), channel_id=1, source_target_pairs={{0,2},{2,0},{4,6},{6,4},{8,10},{10,8},{12,14},{14,12},{16,18},{18,... | collective-permute-start | bytes 3379208 | tf_op jit(solution)/shard_map/ppermute | solution.py:354
  125.3 3.7 %collective-permute-start.20 = (bf16[400,1408]{1,0:T(8,128)(2,1)S(1)}, bf16[400,1408]{1,0:T(8,128)(2,1)S(1)}, u32[]{:S(2)}, u32[]{:S(2)}) collective-permute-start(bf16[400,1408]{1,0:T(8,128)(2,1)S(1)} %collective-permute-done.18.refs_5_), channel_id=1, source_target_pairs={{0,2},{2,0},{4,6},{6,4},{8,10},{10,8},{12,14},{14,12},{16,18},{18,... | collective-permute-start | bytes 3379208 | tf_op jit(solution)/shard_map/ppermute | solution.py:354
  125.9 3.2 collective-permute-start.21
  155.0 39.5 %collective-permute-start.25 = (bf16[6016,128]{1,0:T(8,128)(2,1)}, bf16[6016,128]{1,0:T(8,128)(2,1)S(1)}, u32[]{:S(2)}, u32[]{:S(2)}) collective-permute-start(bf16[6016,128]{1,0:T(8,128)(2,1)} %get-tuple-element.242.refs_2_.refs_6_.refs_10_.logit1), channel_id=1, source_target_pairs={{0,1},{1,0},{2,3},{3,2},{4,5},{5,4},{6,7},{7,6},{8,9},{9,8},{10,11... | collective-permute-start | bytes 4620296 | tf_op jit(solution)/shard_map/ppermute | solution.py:354
  176.1 1.9 collective-permute-start.22
  176.2 6.9 %collective-permute-start.23 = (bf16[4,144,128]{2,1,0:T(8,128)(2,1)}, bf16[4,144,128]{2,1,0:T(8,128)(2,1)S(1)}, u32[]{:S(2)}, u32[]{:S(2)}) collective-permute-start(bf16[4,144,128]{2,1,0:T(8,128)(2,1)} %get-tuple-element.229), channel_id=1, source_target_pairs={{0,4},{2,6},{4,0},{6,2},{8,12},{10,14},{12,8},{14,10},{16,20},{18,... | collective-permute-start | bytes 442376 | tf_op jit(solution)/shard_map/ppermute | solution.py:354
  177.7 7.7 %collective-permute-start.24 = (bf16[4,144,128]{2,1,0:T(8,128)(2,1)}, bf16[4,144,128]{2,1,0:T(8,128)(2,1)S(1)}, u32[]{:S(2)}, u32[]{:S(2)}) collective-permute-start(bf16[4,144,128]{2,1,0:T(8,128)(2,1)} %get-tuple-element.230), channel_id=1, source_target_pairs={{0,6},{2,4},{4,2},{6,0},{8,14},{10,12},{12,10},{14,8},{16,22},{18,... | collective-permute-start | bytes 442376 | tf_op jit(solution)/shard_map/ppermute | solution.py:354
  188.0 6.5 %collective-permute-start.26 = (bf16[4,144,128]{2,1,0:T(8,128)(2,1)}, bf16[4,144,128]{2,1,0:T(8,128)(2,1)S(1)}, u32[]{:S(2)}, u32[]{:S(2)}) collective-permute-start(bf16[4,144,128]{2,1,0:T(8,128)(2,1)} %group.3.refs_0_), channel_id=1, source_target_pairs={{0,8},{2,10},{4,12},{6,14},{8,0},{10,2},{12,4},{14,6},{16,24},{18,... | collective-permute-start | bytes 442376 | tf_op jit(solution)/shard_map/ppermute | solution.py:354
  194.5 7.1 %copy-start.40 = (bf16[4,144,128]{2,1,0:T(8,128)(2,1)}, bf16[4,144,128]{2,1,0:T(8,128)(2,1)S(1)}, u32[]{:S(2)}) copy-start(bf16[4,144,128]{2,1,0:T(8,128)(2,1)S(1)} %collective-permute-done.26.refs_1_) | copy-start | bytes 442372
  203.0 34.6 %collective-permute-start.32 = (bf16[128,5632]{1,0:T(8,128)(2,1)S(1)}, bf16[128,5632]{1,0:T(8,128)(2,1)S(1)}, u32[]{:S(2)}, u32[]{:S(2)}) collective-permute-start(bf16[128,5632]{1,0:T(8,128)(2,1)S(1)} %copy-done.20), channel_id=1, source_target_pairs={{0,1},{1,0},{2,3},{3,2},{4,5},{5,4},{6,7},{7,6},{8,9},{9,8},{10,11... | collective-permute-start | bytes 4325384 | tf_op jit(solution)/shard_map/ppermute | solution.py:354
  204.4 13.8 %collective-permute-start.27 = (bf16[4,144,128]{2,1,0:T(8,128)(2,1)S(1)}, bf16[4,144,128]{2,1,0:T(8,128)(2,1)S(1)}, u32[]{:S(2)}, u32[]{:S(2)}) collective-permute-start(bf16[4,144,128]{2,1,0:T(8,128)(2,1)S(1)} %copy-done.34), channel_id=1, source_target_pairs={{0,16},{2,18},{4,20},{6,22},{8,24},{10,26},{12,28},{14,30},{16,0},... | collective-permute-start | bytes 442376 | tf_op jit(solution)/shard_map/ppermute | solution.py:354
  207.2 11.1 %collective-permute-start.28 = (bf16[4,144,128]{2,1,0:T(8,128)(2,1)S(1)}, bf16[4,144,128]{2,1,0:T(8,128)(2,1)S(1)}, u32[]{:S(2)}, u32[]{:S(2)}) collective-permute-start(bf16[4,144,128]{2,1,0:T(8,128)(2,1)S(1)} %copy-done.34), channel_id=1, source_target_pairs={{0,24},{2,26},{4,28},{6,30},{8,16},{10,18},{12,20},{14,22},{16,8},... | collective-permute-start | bytes 442376 | tf_op jit(solution)/shard_map/ppermute | solution.py:354
  222.3 1.9 collective-permute-start.29
  222.3 6.6 %collective-permute-start.30 = (bf16[4,128,128]{2,1,0:T(8,128)(2,1)}, bf16[4,128,128]{2,1,0:T(8,128)(2,1)S(1)}, u32[]{:S(2)}, u32[]{:S(2)}) collective-permute-start(bf16[4,128,128]{2,1,0:T(8,128)(2,1)} %get-tuple-element.252), channel_id=1, source_target_pairs={{0,4},{2,6},{4,0},{6,2},{8,12},{10,14},{12,8},{14,10},{16,20},{18,... | collective-permute-start | bytes 393224 | tf_op jit(solution)/shard_map/ppermute | solution.py:354
  223.8 7.0 %collective-permute-start.31 = (bf16[4,128,128]{2,1,0:T(8,128)(2,1)}, bf16[4,128,128]{2,1,0:T(8,128)(2,1)S(1)}, u32[]{:S(2)}, u32[]{:S(2)}) collective-permute-start(bf16[4,128,128]{2,1,0:T(8,128)(2,1)} %get-tuple-element.253), channel_id=1, source_target_pairs={{0,6},{2,4},{4,2},{6,0},{8,14},{10,12},{12,10},{14,8},{16,22},{18,... | collective-permute-start | bytes 393224 | tf_op jit(solution)/shard_map/ppermute | solution.py:354
  224.2 6.6 %copy-start.46 = (bf16[4,128,128]{2,1,0:T(8,128)(2,1)}, bf16[4,128,128]{2,1,0:T(8,128)(2,1)S(1)}, u32[]{:S(2)}) copy-start(bf16[4,128,128]{2,1,0:T(8,128)(2,1)S(1)} %collective-permute-done.29.r1) | copy-start | bytes 393220
  238.8 5.4 %copy-start.36 = (bf16[144,1024]{1,0:T(8,128)(2,1)S(1)}, bf16[144,1024]{1,0:T(8,128)(2,1)}, u32[]{:S(2)}) copy-start(bf16[144,1024]{1,0:T(8,128)(2,1)} %get-tuple-element.265) | copy-start | bytes 884740
  238.8 5.4 %copy-start.37 = (bf16[144,1024]{1,0:T(8,128)(2,1)S(1)}, bf16[144,1024]{1,0:T(8,128)(2,1)}, u32[]{:S(2)}) copy-start(bf16[144,1024]{1,0:T(8,128)(2,1)} %get-tuple-element.266) | copy-start | bytes 884740
  238.8 5.4 %copy-start.38 = (bf16[144,1024]{1,0:T(8,128)(2,1)S(1)}, bf16[144,1024]{1,0:T(8,128)(2,1)}, u32[]{:S(2)}) copy-start(bf16[144,1024]{1,0:T(8,128)(2,1)} %get-tuple-element.267) | copy-start | bytes 884740
  243.8 8.2 %collective-permute-start.36 = (bf16[8,32,5632]{2,1,0:T(8,128)(2,1)}, bf16[8,32,5632]{2,1,0:T(8,128)(2,1)}, u32[]{:S(2)}, u32[]{:S(2)}) collective-permute-start(bf16[8,32,5632]{2,1,0:T(8,128)(2,1)} %get-tuple-element.269), channel_id=1, source_target_pairs={{0,2},{2,0},{4,6},{6,4},{8,10},{10,8},{12,14},{14,12},{16,18},{18,... | collective-permute-start | bytes 8650760 | tf_op jit(solution)/shard_map/ppermute | solution.py:354
  244.3 4.9 %collective-permute-start.33 = (bf16[8,3072]{1,0:T(8,128)(2,1)S(1)}, bf16[8,3072]{1,0:T(8,128)(2,1)S(1)}, u32[]{:S(2)}, u32[]{:S(2)}) collective-permute-start(bf16[8,3072]{1,0:T(8,128)(2,1)S(1)} %pad_maximum_fusion.3), channel_id=1, source_target_pairs={{2,0},{4,2},{6,4},{8,6},{10,8},{12,10},{14,12},{16,14},{18,16},{20... | collective-permute-start | bytes 147464 | tf_op jit(solution)/shard_map/ppermute | solution.py:1177
  245.6 5.4 %collective-permute-start.34 = (bf16[8,3072]{1,0:T(8,128)(2,1)S(1)}, bf16[8,3072]{1,0:T(8,128)(2,1)S(1)}, u32[]{:S(2)}, u32[]{:S(2)}) collective-permute-start(bf16[8,3072]{1,0:T(8,128)(2,1)S(1)} %pad_maximum_fusion.3), channel_id=1, source_target_pairs={{2,1},{3,0},{4,3},{5,2},{6,5},{7,4},{8,7},{9,6},{10,9},{11,8},{12,... | collective-permute-start | bytes 147464 | tf_op jit(solution)/shard_map/ppermute | solution.py:1182
  247.0 10.1 %copy-start.2 = (bf16[432,1024]{1,0:T(8,128)(2,1)}, bf16[432,1024]{1,0:T(8,128)(2,1)S(1)}, u32[]{:S(2)}) copy-start(bf16[432,1024]{1,0:T(8,128)(2,1)S(1)} %pad_maximum_fusion.1.refs_2_.refs_8_.refs_14_.own) | copy-start | bytes 2654212
  249.1 7.9 %copy-start.26 = (bf16[8,3072]{1,0:T(8,128)(2,1)}, bf16[8,3072]{1,0:T(8,128)(2,1)S(1)}, u32[]{:S(2)}) copy-start(bf16[8,3072]{1,0:T(8,128)(2,1)S(1)} %collective-permute-done.33.refs_4_.refs_10_.refs_16_.extra1) | copy-start | bytes 147460
  251.0 6.0 %copy-start.27 = (bf16[8,3072]{1,0:T(8,128)(2,1)}, bf16[8,3072]{1,0:T(8,128)(2,1)S(1)}, u32[]{:S(2)}) copy-start(bf16[8,3072]{1,0:T(8,128)(2,1)S(1)} %collective-permute-done.34.refs_5_.refs_11_.refs_17_.extra2) | copy-start | bytes 147460
  251.0 21.0 %collective-permute-start.35 = (bf16[432,1024]{1,0:T(8,128)(2,1)S(1)}, bf16[432,1024]{1,0:T(8,128)(2,1)S(1)}, u32[]{:S(2)}, u32[]{:S(2)}) collective-permute-start(bf16[432,1024]{1,0:T(8,128)(2,1)S(1)} %pad_maximum_fusion.1.refs_2_.refs_8_.refs_14_.own), channel_id=1, source_target_pairs={{0,1},{1,0},{2,3},{3,2},{4,5},{5,4},{6,7},{7,6},{8,9},{9,8},{10,11... | collective-permute-start | bytes 2654216 | tf_op jit(solution)/shard_map/ppermute | solution.py:354
  257.0 39.1 %collective-permute-start.40 = (bf16[4,32,5632]{2,1,0:T(8,128)(2,1)}, bf16[4,32,5632]{2,1,0:T(8,128)(2,1)S(1)}, u32[]{:S(2)}, u32[]{:S(2)}) collective-permute-start(bf16[4,32,5632]{2,1,0:T(8,128)(2,1)} %get-tuple-element.273), channel_id=1, source_target_pairs={{0,4},{2,6},{4,0},{6,2},{8,12},{10,14},{12,8},{14,10},{16,20},{18,... | collective-permute-start | bytes 4325384 | tf_op jit(solution)/shard_map/ppermute | solution.py:354
  277.2 3.9 %collective-permute-start.37 = (bf16[8,48,1024]{2,1,0:T(8,128)(2,1)}, bf16[8,48,1024]{2,1,0:T(8,128)(2,1)S(1)}, u32[]{:S(2)}, u32[]{:S(2)}) collective-permute-start(bf16[8,48,1024]{2,1,0:T(8,128)(2,1)} %get-tuple-element.279), channel_id=1, source_target_pairs={{0,2},{2,0},{4,6},{6,4},{8,10},{10,8},{12,14},{14,12},{16,18},{18,... | collective-permute-start | bytes 2359304 | tf_op jit(solution)/shard_map/ppermute | solution.py:354
  279.0 3.2 collective-permute-start.38
  287.2 21.6 %collective-permute-start.41 = (bf16[4,96,1024]{2,1,0:T(8,128)(2,1)}, bf16[4,96,1024]{2,1,0:T(8,128)(2,1)S(1)}, u32[]{:S(2)}, u32[]{:S(2)}) collective-permute-start(bf16[4,96,1024]{2,1,0:T(8,128)(2,1)} %get-tuple-element.283), channel_id=1, source_target_pairs={{0,4},{2,6},{4,0},{6,2},{8,12},{10,14},{12,8},{14,10},{16,20},{18,... | collective-permute-start | bytes 2359304 | tf_op jit(solution)/shard_map/ppermute | solution.py:354
  295.3 7.2 %collective-permute-start.39 = (bf16[128,512]{1,0:T(8,128)(2,1)}, bf16[128,512]{1,0:T(8,128)(2,1)S(1)}, u32[]{:S(2)}, u32[]{:S(2)}) collective-permute-start(bf16[128,512]{1,0:T(8,128)(2,1)} %get-tuple-element.286), channel_id=1, source_target_pairs={{0,1},{1,0},{2,3},{3,2},{4,5},{5,4},{6,7},{7,6},{8,9},{9,8},{10,11... | collective-permute-start | bytes 393224 | tf_op jit(solution)/shard_map/ppermute | solution.py:354
  300.0 18.7 %collective-permute-start.44 = (bf16[2,32,5632]{2,1,0:T(8,128)(2,1)}, bf16[2,32,5632]{2,1,0:T(8,128)(2,1)S(1)}, u32[]{:S(2)}, u32[]{:S(2)}) collective-permute-start(bf16[2,32,5632]{2,1,0:T(8,128)(2,1)} %get-tuple-element.289), channel_id=1, source_target_pairs={{0,8},{2,10},{4,12},{6,14},{8,0},{10,2},{12,4},{14,6},{16,24},{18,... | collective-permute-start | bytes 2162696 | tf_op jit(solution)/shard_map/ppermute | solution.py:354
  311.9 21.4 %collective-permute-start.42 = (bf16[2,96,1024]{2,1,0:T(8,128)(2,1)}, bf16[2,96,1024]{2,1,0:T(8,128)(2,1)S(1)}, u32[]{:S(2)}, u32[]{:S(2)}) collective-permute-start(bf16[2,96,1024]{2,1,0:T(8,128)(2,1)} %get-tuple-element.301), channel_id=1, source_target_pairs={{0,8},{2,10},{4,12},{6,14},{8,0},{10,2},{12,4},{14,6},{16,24},{18,... | collective-permute-start | bytes 1179656 | tf_op jit(solution)/shard_map/ppermute | solution.py:354
  318.7 7.0 %collective-permute-start.43 = (f32[16,480]{1,0:T(8,128)S(1)}, f32[16,480]{1,0:T(8,128)S(1)}, u32[]{:S(2)}, u32[]{:S(2)}) collective-permute-start(f32[16,480]{1,0:T(8,128)S(1)} %bitcast.57), channel_id=1, source_target_pairs={{0,1},{1,0},{2,3},{3,2},{4,5},{5,4},{6,7},{7,6},{8,9},{9,8},{10,11... | collective-permute-start | bytes 92168 | tf_op jit(solution)/shard_map/ppermute | solution.py:354
  318.7 11.1 %copy-start.22 = (bf16[152,1024]{1,0:T(8,128)(2,1)S(1)}, bf16[152,1024]{1,0:T(8,128)(2,1)}, u32[]{:S(2)}) copy-start(bf16[152,1024]{1,0:T(8,128)(2,1)} %reduce-scatter.2.cloned.1.call-done) | copy-start | bytes 933892
  321.8 31.0 %collective-permute-start.46 = (bf16[1,32,5632]{2,1,0:T(8,128)(2,1)}, bf16[1,32,5632]{2,1,0:T(8,128)(2,1)S(1)}, u32[]{:S(2)}, u32[]{:S(2)}) collective-permute-start(bf16[1,32,5632]{2,1,0:T(8,128)(2,1)} %get-tuple-element.304), channel_id=1, source_target_pairs={{0,16},{2,18},{4,20},{6,22},{8,24},{10,26},{12,28},{14,30},{16,0},... | collective-permute-start | bytes 1081352 | tf_op jit(solution)/shard_map/ppermute | solution.py:354
  326.4 21.2 %all-to-all-start = ((f32[16,1,480]{2,1,0:T(1,128)}), f32[16,1,480]{2,1,0:T(1,128)S(1)}, u32[]{:S(2)}, u32[]{:S(2)}) async-start(f32[16,1,480]{2,1,0:T(1,128)} %all_to_all.8), calls=%async_computation.1 | async-start | bytes 65536 | tf_op jit(solution)/shard_map/all_to_all | solution.py:1463
  336.1 16.7 %copy-start.35 = (bf16[1,32,5632]{2,1,0:T(8,128)(2,1)S(1)}, bf16[1,32,5632]{2,1,0:T(8,128)(2,1)}, u32[]{:S(2)}) copy-start(bf16[1,32,5632]{2,1,0:T(8,128)(2,1)} %get-tuple-element.311) | copy-start | bytes 1081348
  336.9 14.1 %collective-permute-start.45 = (bf16[1,96,1024]{2,1,0:T(8,128)(2,1)}, bf16[1,96,1024]{2,1,0:T(8,128)(2,1)S(1)}, u32[]{:S(2)}, u32[]{:S(2)}) collective-permute-start(bf16[1,96,1024]{2,1,0:T(8,128)(2,1)} %get-tuple-element.309), channel_id=1, source_target_pairs={{0,16},{2,18},{4,20},{6,22},{8,24},{10,26},{12,28},{14,30},{16,0},... | collective-permute-start | bytes 589832 | tf_op jit(solution)/shard_map/ppermute | solution.py:354
  (36 other events, 65.3 us)
Sparse Core Ops, SparseCore 0:
  201.8 81.5 reduce-scatter.1
